TPU v7x, 32 devices: a whole 2x2x4 slice. The times are simulated.
32 devices in a mesh: dp: 16 (over z, x, core), mp: 2 (over y).
Axes of the slice: x: 2, y: 2, z: 4, core: 2. Of those that a mesh axis runs over, the one named last changes fastest.
Arguments:
- acc_grads: bfloat16 [16, 2, 128, 49152], P('dp', None, None, 'mp'), may hold values from -6 to 6
- activations: bfloat16 [2048, 2, 128], P('dp')
- cotangent: bfloat16 [2048, 2, 49152], P('dp', None, 'mp')
- params: float32 [2, 128, 49152], P(None, 'dp', 'mp'), may hold values from -6 to 6
- first_moment: float32 [2, 128, 49152], P(None, 'dp', 'mp'), may hold values from -4 to 4
- second_moment: float32 [2, 128, 49152], P(None, 'dp', 'mp'), may hold values from 0.25 to 1
- step: int32 [1], replicated, may hold values from 1 to 16
Outputs:
- new_params: float32 [2, 128, 49152], P(None, 'dp', 'mp')
- new_first: float32 [2, 128, 49152], P(None, 'dp', 'mp')
- new_second: float32 [2, 128, 49152], P(None, 'dp', 'mp')
- copy_params: float32 [2, 128, 49152], P(None, 'dp', 'mp')
- copy_first: float32 [2, 128, 49152], P(None, 'dp', 'mp')
- copy_second: float32 [2, 128, 49152], P(None, 'dp', 'mp')
All inputs are finite; a program needn't handle non-finite values.
Results may differ from a plain program's by a relative error of at most 0.0014.
Values sent between devices are 32-bit elements; how exact they have to be, the bound alone decides.
No kernel may reach another device: no remote copies, remote signals or barrier semaphores. Data moves between devices by JAX's collectives and lax.ppermute only.
A program may use at most 128 MiB of HBM per device.

v0:
```python
import jax
import jax.numpy as jnp
from jax import lax
from jax.sharding import PartitionSpec as P

HID = 49152


beta_one = 0.9
beta_two = 0.95
learn_rate = 0.1
decay_rate = 0.1
epsilon = 1e-08


def passed_along(value, axis, by):
    peers = lax.axis_size(axis)
    return lax.ppermute(value, axis, [(i, (i + by) % peers) for i in range(peers)])


def adamw_update(weights, first, second, grad, factor, count):
    scaled = factor * grad
    first_new = beta_one * first + (1.0 - beta_one) * scaled
    second_new = beta_two * second + (1.0 - beta_two) * scaled * scaled
    first_hat = first_new / (1.0 - jnp.power(jnp.float32(beta_one), count))
    second_hat = second_new / (1.0 - jnp.power(jnp.float32(beta_two), count))
    weights_new = weights - learn_rate * (
        first_hat / (jnp.sqrt(second_hat) + epsilon) + decay_rate * weights
    )
    return (weights_new, first_new, second_new)


def local_term(earlier, inputs, outgrad):
    product = jnp.einsum("tr,tc->rc", inputs, outgrad, preferred_element_type=jnp.float32)
    rounded = lax.optimization_barrier((earlier.astype(jnp.float32) + product).astype(jnp.bfloat16))
    return rounded.astype(jnp.float32)


def local(acc_grads, activations, cotangent, params, first_moment, second_moment, step):
    earlier = acc_grads[0]
    layer_count = earlier.shape[0]
    row_count = earlier.shape[1]
    old_copy = passed_along((params, first_moment, second_moment), "dp", 1)
    terms = jnp.stack(
        [
            local_term(earlier[layer], activations[:, layer, :], cotangent[:, layer, :])
            for layer in range(layer_count)
        ],
        axis=0,
    )
    grad = lax.psum_scatter(terms, "dp", scatter_dimension=1, tiled=True)
    squares = lax.psum(jnp.sum(grad * grad), ("dp", "mp"))
    bound = jnp.sqrt(jnp.float32(layer_count * row_count * HID))
    factor = jnp.minimum(jnp.float32(1.0), bound / (jnp.sqrt(squares) + 1e-06))
    count = step[0].astype(jnp.float32)
    new_params, new_first, new_second = adamw_update(
        params, first_moment, second_moment, grad, factor, count
    )
    peer_grad = passed_along(grad, "dp", 1)
    copy_params, copy_first, copy_second = adamw_update(
        old_copy[0], old_copy[1], old_copy[2], peer_grad, factor, count
    )
    return (new_params, new_first, new_second, copy_params, copy_first, copy_second)


def solution(mesh):
    placed = (
        P("dp", None, None, "mp"),
        P("dp", None, None),
        P("dp", None, "mp"),
        P(None, "dp", "mp"),
        P(None, "dp", "mp"),
        P(None, "dp", "mp"),
        P(),
    )
    return jax.shard_map(
        local,
        mesh=mesh,
        in_specs=placed,
        out_specs=(
            P(None, "dp", "mp"),
            P(None, "dp", "mp"),
            P(None, "dp", "mp"),
            P(None, "dp", "mp"),
            P(None, "dp", "mp"),
            P(None, "dp", "mp"),
        ),
        check_vma=False,
    )
```

profile of v0, /device:TPU:0, one launch (start us, length us, event | category | flops | bytes accessed | tf_op | source)
XLA Modules:
  0.0 421.6 jit_solution(1744839833261156684)
XLA Ops:
  7.2 0.0 copy-start.2
  7.2 0.0 reduce-scatter.2.cloned.1.call-start
  7.2 38.4 %fusion.6 = (bf16[128,1,24576]{2,1,0:T(2,128)(2,1)}, bf16[128,1,24576]{2,1,0:T(2,128)(2,1)S(1)}) fusion(bf16[128,2,24576]{2,1,0:T(2,128)(2,1)} %param.9), kind=kLoop, calls=%fused_computation.18 | loop fusion | bytes 25165824 | tf_op jit(solution)/shard_map/slice | solution.py:46
  45.6 0.0 copy-done.2
  45.6 0.1 fusion.7
  45.7 17.3 %fusion = bf16[128,24576]{1,0:T(8,128)(2,1)} fusion(bf16[128,1,24576]{2,1,0:T(2,128)(2,1)} %get-tuple-element.12, bf16[1,2,128,24576]{3,2,1,0:T(8,128)(2,1)} %param.7, bf16[128,1,128]{2,1,0:T(2,128)(2,1)S(1)} %get-tuple-element.14), kind=kOutput, calls=%fused_computation.2 | convolution fusion | flops 814743552 | bytes 18907136 | tf_op jit(solution)/shard_map/tr,tc->rc/dot_general | solution.py:34
  63.0 11.9 %fusion.1 = bf16[128,24576]{1,0:T(8,128)(2,1)} fusion(bf16[128,1,24576]{2,1,0:T(2,128)(2,1)S(1)} %get-tuple-element.13, bf16[1,2,128,24576]{3,2,1,0:T(8,128)(2,1)} %param.7, bf16[128,1,128]{2,1,0:T(2,128)(2,1)S(1)} %get-tuple-element.15), kind=kOutput, calls=%fused_computation.3 | convolution fusion | flops 814743552 | bytes 18907136 | tf_op jit(solution)/shard_map/tr,tc->rc/dot_general | solution.py:34
  74.9 13.8 %maximum_convert_fusion = f32[2,128,24576]{2,1,0:T(8,128)} fusion(bf16[1,128,24576]{2,1,0:T(8,128)(2,1)} %bitcast.23, bf16[1,128,24576]{2,1,0:T(8,128)(2,1)} %bitcast.22), kind=kLoop, calls=%fused_computation.4 | loop fusion | flops 12582912 | bytes 37748736 | tf_op jit(solution)/shard_map/stack | solution.py:44
  88.7 0.0 reduce-scatter.2.cloned.1.call-update
  88.7 1.4 copy-done.1
  90.1 0.5 collective-permute-start
  90.5 2.6 collective-permute-start.1
  93.1 0.0 collective-permute-start.3
  93.9 250.1 %reduce-scatter.2.cloned.1.call-done = f32[2,8,24576]{2,1,0:T(8,128)} async-done(((f32[2,128,24576]{2,1,0:T(8,128)}), f32[2,8,24576]{2,1,0:T(8,128)}) %reduce-scatter.2.cloned.1.call-update) | async-done | bytes 1572880 | tf_op jit(solution)/shard_map/reduce_scatter | solution.py:51
  344.0 2.5 multiply_reduce_fusion
  346.5 39.5 %psum.7 = f32[]{:T(128)} all-reduce(f32[]{:T(128)} %multiply_reduce_fusion), channel_id=1, replica_groups=mesh['dp'=16,'mp'=2] {'dp','mp'}, use_global_device_ids=true, to_apply=%region_2.0 | all-reduce | flops 1 | bytes 8 | tf_op jit(solution)/shard_map/psum | solution.py:52
  386.8 0.0 copy-done
  386.8 0.1 collective-permute-start.2
  386.9 4.8 %multiply_subtract_fusion.1 = (f32[2,8,24576]{2,1,0:T(8,128)}, f32[2,8,24576]{2,1,0:T(8,128)}, f32[2,8,24576]{2,1,0:T(8,128)}) fusion(f32[2,8,24576]{2,1,0:T(8,128)S(1)} %copy-done.1, f32[]{:T(128)} %bitcast.9, f32[]{:T(128)} %bitcast.8, f32[2,8,24576]{2,1,0:T(8,128)S(1)} %copy-done, f32[]{:T(128)S(6)} %min.3, f32[2,8,24576]{2,1,0:T(8,128)} %param.12, ...), kind=kLoop, calls=%fused_computation.13 | loop fusion | flops 6291456 | bytes 11010060 | tf_op jit(solution)/shard_map/sub | solution.py:27
  391.7 0.0 collective-permute-done
  391.7 0.0 collective-permute-done.1
  391.7 0.0 collective-permute-done.3
  391.7 17.7 %collective-permute-done.2 = f32[2,8,24576]{2,1,0:T(8,128)S(1)} collective-permute-done((f32[2,8,24576]{2,1,0:T(8,128)S(1)}, f32[2,8,24576]{2,1,0:T(8,128)S(1)}, u32[]{:S(2)}, u32[]{:S(2)}) %collective-permute-start.2) | collective-permute-done | bytes 1572896 | tf_op jit(solution)/shard_map/ppermute | solution.py:18
  409.4 5.3 %multiply_subtract_fusion = (f32[2,8,24576]{2,1,0:T(8,128)}, f32[2,8,24576]{2,1,0:T(8,128)}, f32[2,8,24576]{2,1,0:T(8,128)}) fusion(f32[2,8,24576]{2,1,0:T(8,128)} %collective-permute-done, f32[]{:T(128)} %bitcast.9, f32[]{:T(128)} %bitcast.8, f32[2,8,24576]{2,1,0:T(8,128)S(1)} %collective-permute-done.2, f32[]{:T(128)S(6)} %min.3, ...), kind=kLoop, calls=%fused_computation.11 | loop fusion | flops 6291456 | bytes 11010060 | tf_op jit(solution)/shard_map/sub | solution.py:27
  (2 shorter events, 0.0 us)
Async XLA Ops:
  7.2 38.4 %copy-start.2 = (bf16[128,2,128]{2,1,0:T(2,128)(2,1)S(1)}, bf16[128,2,128]{2,1,0:T(2,128)(2,1)}, u32[]{:S(2)}) copy-start(bf16[128,2,128]{2,1,0:T(2,128)(2,1)} %param.8) | copy-start | bytes 196612
  7.2 336.8 %reduce-scatter.2.cloned.1.call-start = ((), (), s32[]{:S(2)}) async-start(), calls=%async_computation.1 | async-start | bytes 26738688 | tf_op jit(solution)/shard_map/reduce_scatter | solution.py:51
  88.7 1.4 copy-start.1
  90.1 301.6 %collective-permute-start = (f32[2,8,24576]{2,1,0:T(8,128)S(1)}, f32[2,8,24576]{2,1,0:T(8,128)}, u32[]{:S(2)}, u32[]{:S(2)}) collective-permute-start(f32[2,8,24576]{2,1,0:T(8,128)S(1)} %copy-done.1), channel_id=1, source_target_pairs={{0,2},{2,4},{4,6},{6,8},{8,10},{10,12},{12,14},{14,16},{16,18},{18... | collective-permute-start | bytes 4718600 | tf_op jit(solution)/shard_map/ppermute | solution.py:18
  90.5 301.2 %collective-permute-start.1 = (f32[2,8,24576]{2,1,0:T(8,128)}, f32[2,8,24576]{2,1,0:T(8,128)}, u32[]{:S(2)}, u32[]{:S(2)}) collective-permute-start(f32[2,8,24576]{2,1,0:T(8,128)} %param.11), channel_id=1, source_target_pairs={{0,2},{2,4},{4,6},{6,8},{8,10},{10,12},{12,14},{14,16},{16,18},{18... | collective-permute-start | bytes 4718600 | tf_op jit(solution)/shard_map/ppermute | solution.py:18
  93.1 298.6 %collective-permute-start.3 = (f32[2,8,24576]{2,1,0:T(8,128)}, f32[2,8,24576]{2,1,0:T(8,128)}, u32[]{:S(2)}, u32[]{:S(2)}) collective-permute-start(f32[2,8,24576]{2,1,0:T(8,128)} %param.12), channel_id=1, source_target_pairs={{0,2},{2,4},{4,6},{6,8},{8,10},{10,12},{12,14},{14,16},{16,18},{18... | collective-permute-start | bytes 4718600 | tf_op jit(solution)/shard_map/ppermute | solution.py:18
  344.0 42.8 %copy-start = (f32[2,8,24576]{2,1,0:T(8,128)S(1)}, f32[2,8,24576]{2,1,0:T(8,128)}, u32[]{:S(2)}) copy-start(f32[2,8,24576]{2,1,0:T(8,128)} %reduce-scatter.2.cloned.1.call-done) | copy-start | bytes 4718596
  386.8 22.6 %collective-permute-start.2 = (f32[2,8,24576]{2,1,0:T(8,128)S(1)}, f32[2,8,24576]{2,1,0:T(8,128)S(1)}, u32[]{:S(2)}, u32[]{:S(2)}) collective-permute-start(f32[2,8,24576]{2,1,0:T(8,128)S(1)} %copy-done), channel_id=1, source_target_pairs={{0,2},{2,4},{4,6},{6,8},{8,10},{10,12},{12,14},{14,16},{16,18},{18... | collective-permute-start | bytes 4718600 | tf_op jit(solution)/shard_map/ppermute | solution.py:18
Sparse Core Ops, SparseCore 0:
  88.8 255.1 reduce-scatter.1
where the time goes:
time: 422 us
  waiting for transfers between devices  268 us (64%)
  local copies, waits for them, and re-layouts  39.9 us (9%)
  blocking collectives  39.5 us (9%)
  matrix products  29.2 us (7%)
  other arithmetic  26.4 us (6%)
  between operations  15.6 us (4%)
    reduce_scatter x1, waiting for transfers between devices, local(): grad = lax.psum_scatter(terms, 'dp', scatter_dimension=1, tiled=True)  250 us
    psum x1, blocking collectives, local(): squares = lax.psum(jnp.sum(grad * grad), ('dp', 'mp'))  39.5 us
    slice x1, local copies, waits for them, and re-layouts, local(): cotangent[:, layer, :]  38.4 us
    dot_general x2, matrix products, local_term(): jnp.einsum('tr,tc->rc', inputs, outgrad, preferred_element_type=jnp.float32)  29.2 us
    ppermute x4, waiting for transfers between devices, passed_along(): lax.ppermute(value, axis, [(i, (i + by) % peers) for i in range(peers)])  17.7 us
    another operation x1, other arithmetic, local(): jnp.stack([local_term(earlier[layer], activations[:, layer, :], cotangent...  13.8 us
    sub x2, other arithmetic, adamw_update(): weights - learn_rate * (first_hat / (jnp.sqrt(second_hat) + epsilon) + de...  10.1 us
  transfers between devices with their start and end apart: 5, of which 2 were waited for; matrix products, arithmetic and copies ran while one was open for 2% of the time, Pallas kernels for 0%

commit v1 on v0

v1 whole, which is shorter than its diff:
```python
import functools

import jax
import jax.numpy as jnp
from jax import lax
from jax.experimental import pallas as pl
from jax.experimental.pallas import tpu as pltpu
from jax.sharding import PartitionSpec as P

beta_one = 0.9
beta_two = 0.95
learn_rate = 0.1
decay_rate = 0.1
epsilon = 1e-08

streams = 4
lanes = 128
room = pltpu.CompilerParams(vmem_limit_bytes=48 * 2**20)


def block_of(columns, most):
    best = lanes
    for size in range(lanes, min(columns, most) + 1, lanes):
        if columns % size == 0:
            best = size
    return best


def adamw_update(weights, first, second, grad, factor, first_scale, second_scale):
    scaled = factor * grad
    first_new = beta_one * first + (1.0 - beta_one) * scaled
    second_new = beta_two * second + (1.0 - beta_two) * scaled * scaled
    first_hat = first_new / first_scale
    second_hat = second_new / second_scale
    weights_new = weights - learn_rate * (
        first_hat / (jnp.sqrt(second_hat) + epsilon) + decay_rate * weights
    )
    return (weights_new, first_new, second_new)


def terms_kernel(order, layers, core_ref, inputs_ref, earlier_ref, outgrad_ref, keep_ref, give_ref):
    core = core_ref[0]
    tokens, _, columns = outgrad_ref.shape
    rows = earlier_ref.shape[2]
    outgrad = outgrad_ref[...].reshape(tokens * layers, columns)
    product = jnp.dot(inputs_ref[...], outgrad, preferred_element_type=jnp.float32)
    chips = len(order)
    for layer in range(layers):
        total = earlier_ref[0, layer].astype(jnp.float32) + product[layer * rows : (layer + 1) * rows]
        term = total.astype(jnp.bfloat16).astype(jnp.float32)
        term = term.reshape(chips, 2, rows // (2 * chips), columns)
        for place, chip in enumerate(order):
            keep_ref[place, layer] = jnp.where(core == 0, term[chip, 0], term[chip, 1])
            give_ref[place, layer] = jnp.where(core == 0, term[chip, 1], term[chip, 0])


def make_terms(core, inputs, earlier, outgrad, order, start, width):
    _, layers, rows, _ = earlier.shape
    tokens = outgrad.shape[0]
    chips = len(order)
    own = rows // (2 * chips)
    size = block_of(width, 2048)
    first = start // size
    return pl.pallas_call(
        functools.partial(terms_kernel, order, layers),
        grid_spec=pltpu.PrefetchScalarGridSpec(
            num_scalar_prefetch=1,
            grid=(width // size,),
            in_specs=[
                pl.BlockSpec(inputs.shape, lambda i, core: (0, 0)),
                pl.BlockSpec((1, layers, rows, size), lambda i, core: (0, 0, 0, first + i)),
                pl.BlockSpec((tokens, layers, size), lambda i, core: (0, 0, first + i)),
            ],
            out_specs=[pl.BlockSpec((chips, layers, own, size), lambda i, core: (0, 0, 0, i))] * 2,
        ),
        out_shape=[jax.ShapeDtypeStruct((chips, layers, own, width), jnp.float32)] * 2,
        compiler_params=room,
        name="terms",
    )(core, inputs, earlier, outgrad)


def first_kernel(shard_ref, keep_ref, theirs_ref, out_ref):
    out_ref[...] = keep_ref[0] + theirs_ref[0]


def step_kernel(shard_ref, keep_ref, theirs_ref, arrived_ref, out_ref):
    out_ref[...] = arrived_ref[...] + (keep_ref[0] + theirs_ref[0])


def last_kernel(shard_ref, keep_ref, theirs_ref, arrived_ref, out_ref, squares_ref):
    grad = arrived_ref[...] + (keep_ref[0] + theirs_ref[0])
    out_ref[...] = grad
    layers, own, columns = grad.shape
    squares = jnp.sum((grad * grad).reshape(layers, own, columns // lanes, lanes), axis=(0, 2))

    @pl.when(pl.program_id(0) == 0)
    def _():
        squares_ref[...] = squares

    @pl.when(pl.program_id(0) > 0)
    def _():
        squares_ref[...] += squares


def ring_add(shards, step, keep, theirs, arrived, last):
    _, layers, own, width = keep.shape
    size = block_of(width, 3072)
    chosen = pl.BlockSpec((1, layers, own, size), lambda i, shards: (shards[step], 0, 0, i))
    whole = pl.BlockSpec((layers, own, size), lambda i, shards: (0, 0, i))
    summed = jax.ShapeDtypeStruct((layers, own, width), jnp.float32)
    out_shape, out_specs = summed, whole
    body = step_kernel
    if arrived is None:
        body = first_kernel
    elif last:
        body = last_kernel
        out_shape = [summed, jax.ShapeDtypeStruct((own, lanes), jnp.float32)]
        out_specs = [whole, pl.BlockSpec((own, lanes), lambda i, shards: (0, 0))]
    rest = [] if arrived is None else [arrived]
    return pl.pallas_call(
        body,
        grid_spec=pltpu.PrefetchScalarGridSpec(
            num_scalar_prefetch=1,
            grid=(width // size,),
            in_specs=[chosen, chosen] + [whole] * len(rest),
            out_specs=out_specs,
        ),
        out_shape=out_shape,
        compiler_params=room,
        name="ring_add",
    )(shards, keep, theirs, *rest)


def update_kernel(count, bound, scales_ref, squares_ref, weights_ref, first_ref, second_ref, *rest):
    grads, outs = rest[:count], rest[count:]
    step = pl.program_id(0)
    per = pl.num_programs(0) // count
    factor = jnp.minimum(
        jnp.float32(1.0), bound / (jnp.sqrt(jnp.sum(squares_ref[...])) + jnp.float32(1e-06))
    )
    for index, grad_ref in enumerate(grads):

        @pl.when(step // per == index)
        def _(grad_ref=grad_ref):
            new = adamw_update(
                weights_ref[...],
                first_ref[...],
                second_ref[...],
                grad_ref[...],
                factor,
                scales_ref[0],
                scales_ref[1],
            )
            for out_ref, value in zip(outs, new):
                out_ref[...] = value


def update(scales, squares, state, grads, bound):
    layers, own, columns = state[0].shape
    width = grads[0].shape[-1]
    count = len(grads)
    size = block_of(width, 3072)
    per = width // size
    block = pl.BlockSpec((layers, own, size), lambda i: (0, 0, i))
    return pl.pallas_call(
        functools.partial(update_kernel, count, bound),
        grid=(columns // size,),
        in_specs=[
            pl.BlockSpec(memory_space=pltpu.SMEM),
            pl.BlockSpec(squares.shape, lambda i: (0, 0)),
        ]
        + [block] * 3
        + [
            pl.BlockSpec(
                (layers, own, size), lambda i, k=k: (0, 0, jnp.clip(i - k * per, 0, per - 1))
            )
            for k in range(count)
        ],
        out_specs=[block] * 3,
        out_shape=[jax.ShapeDtypeStruct((layers, own, columns), jnp.float32)] * 3,
        compiler_params=room,
        name="update",
    )(scales, squares, *state, *grads)


def total_over(value, axis):
    peers = lax.axis_size(axis)
    if peers & (peers - 1):
        return lax.psum(value, axis)
    bit = 1
    while bit < peers:
        value = value + lax.ppermute(value, axis, [(i, i ^ bit) for i in range(peers)])
        bit *= 2
    return value


def local(acc_grads, activations, cotangent, params, first_moment, second_moment, step):
    _, layers, rows, columns = acc_grads.shape
    tokens = activations.shape[0]
    peers = lax.axis_size("dp")
    chips = peers // 2
    half = chips // 2
    order = [2 * z for z in range(half)] + [2 * z + 1 for z in reversed(range(half))]
    forward = [
        (2 * order[r] + core, 2 * order[(r + 1) % chips] + core)
        for r in range(chips)
        for core in range(2)
    ]
    backward = [(target, source) for source, target in forward]
    swap = [(i, i ^ 1) for i in range(peers)]
    onward = [(i, (i + 1) % peers) for i in range(peers)]

    index = lax.axis_index("dp")
    core, chip = index % 2, index // 2
    place = jnp.where(chip % 2 == 0, chip // 2, chips - 1 - chip // 2)
    hops = jnp.arange(1, chips + 1, dtype=jnp.int32)
    shards = [jnp.mod(place - hops, chips), jnp.mod(place + hops, chips)]
    core = core.reshape(1)

    state = (params, first_moment, second_moment)
    old_copy = [lax.ppermute(value, "dp", onward) for value in state]

    same = jnp.eye(layers, dtype=activations.dtype)
    inputs = activations.transpose(1, 2, 0)[:, :, :, None] * same[:, None, None, :]
    inputs = inputs.reshape(layers * rows, tokens * layers)

    width = columns // streams
    keep, theirs = [], []
    for k in range(streams):
        mine, give = make_terms(core, inputs, acc_grads, cotangent, order, k * width, width)
        keep.append(mine)
        theirs.append(lax.ppermute(give, "dp", swap))

    sums = [None] * streams
    squares = None
    for hop in range(chips):
        for k in range(streams):
            last = hop == chips - 1
            out = ring_add(shards[k % 2], hop, keep[k], theirs[k], sums[k], last)
            if last:
                sums[k], part = out
                squares = part if squares is None else squares + part
            else:
                sums[k] = lax.ppermute(out, "dp", backward if k % 2 else forward)

    peer_grads = [lax.ppermute(value, "dp", onward) for value in sums]
    squares = total_over(total_over(squares, "dp"), "mp")
    bound = float((layers * rows * columns * lax.axis_size("mp")) ** 0.5)
    count = step.astype(jnp.float32)
    scales = jnp.concatenate(
        [
            1.0 - jnp.power(jnp.float32(beta_one), count),
            1.0 - jnp.power(jnp.float32(beta_two), count),
        ]
    )
    new = update(scales, squares, state, sums, bound)
    copies = update(scales, squares, old_copy, peer_grads, bound)
    return (*new, *copies)


def solution(mesh):
    owned = P(None, "dp", "mp")
    return jax.shard_map(
        local,
        mesh=mesh,
        in_specs=(
            P("dp", None, None, "mp"),
            P("dp", None, None),
            P("dp", None, "mp"),
            owned,
            owned,
            owned,
            P(),
        ),
        out_specs=(owned,) * 6,
        check_vma=False,
    )
```

time: 422 us -> 266 us (0.63)
  waiting for transfers between devices: 268 us -> 113 us
  Pallas kernels: 0 us -> 102 us
  blocking collectives: 39.5 us -> 0 us
  starting transfers between devices: 3.18 us -> 36.7 us
  local copies, waits for them, and re-layouts: 39.9 us -> 10.3 us
  matrix products: 29.2 us -> 0 us
  other arithmetic: 26.4 us -> 1.14 us
  between operations: 15.6 us -> 1.79 us
    reduce_scatter x1 -> x0, waiting for transfers between devices: 250 us -> none  [local(): grad = lax.psum_scatter(terms, 'dp', scatter_dimension=1, tiled=True)]
    pallas_call x0 -> x38, Pallas kernels: none -> 102 us  [the longest x32 61.5 us: ring_add(): pl.pallas_call(body, grid_spec=pltpu.PrefetchScalarGridSpec(num_scalar_pr...]
    ppermute x4 -> x44, waiting for transfers between devices: 17.7 us -> 113 us  [the longest x28 86.8 us: local(): sums[k] = lax.ppermute(out, 'dp', backward if k % 2 else forward)]
    psum x1 -> x0, blocking collectives: 39.5 us -> none  [local(): squares = lax.psum(jnp.sum(grad * grad), ('dp', 'mp'))]
    slice x2 -> x0, local copies, waits for them, and re-layouts: 38.5 us -> none  [the longest x1 38.4 us: local(): cotangent[:, layer, :]]
    ppermute x4 -> x44, starting transfers between devices: 3.14 us -> 36.7 us  [the longest x28 30 us: local(): sums[k] = lax.ppermute(out, 'dp', backward if k % 2 else forward)]
    dot_general x2 -> x0, matrix products: 29.2 us -> none  [local_term(): jnp.einsum('tr,tc->rc', inputs, outgrad, preferred_element_type=jnp.float32)]
    another operation x1 -> x0, other arithmetic: 13.8 us -> none  [local(): jnp.stack([local_term(earlier[layer], activations[:, layer, :], cotangent...]
  transfers between devices with their start and end apart: 5 -> 44, of which waited for: 2 -> 22; matrix products, arithmetic and copies ran while one was open for 2% -> 0% of each run, Pallas kernels for 0% -> 33%
where the time goes in v1:
time: 266 us; the launch traced here: 265 us
  waiting for transfers between devices  113 us (42%)
  Pallas kernels  102 us (38%)
  starting transfers between devices  36.7 us (14%)
  local copies, waits for them, and re-layouts  10.3 us (4%)
    ppermute x28, waiting for transfers between devices, local(): sums[k] = lax.ppermute(out, 'dp', backward if k % 2 else forward)  86.8 us
    pallas_call x32, Pallas kernels, ring_add(): pl.pallas_call(body, grid_spec=pltpu.PrefetchScalarGridSpec(num_scalar_pr...  61.5 us
    ppermute x28, starting transfers between devices, local(): sums[k] = lax.ppermute(out, 'dp', backward if k % 2 else forward)  30 us
    pallas_call x4, Pallas kernels, make_terms(): pl.pallas_call(functools.partial(terms_kernel, order, layers), grid_spec=...  25 us
    pallas_call x2, Pallas kernels, update(): pl.pallas_call(functools.partial(update_kernel, count, bound), grid=(colu...  15.5 us
    ppermute x5, waiting for transfers between devices, total_over(): lax.ppermute(value, axis, [(i, i ^ bit) for i in range(peers)])  14.1 us
    ppermute x4, waiting for transfers between devices, local(): peer_grads = [lax.ppermute(value, 'dp', onward) for value in sums]  12.2 us
    unnamed x45, local copies, waits for them, and re-layouts  10.2 us
  transfers between devices with their start and end apart: 44, of which 22 were waited for; matrix products, arithmetic and copies ran while one was open for 0% of the time, Pallas kernels for 33%

profile of v1, /device:TPU:0, one launch (start us, length us, event | category | flops | bytes accessed | tf_op | source)
XLA Modules:
  0.0 265.0 jit_solution(15287709404595207589)
XLA Ops:
  1.8 6.1 %terms.5 = (f32[8,2,8,6144]{3,2,1,0:T(8,128)S(1)}, f32[8,2,8,6144]{3,2,1,0:T(8,128)}) custom-call(s32[1]{0:T(128)} %bitcast.core_ref, bf16[256,256]{1,0:T(8,128)(2,1)S(1)} %copy.14.inputs_ref, bf16[1,2,128,24576]{3,2,1,0:T(8,128)(2,1)} %earlier_ref.7, bf16[128,2,24576]{2,1,0:T(2,128)(2,1)} %outgrad_ref.7), custom_call_target="tpu_custom_call" | custom-call | tf_op jit(solution)/shard_map/terms/pallas_call | solution.py:64
  10.0 6.1 %terms.4 = (f32[8,2,8,6144]{3,2,1,0:T(8,128)S(1)}, f32[8,2,8,6144]{3,2,1,0:T(8,128)}) custom-call(s32[1]{0:T(128)} %bitcast.core_ref, bf16[256,256]{1,0:T(8,128)(2,1)S(1)} %copy.14.inputs_ref, bf16[1,2,128,24576]{3,2,1,0:T(8,128)(2,1)} %earlier_ref.7, bf16[128,2,24576]{2,1,0:T(2,128)(2,1)} %outgrad_ref.7), custom_call_target="tpu_custom_call" | custom-call | tf_op jit(solution)/shard_map/terms/pallas_call | solution.py:64
  17.8 6.1 %terms.6 = (f32[8,2,8,6144]{3,2,1,0:T(8,128)S(1)}, f32[8,2,8,6144]{3,2,1,0:T(8,128)}) custom-call(s32[1]{0:T(128)} %bitcast.core_ref, bf16[256,256]{1,0:T(8,128)(2,1)S(1)} %copy.14.inputs_ref, bf16[1,2,128,24576]{3,2,1,0:T(8,128)(2,1)} %earlier_ref.7, bf16[128,2,24576]{2,1,0:T(2,128)(2,1)} %outgrad_ref.7), custom_call_target="tpu_custom_call" | custom-call | tf_op jit(solution)/shard_map/terms/pallas_call | solution.py:64
  24.3 6.7 %terms.7 = (f32[8,2,8,6144]{3,2,1,0:T(8,128)S(1)}, f32[8,2,8,6144]{3,2,1,0:T(8,128)}) custom-call(s32[1]{0:T(128)} %bitcast.core_ref, bf16[256,256]{1,0:T(8,128)(2,1)S(1)} %copy.14.inputs_ref, bf16[1,2,128,24576]{3,2,1,0:T(8,128)(2,1)} %earlier_ref.7, bf16[128,2,24576]{2,1,0:T(2,128)(2,1)} %outgrad_ref.7), custom_call_target="tpu_custom_call" | custom-call | tf_op jit(solution)/shard_map/terms/pallas_call | solution.py:64
  35.4 2.6 collective-permute-start.9
  53.8 6.6 %collective-permute-done.17.arrived_ref = f32[2,8,6144]{2,1,0:T(8,128)S(1)} collective-permute-done((f32[2,8,6144]{2,1,0:T(8,128)S(1)}, f32[2,8,6144]{2,1,0:T(8,128)S(1)}, u32[]{:S(2)}, u32[]{:S(2)}) %collective-permute-start.17) | collective-permute-done | bytes 393248 | tf_op jit(solution)/shard_map/ppermute | solution.py:244
  71.5 5.8 %collective-permute-done.18.arrived_ref = f32[2,8,6144]{2,1,0:T(8,128)S(1)} collective-permute-done((f32[2,8,6144]{2,1,0:T(8,128)S(1)}, f32[2,8,6144]{2,1,0:T(8,128)S(1)}, u32[]{:S(2)}, u32[]{:S(2)}) %collective-permute-start.18) | collective-permute-done | bytes 393248 | tf_op jit(solution)/shard_map/ppermute | solution.py:244
  88.3 5.8 %collective-permute-done.19.arrived_ref = f32[2,8,6144]{2,1,0:T(8,128)S(1)} collective-permute-done((f32[2,8,6144]{2,1,0:T(8,128)S(1)}, f32[2,8,6144]{2,1,0:T(8,128)S(1)}, u32[]{:S(2)}, u32[]{:S(2)}) %collective-permute-start.19) | collective-permute-done | bytes 393248 | tf_op jit(solution)/shard_map/ppermute | solution.py:244
  105.8 5.2 %collective-permute-done.20.arrived_ref = f32[2,8,6144]{2,1,0:T(8,128)S(1)} collective-permute-done((f32[2,8,6144]{2,1,0:T(8,128)S(1)}, f32[2,8,6144]{2,1,0:T(8,128)S(1)}, u32[]{:S(2)}, u32[]{:S(2)}) %collective-permute-start.20) | collective-permute-done | bytes 393248 | tf_op jit(solution)/shard_map/ppermute | solution.py:244
  124.0 3.2 %collective-permute-done.21.arrived_ref = f32[2,8,6144]{2,1,0:T(8,128)} collective-permute-done((f32[2,8,6144]{2,1,0:T(8,128)}, f32[2,8,6144]{2,1,0:T(8,128)}, u32[]{:S(2)}, u32[]{:S(2)}) %collective-permute-start.21) | collective-permute-done | bytes 393248 | tf_op jit(solution)/shard_map/ppermute | solution.py:244
  127.2 2.5 ring_add.53
  132.8 3.2 %collective-permute-done.14.arrived_ref = f32[2,8,6144]{2,1,0:T(8,128)} collective-permute-done((f32[2,8,6144]{2,1,0:T(8,128)}, f32[2,8,6144]{2,1,0:T(8,128)}, u32[]{:S(2)}, u32[]{:S(2)}) %collective-permute-start.14) | collective-permute-done | bytes 393248 | tf_op jit(solution)/shard_map/ppermute | solution.py:244
  141.2 2.8 %collective-permute-start.39 = (f32[2,8,24576]{2,1,0:T(8,128)}, f32[2,8,24576]{2,1,0:T(8,128)}, u32[]{:S(2)}, u32[]{:S(2)}) collective-permute-start(f32[2,8,24576]{2,1,0:T(8,128)} %second_ref.1), channel_id=1, source_target_pairs={{0,2},{2,4},{4,6},{6,8},{8,10},{10,12},{12,14},{14,16},{16,18},{18... | collective-permute-start | bytes 4718600 | tf_op jit(solution)/shard_map/ppermute | solution.py:221
  150.0 27.2 %collective-permute-done.22.arrived_ref = f32[2,8,6144]{2,1,0:T(8,128)} collective-permute-done((f32[2,8,6144]{2,1,0:T(8,128)}, f32[2,8,6144]{2,1,0:T(8,128)}, u32[]{:S(2)}, u32[]{:S(2)}) %collective-permute-start.22) | collective-permute-done | bytes 393248 | tf_op jit(solution)/shard_map/ppermute | solution.py:244
  184.4 4.8 %collective-permute-done.15.arrived_ref = f32[2,8,6144]{2,1,0:T(8,128)S(1)} collective-permute-done((f32[2,8,6144]{2,1,0:T(8,128)}, f32[2,8,6144]{2,1,0:T(8,128)S(1)}, u32[]{:S(2)}, u32[]{:S(2)}) %collective-permute-start.15) | collective-permute-done | bytes 393248 | tf_op jit(solution)/shard_map/ppermute | solution.py:244
  189.2 17.1 %collective-permute-done.7.arrived_ref = f32[2,8,6144]{2,1,0:T(8,128)S(1)} collective-permute-done((f32[2,8,6144]{2,1,0:T(8,128)}, f32[2,8,6144]{2,1,0:T(8,128)S(1)}, u32[]{:S(2)}, u32[]{:S(2)}) %collective-permute-start.7) | collective-permute-done | bytes 393248 | tf_op jit(solution)/shard_map/ppermute | solution.py:244
  221.4 3.3 %collective-permute-done.33 = f32[8,128]{1,0:T(8,128)S(1)} collective-permute-done((f32[8,128]{1,0:T(8,128)S(1)}, f32[8,128]{1,0:T(8,128)S(1)}, u32[]{:S(2)}, u32[]{:S(2)}) %collective-permute-start.33) | collective-permute-done | bytes 4128 | tf_op jit(solution)/shard_map/ppermute | solution.py:192
  224.8 3.5 %collective-permute-done.34 = f32[8,128]{1,0:T(8,128)S(1)} collective-permute-done((f32[8,128]{1,0:T(8,128)S(1)}, f32[8,128]{1,0:T(8,128)S(1)}, u32[]{:S(2)}, u32[]{:S(2)}) %collective-permute-start.34) | collective-permute-done | bytes 4128 | tf_op jit(solution)/shard_map/ppermute | solution.py:192
  228.4 4.5 %collective-permute-done.35 = f32[8,128]{1,0:T(8,128)S(1)} collective-permute-done((f32[8,128]{1,0:T(8,128)S(1)}, f32[8,128]{1,0:T(8,128)S(1)}, u32[]{:S(2)}, u32[]{:S(2)}) %collective-permute-start.35) | collective-permute-done | bytes 4128 | tf_op jit(solution)/shard_map/ppermute | solution.py:192
  237.3 7.4 %update.2 = (f32[2,8,24576]{2,1,0:T(8,128)}, f32[2,8,24576]{2,1,0:T(8,128)}, f32[2,8,24576]{2,1,0:T(8,128)}) custom-call(f32[2]{0:T(128)S(1)} %pad_maximum_fusion.scales_ref, f32[8,128]{1,0:T(8,128)S(1)} %add.65.squares_ref, f32[2,8,24576]{2,1,0:T(8,128)S(1)} %copy-done.14, f32[2,8,24576]{2,1,0:T(8,128)S(1)} %copy-done.15, f32[2,8,24576]{2,1,0:T(8,128)} %second_ref.1, ...), custom_call_target="tpu_custom_call" | custom-call | tf_op jit(solution)/shard_map/update/pallas_call | solution.py:165
  244.8 3.8 %collective-permute-done.40.rest_0_ = f32[2,8,6144]{2,1,0:T(8,128)S(1)} collective-permute-done((f32[2,8,6144]{2,1,0:T(8,128)S(1)}, f32[2,8,6144]{2,1,0:T(8,128)S(1)}, u32[]{:S(2)}, u32[]{:S(2)}) %collective-permute-start.40) | collective-permute-done | bytes 393248 | tf_op jit(solution)/shard_map/ppermute | solution.py:246
  248.5 4.2 %collective-permute-done.42.rest_2_ = f32[2,8,6144]{2,1,0:T(8,128)S(1)} collective-permute-done((f32[2,8,6144]{2,1,0:T(8,128)S(1)}, f32[2,8,6144]{2,1,0:T(8,128)S(1)}, u32[]{:S(2)}, u32[]{:S(2)}) %collective-permute-start.42) | collective-permute-done | bytes 393248 | tf_op jit(solution)/shard_map/ppermute | solution.py:246
  252.7 4.2 %collective-permute-done.43.rest_3_ = f32[2,8,6144]{2,1,0:T(8,128)S(1)} collective-permute-done((f32[2,8,6144]{2,1,0:T(8,128)S(1)}, f32[2,8,6144]{2,1,0:T(8,128)S(1)}, u32[]{:S(2)}, u32[]{:S(2)}) %collective-permute-start.43) | collective-permute-done | bytes 393248 | tf_op jit(solution)/shard_map/ppermute | solution.py:246
  257.0 8.0 %update.3 = (f32[2,8,24576]{2,1,0:T(8,128)}, f32[2,8,24576]{2,1,0:T(8,128)}, f32[2,8,24576]{2,1,0:T(8,128)}) custom-call(f32[2]{0:T(128)S(1)} %pad_maximum_fusion.scales_ref, f32[8,128]{1,0:T(8,128)S(1)} %add.65.squares_ref, f32[2,8,24576]{2,1,0:T(8,128)} %collective-permute-done.37.weights_ref, f32[2,8,24576]{2,1,0:T(8,128)} %collective-permute-done.38.first_ref, ...), custom_call_target="tpu_custom_call" | custom-call | tf_op jit(solution)/shard_map/update/pallas_call | solution.py:165
  (159 shorter events, 112.3 us)
Async XLA Ops:
  9.5 22.0 %collective-permute-start.8 = (f32[8,2,8,6144]{3,2,1,0:T(8,128)}, f32[8,2,8,6144]{3,2,1,0:T(8,128)}, u32[]{:S(2)}, u32[]{:S(2)}) collective-permute-start(f32[8,2,8,6144]{3,2,1,0:T(8,128)} %get-tuple-element.32), channel_id=1, source_target_pairs={{0,2},{2,0},{4,6},{6,4},{8,10},{10,8},{12,14},{14,12},{16,18},{18,... | collective-permute-start | bytes 9437192 | tf_op jit(solution)/shard_map/ppermute | solution.py:232
  17.7 20.3 %collective-permute-start = (f32[8,2,8,6144]{3,2,1,0:T(8,128)}, f32[8,2,8,6144]{3,2,1,0:T(8,128)}, u32[]{:S(2)}, u32[]{:S(2)}) collective-permute-start(f32[8,2,8,6144]{3,2,1,0:T(8,128)} %get-tuple-element.29), channel_id=1, source_target_pairs={{0,2},{2,0},{4,6},{6,4},{8,10},{10,8},{12,14},{14,12},{16,18},{18,... | collective-permute-start | bytes 9437192 | tf_op jit(solution)/shard_map/ppermute | solution.py:232
  23.9 16.3 %collective-permute-start.16 = (f32[8,2,8,6144]{3,2,1,0:T(8,128)}, f32[8,2,8,6144]{3,2,1,0:T(8,128)}, u32[]{:S(2)}, u32[]{:S(2)}) collective-permute-start(f32[8,2,8,6144]{3,2,1,0:T(8,128)} %get-tuple-element.35), channel_id=1, source_target_pairs={{0,2},{2,0},{4,6},{6,4},{8,10},{10,8},{12,14},{14,12},{16,18},{18,... | collective-permute-start | bytes 9437192 | tf_op jit(solution)/shard_map/ppermute | solution.py:232
  41.8 18.6 %collective-permute-start.17 = (f32[2,8,6144]{2,1,0:T(8,128)S(1)}, f32[2,8,6144]{2,1,0:T(8,128)S(1)}, u32[]{:S(2)}, u32[]{:S(2)}) collective-permute-start(f32[2,8,6144]{2,1,0:T(8,128)S(1)} %ring_add.48), channel_id=1, source_target_pairs={{0,8},{2,10},{8,16},{10,18},{16,24},{18,26},{24,28},{26,30},{28,20... | collective-permute-start | bytes 1179656 | tf_op jit(solution)/shard_map/ppermute | solution.py:244
  45.8 16.4 %collective-permute-start.25 = (f32[2,8,6144]{2,1,0:T(8,128)S(1)}, f32[2,8,6144]{2,1,0:T(8,128)S(1)}, u32[]{:S(2)}, u32[]{:S(2)}) collective-permute-start(f32[2,8,6144]{2,1,0:T(8,128)S(1)} %ring_add.56), channel_id=1, source_target_pairs={{8,0},{10,2},{16,8},{18,10},{24,16},{26,18},{28,24},{30,26},{20,28... | collective-permute-start | bytes 1179656 | tf_op jit(solution)/shard_map/ppermute | solution.py:244
  49.5 16.4 %collective-permute-start.10 = (f32[2,8,6144]{2,1,0:T(8,128)S(1)}, f32[2,8,6144]{2,1,0:T(8,128)S(1)}, u32[]{:S(2)}, u32[]{:S(2)}) collective-permute-start(f32[2,8,6144]{2,1,0:T(8,128)S(1)} %ring_add.41), channel_id=1, source_target_pairs={{8,0},{10,2},{16,8},{18,10},{24,16},{26,18},{28,24},{30,26},{20,28... | collective-permute-start | bytes 1179656 | tf_op jit(solution)/shard_map/ppermute | solution.py:244
  53.7 15.6 %collective-permute-start.2 = (f32[2,8,6144]{2,1,0:T(8,128)S(1)}, f32[2,8,6144]{2,1,0:T(8,128)S(1)}, u32[]{:S(2)}, u32[]{:S(2)}) collective-permute-start(f32[2,8,6144]{2,1,0:T(8,128)S(1)} %ring_add.33), channel_id=1, source_target_pairs={{0,8},{2,10},{8,16},{10,18},{16,24},{18,26},{24,28},{26,30},{28,20... | collective-permute-start | bytes 1179656 | tf_op jit(solution)/shard_map/ppermute | solution.py:244
  62.1 15.2 %collective-permute-start.18 = (f32[2,8,6144]{2,1,0:T(8,128)S(1)}, f32[2,8,6144]{2,1,0:T(8,128)S(1)}, u32[]{:S(2)}, u32[]{:S(2)}) collective-permute-start(f32[2,8,6144]{2,1,0:T(8,128)S(1)} %ring_add.49), channel_id=1, source_target_pairs={{0,8},{2,10},{8,16},{10,18},{16,24},{18,26},{24,28},{26,30},{28,20... | collective-permute-start | bytes 1179656 | tf_op jit(solution)/shard_map/ppermute | solution.py:244
  79.0 15.2 %collective-permute-start.19 = (f32[2,8,6144]{2,1,0:T(8,128)S(1)}, f32[2,8,6144]{2,1,0:T(8,128)S(1)}, u32[]{:S(2)}, u32[]{:S(2)}) collective-permute-start(f32[2,8,6144]{2,1,0:T(8,128)S(1)} %ring_add.50), channel_id=1, source_target_pairs={{0,8},{2,10},{8,16},{10,18},{16,24},{18,26},{24,28},{26,30},{28,20... | collective-permute-start | bytes 1179656 | tf_op jit(solution)/shard_map/ppermute | solution.py:244
  95.8 15.2 %collective-permute-start.20 = (f32[2,8,6144]{2,1,0:T(8,128)S(1)}, f32[2,8,6144]{2,1,0:T(8,128)S(1)}, u32[]{:S(2)}, u32[]{:S(2)}) collective-permute-start(f32[2,8,6144]{2,1,0:T(8,128)S(1)} %ring_add.51), channel_id=1, source_target_pairs={{0,8},{2,10},{8,16},{10,18},{16,24},{18,26},{24,28},{26,30},{28,20... | collective-permute-start | bytes 1179656 | tf_op jit(solution)/shard_map/ppermute | solution.py:244
  97.7 15.7 %collective-permute-start.28 = (f32[2,8,6144]{2,1,0:T(8,128)S(1)}, f32[2,8,6144]{2,1,0:T(8,128)S(1)}, u32[]{:S(2)}, u32[]{:S(2)}) collective-permute-start(f32[2,8,6144]{2,1,0:T(8,128)S(1)} %ring_add.59), channel_id=1, source_target_pairs={{8,0},{10,2},{16,8},{18,10},{24,16},{26,18},{28,24},{30,26},{20,28... | collective-permute-start | bytes 1179656 | tf_op jit(solution)/shard_map/ppermute | solution.py:244
  101.3 16.3 %collective-permute-start.13 = (f32[2,8,6144]{2,1,0:T(8,128)S(1)}, f32[2,8,6144]{2,1,0:T(8,128)S(1)}, u32[]{:S(2)}, u32[]{:S(2)}) collective-permute-start(f32[2,8,6144]{2,1,0:T(8,128)S(1)} %ring_add.44), channel_id=1, source_target_pairs={{8,0},{10,2},{16,8},{18,10},{24,16},{26,18},{28,24},{30,26},{20,28... | collective-permute-start | bytes 1179656 | tf_op jit(solution)/shard_map/ppermute | solution.py:244
  105.3 16.3 %collective-permute-start.5 = (f32[2,8,6144]{2,1,0:T(8,128)}, f32[2,8,6144]{2,1,0:T(8,128)}, u32[]{:S(2)}, u32[]{:S(2)}) collective-permute-start(f32[2,8,6144]{2,1,0:T(8,128)} %ring_add.36), channel_id=1, source_target_pairs={{0,8},{2,10},{8,16},{10,18},{16,24},{18,26},{24,28},{26,30},{28,20... | collective-permute-start | bytes 1179656 | tf_op jit(solution)/shard_map/ppermute | solution.py:244
  120.0 16.0 %collective-permute-start.14 = (f32[2,8,6144]{2,1,0:T(8,128)}, f32[2,8,6144]{2,1,0:T(8,128)}, u32[]{:S(2)}, u32[]{:S(2)}) collective-permute-start(f32[2,8,6144]{2,1,0:T(8,128)} %ring_add.45), channel_id=1, source_target_pairs={{8,0},{10,2},{16,8},{18,10},{24,16},{26,18},{28,24},{30,26},{20,28... | collective-permute-start | bytes 1179656 | tf_op jit(solution)/shard_map/ppermute | solution.py:244
  121.6 112.8 %collective-permute-start.37 = (f32[2,8,24576]{2,1,0:T(8,128)S(1)}, f32[2,8,24576]{2,1,0:T(8,128)}, u32[]{:S(2)}, u32[]{:S(2)}) collective-permute-start(f32[2,8,24576]{2,1,0:T(8,128)S(1)} %copy-done.14), channel_id=1, source_target_pairs={{0,2},{2,4},{4,6},{6,8},{8,10},{10,12},{12,14},{14,16},{16,18},{18... | collective-permute-start | bytes 4718600 | tf_op jit(solution)/shard_map/ppermute | solution.py:221
  123.5 16.9 %collective-permute-start.6 = (f32[2,8,6144]{2,1,0:T(8,128)S(1)}, f32[2,8,6144]{2,1,0:T(8,128)S(1)}, u32[]{:S(2)}, u32[]{:S(2)}) collective-permute-start(f32[2,8,6144]{2,1,0:T(8,128)S(1)} %ring_add.37), channel_id=1, source_target_pairs={{0,8},{2,10},{8,16},{10,18},{16,24},{18,26},{24,28},{26,30},{28,20... | collective-permute-start | bytes 1179656 | tf_op jit(solution)/shard_map/ppermute | solution.py:244
  127.2 107.6 %collective-permute-start.38 = (f32[2,8,24576]{2,1,0:T(8,128)S(1)}, f32[2,8,24576]{2,1,0:T(8,128)}, u32[]{:S(2)}, u32[]{:S(2)}) collective-permute-start(f32[2,8,24576]{2,1,0:T(8,128)S(1)} %copy-done.15), channel_id=1, source_target_pairs={{0,2},{2,4},{4,6},{6,8},{8,10},{10,12},{12,14},{14,16},{16,18},{18... | collective-permute-start | bytes 4718600 | tf_op jit(solution)/shard_map/ppermute | solution.py:221
  129.7 47.4 %collective-permute-start.22 = (f32[2,8,6144]{2,1,0:T(8,128)}, f32[2,8,6144]{2,1,0:T(8,128)}, u32[]{:S(2)}, u32[]{:S(2)}) collective-permute-start(f32[2,8,6144]{2,1,0:T(8,128)} %ring_add.53), channel_id=1, source_target_pairs={{0,8},{2,10},{8,16},{10,18},{16,24},{18,26},{24,28},{26,30},{28,20... | collective-permute-start | bytes 1179656 | tf_op jit(solution)/shard_map/ppermute | solution.py:244
  136.0 43.3 %collective-permute-start.30 = (f32[2,8,6144]{2,1,0:T(8,128)}, f32[2,8,6144]{2,1,0:T(8,128)}, u32[]{:S(2)}, u32[]{:S(2)}) collective-permute-start(f32[2,8,6144]{2,1,0:T(8,128)} %copy-done.18), channel_id=1, source_target_pairs={{8,0},{10,2},{16,8},{18,10},{24,16},{26,18},{28,24},{30,26},{20,28... | collective-permute-start | bytes 1179656 | tf_op jit(solution)/shard_map/ppermute | solution.py:244
  141.2 103.6 %collective-permute-start.39 = (f32[2,8,24576]{2,1,0:T(8,128)}, f32[2,8,24576]{2,1,0:T(8,128)}, u32[]{:S(2)}, u32[]{:S(2)}) collective-permute-start(f32[2,8,24576]{2,1,0:T(8,128)} %second_ref.1), channel_id=1, source_target_pairs={{0,2},{2,4},{4,6},{6,8},{8,10},{10,12},{12,14},{14,16},{16,18},{18... | collective-permute-start | bytes 4718600 | tf_op jit(solution)/shard_map/ppermute | solution.py:221
  179.3 27.0 %collective-permute-start.7 = (f32[2,8,6144]{2,1,0:T(8,128)}, f32[2,8,6144]{2,1,0:T(8,128)S(1)}, u32[]{:S(2)}, u32[]{:S(2)}) collective-permute-start(f32[2,8,6144]{2,1,0:T(8,128)} %ring_add.38), channel_id=1, source_target_pairs={{0,8},{2,10},{8,16},{10,18},{16,24},{18,26},{24,28},{26,30},{28,20... | collective-permute-start | bytes 1179656 | tf_op jit(solution)/shard_map/ppermute | solution.py:244
  189.2 25.4 %collective-permute-start.23 = (f32[2,8,6144]{2,1,0:T(8,128)}, f32[2,8,6144]{2,1,0:T(8,128)}, u32[]{:S(2)}, u32[]{:S(2)}) collective-permute-start(f32[2,8,6144]{2,1,0:T(8,128)} %ring_add.54), channel_id=1, source_target_pairs={{0,8},{2,10},{8,16},{10,18},{16,24},{18,26},{24,28},{26,30},{28,20... | collective-permute-start | bytes 1179656 | tf_op jit(solution)/shard_map/ppermute | solution.py:244
  234.8 17.9 %collective-permute-start.42 = (f32[2,8,6144]{2,1,0:T(8,128)S(1)}, f32[2,8,6144]{2,1,0:T(8,128)S(1)}, u32[]{:S(2)}, u32[]{:S(2)}) collective-permute-start(f32[2,8,6144]{2,1,0:T(8,128)S(1)} %get-tuple-element.42.rest_2_), channel_id=1, source_target_pairs={{0,2},{2,4},{4,6},{6,8},{8,10},{10,12},{12,14},{14,16},{16,18},{18... | collective-permute-start | bytes 1179656 | tf_op jit(solution)/shard_map/ppermute | solution.py:246
  236.5 20.5 %collective-permute-start.43 = (f32[2,8,6144]{2,1,0:T(8,128)S(1)}, f32[2,8,6144]{2,1,0:T(8,128)S(1)}, u32[]{:S(2)}, u32[]{:S(2)}) collective-permute-start(f32[2,8,6144]{2,1,0:T(8,128)S(1)} %get-tuple-element.43.rest_3_), channel_id=1, source_target_pairs={{0,2},{2,4},{4,6},{6,8},{8,10},{10,12},{12,14},{14,16},{16,18},{18... | collective-permute-start | bytes 1179656 | tf_op jit(solution)/shard_map/ppermute | solution.py:246
  (42 other events, 328.4 us)

commit v2 on v1

--- a/solution.py
+++ b/solution.py
@@ -1,4 +1,5 @@
 import functools
+import math
 
 import jax
 import jax.numpy as jnp
@@ -13,7 +14,7 @@
 decay_rate = 0.1
 epsilon = 1e-08
 
-streams = 4
+streams = 2
 lanes = 128
 room = pltpu.CompilerParams(vmem_limit_bytes=48 * 2**20)
 
@@ -24,6 +25,11 @@
         if columns % size == 0:
             best = size
     return best
+
+
+def cost_of(*arrays):
+    moved = sum(math.prod(a.shape) * jnp.dtype(a.dtype).itemsize for a in arrays)
+    return pl.CostEstimate(flops=0, bytes_accessed=moved, transcendentals=0)
 
 
 def adamw_update(weights, first, second, grad, factor, first_scale, second_scale):
@@ -75,20 +81,27 @@
         ),
         out_shape=[jax.ShapeDtypeStruct((chips, layers, own, width), jnp.float32)] * 2,
         compiler_params=room,
+        cost_estimate=cost_of(
+            jax.ShapeDtypeStruct((layers, rows + tokens, width), earlier.dtype),
+            jax.ShapeDtypeStruct((layers, rows, width), jnp.float32),
+        ),
         name="terms",
     )(core, inputs, earlier, outgrad)
 
 
-def first_kernel(shard_ref, keep_ref, theirs_ref, out_ref):
+def plain_kernel(shard_ref, keep_ref, theirs_ref, *rest):
+    out_ref = rest[-1]
     out_ref[...] = keep_ref[0] + theirs_ref[0]
 
 
-def step_kernel(shard_ref, keep_ref, theirs_ref, arrived_ref, out_ref):
+def step_kernel(shard_ref, keep_ref, theirs_ref, arrived_ref, *rest):
+    out_ref = rest[-1]
     out_ref[...] = arrived_ref[...] + (keep_ref[0] + theirs_ref[0])
 
 
-def last_kernel(shard_ref, keep_ref, theirs_ref, arrived_ref, out_ref, squares_ref):
-    grad = arrived_ref[...] + (keep_ref[0] + theirs_ref[0])
+def last_kernel(shard_ref, keep_ref, theirs_ref, up_ref, down_ref, *rest):
+    out_ref, squares_ref = rest[-2:]
+    grad = (up_ref[...] + down_ref[...]) + (keep_ref[0] + theirs_ref[0])
     out_ref[...] = grad
     layers, own, columns = grad.shape
     squares = jnp.sum((grad * grad).reshape(layers, own, columns // lanes, lanes), axis=(0, 2))
@@ -102,33 +115,31 @@
         squares_ref[...] += squares
 
 
-def ring_add(shards, step, keep, theirs, arrived, last):
+def shard_sum(body, shards, which, keep, theirs, *arrived, after=()):
     _, layers, own, width = keep.shape
     size = block_of(width, 3072)
-    chosen = pl.BlockSpec((1, layers, own, size), lambda i, shards: (shards[step], 0, 0, i))
+    chosen = pl.BlockSpec((1, layers, own, size), lambda i, shards: (shards[which], 0, 0, i))
     whole = pl.BlockSpec((layers, own, size), lambda i, shards: (0, 0, i))
     summed = jax.ShapeDtypeStruct((layers, own, width), jnp.float32)
     out_shape, out_specs = summed, whole
-    body = step_kernel
-    if arrived is None:
-        body = first_kernel
-    elif last:
-        body = last_kernel
+    if body is last_kernel:
         out_shape = [summed, jax.ShapeDtypeStruct((own, lanes), jnp.float32)]
         out_specs = [whole, pl.BlockSpec((own, lanes), lambda i, shards: (0, 0))]
-    rest = [] if arrived is None else [arrived]
     return pl.pallas_call(
         body,
         grid_spec=pltpu.PrefetchScalarGridSpec(
             num_scalar_prefetch=1,
             grid=(width // size,),
-            in_specs=[chosen, chosen] + [whole] * len(rest),
+            in_specs=[chosen, chosen]
+            + [whole] * len(arrived)
+            + [pl.BlockSpec(memory_space=pl.ANY)] * len(after),
             out_specs=out_specs,
         ),
         out_shape=out_shape,
         compiler_params=room,
-        name="ring_add",
-    )(shards, keep, theirs, *rest)
+        cost_estimate=cost_of(*[summed] * (3 + len(arrived))),
+        name="shard_sum",
+    )(shards, keep, theirs, *arrived, *after)
 
 
 def update_kernel(count, bound, scales_ref, squares_ref, weights_ref, first_ref, second_ref, *rest):
@@ -179,6 +190,7 @@
         out_specs=[block] * 3,
         out_shape=[jax.ShapeDtypeStruct((layers, own, columns), jnp.float32)] * 3,
         compiler_params=room,
+        cost_estimate=cost_of(*[state[0]] * 7),
         name="update",
     )(scales, squares, *state, *grads)
 
@@ -201,21 +213,24 @@
     chips = peers // 2
     half = chips // 2
     order = [2 * z for z in range(half)] + [2 * z + 1 for z in reversed(range(half))]
-    forward = [
-        (2 * order[r] + core, 2 * order[(r + 1) % chips] + core)
-        for r in range(chips)
-        for core in range(2)
-    ]
-    backward = [(target, source) for source, target in forward]
+
+    def hop(by):
+        return [
+            (2 * order[r] + core, 2 * order[(r + by) % chips] + core)
+            for r in range(chips)
+            for core in range(2)
+        ]
+
     swap = [(i, i ^ 1) for i in range(peers)]
     onward = [(i, (i + 1) % peers) for i in range(peers)]
 
     index = lax.axis_index("dp")
     core, chip = index % 2, index // 2
     place = jnp.where(chip % 2 == 0, chip // 2, chips - 1 - chip // 2)
-    hops = jnp.arange(1, chips + 1, dtype=jnp.int32)
-    shards = [jnp.mod(place - hops, chips), jnp.mod(place + hops, chips)]
-    core = core.reshape(1)
+    hops = jnp.arange(half + 1, dtype=jnp.int32)
+    tables = [
+        jnp.concatenate([jnp.mod(place + by * hops, chips), core.reshape(1)]) for by in (1, -1)
+    ]
 
     state = (params, first_moment, second_moment)
     old_copy = [lax.ppermute(value, "dp", onward) for value in state]
@@ -225,25 +240,34 @@
     inputs = inputs.reshape(layers * rows, tokens * layers)
 
     width = columns // streams
-    keep, theirs = [], []
+    keep, theirs, sent, grads, peer_grads = ([None] * streams for _ in range(5))
     for k in range(streams):
-        mine, give = make_terms(core, inputs, acc_grads, cotangent, order, k * width, width)
-        keep.append(mine)
-        theirs.append(lax.ppermute(give, "dp", swap))
-
-    sums = [None] * streams
+        keep[k], give = make_terms(
+            core.reshape(1), inputs, acc_grads, cotangent, order, k * width, width
+        )
+        theirs[k] = lax.ppermute(give, "dp", swap)
+    for k in range(streams):
+        total = shard_sum(plain_kernel, tables[0], half, keep[k], theirs[k], after=old_copy[k : k + 1])
+        sent[k] = [None, None]
+        sent[k][k % 2] = lax.ppermute(total, "dp", hop(-1 if k % 2 else 1))
+    waiting = old_copy[streams:]
+    for away in range(half - 1, 0, -1):
+        for k in range(streams):
+            for way, by in enumerate((1, -1)):
+                arrived, after = [], ()
+                if sent[k][way] is not None:
+                    arrived, after, waiting = [sent[k][way]], waiting, ()
+                body = step_kernel if arrived else plain_kernel
+                total = shard_sum(
+                    body, tables[way], away, keep[k], theirs[k], *arrived, after=after
+                )
+                sent[k][way] = lax.ppermute(total, "dp", hop(by))
     squares = None
-    for hop in range(chips):
-        for k in range(streams):
-            last = hop == chips - 1
-            out = ring_add(shards[k % 2], hop, keep[k], theirs[k], sums[k], last)
-            if last:
-                sums[k], part = out
-                squares = part if squares is None else squares + part
-            else:
-                sums[k] = lax.ppermute(out, "dp", backward if k % 2 else forward)
-
-    peer_grads = [lax.ppermute(value, "dp", onward) for value in sums]
+    for k in range(streams):
+        grads[k], part = shard_sum(last_kernel, tables[0], 0, keep[k], theirs[k], *sent[k])
+        peer_grads[k] = lax.ppermute(grads[k], "dp", onward)
+        squares = part if squares is None else squares + part
+
     squares = total_over(total_over(squares, "dp"), "mp")
     bound = float((layers * rows * columns * lax.axis_size("mp")) ** 0.5)
     count = step.astype(jnp.float32)
@@ -253,7 +277,7 @@
             1.0 - jnp.power(jnp.float32(beta_two), count),
         ]
     )
-    new = update(scales, squares, state, sums, bound)
+    new = update(scales, squares, state, grads, bound)
     copies = update(scales, squares, old_copy, peer_grads, bound)
     return (*new, *copies)
 

time: 266 us -> 250 us (0.940)
  Pallas kernels: 102 us -> 86.2 us
  starting transfers between devices: 36.7 us -> 51.6 us
  local copies, waits for them, and re-layouts: 10.3 us -> 0.12 us
  waiting for transfers between devices: 113 us -> 108 us
    ppermute x36 -> x18, waiting for transfers between devices: 99 us -> 58.7 us  [the longest x12 49.1 us: local(): sent[k][way] = lax.ppermute(total, 'dp', hop(by))]
    ppermute x3, waiting for transfers between devices: 0.01 us -> 38.4 us  [local(): old_copy = [lax.ppermute(value, 'dp', onward) for value in state]]
    ppermute x5, starting transfers between devices: 1.95 us -> 16 us  [total_over(): lax.ppermute(value, axis, [(i, i ^ bit) for i in range(peers)])]
    pallas_call x32 -> x16, Pallas kernels: 61.5 us -> 47.8 us  [shard_sum(): pl.pallas_call(body, grid_spec=pltpu.PrefetchScalarGridSpec(num_scalar_pr...]
    unnamed x45 -> x1, local copies, waits for them, and re-layouts: 10.2 us -> 0.02 us
    ppermute x5, waiting for transfers between devices: 14.1 us -> 10.4 us  [total_over(): lax.ppermute(value, axis, [(i, i ^ bit) for i in range(peers)])]
    pallas_call x4 -> x2, Pallas kernels: 25 us -> 22.8 us  [make_terms(): pl.pallas_call(functools.partial(terms_kernel, order, layers), grid_spec=...]
    ppermute x36 -> x18, starting transfers between devices: 31.9 us -> 32.5 us  [the longest x2 12.9 us: local(): peer_grads[k] = lax.ppermute(grads[k], 'dp', onward)]
  transfers between devices with their start and end apart: 44 -> 26, of which waited for: 22 -> 16; matrix products, arithmetic and copies ran while one was open for 0% -> 0% of each run, Pallas kernels for 33% -> 27%
where the time goes in v2:
time: 250 us; the launch traced here: 248 us
  waiting for transfers between devices  108 us (43%)
  Pallas kernels  86.2 us (34%)
  starting transfers between devices  51.6 us (21%)
    ppermute x12, waiting for transfers between devices, local(): sent[k][way] = lax.ppermute(total, 'dp', hop(by))  49.1 us
    pallas_call x16, Pallas kernels, shard_sum(): pl.pallas_call(body, grid_spec=pltpu.PrefetchScalarGridSpec(num_scalar_pr...  47.8 us
    ppermute x3, waiting for transfers between devices, local(): old_copy = [lax.ppermute(value, 'dp', onward) for value in state]  38.4 us
    pallas_call x2, Pallas kernels, make_terms(): pl.pallas_call(functools.partial(terms_kernel, order, layers), grid_spec=...  22.8 us
    ppermute x5, starting transfers between devices, total_over(): lax.ppermute(value, axis, [(i, i ^ bit) for i in range(peers)])  16 us
    pallas_call x2, Pallas kernels, update(): pl.pallas_call(functools.partial(update_kernel, count, bound), grid=(colu...  15.5 us
    ppermute x2, starting transfers between devices, local(): peer_grads[k] = lax.ppermute(grads[k], 'dp', onward)  12.9 us
    ppermute x12, starting transfers between devices, local(): sent[k][way] = lax.ppermute(total, 'dp', hop(by))  10.4 us
  transfers between devices with their start and end apart: 26, of which 16 were waited for; matrix products, arithmetic and copies ran while one was open for 0% of the time, Pallas kernels for 27%

profile of v2, /device:TPU:0, one launch (start us, length us, event | category | flops | bytes accessed | tf_op | source)
XLA Modules:
  0.0 248.3 jit_solution(13525868179955301258)
XLA Ops:
  1.8 11.4 %terms.3 = (f32[8,2,8,12288]{3,2,1,0:T(8,128)}, f32[8,2,8,12288]{3,2,1,0:T(8,128)}) custom-call(s32[1]{0:T(128)} %bitcast.core_ref, bf16[256,256]{1,0:T(8,128)(2,1)S(1)} %copy.14.inputs_ref, bf16[1,2,128,24576]{3,2,1,0:T(8,128)(2,1)} %earlier_ref.3, bf16[128,2,24576]{2,1,0:T(2,128)(2,1)} %outgrad_ref.3), custom_call_target="tpu_custom_call" | custom-call | bytes 25165824 | tf_op jit(solution)/shard_map/terms/pallas_call | solution.py:70
  13.7 11.4 %terms.2 = (f32[8,2,8,12288]{3,2,1,0:T(8,128)}, f32[8,2,8,12288]{3,2,1,0:T(8,128)}) custom-call(s32[1]{0:T(128)} %bitcast.core_ref, bf16[256,256]{1,0:T(8,128)(2,1)S(1)} %copy.14.inputs_ref, bf16[1,2,128,24576]{3,2,1,0:T(8,128)(2,1)} %earlier_ref.3, bf16[128,2,24576]{2,1,0:T(2,128)(2,1)} %outgrad_ref.3), custom_call_target="tpu_custom_call" | custom-call | bytes 25165824 | tf_op jit(solution)/shard_map/terms/pallas_call | solution.py:70
  28.3 20.7 %collective-permute-done.14.rest_0_.first_ref = f32[2,8,24576]{2,1,0:T(8,128)S(1)} collective-permute-done((f32[2,8,24576]{2,1,0:T(8,128)}, f32[2,8,24576]{2,1,0:T(8,128)S(1)}, u32[]{:S(2)}, u32[]{:S(2)}) %collective-permute-start.14) | collective-permute-done | bytes 1572896 | tf_op jit(solution)/shard_map/ppermute | solution.py:236
  52.1 13.8 %collective-permute-done.1.rest_0_.weights_ref = f32[2,8,24576]{2,1,0:T(8,128)S(1)} collective-permute-done((f32[2,8,24576]{2,1,0:T(8,128)}, f32[2,8,24576]{2,1,0:T(8,128)S(1)}, u32[]{:S(2)}, u32[]{:S(2)}) %collective-permute-start.1) | collective-permute-done | bytes 1572896 | tf_op jit(solution)/shard_map/ppermute | solution.py:236
  68.9 8.6 %collective-permute-start.2 = (f32[2,8,12288]{2,1,0:T(8,128)S(1)}, f32[2,8,12288]{2,1,0:T(8,128)S(1)}, u32[]{:S(2)}, u32[]{:S(2)}) collective-permute-start(f32[2,8,12288]{2,1,0:T(8,128)S(1)} %shard_sum.16), channel_id=1, source_target_pairs={{0,8},{2,10},{8,16},{10,18},{16,24},{18,26},{24,28},{26,30},{28,20... | collective-permute-start | bytes 2359304 | tf_op jit(solution)/shard_map/ppermute | solution.py:252
  82.1 3.0 %shard_sum.28 = f32[2,8,12288]{2,1,0:T(8,128)S(1)} custom-call(s32[6]{0:T(128)S(1)} %pad_add_fusion.1.shard_ref, f32[8,2,8,12288]{3,2,1,0:T(8,128)} %get-tuple-element.23.keep_ref, f32[8,2,8,12288]{3,2,1,0:T(8,128)} %collective-permute-done.10.theirs_ref, f32[2,8,12288]{2,1,0:T(8,128)S(1)} %collective-permute-done.15.arrived_ref), custom_call_target="tpu_custom_call" | custom-call | bytes 3145728 | tf_op jit(solution)/shard_map/shard_sum/pallas_call | solution.py:128
  88.6 3.9 %collective-permute-done.3.rest_0_.second_ref = f32[2,8,24576]{2,1,0:T(8,128)} collective-permute-done((f32[2,8,24576]{2,1,0:T(8,128)}, f32[2,8,24576]{2,1,0:T(8,128)}, u32[]{:S(2)}, u32[]{:S(2)}) %collective-permute-start.3) | collective-permute-done | bytes 1572896 | tf_op jit(solution)/shard_map/ppermute | solution.py:236
  92.5 9.6 %collective-permute-done.2.arrived_ref = f32[2,8,12288]{2,1,0:T(8,128)S(1)} collective-permute-done((f32[2,8,12288]{2,1,0:T(8,128)S(1)}, f32[2,8,12288]{2,1,0:T(8,128)S(1)}, u32[]{:S(2)}, u32[]{:S(2)}) %collective-permute-start.2) | collective-permute-done | bytes 786464 | tf_op jit(solution)/shard_map/ppermute | solution.py:252
  105.1 13.2 %collective-permute-done.11.arrived_ref = f32[2,8,12288]{2,1,0:T(8,128)S(1)} collective-permute-done((f32[2,8,12288]{2,1,0:T(8,128)S(1)}, f32[2,8,12288]{2,1,0:T(8,128)S(1)}, u32[]{:S(2)}, u32[]{:S(2)}) %collective-permute-start.11) | collective-permute-done | bytes 786464 | tf_op jit(solution)/shard_map/ppermute | solution.py:264
  121.4 3.0 %shard_sum.29 = f32[2,8,12288]{2,1,0:T(8,128)S(1)} custom-call(s32[6]{0:T(128)S(1)} %pad_add_fusion.1.shard_ref, f32[8,2,8,12288]{3,2,1,0:T(8,128)} %get-tuple-element.23.keep_ref, f32[8,2,8,12288]{3,2,1,0:T(8,128)} %collective-permute-done.10.theirs_ref, f32[2,8,12288]{2,1,0:T(8,128)S(1)} %collective-permute-done.16.arrived_ref), custom_call_target="tpu_custom_call" | custom-call | bytes 3145728 | tf_op jit(solution)/shard_map/shard_sum/pallas_call | solution.py:128
  134.5 13.2 %collective-permute-done.12.arrived_ref = f32[2,8,12288]{2,1,0:T(8,128)S(1)} collective-permute-done((f32[2,8,12288]{2,1,0:T(8,128)S(1)}, f32[2,8,12288]{2,1,0:T(8,128)S(1)}, u32[]{:S(2)}, u32[]{:S(2)}) %collective-permute-start.12) | collective-permute-done | bytes 786464 | tf_op jit(solution)/shard_map/ppermute | solution.py:264
  150.8 3.0 %shard_sum.30 = f32[2,8,12288]{2,1,0:T(8,128)S(1)} custom-call(s32[6]{0:T(128)S(1)} %pad_add_fusion.1.shard_ref, f32[8,2,8,12288]{3,2,1,0:T(8,128)} %get-tuple-element.23.keep_ref, f32[8,2,8,12288]{3,2,1,0:T(8,128)} %collective-permute-done.10.theirs_ref, f32[2,8,12288]{2,1,0:T(8,128)S(1)} %collective-permute-done.17.arrived_ref), custom_call_target="tpu_custom_call" | custom-call | bytes 3145728 | tf_op jit(solution)/shard_map/shard_sum/pallas_call | solution.py:128
  155.8 5.9 %collective-permute-done.8.arrived_ref = f32[2,8,12288]{2,1,0:T(8,128)S(1)} collective-permute-done((f32[2,8,12288]{2,1,0:T(8,128)S(1)}, f32[2,8,12288]{2,1,0:T(8,128)S(1)}, u32[]{:S(2)}, u32[]{:S(2)}) %collective-permute-start.8) | collective-permute-done | bytes 786464 | tf_op jit(solution)/shard_map/ppermute | solution.py:264
  169.8 11.6 %collective-permute-done.13.up_ref = f32[2,8,12288]{2,1,0:T(8,128)S(1)} collective-permute-done((f32[2,8,12288]{2,1,0:T(8,128)S(1)}, f32[2,8,12288]{2,1,0:T(8,128)S(1)}, u32[]{:S(2)}, u32[]{:S(2)}) %collective-permute-start.13) | collective-permute-done | bytes 786464 | tf_op jit(solution)/shard_map/ppermute | solution.py:264
  181.4 3.1 %shard_sum.31 = (f32[2,8,12288]{2,1,0:T(8,128)S(1)}, f32[8,128]{1,0:T(8,128)S(1)}) custom-call(s32[6]{0:T(128)S(1)} %pad_add_fusion.shard_ref, f32[8,2,8,12288]{3,2,1,0:T(8,128)} %get-tuple-element.23.keep_ref, f32[8,2,8,12288]{3,2,1,0:T(8,128)} %collective-permute-done.10.theirs_ref, f32[2,8,12288]{2,1,0:T(8,128)S(1)} %collective-permute-done.13.up_ref, ...), custom_call_target="tpu_custom_call" | custom-call | bytes 3932160 | tf_op jit(solution)/shard_map/shard_sum/pallas_call | solution.py:128
  184.5 8.8 %collective-permute-start.25 = (f32[2,8,12288]{2,1,0:T(8,128)S(1)}, f32[2,8,12288]{2,1,0:T(8,128)S(1)}, u32[]{:S(2)}, u32[]{:S(2)}) collective-permute-start(f32[2,8,12288]{2,1,0:T(8,128)S(1)} %get-tuple-element.27.rest_1_), channel_id=1, source_target_pairs={{0,2},{2,4},{4,6},{6,8},{8,10},{10,12},{12,14},{14,16},{16,18},{18... | collective-permute-start | bytes 2359304 | tf_op jit(solution)/shard_map/ppermute | solution.py:268
  195.0 3.3 %collective-permute-done.6.up_ref = f32[2,8,12288]{2,1,0:T(8,128)S(1)} collective-permute-done((f32[2,8,12288]{2,1,0:T(8,128)S(1)}, f32[2,8,12288]{2,1,0:T(8,128)S(1)}, u32[]{:S(2)}, u32[]{:S(2)}) %collective-permute-start.6) | collective-permute-done | bytes 786464 | tf_op jit(solution)/shard_map/ppermute | solution.py:264
  198.3 3.1 %shard_sum.23 = (f32[2,8,12288]{2,1,0:T(8,128)S(1)}, f32[8,128]{1,0:T(8,128)S(1)}) custom-call(s32[6]{0:T(128)S(1)} %pad_add_fusion.shard_ref, f32[8,2,8,12288]{3,2,1,0:T(8,128)} %get-tuple-element.20.keep_ref, f32[8,2,8,12288]{3,2,1,0:T(8,128)} %collective-permute-done.theirs_ref, f32[2,8,12288]{2,1,0:T(8,128)S(1)} %collective-permute-done.6.up_ref, ...), custom_call_target="tpu_custom_call" | custom-call | bytes 3932160 | tf_op jit(solution)/shard_map/shard_sum/pallas_call | solution.py:128
  201.4 4.2 %collective-permute-start.24 = (f32[2,8,12288]{2,1,0:T(8,128)S(1)}, f32[2,8,12288]{2,1,0:T(8,128)S(1)}, u32[]{:S(2)}, u32[]{:S(2)}) collective-permute-start(f32[2,8,12288]{2,1,0:T(8,128)S(1)} %get-tuple-element.26.rest_0_), channel_id=1, source_target_pairs={{0,2},{2,4},{4,6},{6,8},{8,10},{10,12},{12,14},{14,16},{16,18},{18... | collective-permute-start | bytes 2359304 | tf_op jit(solution)/shard_map/ppermute | solution.py:268
  207.5 9.8 %collective-permute-start.20 = (f32[8,128]{1,0:T(8,128)S(1)}, f32[8,128]{1,0:T(8,128)S(1)}, u32[]{:S(2)}, u32[]{:S(2)}) collective-permute-start(f32[8,128]{1,0:T(8,128)S(1)} %add.55), channel_id=1, source_target_pairs={{0,4},{2,6},{4,0},{6,2},{8,12},{10,14},{12,8},{14,10},{16,20},{18,... | collective-permute-start | bytes 12296 | tf_op jit(solution)/shard_map/ppermute | solution.py:204
  219.4 3.6 %collective-permute-done.21 = f32[8,128]{1,0:T(8,128)S(1)} collective-permute-done((f32[8,128]{1,0:T(8,128)S(1)}, f32[8,128]{1,0:T(8,128)S(1)}, u32[]{:S(2)}, u32[]{:S(2)}) %collective-permute-start.21) | collective-permute-done | bytes 4128 | tf_op jit(solution)/shard_map/ppermute | solution.py:204
  223.0 4.6 %collective-permute-start.22 = (f32[8,128]{1,0:T(8,128)S(1)}, f32[8,128]{1,0:T(8,128)S(1)}, u32[]{:S(2)}, u32[]{:S(2)}) collective-permute-start(f32[8,128]{1,0:T(8,128)S(1)} %add.57), channel_id=1, source_target_pairs={{0,16},{2,18},{4,20},{6,22},{8,24},{10,26},{12,28},{14,30},{16,0},... | collective-permute-start | bytes 12296 | tf_op jit(solution)/shard_map/ppermute | solution.py:204
  232.8 8.1 %update.2 = (f32[2,8,24576]{2,1,0:T(8,128)}, f32[2,8,24576]{2,1,0:T(8,128)}, f32[2,8,24576]{2,1,0:T(8,128)}) custom-call(f32[2]{0:T(128)S(1)} %pad_maximum_fusion.scales_ref, f32[8,128]{1,0:T(8,128)S(1)} %add.59.squares_ref, f32[2,8,24576]{2,1,0:T(8,128)} %weights_ref.1, f32[2,8,24576]{2,1,0:T(8,128)} %first_ref.1, f32[2,8,24576]{2,1,0:T(8,128)} %second_ref.1, ...), custom_call_target="tpu_custom_call" | custom-call | bytes 11010048 | tf_op jit(solution)/shard_map/update/pallas_call | solution.py:176
  240.9 7.4 %update.3 = (f32[2,8,24576]{2,1,0:T(8,128)}, f32[2,8,24576]{2,1,0:T(8,128)}, f32[2,8,24576]{2,1,0:T(8,128)}) custom-call(f32[2]{0:T(128)S(1)} %pad_maximum_fusion.scales_ref, f32[8,128]{1,0:T(8,128)S(1)} %add.59.squares_ref, f32[2,8,24576]{2,1,0:T(8,128)S(1)} %collective-permute-done.1.rest_0_.weights_ref, ...), custom_call_target="tpu_custom_call" | custom-call | bytes 11010048 | tf_op jit(solution)/shard_map/update/pallas_call | solution.py:176
  (63 shorter events, 58.5 us)
Async XLA Ops:
  13.2 35.8 %collective-permute-start.10 = (f32[8,2,8,12288]{3,2,1,0:T(8,128)}, f32[8,2,8,12288]{3,2,1,0:T(8,128)}, u32[]{:S(2)}, u32[]{:S(2)}) collective-permute-start(f32[8,2,8,12288]{3,2,1,0:T(8,128)} %get-tuple-element.24), channel_id=1, source_target_pairs={{0,2},{2,0},{4,6},{6,4},{8,10},{10,8},{12,14},{14,12},{16,18},{18,... | collective-permute-start | bytes 18874376 | tf_op jit(solution)/shard_map/ppermute | solution.py:248
  25.1 40.8 %collective-permute-start = (f32[8,2,8,12288]{3,2,1,0:T(8,128)}, f32[8,2,8,12288]{3,2,1,0:T(8,128)}, u32[]{:S(2)}, u32[]{:S(2)}) collective-permute-start(f32[8,2,8,12288]{3,2,1,0:T(8,128)} %get-tuple-element.21), channel_id=1, source_target_pairs={{0,2},{2,0},{4,6},{6,4},{8,10},{10,8},{12,14},{14,12},{16,18},{18,... | collective-permute-start | bytes 18874376 | tf_op jit(solution)/shard_map/ppermute | solution.py:248
  25.2 23.9 %collective-permute-start.14 = (f32[2,8,24576]{2,1,0:T(8,128)}, f32[2,8,24576]{2,1,0:T(8,128)S(1)}, u32[]{:S(2)}, u32[]{:S(2)}) collective-permute-start(f32[2,8,24576]{2,1,0:T(8,128)} %first_ref.1), channel_id=1, source_target_pairs={{0,2},{2,4},{4,6},{6,8},{8,10},{10,12},{12,14},{14,16},{16,18},{18... | collective-permute-start | bytes 4718600 | tf_op jit(solution)/shard_map/ppermute | solution.py:236
  25.6 40.3 %collective-permute-start.1 = (f32[2,8,24576]{2,1,0:T(8,128)}, f32[2,8,24576]{2,1,0:T(8,128)S(1)}, u32[]{:S(2)}, u32[]{:S(2)}) collective-permute-start(f32[2,8,24576]{2,1,0:T(8,128)} %weights_ref.1), channel_id=1, source_target_pairs={{0,2},{2,4},{4,6},{6,8},{8,10},{10,12},{12,14},{14,16},{16,18},{18... | collective-permute-start | bytes 4718600 | tf_op jit(solution)/shard_map/ppermute | solution.py:236
  28.2 64.3 %collective-permute-start.3 = (f32[2,8,24576]{2,1,0:T(8,128)}, f32[2,8,24576]{2,1,0:T(8,128)}, u32[]{:S(2)}, u32[]{:S(2)}) collective-permute-start(f32[2,8,24576]{2,1,0:T(8,128)} %second_ref.1), channel_id=1, source_target_pairs={{0,2},{2,4},{4,6},{6,8},{8,10},{10,12},{12,14},{14,16},{16,18},{18... | collective-permute-start | bytes 4718600 | tf_op jit(solution)/shard_map/ppermute | solution.py:236
  52.0 30.1 %collective-permute-start.15 = (f32[2,8,12288]{2,1,0:T(8,128)S(1)}, f32[2,8,12288]{2,1,0:T(8,128)S(1)}, u32[]{:S(2)}, u32[]{:S(2)}) collective-permute-start(f32[2,8,12288]{2,1,0:T(8,128)S(1)} %shard_sum.27), channel_id=1, source_target_pairs={{0,4},{2,6},{8,0},{10,2},{16,8},{18,10},{24,16},{26,18},{28,24},{3... | collective-permute-start | bytes 2359304 | tf_op jit(solution)/shard_map/ppermute | solution.py:252
  68.9 33.2 %collective-permute-start.2 = (f32[2,8,12288]{2,1,0:T(8,128)S(1)}, f32[2,8,12288]{2,1,0:T(8,128)S(1)}, u32[]{:S(2)}, u32[]{:S(2)}) collective-permute-start(f32[2,8,12288]{2,1,0:T(8,128)S(1)} %shard_sum.16), channel_id=1, source_target_pairs={{0,8},{2,10},{8,16},{10,18},{16,24},{18,26},{24,28},{26,30},{28,20... | collective-permute-start | bytes 2359304 | tf_op jit(solution)/shard_map/ppermute | solution.py:252
  80.5 37.8 %collective-permute-start.11 = (f32[2,8,12288]{2,1,0:T(8,128)S(1)}, f32[2,8,12288]{2,1,0:T(8,128)S(1)}, u32[]{:S(2)}, u32[]{:S(2)}) collective-permute-start(f32[2,8,12288]{2,1,0:T(8,128)S(1)} %shard_sum.24), channel_id=1, source_target_pairs={{0,8},{2,10},{8,16},{10,18},{16,24},{18,26},{24,28},{26,30},{28,20... | collective-permute-start | bytes 2359304 | tf_op jit(solution)/shard_map/ppermute | solution.py:264
  85.1 36.3 %collective-permute-start.16 = (f32[2,8,12288]{2,1,0:T(8,128)S(1)}, f32[2,8,12288]{2,1,0:T(8,128)S(1)}, u32[]{:S(2)}, u32[]{:S(2)}) collective-permute-start(f32[2,8,12288]{2,1,0:T(8,128)S(1)} %shard_sum.28), channel_id=1, source_target_pairs={{0,4},{2,6},{8,0},{10,2},{16,8},{18,10},{24,16},{26,18},{28,24},{3... | collective-permute-start | bytes 2359304 | tf_op jit(solution)/shard_map/ppermute | solution.py:264
  88.5 37.9 %collective-permute-start.7 = (f32[2,8,12288]{2,1,0:T(8,128)S(1)}, f32[2,8,12288]{2,1,0:T(8,128)S(1)}, u32[]{:S(2)}, u32[]{:S(2)}) collective-permute-start(f32[2,8,12288]{2,1,0:T(8,128)S(1)} %shard_sum.20), channel_id=1, source_target_pairs={{0,4},{2,6},{8,0},{10,2},{16,8},{18,10},{24,16},{26,18},{28,24},{3... | collective-permute-start | bytes 2359304 | tf_op jit(solution)/shard_map/ppermute | solution.py:264
  105.1 25.8 %collective-permute-start.4 = (f32[2,8,12288]{2,1,0:T(8,128)S(1)}, f32[2,8,12288]{2,1,0:T(8,128)S(1)}, u32[]{:S(2)}, u32[]{:S(2)}) collective-permute-start(f32[2,8,12288]{2,1,0:T(8,128)S(1)} %shard_sum.17), channel_id=1, source_target_pairs={{0,8},{2,10},{8,16},{10,18},{16,24},{18,26},{24,28},{26,30},{28,20... | collective-permute-start | bytes 2359304 | tf_op jit(solution)/shard_map/ppermute | solution.py:264
  121.3 26.4 %collective-permute-start.12 = (f32[2,8,12288]{2,1,0:T(8,128)S(1)}, f32[2,8,12288]{2,1,0:T(8,128)S(1)}, u32[]{:S(2)}, u32[]{:S(2)}) collective-permute-start(f32[2,8,12288]{2,1,0:T(8,128)S(1)} %shard_sum.25), channel_id=1, source_target_pairs={{0,8},{2,10},{8,16},{10,18},{16,24},{18,26},{24,28},{26,30},{28,20... | collective-permute-start | bytes 2359304 | tf_op jit(solution)/shard_map/ppermute | solution.py:264
  124.4 26.4 %collective-permute-start.17 = (f32[2,8,12288]{2,1,0:T(8,128)S(1)}, f32[2,8,12288]{2,1,0:T(8,128)S(1)}, u32[]{:S(2)}, u32[]{:S(2)}) collective-permute-start(f32[2,8,12288]{2,1,0:T(8,128)S(1)} %shard_sum.29), channel_id=1, source_target_pairs={{0,4},{2,6},{8,0},{10,2},{16,8},{18,10},{24,16},{26,18},{28,24},{3... | collective-permute-start | bytes 2359304 | tf_op jit(solution)/shard_map/ppermute | solution.py:264
  129.4 32.3 %collective-permute-start.8 = (f32[2,8,12288]{2,1,0:T(8,128)S(1)}, f32[2,8,12288]{2,1,0:T(8,128)S(1)}, u32[]{:S(2)}, u32[]{:S(2)}) collective-permute-start(f32[2,8,12288]{2,1,0:T(8,128)S(1)} %shard_sum.21), channel_id=1, source_target_pairs={{0,4},{2,6},{8,0},{10,2},{16,8},{18,10},{24,16},{26,18},{28,24},{3... | collective-permute-start | bytes 2359304 | tf_op jit(solution)/shard_map/ppermute | solution.py:264
  133.8 32.9 %collective-permute-start.5 = (f32[2,8,12288]{2,1,0:T(8,128)S(1)}, f32[2,8,12288]{2,1,0:T(8,128)S(1)}, u32[]{:S(2)}, u32[]{:S(2)}) collective-permute-start(f32[2,8,12288]{2,1,0:T(8,128)S(1)} %shard_sum.18), channel_id=1, source_target_pairs={{0,8},{2,10},{8,16},{10,18},{16,24},{18,26},{24,28},{26,30},{28,20... | collective-permute-start | bytes 2359304 | tf_op jit(solution)/shard_map/ppermute | solution.py:264
  150.7 30.7 %collective-permute-start.13 = (f32[2,8,12288]{2,1,0:T(8,128)S(1)}, f32[2,8,12288]{2,1,0:T(8,128)S(1)}, u32[]{:S(2)}, u32[]{:S(2)}) collective-permute-start(f32[2,8,12288]{2,1,0:T(8,128)S(1)} %shard_sum.26), channel_id=1, source_target_pairs={{0,8},{2,10},{8,16},{10,18},{16,24},{18,26},{24,28},{26,30},{28,20... | collective-permute-start | bytes 2359304 | tf_op jit(solution)/shard_map/ppermute | solution.py:264
  153.8 27.7 %collective-permute-start.18 = (f32[2,8,12288]{2,1,0:T(8,128)S(1)}, f32[2,8,12288]{2,1,0:T(8,128)S(1)}, u32[]{:S(2)}, u32[]{:S(2)}) collective-permute-start(f32[2,8,12288]{2,1,0:T(8,128)S(1)} %shard_sum.30), channel_id=1, source_target_pairs={{0,4},{2,6},{8,0},{10,2},{16,8},{18,10},{24,16},{26,18},{28,24},{3... | collective-permute-start | bytes 2359304 | tf_op jit(solution)/shard_map/ppermute | solution.py:264
  164.7 30.3 %collective-permute-start.9 = (f32[2,8,12288]{2,1,0:T(8,128)S(1)}, f32[2,8,12288]{2,1,0:T(8,128)S(1)}, u32[]{:S(2)}, u32[]{:S(2)}) collective-permute-start(f32[2,8,12288]{2,1,0:T(8,128)S(1)} %shard_sum.22), channel_id=1, source_target_pairs={{0,4},{2,6},{8,0},{10,2},{16,8},{18,10},{24,16},{26,18},{28,24},{3... | collective-permute-start | bytes 2359304 | tf_op jit(solution)/shard_map/ppermute | solution.py:264
  169.8 28.5 %collective-permute-start.6 = (f32[2,8,12288]{2,1,0:T(8,128)S(1)}, f32[2,8,12288]{2,1,0:T(8,128)S(1)}, u32[]{:S(2)}, u32[]{:S(2)}) collective-permute-start(f32[2,8,12288]{2,1,0:T(8,128)S(1)} %shard_sum.19), channel_id=1, source_target_pairs={{0,8},{2,10},{8,16},{10,18},{16,24},{18,26},{24,28},{26,30},{28,20... | collective-permute-start | bytes 2359304 | tf_op jit(solution)/shard_map/ppermute | solution.py:264
  184.5 56.3 %collective-permute-start.25 = (f32[2,8,12288]{2,1,0:T(8,128)S(1)}, f32[2,8,12288]{2,1,0:T(8,128)S(1)}, u32[]{:S(2)}, u32[]{:S(2)}) collective-permute-start(f32[2,8,12288]{2,1,0:T(8,128)S(1)} %get-tuple-element.27.rest_1_), channel_id=1, source_target_pairs={{0,2},{2,4},{4,6},{6,8},{8,10},{10,12},{12,14},{14,16},{16,18},{18... | collective-permute-start | bytes 2359304 | tf_op jit(solution)/shard_map/ppermute | solution.py:268
  201.4 39.5 %collective-permute-start.24 = (f32[2,8,12288]{2,1,0:T(8,128)S(1)}, f32[2,8,12288]{2,1,0:T(8,128)S(1)}, u32[]{:S(2)}, u32[]{:S(2)}) collective-permute-start(f32[2,8,12288]{2,1,0:T(8,128)S(1)} %get-tuple-element.26.rest_0_), channel_id=1, source_target_pairs={{0,2},{2,4},{4,6},{6,8},{8,10},{10,12},{12,14},{14,16},{16,18},{18... | collective-permute-start | bytes 2359304 | tf_op jit(solution)/shard_map/ppermute | solution.py:268
  207.5 11.9 %collective-permute-start.20 = (f32[8,128]{1,0:T(8,128)S(1)}, f32[8,128]{1,0:T(8,128)S(1)}, u32[]{:S(2)}, u32[]{:S(2)}) collective-permute-start(f32[8,128]{1,0:T(8,128)S(1)} %add.55), channel_id=1, source_target_pairs={{0,4},{2,6},{4,0},{6,2},{8,12},{10,14},{12,8},{14,10},{16,20},{18,... | collective-permute-start | bytes 12296 | tf_op jit(solution)/shard_map/ppermute | solution.py:204
  223.0 6.2 %collective-permute-start.22 = (f32[8,128]{1,0:T(8,128)S(1)}, f32[8,128]{1,0:T(8,128)S(1)}, u32[]{:S(2)}, u32[]{:S(2)}) collective-permute-start(f32[8,128]{1,0:T(8,128)S(1)} %add.57), channel_id=1, source_target_pairs={{0,16},{2,18},{4,20},{6,22},{8,24},{10,26},{12,28},{14,30},{16,0},... | collective-permute-start | bytes 12296 | tf_op jit(solution)/shard_map/ppermute | solution.py:204
  229.2 3.6 %collective-permute-start.23 = (f32[8,128]{1,0:T(8,128)S(1)}, f32[8,128]{1,0:T(8,128)S(1)}, u32[]{:S(2)}, u32[]{:S(2)}) collective-permute-start(f32[8,128]{1,0:T(8,128)S(1)} %add.58), channel_id=1, source_target_pairs={{0,1},{1,0},{2,3},{3,2},{4,5},{5,4},{6,7},{7,6},{8,9},{9,8},{10,11... | collective-permute-start | bytes 12296 | tf_op jit(solution)/shard_map/ppermute | solution.py:204
  (2 other events, 5.5 us)

commit v3 on v2

--- a/solution.py
+++ b/solution.py
@@ -16,7 +16,7 @@
 
 streams = 2
 lanes = 128
-room = pltpu.CompilerParams(vmem_limit_bytes=48 * 2**20)
+room = pltpu.CompilerParams(vmem_limit_bytes=60 * 2**20)
 
 
 def block_of(columns, most):
@@ -44,7 +44,8 @@
     return (weights_new, first_new, second_new)
 
 
-def terms_kernel(order, layers, core_ref, inputs_ref, earlier_ref, outgrad_ref, keep_ref, give_ref):
+def terms_kernel(order, layers, core_ref, inputs_ref, earlier_ref, outgrad_ref, *rest):
+    keep_ref, give_ref = rest[-2:]
     core = core_ref[0]
     tokens, _, columns = outgrad_ref.shape
     rows = earlier_ref.shape[2]
@@ -60,12 +61,12 @@
             give_ref[place, layer] = jnp.where(core == 0, term[chip, 1], term[chip, 0])
 
 
-def make_terms(core, inputs, earlier, outgrad, order, start, width):
+def make_terms(core, inputs, earlier, outgrad, order, start, width, after=()):
     _, layers, rows, _ = earlier.shape
     tokens = outgrad.shape[0]
     chips = len(order)
     own = rows // (2 * chips)
-    size = block_of(width, 2048)
+    size = block_of(width, 6144)
     first = start // size
     return pl.pallas_call(
         functools.partial(terms_kernel, order, layers),
@@ -76,7 +77,8 @@
                 pl.BlockSpec(inputs.shape, lambda i, core: (0, 0)),
                 pl.BlockSpec((1, layers, rows, size), lambda i, core: (0, 0, 0, first + i)),
                 pl.BlockSpec((tokens, layers, size), lambda i, core: (0, 0, first + i)),
-            ],
+            ]
+            + [pl.BlockSpec(memory_space=pl.ANY)] * len(after),
             out_specs=[pl.BlockSpec((chips, layers, own, size), lambda i, core: (0, 0, 0, i))] * 2,
         ),
         out_shape=[jax.ShapeDtypeStruct((chips, layers, own, width), jnp.float32)] * 2,
@@ -86,7 +88,7 @@
             jax.ShapeDtypeStruct((layers, rows, width), jnp.float32),
         ),
         name="terms",
-    )(core, inputs, earlier, outgrad)
+    )(core, inputs, earlier, outgrad, *after)
 
 
 def plain_kernel(shard_ref, keep_ref, theirs_ref, *rest):
@@ -117,7 +119,7 @@
 
 def shard_sum(body, shards, which, keep, theirs, *arrived, after=()):
     _, layers, own, width = keep.shape
-    size = block_of(width, 3072)
+    size = block_of(width, 6144)
     chosen = pl.BlockSpec((1, layers, own, size), lambda i, shards: (shards[which], 0, 0, i))
     whole = pl.BlockSpec((layers, own, size), lambda i, shards: (0, 0, i))
     summed = jax.ShapeDtypeStruct((layers, own, width), jnp.float32)
@@ -170,7 +172,7 @@
     layers, own, columns = state[0].shape
     width = grads[0].shape[-1]
     count = len(grads)
-    size = block_of(width, 3072)
+    size = block_of(width, 12288)
     per = width // size
     block = pl.BlockSpec((layers, own, size), lambda i: (0, 0, i))
     return pl.pallas_call(
@@ -243,14 +245,15 @@
     keep, theirs, sent, grads, peer_grads = ([None] * streams for _ in range(5))
     for k in range(streams):
         keep[k], give = make_terms(
-            core.reshape(1), inputs, acc_grads, cotangent, order, k * width, width
+            core.reshape(1), inputs, acc_grads, cotangent, order, k * width, width,
+            after=old_copy[:1] if k == 1 else (),
         )
         theirs[k] = lax.ppermute(give, "dp", swap)
     for k in range(streams):
-        total = shard_sum(plain_kernel, tables[0], half, keep[k], theirs[k], after=old_copy[k : k + 1])
+        total = shard_sum(plain_kernel, tables[0], half, keep[k], theirs[k], after=old_copy[1:2] if k == 1 else ())
         sent[k] = [None, None]
         sent[k][k % 2] = lax.ppermute(total, "dp", hop(-1 if k % 2 else 1))
-    waiting = old_copy[streams:]
+    waiting = old_copy[2:]
     for away in range(half - 1, 0, -1):
         for k in range(streams):
             for way, by in enumerate((1, -1)):

time: 250 us -> 243 us (0.972)
  starting transfers between devices: 51.6 us -> 25.3 us
  local copies, waits for them, and re-layouts: 0.12 us -> 13.7 us
  waiting for transfers between devices: 108 us -> 119 us
  Pallas kernels: 86.2 us -> 77.4 us
  other arithmetic: 1.29 us -> 4.25 us
    unnamed x1 -> x35, local copies, waits for them, and re-layouts: 0.02 us -> 12.9 us
    ppermute x2, starting transfers between devices: 12.9 us -> 0.04 us  [local(): peer_grads[k] = lax.ppermute(grads[k], 'dp', onward)]
    ppermute x2, starting transfers between devices: 8.61 us -> 0.44 us  [local(): sent[k][k % 2] = lax.ppermute(total, 'dp', hop(-1 if k % 2 else 1))]
    ppermute x3, waiting for transfers between devices: 38.4 us -> 46.1 us  [local(): old_copy = [lax.ppermute(value, 'dp', onward) for value in state]]
    pallas_call x2, Pallas kernels: 15.5 us -> 10.5 us  [update(): pl.pallas_call(functools.partial(update_kernel, count, bound), grid=(colu...]
    ppermute x12, waiting for transfers between devices: 49.1 us -> 53.9 us  [local(): sent[k][way] = lax.ppermute(total, 'dp', hop(by))]
    pallas_call x2, Pallas kernels: 22.8 us -> 18.1 us  [make_terms(): pl.pallas_call(functools.partial(terms_kernel, order, layers), grid_spec=...]
    ppermute x5, starting transfers between devices: 16 us -> 12.2 us  [total_over(): lax.ppermute(value, axis, [(i, i ^ bit) for i in range(peers)])]
  transfers between devices with their start and end apart: 26 -> 26, of which waited for: 16 -> 17; matrix products, arithmetic and copies ran while one was open for 0% -> 2% of each run, Pallas kernels for 27% -> 30%
where the time goes in v3:
time: 243 us; the launch traced here: 241 us
  waiting for transfers between devices  119 us (49%)
  Pallas kernels  77.4 us (32%)
  starting transfers between devices  25.3 us (10%)
  local copies, waits for them, and re-layouts  13.7 us (6%)
  other arithmetic  4.25 us (2%)
    ppermute x12, waiting for transfers between devices, local(): sent[k][way] = lax.ppermute(total, 'dp', hop(by))  53.9 us
    pallas_call x16, Pallas kernels, shard_sum(): pl.pallas_call(body, grid_spec=pltpu.PrefetchScalarGridSpec(num_scalar_pr...  48.9 us
    ppermute x3, waiting for transfers between devices, local(): old_copy = [lax.ppermute(value, 'dp', onward) for value in state]  46.1 us
    pallas_call x2, Pallas kernels, make_terms(): pl.pallas_call(functools.partial(terms_kernel, order, layers), grid_spec=...  18.1 us
    unnamed x35, local copies, waits for them, and re-layouts  12.9 us
    ppermute x5, starting transfers between devices, total_over(): lax.ppermute(value, axis, [(i, i ^ bit) for i in range(peers)])  12.2 us
    pallas_call x2, Pallas kernels, update(): pl.pallas_call(functools.partial(update_kernel, count, bound), grid=(colu...  10.5 us
    ppermute x5, waiting for transfers between devices, total_over(): lax.ppermute(value, axis, [(i, i ^ bit) for i in range(peers)])  10.2 us
  transfers between devices with their start and end apart: 26, of which 17 were waited for; matrix products, arithmetic and copies ran while one was open for 2% of the time, Pallas kernels for 30%

profile of v3, /device:TPU:0, one launch (start us, length us, event | category | flops | bytes accessed | tf_op | source)
XLA Modules:
  0.0 240.8 jit_solution(1051016939340321606)
XLA Ops:
  2.9 9.1 %terms.2 = (f32[8,2,8,12288]{3,2,1,0:T(8,128)}, f32[8,2,8,12288]{3,2,1,0:T(8,128)}) custom-call(s32[1]{0:T(128)} %bitcast.core_ref, bf16[256,256]{1,0:T(8,128)(2,1)} %copy.14.inputs_ref, bf16[1,2,128,24576]{3,2,1,0:T(8,128)(2,1)} %earlier_ref.3, bf16[128,2,24576]{2,1,0:T(2,128)(2,1)} %outgrad_ref.3), custom_call_target="tpu_custom_call" | custom-call | bytes 25165824 | tf_op jit(solution)/shard_map/terms/pallas_call | solution.py:71
  14.6 9.8 %collective-permute-done.9.rest_0_.weights_ref = f32[2,8,24576]{2,1,0:T(8,128)S(1)} collective-permute-done((f32[2,8,24576]{2,1,0:T(8,128)}, f32[2,8,24576]{2,1,0:T(8,128)S(1)}, u32[]{:S(2)}, u32[]{:S(2)}) %collective-permute-start.9) | collective-permute-done | bytes 1572896 | tf_op jit(solution)/shard_map/ppermute | solution.py:238
  25.6 9.0 %terms.3 = (f32[8,2,8,12288]{3,2,1,0:T(8,128)}, f32[8,2,8,12288]{3,2,1,0:T(8,128)}) custom-call(s32[1]{0:T(128)} %bitcast.core_ref, bf16[256,256]{1,0:T(8,128)(2,1)} %copy.14.inputs_ref, bf16[1,2,128,24576]{3,2,1,0:T(8,128)(2,1)} %earlier_ref.3, bf16[128,2,24576]{2,1,0:T(2,128)(2,1)} %outgrad_ref.3, f32[2,8,24576]{2,1,0:T(8,128)} %copy-done), custom_call_target="tpu_custom_call" | custom-call | bytes 25165824 | tf_op jit(solution)/shard_map/terms/pallas_call | solution.py:71
  39.1 26.9 %collective-permute-done.14.rest_0_.first_ref = f32[2,8,24576]{2,1,0:T(8,128)S(1)} collective-permute-done((f32[2,8,24576]{2,1,0:T(8,128)}, f32[2,8,24576]{2,1,0:T(8,128)S(1)}, u32[]{:S(2)}, u32[]{:S(2)}) %collective-permute-start.14) | collective-permute-done | bytes 1572896 | tf_op jit(solution)/shard_map/ppermute | solution.py:238
  73.3 9.4 %collective-permute-done.2.rest_0_.second_ref = f32[2,8,24576]{2,1,0:T(8,128)S(1)} collective-permute-done((f32[2,8,24576]{2,1,0:T(8,128)}, f32[2,8,24576]{2,1,0:T(8,128)S(1)}, u32[]{:S(2)}, u32[]{:S(2)}) %collective-permute-start.2) | collective-permute-done | bytes 1572896 | tf_op jit(solution)/shard_map/ppermute | solution.py:238
  82.8 8.4 %collective-permute-done.1.arrived_ref = f32[2,8,12288]{2,1,0:T(8,128)} collective-permute-done((f32[2,8,12288]{2,1,0:T(8,128)}, f32[2,8,12288]{2,1,0:T(8,128)}, u32[]{:S(2)}, u32[]{:S(2)}) %collective-permute-start.1) | collective-permute-done | bytes 786464 | tf_op jit(solution)/shard_map/ppermute | solution.py:255
  91.2 3.1 %shard_sum.17 = f32[2,8,12288]{2,1,0:T(8,128)} custom-call(s32[6]{0:T(128)} %pad_add_fusion.shard_ref, f32[8,2,8,12288]{3,2,1,0:T(8,128)} %get-tuple-element.20.keep_ref, f32[8,2,8,12288]{3,2,1,0:T(8,128)} %collective-permute-done.theirs_ref, f32[2,8,12288]{2,1,0:T(8,128)} %collective-permute-done.1.arrived_ref, f32[2,8,24576]{2,1,0:T(8,128)} %copy-done.2), custom_call_target="tpu_custom_call" | custom-call | bytes 3145728 | tf_op jit(solution)/shard_map/shard_sum/pallas_call | solution.py:130
  104.1 3.1 %shard_sum.21 = f32[2,8,12288]{2,1,0:T(8,128)} custom-call(s32[6]{0:T(128)} %pad_add_fusion.1.shard_ref, f32[8,2,8,12288]{3,2,1,0:T(8,128)} %get-tuple-element.20.keep_ref, f32[8,2,8,12288]{3,2,1,0:T(8,128)} %collective-permute-done.theirs_ref, f32[2,8,12288]{2,1,0:T(8,128)} %copy-done.13), custom_call_target="tpu_custom_call" | custom-call | bytes 3145728 | tf_op jit(solution)/shard_map/shard_sum/pallas_call | solution.py:130
  109.6 5.4 %collective-permute-done.3.arrived_ref = f32[2,8,12288]{2,1,0:T(8,128)} collective-permute-done((f32[2,8,12288]{2,1,0:T(8,128)}, f32[2,8,12288]{2,1,0:T(8,128)}, u32[]{:S(2)}, u32[]{:S(2)}) %collective-permute-start.3) | collective-permute-done | bytes 786464 | tf_op jit(solution)/shard_map/ppermute | solution.py:267
  115.0 3.1 %shard_sum.18 = f32[2,8,12288]{2,1,0:T(8,128)} custom-call(s32[6]{0:T(128)} %pad_add_fusion.shard_ref, f32[8,2,8,12288]{3,2,1,0:T(8,128)} %get-tuple-element.20.keep_ref, f32[8,2,8,12288]{3,2,1,0:T(8,128)} %collective-permute-done.theirs_ref, f32[2,8,12288]{2,1,0:T(8,128)} %collective-permute-done.3.arrived_ref), custom_call_target="tpu_custom_call" | custom-call | bytes 3145728 | tf_op jit(solution)/shard_map/shard_sum/pallas_call | solution.py:130
  118.0 13.7 %collective-permute-done.11.arrived_ref = f32[2,8,12288]{2,1,0:T(8,128)S(1)} collective-permute-done((f32[2,8,12288]{2,1,0:T(8,128)}, f32[2,8,12288]{2,1,0:T(8,128)S(1)}, u32[]{:S(2)}, u32[]{:S(2)}) %collective-permute-start.11) | collective-permute-done | bytes 786464 | tf_op jit(solution)/shard_map/ppermute | solution.py:267
  132.6 3.1 %shard_sum.25 = f32[2,8,12288]{2,1,0:T(8,128)} custom-call(s32[6]{0:T(128)} %pad_add_fusion.shard_ref, f32[8,2,8,12288]{3,2,1,0:T(8,128)} %get-tuple-element.23.keep_ref, f32[8,2,8,12288]{3,2,1,0:T(8,128)} %collective-permute-done.10.theirs_ref, f32[2,8,12288]{2,1,0:T(8,128)} %copy-done.6), custom_call_target="tpu_custom_call" | custom-call | bytes 3145728 | tf_op jit(solution)/shard_map/shard_sum/pallas_call | solution.py:130
  136.5 3.1 %shard_sum.29 = f32[2,8,12288]{2,1,0:T(8,128)} custom-call(s32[6]{0:T(128)} %pad_add_fusion.1.shard_ref, f32[8,2,8,12288]{3,2,1,0:T(8,128)} %get-tuple-element.23.keep_ref, f32[8,2,8,12288]{3,2,1,0:T(8,128)} %collective-permute-done.10.theirs_ref, f32[2,8,12288]{2,1,0:T(8,128)} %copy-done.7), custom_call_target="tpu_custom_call" | custom-call | bytes 3145728 | tf_op jit(solution)/shard_map/shard_sum/pallas_call | solution.py:130
  142.5 3.1 %shard_sum.22 = f32[2,8,12288]{2,1,0:T(8,128)} custom-call(s32[6]{0:T(128)} %pad_add_fusion.1.shard_ref, f32[8,2,8,12288]{3,2,1,0:T(8,128)} %get-tuple-element.20.keep_ref, f32[8,2,8,12288]{3,2,1,0:T(8,128)} %collective-permute-done.theirs_ref, f32[2,8,12288]{2,1,0:T(8,128)} %copy-done.8), custom_call_target="tpu_custom_call" | custom-call | bytes 3145728 | tf_op jit(solution)/shard_map/shard_sum/pallas_call | solution.py:130
  152.5 13.0 %collective-permute-done.12.arrived_ref = f32[2,8,12288]{2,1,0:T(8,128)} collective-permute-done((f32[2,8,12288]{2,1,0:T(8,128)}, f32[2,8,12288]{2,1,0:T(8,128)}, u32[]{:S(2)}, u32[]{:S(2)}) %collective-permute-start.12) | collective-permute-done | bytes 786464 | tf_op jit(solution)/shard_map/ppermute | solution.py:267
  165.5 3.1 %shard_sum.26 = f32[2,8,12288]{2,1,0:T(8,128)} custom-call(s32[6]{0:T(128)} %pad_add_fusion.shard_ref, f32[8,2,8,12288]{3,2,1,0:T(8,128)} %get-tuple-element.23.keep_ref, f32[8,2,8,12288]{3,2,1,0:T(8,128)} %collective-permute-done.10.theirs_ref, f32[2,8,12288]{2,1,0:T(8,128)} %collective-permute-done.12.arrived_ref), custom_call_target="tpu_custom_call" | custom-call | bytes 3145728 | tf_op jit(solution)/shard_map/shard_sum/pallas_call | solution.py:130
  175.4 6.8 %collective-permute-done.5.up_ref = f32[2,8,12288]{2,1,0:T(8,128)S(1)} collective-permute-done((f32[2,8,12288]{2,1,0:T(8,128)}, f32[2,8,12288]{2,1,0:T(8,128)S(1)}, u32[]{:S(2)}, u32[]{:S(2)}) %collective-permute-start.5) | collective-permute-done | bytes 786464 | tf_op jit(solution)/shard_map/ppermute | solution.py:267
  183.1 3.4 %shard_sum.23 = (f32[2,8,12288]{2,1,0:T(8,128)}, f32[8,128]{1,0:T(8,128)}) custom-call(s32[6]{0:T(128)} %pad_add_fusion.shard_ref, f32[8,2,8,12288]{3,2,1,0:T(8,128)} %get-tuple-element.20.keep_ref, f32[8,2,8,12288]{3,2,1,0:T(8,128)} %collective-permute-done.theirs_ref, f32[2,8,12288]{2,1,0:T(8,128)} %copy-done.10, f32[2,8,12288]{2,1,0:T(8,128)} %copy-done.3), custom_call_target="tpu_custom_call" | custom-call | bytes 3932160 | tf_op jit(solution)/shard_map/shard_sum/pallas_call | solution.py:130
  186.6 11.6 %collective-permute-done.13.up_ref = f32[2,8,12288]{2,1,0:T(8,128)S(1)} collective-permute-done((f32[2,8,12288]{2,1,0:T(8,128)}, f32[2,8,12288]{2,1,0:T(8,128)S(1)}, u32[]{:S(2)}, u32[]{:S(2)}) %collective-permute-start.13) | collective-permute-done | bytes 786464 | tf_op jit(solution)/shard_map/ppermute | solution.py:267
  200.0 3.4 %shard_sum.31 = (f32[2,8,12288]{2,1,0:T(8,128)}, f32[8,128]{1,0:T(8,128)}) custom-call(s32[6]{0:T(128)} %pad_add_fusion.shard_ref, f32[8,2,8,12288]{3,2,1,0:T(8,128)} %get-tuple-element.23.keep_ref, f32[8,2,8,12288]{3,2,1,0:T(8,128)} %collective-permute-done.10.theirs_ref, f32[2,8,12288]{2,1,0:T(8,128)} %copy-done.4, f32[2,8,12288]{2,1,0:T(8,128)} %copy-done.11), custom_call_target="tpu_custom_call" | custom-call | bytes 3932160 | tf_op jit(solution)/shard_map/shard_sum/pallas_call | solution.py:130
  209.8 8.4 %collective-permute-start.21 = (f32[8,128]{1,0:T(8,128)S(1)}, f32[8,128]{1,0:T(8,128)S(1)}, u32[]{:S(2)}, u32[]{:S(2)}) collective-permute-start(f32[8,128]{1,0:T(8,128)S(1)} %add.56), channel_id=1, source_target_pairs={{0,8},{2,10},{4,12},{6,14},{8,0},{10,2},{12,4},{14,6},{16,24},{18,... | collective-permute-start | bytes 12296 | tf_op jit(solution)/shard_map/ppermute | solution.py:206
  220.6 3.8 %collective-permute-done.22 = f32[8,128]{1,0:T(8,128)S(1)} collective-permute-done((f32[8,128]{1,0:T(8,128)S(1)}, f32[8,128]{1,0:T(8,128)S(1)}, u32[]{:S(2)}, u32[]{:S(2)}) %collective-permute-start.22) | collective-permute-done | bytes 4128 | tf_op jit(solution)/shard_map/ppermute | solution.py:206
  228.5 5.2 %update.2 = (f32[2,8,24576]{2,1,0:T(8,128)}, f32[2,8,24576]{2,1,0:T(8,128)}, f32[2,8,24576]{2,1,0:T(8,128)}) custom-call(f32[2]{0:T(128)} %pad_maximum_fusion.scales_ref, f32[8,128]{1,0:T(8,128)} %add.59.squares_ref, f32[2,8,24576]{2,1,0:T(8,128)} %weights_ref.1, f32[2,8,24576]{2,1,0:T(8,128)} %first_ref.1, f32[2,8,24576]{2,1,0:T(8,128)} %second_ref.1, ...), custom_call_target="tpu_custom_call" | custom-call | bytes 11010048 | tf_op jit(solution)/shard_map/update/pallas_call | solution.py:178
  235.6 5.2 %update.3 = (f32[2,8,24576]{2,1,0:T(8,128)}, f32[2,8,24576]{2,1,0:T(8,128)}, f32[2,8,24576]{2,1,0:T(8,128)}) custom-call(f32[2]{0:T(128)} %pad_maximum_fusion.scales_ref, f32[8,128]{1,0:T(8,128)} %add.59.squares_ref, f32[2,8,24576]{2,1,0:T(8,128)} %copy-done, f32[2,8,24576]{2,1,0:T(8,128)} %copy-done.1, f32[2,8,24576]{2,1,0:T(8,128)} %copy-done.2, ...), custom_call_target="tpu_custom_call" | custom-call | bytes 11010048 | tf_op jit(solution)/shard_map/update/pallas_call | solution.py:178
  (97 shorter events, 65.3 us)
Async XLA Ops:
  0.6 23.8 %collective-permute-start.9 = (f32[2,8,24576]{2,1,0:T(8,128)}, f32[2,8,24576]{2,1,0:T(8,128)S(1)}, u32[]{:S(2)}, u32[]{:S(2)}) collective-permute-start(f32[2,8,24576]{2,1,0:T(8,128)} %weights_ref.1), channel_id=1, source_target_pairs={{0,2},{2,4},{4,6},{6,8},{8,10},{10,12},{12,14},{14,16},{16,18},{18... | collective-permute-start | bytes 4718600 | tf_op jit(solution)/shard_map/ppermute | solution.py:238
  12.0 23.8 %collective-permute-start = (f32[8,2,8,12288]{3,2,1,0:T(8,128)}, f32[8,2,8,12288]{3,2,1,0:T(8,128)}, u32[]{:S(2)}, u32[]{:S(2)}) collective-permute-start(f32[8,2,8,12288]{3,2,1,0:T(8,128)} %get-tuple-element.21), channel_id=1, source_target_pairs={{0,2},{2,0},{4,6},{6,4},{8,10},{10,8},{12,14},{14,12},{16,18},{18,... | collective-permute-start | bytes 18874376 | tf_op jit(solution)/shard_map/ppermute | solution.py:251
  34.6 31.3 %collective-permute-start.10 = (f32[8,2,8,12288]{3,2,1,0:T(8,128)}, f32[8,2,8,12288]{3,2,1,0:T(8,128)}, u32[]{:S(2)}, u32[]{:S(2)}) collective-permute-start(f32[8,2,8,12288]{3,2,1,0:T(8,128)} %get-tuple-element.24), channel_id=1, source_target_pairs={{0,2},{2,0},{4,6},{6,4},{8,10},{10,8},{12,14},{14,12},{16,18},{18,... | collective-permute-start | bytes 18874376 | tf_op jit(solution)/shard_map/ppermute | solution.py:251
  34.6 31.3 %collective-permute-start.14 = (f32[2,8,24576]{2,1,0:T(8,128)}, f32[2,8,24576]{2,1,0:T(8,128)S(1)}, u32[]{:S(2)}, u32[]{:S(2)}) collective-permute-start(f32[2,8,24576]{2,1,0:T(8,128)} %first_ref.1), channel_id=1, source_target_pairs={{0,2},{2,4},{4,6},{6,8},{8,10},{10,12},{12,14},{14,16},{16,18},{18... | collective-permute-start | bytes 4718600 | tf_op jit(solution)/shard_map/ppermute | solution.py:238
  35.1 47.7 %collective-permute-start.2 = (f32[2,8,24576]{2,1,0:T(8,128)}, f32[2,8,24576]{2,1,0:T(8,128)S(1)}, u32[]{:S(2)}, u32[]{:S(2)}) collective-permute-start(f32[2,8,24576]{2,1,0:T(8,128)} %second_ref.1), channel_id=1, source_target_pairs={{0,2},{2,4},{4,6},{6,8},{8,10},{10,12},{12,14},{14,16},{16,18},{18... | collective-permute-start | bytes 4718600 | tf_op jit(solution)/shard_map/ppermute | solution.py:238
  38.6 52.5 %collective-permute-start.1 = (f32[2,8,12288]{2,1,0:T(8,128)}, f32[2,8,12288]{2,1,0:T(8,128)}, u32[]{:S(2)}, u32[]{:S(2)}) collective-permute-start(f32[2,8,12288]{2,1,0:T(8,128)} %shard_sum.16), channel_id=1, source_target_pairs={{0,8},{2,10},{8,16},{10,18},{16,24},{18,26},{24,28},{26,30},{28,20... | collective-permute-start | bytes 2359304 | tf_op jit(solution)/shard_map/ppermute | solution.py:255
  69.9 27.2 %collective-permute-start.15 = (f32[2,8,12288]{2,1,0:T(8,128)}, f32[2,8,12288]{2,1,0:T(8,128)S(1)}, u32[]{:S(2)}, u32[]{:S(2)}) collective-permute-start(f32[2,8,12288]{2,1,0:T(8,128)} %shard_sum.27), channel_id=1, source_target_pairs={{0,4},{2,6},{8,0},{10,2},{16,8},{18,10},{24,16},{26,18},{28,24},{3... | collective-permute-start | bytes 2359304 | tf_op jit(solution)/shard_map/ppermute | solution.py:255
  73.3 29.9 %collective-permute-start.6 = (f32[2,8,12288]{2,1,0:T(8,128)}, f32[2,8,12288]{2,1,0:T(8,128)S(1)}, u32[]{:S(2)}, u32[]{:S(2)}) collective-permute-start(f32[2,8,12288]{2,1,0:T(8,128)} %shard_sum.20), channel_id=1, source_target_pairs={{0,4},{2,6},{8,0},{10,2},{16,8},{18,10},{24,16},{26,18},{28,24},{3... | collective-permute-start | bytes 2359304 | tf_op jit(solution)/shard_map/ppermute | solution.py:267
  94.2 20.7 %collective-permute-start.3 = (f32[2,8,12288]{2,1,0:T(8,128)}, f32[2,8,12288]{2,1,0:T(8,128)}, u32[]{:S(2)}, u32[]{:S(2)}) collective-permute-start(f32[2,8,12288]{2,1,0:T(8,128)} %shard_sum.17), channel_id=1, source_target_pairs={{0,8},{2,10},{8,16},{10,18},{16,24},{18,26},{24,28},{26,30},{28,20... | collective-permute-start | bytes 2359304 | tf_op jit(solution)/shard_map/ppermute | solution.py:267
  97.1 34.6 %collective-permute-start.11 = (f32[2,8,12288]{2,1,0:T(8,128)}, f32[2,8,12288]{2,1,0:T(8,128)S(1)}, u32[]{:S(2)}, u32[]{:S(2)}) collective-permute-start(f32[2,8,12288]{2,1,0:T(8,128)} %shard_sum.24), channel_id=1, source_target_pairs={{0,8},{2,10},{8,16},{10,18},{16,24},{18,26},{24,28},{26,30},{28,20... | collective-permute-start | bytes 2359304 | tf_op jit(solution)/shard_map/ppermute | solution.py:267
  101.0 34.6 %collective-permute-start.16 = (f32[2,8,12288]{2,1,0:T(8,128)}, f32[2,8,12288]{2,1,0:T(8,128)S(1)}, u32[]{:S(2)}, u32[]{:S(2)}) collective-permute-start(f32[2,8,12288]{2,1,0:T(8,128)} %shard_sum.28), channel_id=1, source_target_pairs={{0,4},{2,6},{8,0},{10,2},{16,8},{18,10},{24,16},{26,18},{28,24},{3... | collective-permute-start | bytes 2359304 | tf_op jit(solution)/shard_map/ppermute | solution.py:267
  107.2 34.5 %collective-permute-start.7 = (f32[2,8,12288]{2,1,0:T(8,128)}, f32[2,8,12288]{2,1,0:T(8,128)S(1)}, u32[]{:S(2)}, u32[]{:S(2)}) collective-permute-start(f32[2,8,12288]{2,1,0:T(8,128)} %shard_sum.21), channel_id=1, source_target_pairs={{0,4},{2,6},{8,0},{10,2},{16,8},{18,10},{24,16},{26,18},{28,24},{3... | collective-permute-start | bytes 2359304 | tf_op jit(solution)/shard_map/ppermute | solution.py:267
  118.0 30.5 %collective-permute-start.4 = (f32[2,8,12288]{2,1,0:T(8,128)}, f32[2,8,12288]{2,1,0:T(8,128)S(1)}, u32[]{:S(2)}, u32[]{:S(2)}) collective-permute-start(f32[2,8,12288]{2,1,0:T(8,128)} %shard_sum.18), channel_id=1, source_target_pairs={{0,8},{2,10},{8,16},{10,18},{16,24},{18,26},{24,28},{26,30},{28,20... | collective-permute-start | bytes 2359304 | tf_op jit(solution)/shard_map/ppermute | solution.py:267
  135.7 29.9 %collective-permute-start.12 = (f32[2,8,12288]{2,1,0:T(8,128)}, f32[2,8,12288]{2,1,0:T(8,128)}, u32[]{:S(2)}, u32[]{:S(2)}) collective-permute-start(f32[2,8,12288]{2,1,0:T(8,128)} %shard_sum.25), channel_id=1, source_target_pairs={{0,8},{2,10},{8,16},{10,18},{16,24},{18,26},{24,28},{26,30},{28,20... | collective-permute-start | bytes 2359304 | tf_op jit(solution)/shard_map/ppermute | solution.py:267
  139.6 29.0 %collective-permute-start.17 = (f32[2,8,12288]{2,1,0:T(8,128)}, f32[2,8,12288]{2,1,0:T(8,128)S(1)}, u32[]{:S(2)}, u32[]{:S(2)}) collective-permute-start(f32[2,8,12288]{2,1,0:T(8,128)} %shard_sum.29), channel_id=1, source_target_pairs={{0,4},{2,6},{8,0},{10,2},{16,8},{18,10},{24,16},{26,18},{28,24},{3... | collective-permute-start | bytes 2359304 | tf_op jit(solution)/shard_map/ppermute | solution.py:267
  145.6 29.8 %collective-permute-start.8 = (f32[2,8,12288]{2,1,0:T(8,128)}, f32[2,8,12288]{2,1,0:T(8,128)S(1)}, u32[]{:S(2)}, u32[]{:S(2)}) collective-permute-start(f32[2,8,12288]{2,1,0:T(8,128)} %shard_sum.22), channel_id=1, source_target_pairs={{0,4},{2,6},{8,0},{10,2},{16,8},{18,10},{24,16},{26,18},{28,24},{3... | collective-permute-start | bytes 2359304 | tf_op jit(solution)/shard_map/ppermute | solution.py:267
  152.5 29.8 %collective-permute-start.5 = (f32[2,8,12288]{2,1,0:T(8,128)}, f32[2,8,12288]{2,1,0:T(8,128)S(1)}, u32[]{:S(2)}, u32[]{:S(2)}) collective-permute-start(f32[2,8,12288]{2,1,0:T(8,128)} %shard_sum.19), channel_id=1, source_target_pairs={{0,8},{2,10},{8,16},{10,18},{16,24},{18,26},{24,28},{26,30},{28,20... | collective-permute-start | bytes 2359304 | tf_op jit(solution)/shard_map/ppermute | solution.py:267
  168.6 29.6 %collective-permute-start.13 = (f32[2,8,12288]{2,1,0:T(8,128)}, f32[2,8,12288]{2,1,0:T(8,128)S(1)}, u32[]{:S(2)}, u32[]{:S(2)}) collective-permute-start(f32[2,8,12288]{2,1,0:T(8,128)} %shard_sum.26), channel_id=1, source_target_pairs={{0,8},{2,10},{8,16},{10,18},{16,24},{18,26},{24,28},{26,30},{28,20... | collective-permute-start | bytes 2359304 | tf_op jit(solution)/shard_map/ppermute | solution.py:267
  172.6 25.6 %collective-permute-start.18 = (f32[2,8,12288]{2,1,0:T(8,128)}, f32[2,8,12288]{2,1,0:T(8,128)S(1)}, u32[]{:S(2)}, u32[]{:S(2)}) collective-permute-start(f32[2,8,12288]{2,1,0:T(8,128)} %shard_sum.30), channel_id=1, source_target_pairs={{0,4},{2,6},{8,0},{10,2},{16,8},{18,10},{24,16},{26,18},{28,24},{3... | collective-permute-start | bytes 2359304 | tf_op jit(solution)/shard_map/ppermute | solution.py:267
  186.6 47.2 %collective-permute-start.24 = (f32[2,8,12288]{2,1,0:T(8,128)}, f32[2,8,12288]{2,1,0:T(8,128)S(1)}, u32[]{:S(2)}, u32[]{:S(2)}) collective-permute-start(f32[2,8,12288]{2,1,0:T(8,128)} %get-tuple-element.26.rest_0_), channel_id=1, source_target_pairs={{0,2},{2,4},{4,6},{6,8},{8,10},{10,12},{12,14},{14,16},{16,18},{18... | collective-permute-start | bytes 2359304 | tf_op jit(solution)/shard_map/ppermute | solution.py:271
  203.4 30.4 %collective-permute-start.25 = (f32[2,8,12288]{2,1,0:T(8,128)}, f32[2,8,12288]{2,1,0:T(8,128)S(1)}, u32[]{:S(2)}, u32[]{:S(2)}) collective-permute-start(f32[2,8,12288]{2,1,0:T(8,128)} %get-tuple-element.27.rest_1_), channel_id=1, source_target_pairs={{0,2},{2,4},{4,6},{6,8},{8,10},{10,12},{12,14},{14,16},{16,18},{18... | collective-permute-start | bytes 2359304 | tf_op jit(solution)/shard_map/ppermute | solution.py:271
  205.8 4.0 %collective-permute-start.20 = (f32[8,128]{1,0:T(8,128)S(1)}, f32[8,128]{1,0:T(8,128)S(1)}, u32[]{:S(2)}, u32[]{:S(2)}) collective-permute-start(f32[8,128]{1,0:T(8,128)S(1)} %add.55), channel_id=1, source_target_pairs={{0,4},{2,6},{4,0},{6,2},{8,12},{10,14},{12,8},{14,10},{16,20},{18,... | collective-permute-start | bytes 12296 | tf_op jit(solution)/shard_map/ppermute | solution.py:206
  209.8 10.0 %collective-permute-start.21 = (f32[8,128]{1,0:T(8,128)S(1)}, f32[8,128]{1,0:T(8,128)S(1)}, u32[]{:S(2)}, u32[]{:S(2)}) collective-permute-start(f32[8,128]{1,0:T(8,128)S(1)} %add.56), channel_id=1, source_target_pairs={{0,8},{2,10},{4,12},{6,14},{8,0},{10,2},{12,4},{14,6},{16,24},{18,... | collective-permute-start | bytes 12296 | tf_op jit(solution)/shard_map/ppermute | solution.py:206
  219.8 4.5 %collective-permute-start.22 = (f32[8,128]{1,0:T(8,128)S(1)}, f32[8,128]{1,0:T(8,128)S(1)}, u32[]{:S(2)}, u32[]{:S(2)}) collective-permute-start(f32[8,128]{1,0:T(8,128)S(1)} %add.57), channel_id=1, source_target_pairs={{0,16},{2,18},{4,20},{6,22},{8,24},{10,26},{12,28},{14,30},{16,0},... | collective-permute-start | bytes 12296 | tf_op jit(solution)/shard_map/ppermute | solution.py:206
  (19 other events, 50.4 us)

commit v4 on v2

--- a/solution.py
+++ b/solution.py
@@ -16,7 +16,7 @@
 
 streams = 2
 lanes = 128
-room = pltpu.CompilerParams(vmem_limit_bytes=48 * 2**20)
+room = pltpu.CompilerParams(vmem_limit_bytes=60 * 2**20)
 
 
 def block_of(columns, most):
@@ -44,7 +44,8 @@
     return (weights_new, first_new, second_new)
 
 
-def terms_kernel(order, layers, core_ref, inputs_ref, earlier_ref, outgrad_ref, keep_ref, give_ref):
+def terms_kernel(order, layers, core_ref, inputs_ref, earlier_ref, outgrad_ref, *rest):
+    keep_ref, gives = rest[-1 - layers], rest[-layers:]
     core = core_ref[0]
     tokens, _, columns = outgrad_ref.shape
     rows = earlier_ref.shape[2]
@@ -57,7 +58,7 @@
         term = term.reshape(chips, 2, rows // (2 * chips), columns)
         for place, chip in enumerate(order):
             keep_ref[place, layer] = jnp.where(core == 0, term[chip, 0], term[chip, 1])
-            give_ref[place, layer] = jnp.where(core == 0, term[chip, 1], term[chip, 0])
+            gives[layer][place] = jnp.where(core == 0, term[chip, 1], term[chip, 0])
 
 
 def make_terms(core, inputs, earlier, outgrad, order, start, width):
@@ -65,7 +66,7 @@
     tokens = outgrad.shape[0]
     chips = len(order)
     own = rows // (2 * chips)
-    size = block_of(width, 2048)
+    size = block_of(width, 6144)
     first = start // size
     return pl.pallas_call(
         functools.partial(terms_kernel, order, layers),
@@ -77,9 +78,11 @@
                 pl.BlockSpec((1, layers, rows, size), lambda i, core: (0, 0, 0, first + i)),
                 pl.BlockSpec((tokens, layers, size), lambda i, core: (0, 0, first + i)),
             ],
-            out_specs=[pl.BlockSpec((chips, layers, own, size), lambda i, core: (0, 0, 0, i))] * 2,
+            out_specs=[pl.BlockSpec((chips, layers, own, size), lambda i, core: (0, 0, 0, i))]
+            + [pl.BlockSpec((chips, own, size), lambda i, core: (0, 0, i))] * layers,
         ),
-        out_shape=[jax.ShapeDtypeStruct((chips, layers, own, width), jnp.float32)] * 2,
+        out_shape=[jax.ShapeDtypeStruct((chips, layers, own, width), jnp.float32)]
+        + [jax.ShapeDtypeStruct((chips, own, width), jnp.float32)] * layers,
         compiler_params=room,
         cost_estimate=cost_of(
             jax.ShapeDtypeStruct((layers, rows + tokens, width), earlier.dtype),
@@ -89,21 +92,26 @@
     )(core, inputs, earlier, outgrad)
 
 
-def plain_kernel(shard_ref, keep_ref, theirs_ref, *rest):
-    out_ref = rest[-1]
-    out_ref[...] = keep_ref[0] + theirs_ref[0]
-
-
-def step_kernel(shard_ref, keep_ref, theirs_ref, arrived_ref, *rest):
-    out_ref = rest[-1]
-    out_ref[...] = arrived_ref[...] + (keep_ref[0] + theirs_ref[0])
-
-
-def last_kernel(shard_ref, keep_ref, theirs_ref, up_ref, down_ref, *rest):
+def both_cores(keep_ref, theirs):
+    return jnp.stack([keep_ref[0, layer] + theirs_ref[0] for layer, theirs_ref in enumerate(theirs)])
+
+
+def plain_kernel(layers, shard_ref, keep_ref, *rest):
+    theirs, out_ref = rest[:layers], rest[-1]
+    out_ref[...] = both_cores(keep_ref, theirs)
+
+
+def step_kernel(layers, shard_ref, keep_ref, *rest):
+    theirs, arrived_ref, out_ref = rest[:layers], rest[layers], rest[-1]
+    out_ref[...] = arrived_ref[...] + both_cores(keep_ref, theirs)
+
+
+def last_kernel(layers, shard_ref, keep_ref, *rest):
+    theirs, up_ref, down_ref = rest[:layers], rest[layers], rest[layers + 1]
     out_ref, squares_ref = rest[-2:]
-    grad = (up_ref[...] + down_ref[...]) + (keep_ref[0] + theirs_ref[0])
+    grad = (up_ref[...] + down_ref[...]) + both_cores(keep_ref, theirs)
     out_ref[...] = grad
-    layers, own, columns = grad.shape
+    _, own, columns = grad.shape
     squares = jnp.sum((grad * grad).reshape(layers, own, columns // lanes, lanes), axis=(0, 2))
 
     @pl.when(pl.program_id(0) == 0)
@@ -117,8 +125,9 @@
 
 def shard_sum(body, shards, which, keep, theirs, *arrived, after=()):
     _, layers, own, width = keep.shape
-    size = block_of(width, 3072)
+    size = block_of(width, 6144)
     chosen = pl.BlockSpec((1, layers, own, size), lambda i, shards: (shards[which], 0, 0, i))
+    layer = pl.BlockSpec((1, own, size), lambda i, shards: (shards[which], 0, i))
     whole = pl.BlockSpec((layers, own, size), lambda i, shards: (0, 0, i))
     summed = jax.ShapeDtypeStruct((layers, own, width), jnp.float32)
     out_shape, out_specs = summed, whole
@@ -126,11 +135,12 @@
         out_shape = [summed, jax.ShapeDtypeStruct((own, lanes), jnp.float32)]
         out_specs = [whole, pl.BlockSpec((own, lanes), lambda i, shards: (0, 0))]
     return pl.pallas_call(
-        body,
+        functools.partial(body, layers),
         grid_spec=pltpu.PrefetchScalarGridSpec(
             num_scalar_prefetch=1,
             grid=(width // size,),
-            in_specs=[chosen, chosen]
+            in_specs=[chosen]
+            + [layer] * layers
             + [whole] * len(arrived)
             + [pl.BlockSpec(memory_space=pl.ANY)] * len(after),
             out_specs=out_specs,
@@ -139,60 +149,59 @@
         compiler_params=room,
         cost_estimate=cost_of(*[summed] * (3 + len(arrived))),
         name="shard_sum",
-    )(shards, keep, theirs, *arrived, *after)
-
-
-def update_kernel(count, bound, scales_ref, squares_ref, weights_ref, first_ref, second_ref, *rest):
-    grads, outs = rest[:count], rest[count:]
+    )(shards, keep, *theirs, *arrived, *after)
+
+
+def update_kernel(count, bound, scales_ref, squares_ref, *rest):
+    states, grads, outs = (rest[:3], rest[3:6]), rest[6 : 6 + 2 * count], rest[6 + 2 * count :]
     step = pl.program_id(0)
-    per = pl.num_programs(0) // count
+    per = pl.num_programs(0) // (2 * count)
     factor = jnp.minimum(
         jnp.float32(1.0), bound / (jnp.sqrt(jnp.sum(squares_ref[...])) + jnp.float32(1e-06))
     )
     for index, grad_ref in enumerate(grads):
 
         @pl.when(step // per == index)
-        def _(grad_ref=grad_ref):
+        def _(index=index, grad_ref=grad_ref):
+            who = index // count
             new = adamw_update(
-                weights_ref[...],
-                first_ref[...],
-                second_ref[...],
+                *[ref[...] for ref in states[who]],
                 grad_ref[...],
                 factor,
                 scales_ref[0],
                 scales_ref[1],
             )
-            for out_ref, value in zip(outs, new):
+            for out_ref, value in zip(outs[3 * who : 3 * who + 3], new):
                 out_ref[...] = value
 
 
-def update(scales, squares, state, grads, bound):
+def update(scales, squares, state, grads, old_copy, peer_grads, bound):
     layers, own, columns = state[0].shape
     width = grads[0].shape[-1]
     count = len(grads)
-    size = block_of(width, 3072)
-    per = width // size
-    block = pl.BlockSpec((layers, own, size), lambda i: (0, 0, i))
+    size = block_of(width, 12288)
+    per, blocks = width // size, columns // size
+    shape = (layers, own, size)
+
+    def part(first, many, row=0):
+        return pl.BlockSpec(shape, lambda i: (row, 0, jnp.clip(i - first, 0, many - 1)))
+
     return pl.pallas_call(
         functools.partial(update_kernel, count, bound),
-        grid=(columns // size,),
+        grid=(2 * blocks,),
         in_specs=[
             pl.BlockSpec(memory_space=pltpu.SMEM),
             pl.BlockSpec(squares.shape, lambda i: (0, 0)),
         ]
-        + [block] * 3
-        + [
-            pl.BlockSpec(
-                (layers, own, size), lambda i, k=k: (0, 0, jnp.clip(i - k * per, 0, per - 1))
-            )
-            for k in range(count)
-        ],
-        out_specs=[block] * 3,
-        out_shape=[jax.ShapeDtypeStruct((layers, own, columns), jnp.float32)] * 3,
+        + [part(0, blocks)] * 3
+        + [part(blocks, blocks, row) for row in range(3)]
+        + [part(k * per, per) for k in range(2 * count)],
+        out_specs=[part(0, blocks)] * 3 + [part(blocks, blocks)] * 3,
+        out_shape=[jax.ShapeDtypeStruct((layers, own, columns), jnp.float32)] * 6,
         compiler_params=room,
-        cost_estimate=cost_of(*[state[0]] * 7),
+        cost_estimate=cost_of(*[state[0]] * 14),
         name="update",
-    )(scales, squares, *state, *grads)
+    )(scales, squares, *state, *[old_copy] * 3, *grads, *peer_grads)
 
 
 def total_over(value, axis):
@@ -233,7 +242,7 @@
     ]
 
     state = (params, first_moment, second_moment)
-    old_copy = [lax.ppermute(value, "dp", onward) for value in state]
+    old_copy = lax.ppermute(jnp.concatenate(state), "dp", onward)
 
     same = jnp.eye(layers, dtype=activations.dtype)
     inputs = activations.transpose(1, 2, 0)[:, :, :, None] * same[:, None, None, :]
@@ -242,25 +251,22 @@
     width = columns // streams
     keep, theirs, sent, grads, peer_grads = ([None] * streams for _ in range(5))
     for k in range(streams):
-        keep[k], give = make_terms(
+        keep[k], *gives = make_terms(
             core.reshape(1), inputs, acc_grads, cotangent, order, k * width, width
         )
-        theirs[k] = lax.ppermute(give, "dp", swap)
+        theirs[k] = [lax.ppermute(give, "dp", swap) for give in gives]
     for k in range(streams):
-        total = shard_sum(plain_kernel, tables[0], half, keep[k], theirs[k], after=old_copy[k : k + 1])
+        total = shard_sum(
+            plain_kernel, tables[0], half, keep[k], theirs[k], after=() if k else [old_copy]
+        )
         sent[k] = [None, None]
         sent[k][k % 2] = lax.ppermute(total, "dp", hop(-1 if k % 2 else 1))
-    waiting = old_copy[streams:]
     for away in range(half - 1, 0, -1):
         for k in range(streams):
             for way, by in enumerate((1, -1)):
-                arrived, after = [], ()
-                if sent[k][way] is not None:
-                    arrived, after, waiting = [sent[k][way]], waiting, ()
+                arrived = [] if sent[k][way] is None else [sent[k][way]]
                 body = step_kernel if arrived else plain_kernel
-                total = shard_sum(
-                    body, tables[way], away, keep[k], theirs[k], *arrived, after=after
-                )
+                total = shard_sum(body, tables[way], away, keep[k], theirs[k], *arrived)
                 sent[k][way] = lax.ppermute(total, "dp", hop(by))
     squares = None
     for k in range(streams):
@@ -277,9 +283,7 @@
             1.0 - jnp.power(jnp.float32(beta_two), count),
         ]
     )
-    new = update(scales, squares, state, grads, bound)
-    copies = update(scales, squares, old_copy, peer_grads, bound)
-    return (*new, *copies)
+    return tuple(update(scales, squares, state, grads, old_copy, peer_grads, bound))
 
 
 def solution(mesh):

time: 250 us -> 237 us (0.948)
  starting transfers between devices: 51.6 us -> 33.3 us
  local copies, waits for them, and re-layouts: 0.12 us -> 13.1 us
  Pallas kernels: 86.2 us -> 78.1 us
  other arithmetic: 1.29 us -> 8.14 us
  waiting for transfers between devices: 108 us -> 102 us
    ppermute x2, starting transfers between devices: 12.9 us -> 0.03 us  [local(): peer_grads[k] = lax.ppermute(grads[k], 'dp', onward)]
    ppermute x5, starting transfers between devices: 16 us -> 3.48 us  [total_over(): lax.ppermute(value, axis, [(i, i ^ bit) for i in range(peers)])]
    unnamed x1 -> x37, local copies, waits for them, and re-layouts: 0.02 us -> 12.3 us
    ppermute x5, waiting for transfers between devices: 38.5 us -> 29.9 us  [the longest x1 24.8 us: local(): old_copy = lax.ppermute(jnp.concatenate(state), 'dp', onward)]
    ppermute x12, starting transfers between devices: 10.4 us -> 16 us  [local(): sent[k][way] = lax.ppermute(total, 'dp', hop(by))]
    concatenate x0 -> x1, other arithmetic: none -> 4.86 us  [local(): old_copy = lax.ppermute(jnp.concatenate(state), 'dp', onward)]
    pallas_call x2, Pallas kernels: 22.8 us -> 18.1 us  [make_terms(): pl.pallas_call(functools.partial(terms_kernel, order, layers), grid_spec=...]
    pallas_call x18 -> x17, Pallas kernels: 63.3 us -> 60.1 us  [the longest x16 49.7 us: shard_sum(): pl.pallas_call(functools.partial(body, layers), grid_spec=pltpu.PrefetchS...]
  transfers between devices with their start and end apart: 26 -> 26, of which waited for: 16 -> 16; matrix products, arithmetic and copies ran while one was open for 0% -> 2% of each run, Pallas kernels for 27% -> 29%
where the time goes in v4:
time: 237 us; the launch traced here: 236 us
  waiting for transfers between devices  102 us (43%)
  Pallas kernels  78.1 us (33%)
  starting transfers between devices  33.3 us (14%)
  local copies, waits for them, and re-layouts  13.1 us (6%)
  other arithmetic  8.14 us (3%)
    ppermute x12, waiting for transfers between devices, local(): sent[k][way] = lax.ppermute(total, 'dp', hop(by))  52.2 us
    pallas_call x16, Pallas kernels, shard_sum(): pl.pallas_call(functools.partial(body, layers), grid_spec=pltpu.PrefetchS...  49.7 us
    ppermute x1, waiting for transfers between devices, local(): old_copy = lax.ppermute(jnp.concatenate(state), 'dp', onward)  24.8 us
    pallas_call x2, Pallas kernels, make_terms(): pl.pallas_call(functools.partial(terms_kernel, order, layers), grid_spec=...  18.1 us
    ppermute x12, starting transfers between devices, local(): sent[k][way] = lax.ppermute(total, 'dp', hop(by))  16 us
    ppermute x5, waiting for transfers between devices, total_over(): lax.ppermute(value, axis, [(i, i ^ bit) for i in range(peers)])  13.3 us
    unnamed x37, local copies, waits for them, and re-layouts  12.3 us
    pallas_call x1, Pallas kernels, update(): pl.pallas_call(functools.partial(update_kernel, count, bound), grid=(2 *...  10.4 us
  transfers between devices with their start and end apart: 26, of which 16 were waited for; matrix products, arithmetic and copies ran while one was open for 2% of the time, Pallas kernels for 29%

profile of v4, /device:TPU:0, one launch (start us, length us, event | category | flops | bytes accessed | tf_op | source)
XLA Modules:
  0.0 236.4 jit_solution(7504705973129215152)
XLA Ops:
  0.6 4.9 %pad_maximum_fusion = f32[6,8,24576]{2,1,0:T(8,128)} fusion(f32[2,8,24576]{2,1,0:T(8,128)} %rest_2_.1, f32[2,8,24576]{2,1,0:T(8,128)} %rest_1_.1, f32[2,8,24576]{2,1,0:T(8,128)} %rest_0_.1), kind=kLoop, calls=%fused_computation | loop fusion | flops 2359296 | bytes 9437184 | tf_op jit(solution)/shard_map/concatenate | solution.py:245
  6.9 9.1 %terms.3 = (f32[8,2,8,12288]{3,2,1,0:T(8,128)}, f32[8,8,12288]{2,1,0:T(8,128)}, f32[8,8,12288]{2,1,0:T(8,128)}) custom-call(s32[1]{0:T(128)} %bitcast.core_ref, bf16[256,256]{1,0:T(8,128)(2,1)} %copy.14.inputs_ref, bf16[1,2,128,24576]{3,2,1,0:T(8,128)(2,1)} %earlier_ref.3, bf16[128,2,24576]{2,1,0:T(2,128)(2,1)} %outgrad_ref.3), custom_call_target="tpu_custom_call" | custom-call | bytes 25165824 | tf_op jit(solution)/shard_map/terms/pallas_call | solution.py:71
  18.6 9.0 %terms.2 = (f32[8,2,8,12288]{3,2,1,0:T(8,128)}, f32[8,8,12288]{2,1,0:T(8,128)}, f32[8,8,12288]{2,1,0:T(8,128)}) custom-call(s32[1]{0:T(128)} %bitcast.core_ref, bf16[256,256]{1,0:T(8,128)(2,1)} %copy.14.inputs_ref, bf16[1,2,128,24576]{3,2,1,0:T(8,128)(2,1)} %earlier_ref.3, bf16[128,2,24576]{2,1,0:T(2,128)(2,1)} %outgrad_ref.3), custom_call_target="tpu_custom_call" | custom-call | bytes 25165824 | tf_op jit(solution)/shard_map/terms/pallas_call | solution.py:71
  33.2 4.8 %collective-permute-done.rest_0_ = f32[8,8,12288]{2,1,0:T(8,128)S(1)} collective-permute-done((f32[8,8,12288]{2,1,0:T(8,128)}, f32[8,8,12288]{2,1,0:T(8,128)S(1)}, u32[]{:S(2)}, u32[]{:S(2)}) %collective-permute-start) | collective-permute-done | bytes 3145760 | tf_op jit(solution)/shard_map/ppermute | solution.py:257
  38.2 24.8 %collective-permute-done.2.rest_2_.rest_3_.rest_4_.rest_5_ = f32[6,8,24576]{2,1,0:T(8,128)} collective-permute-done((f32[6,8,24576]{2,1,0:T(8,128)}, f32[6,8,24576]{2,1,0:T(8,128)}, u32[]{:S(2)}, u32[]{:S(2)}) %collective-permute-start.2) | collective-permute-done | bytes 4718624 | tf_op jit(solution)/shard_map/ppermute | solution.py:245
  65.9 8.7 %collective-permute-start.3 = (f32[2,8,12288]{2,1,0:T(8,128)}, f32[2,8,12288]{2,1,0:T(8,128)S(1)}, u32[]{:S(2)}, u32[]{:S(2)}) collective-permute-start(f32[2,8,12288]{2,1,0:T(8,128)} %shard_sum.16), channel_id=1, source_target_pairs={{0,8},{2,10},{8,16},{10,18},{16,24},{18,26},{24,28},{26,30},{28,20... | collective-permute-start | bytes 2359304 | tf_op jit(solution)/shard_map/ppermute | solution.py:263
  79.6 3.1 %shard_sum.28 = f32[2,8,12288]{2,1,0:T(8,128)} custom-call(s32[6]{0:T(128)} %pad_add_fusion.1.shard_ref, f32[8,2,8,12288]{3,2,1,0:T(8,128)} %get-tuple-element.20.keep_ref, f32[8,8,12288]{2,1,0:T(8,128)} %collective-permute-done.10.rest_0_, f32[8,8,12288]{2,1,0:T(8,128)} %collective-permute-done.11.rest_1_, f32[2,8,12288]{2,1,0:T(8,128)} %collective-permute-done.15.rest_2_), custom_call_target="tpu_custom_call" | custom-call | bytes 3145728 | tf_op jit(solution)/shard_map/shard_sum/pallas_call | solution.py:137
  86.1 6.8 %collective-permute-done.3.rest_2_ = f32[2,8,12288]{2,1,0:T(8,128)S(1)} collective-permute-done((f32[2,8,12288]{2,1,0:T(8,128)}, f32[2,8,12288]{2,1,0:T(8,128)S(1)}, u32[]{:S(2)}, u32[]{:S(2)}) %collective-permute-start.3) | collective-permute-done | bytes 786464 | tf_op jit(solution)/shard_map/ppermute | solution.py:263
  93.8 3.1 %shard_sum.17 = f32[2,8,12288]{2,1,0:T(8,128)} custom-call(s32[6]{0:T(128)} %pad_add_fusion.shard_ref, f32[8,2,8,12288]{3,2,1,0:T(8,128)} %get-tuple-element.16.keep_ref, f32[8,8,12288]{2,1,0:T(8,128)} %copy-done, f32[8,8,12288]{2,1,0:T(8,128)} %collective-permute-done.1.rest_1_, f32[2,8,12288]{2,1,0:T(8,128)} %copy-done.11), custom_call_target="tpu_custom_call" | custom-call | bytes 3145728 | tf_op jit(solution)/shard_map/shard_sum/pallas_call | solution.py:137
  99.3 10.5 %collective-permute-done.12.rest_2_ = f32[2,8,12288]{2,1,0:T(8,128)S(1)} collective-permute-done((f32[2,8,12288]{2,1,0:T(8,128)}, f32[2,8,12288]{2,1,0:T(8,128)S(1)}, u32[]{:S(2)}, u32[]{:S(2)}) %collective-permute-start.12) | collective-permute-done | bytes 786464 | tf_op jit(solution)/shard_map/ppermute | solution.py:270
  110.6 3.1 %shard_sum.25 = f32[2,8,12288]{2,1,0:T(8,128)} custom-call(s32[6]{0:T(128)} %pad_add_fusion.shard_ref, f32[8,2,8,12288]{3,2,1,0:T(8,128)} %get-tuple-element.20.keep_ref, f32[8,8,12288]{2,1,0:T(8,128)} %collective-permute-done.10.rest_0_, f32[8,8,12288]{2,1,0:T(8,128)} %collective-permute-done.11.rest_1_, f32[2,8,12288]{2,1,0:T(8,128)} %copy-done.12), custom_call_target="tpu_custom_call" | custom-call | bytes 3145728 | tf_op jit(solution)/shard_map/shard_sum/pallas_call | solution.py:137
  117.0 3.1 %shard_sum.29 = f32[2,8,12288]{2,1,0:T(8,128)} custom-call(s32[6]{0:T(128)} %pad_add_fusion.1.shard_ref, f32[8,2,8,12288]{3,2,1,0:T(8,128)} %get-tuple-element.20.keep_ref, f32[8,8,12288]{2,1,0:T(8,128)} %collective-permute-done.10.rest_0_, f32[8,8,12288]{2,1,0:T(8,128)} %collective-permute-done.11.rest_1_, f32[2,8,12288]{2,1,0:T(8,128)} %copy-done.13), custom_call_target="tpu_custom_call" | custom-call | bytes 3145728 | tf_op jit(solution)/shard_map/shard_sum/pallas_call | solution.py:137
  121.0 3.1 %shard_sum.21 = f32[2,8,12288]{2,1,0:T(8,128)} custom-call(s32[6]{0:T(128)} %pad_add_fusion.1.shard_ref, f32[8,2,8,12288]{3,2,1,0:T(8,128)} %get-tuple-element.16.keep_ref, f32[8,8,12288]{2,1,0:T(8,128)} %copy-done, f32[8,8,12288]{2,1,0:T(8,128)} %collective-permute-done.1.rest_1_, f32[2,8,12288]{2,1,0:T(8,128)} %copy-done.7), custom_call_target="tpu_custom_call" | custom-call | bytes 3145728 | tf_op jit(solution)/shard_map/shard_sum/pallas_call | solution.py:137
  133.0 10.5 %collective-permute-done.13.rest_2_ = f32[2,8,12288]{2,1,0:T(8,128)S(1)} collective-permute-done((f32[2,8,12288]{2,1,0:T(8,128)}, f32[2,8,12288]{2,1,0:T(8,128)S(1)}, u32[]{:S(2)}, u32[]{:S(2)}) %collective-permute-start.13) | collective-permute-done | bytes 786464 | tf_op jit(solution)/shard_map/ppermute | solution.py:270
  144.3 3.1 %shard_sum.26 = f32[2,8,12288]{2,1,0:T(8,128)} custom-call(s32[6]{0:T(128)} %pad_add_fusion.shard_ref, f32[8,2,8,12288]{3,2,1,0:T(8,128)} %get-tuple-element.20.keep_ref, f32[8,8,12288]{2,1,0:T(8,128)} %collective-permute-done.10.rest_0_, f32[8,8,12288]{2,1,0:T(8,128)} %collective-permute-done.11.rest_1_, f32[2,8,12288]{2,1,0:T(8,128)} %copy-done.9), custom_call_target="tpu_custom_call" | custom-call | bytes 3145728 | tf_op jit(solution)/shard_map/shard_sum/pallas_call | solution.py:137
  150.7 3.1 %shard_sum.30 = f32[2,8,12288]{2,1,0:T(8,128)} custom-call(s32[6]{0:T(128)} %pad_add_fusion.1.shard_ref, f32[8,2,8,12288]{3,2,1,0:T(8,128)} %get-tuple-element.20.keep_ref, f32[8,8,12288]{2,1,0:T(8,128)} %collective-permute-done.10.rest_0_, f32[8,8,12288]{2,1,0:T(8,128)} %collective-permute-done.11.rest_1_, f32[2,8,12288]{2,1,0:T(8,128)} %copy-done.10), custom_call_target="tpu_custom_call" | custom-call | bytes 3145728 | tf_op jit(solution)/shard_map/shard_sum/pallas_call | solution.py:137
  166.7 10.5 %collective-permute-done.14.rest_2_ = f32[2,8,12288]{2,1,0:T(8,128)S(1)} collective-permute-done((f32[2,8,12288]{2,1,0:T(8,128)}, f32[2,8,12288]{2,1,0:T(8,128)S(1)}, u32[]{:S(2)}, u32[]{:S(2)}) %collective-permute-start.14) | collective-permute-done | bytes 786464 | tf_op jit(solution)/shard_map/ppermute | solution.py:270
  178.9 3.5 %shard_sum.31 = (f32[2,8,12288]{2,1,0:T(8,128)}, f32[8,128]{1,0:T(8,128)}) custom-call(s32[6]{0:T(128)} %pad_add_fusion.shard_ref, f32[8,2,8,12288]{3,2,1,0:T(8,128)} %get-tuple-element.20.keep_ref, f32[8,8,12288]{2,1,0:T(8,128)} %collective-permute-done.10.rest_0_, f32[8,8,12288]{2,1,0:T(8,128)} %collective-permute-done.11.rest_1_, ...), custom_call_target="tpu_custom_call" | custom-call | bytes 3932160 | tf_op jit(solution)/shard_map/shard_sum/pallas_call | solution.py:137
  184.7 15.7 %collective-permute-done.6.rest_2_ = f32[2,8,12288]{2,1,0:T(8,128)S(1)} collective-permute-done((f32[2,8,12288]{2,1,0:T(8,128)}, f32[2,8,12288]{2,1,0:T(8,128)S(1)}, u32[]{:S(2)}, u32[]{:S(2)}) %collective-permute-start.6) | collective-permute-done | bytes 786464 | tf_op jit(solution)/shard_map/ppermute | solution.py:270
  201.3 3.5 %shard_sum.23 = (f32[2,8,12288]{2,1,0:T(8,128)}, f32[8,128]{1,0:T(8,128)}) custom-call(s32[6]{0:T(128)} %pad_add_fusion.shard_ref, f32[8,2,8,12288]{3,2,1,0:T(8,128)} %get-tuple-element.16.keep_ref, f32[8,8,12288]{2,1,0:T(8,128)} %copy-done, f32[8,8,12288]{2,1,0:T(8,128)} %collective-permute-done.1.rest_1_, f32[2,8,12288]{2,1,0:T(8,128)} %copy-done.6, ...), custom_call_target="tpu_custom_call" | custom-call | bytes 3932160 | tf_op jit(solution)/shard_map/shard_sum/pallas_call | solution.py:137
  208.3 3.6 %collective-permute-done.20 = f32[8,128]{1,0:T(8,128)S(1)} collective-permute-done((f32[8,128]{1,0:T(8,128)S(1)}, f32[8,128]{1,0:T(8,128)S(1)}, u32[]{:S(2)}, u32[]{:S(2)}) %collective-permute-start.20) | collective-permute-done | bytes 4128 | tf_op jit(solution)/shard_map/ppermute | solution.py:213
  211.9 3.6 %collective-permute-done.21 = f32[8,128]{1,0:T(8,128)S(1)} collective-permute-done((f32[8,128]{1,0:T(8,128)S(1)}, f32[8,128]{1,0:T(8,128)S(1)}, u32[]{:S(2)}, u32[]{:S(2)}) %collective-permute-start.21) | collective-permute-done | bytes 4128 | tf_op jit(solution)/shard_map/ppermute | solution.py:213
  216.3 3.8 %collective-permute-done.22 = f32[8,128]{1,0:T(8,128)S(1)} collective-permute-done((f32[8,128]{1,0:T(8,128)S(1)}, f32[8,128]{1,0:T(8,128)S(1)}, u32[]{:S(2)}, u32[]{:S(2)}) %collective-permute-start.22) | collective-permute-done | bytes 4128 | tf_op jit(solution)/shard_map/ppermute | solution.py:213
  226.1 10.4 %update.1 = (f32[2,8,24576]{2,1,0:T(8,128)}, f32[2,8,24576]{2,1,0:T(8,128)}, f32[2,8,24576]{2,1,0:T(8,128)}, f32[2,8,24576]{2,1,0:T(8,128)}, f32[2,8,24576]{2,1,0:T(8,128)}, /*index=5*/f32[2,8,24576]{2,1,0:T(8,128)}) custom-call(f32[2]{0:T(128)} %pad_maximum_fusion.1.scales_ref, f32[8,128]{1,0:T(8,128)} %add.59.squares_ref, f32[2,8,24576]{2,1,0:T(8,128)} %rest_0_.1, ...), custom_call_target="tpu_custom_call" | custom-call | bytes 22020096 | tf_op jit(solution)/shard_map/update/pallas_call | solution.py:189
  (99 shorter events, 69.6 us)
Async XLA Ops:
  5.5 57.5 %collective-permute-start.2 = (f32[6,8,24576]{2,1,0:T(8,128)}, f32[6,8,24576]{2,1,0:T(8,128)}, u32[]{:S(2)}, u32[]{:S(2)}) collective-permute-start(f32[6,8,24576]{2,1,0:T(8,128)} %pad_maximum_fusion), channel_id=1, source_target_pairs={{0,2},{2,4},{4,6},{6,8},{8,10},{10,12},{12,14},{14,16},{16,18},{18... | collective-permute-start | bytes 14155784 | tf_op jit(solution)/shard_map/ppermute | solution.py:245
  16.0 12.7 %collective-permute-start.10 = (f32[8,8,12288]{2,1,0:T(8,128)}, f32[8,8,12288]{2,1,0:T(8,128)}, u32[]{:S(2)}, u32[]{:S(2)}) collective-permute-start(f32[8,8,12288]{2,1,0:T(8,128)} %get-tuple-element.21), channel_id=1, source_target_pairs={{0,2},{2,0},{4,6},{6,4},{8,10},{10,8},{12,14},{14,12},{16,18},{18,... | collective-permute-start | bytes 9437192 | tf_op jit(solution)/shard_map/ppermute | solution.py:257
  18.6 10.1 %collective-permute-start.11 = (f32[8,8,12288]{2,1,0:T(8,128)}, f32[8,8,12288]{2,1,0:T(8,128)}, u32[]{:S(2)}, u32[]{:S(2)}) collective-permute-start(f32[8,8,12288]{2,1,0:T(8,128)} %get-tuple-element.22), channel_id=1, source_target_pairs={{0,2},{2,0},{4,6},{6,4},{8,10},{10,8},{12,14},{14,12},{16,18},{18,... | collective-permute-start | bytes 9437192 | tf_op jit(solution)/shard_map/ppermute | solution.py:257
  27.6 10.3 %collective-permute-start = (f32[8,8,12288]{2,1,0:T(8,128)}, f32[8,8,12288]{2,1,0:T(8,128)S(1)}, u32[]{:S(2)}, u32[]{:S(2)}) collective-permute-start(f32[8,8,12288]{2,1,0:T(8,128)} %get-tuple-element.17), channel_id=1, source_target_pairs={{0,2},{2,0},{4,6},{6,4},{8,10},{10,8},{12,14},{14,12},{16,18},{18,... | collective-permute-start | bytes 9437192 | tf_op jit(solution)/shard_map/ppermute | solution.py:257
  28.1 10.1 %collective-permute-start.1 = (f32[8,8,12288]{2,1,0:T(8,128)}, f32[8,8,12288]{2,1,0:T(8,128)}, u32[]{:S(2)}, u32[]{:S(2)}) collective-permute-start(f32[8,8,12288]{2,1,0:T(8,128)} %get-tuple-element.18), channel_id=1, source_target_pairs={{0,2},{2,0},{4,6},{6,4},{8,10},{10,8},{12,14},{14,12},{16,18},{18,... | collective-permute-start | bytes 9437192 | tf_op jit(solution)/shard_map/ppermute | solution.py:257
  31.6 48.0 %collective-permute-start.15 = (f32[2,8,12288]{2,1,0:T(8,128)}, f32[2,8,12288]{2,1,0:T(8,128)}, u32[]{:S(2)}, u32[]{:S(2)}) collective-permute-start(f32[2,8,12288]{2,1,0:T(8,128)} %shard_sum.27), channel_id=1, source_target_pairs={{0,4},{2,6},{8,0},{10,2},{16,8},{18,10},{24,16},{26,18},{28,24},{3... | collective-permute-start | bytes 2359304 | tf_op jit(solution)/shard_map/ppermute | solution.py:263
  65.9 27.0 %collective-permute-start.3 = (f32[2,8,12288]{2,1,0:T(8,128)}, f32[2,8,12288]{2,1,0:T(8,128)S(1)}, u32[]{:S(2)}, u32[]{:S(2)}) collective-permute-start(f32[2,8,12288]{2,1,0:T(8,128)} %shard_sum.16), channel_id=1, source_target_pairs={{0,8},{2,10},{8,16},{10,18},{16,24},{18,26},{24,28},{26,30},{28,20... | collective-permute-start | bytes 2359304 | tf_op jit(solution)/shard_map/ppermute | solution.py:263
  78.1 31.7 %collective-permute-start.12 = (f32[2,8,12288]{2,1,0:T(8,128)}, f32[2,8,12288]{2,1,0:T(8,128)S(1)}, u32[]{:S(2)}, u32[]{:S(2)}) collective-permute-start(f32[2,8,12288]{2,1,0:T(8,128)} %shard_sum.24), channel_id=1, source_target_pairs={{0,8},{2,10},{8,16},{10,18},{16,24},{18,26},{24,28},{26,30},{28,20... | collective-permute-start | bytes 2359304 | tf_op jit(solution)/shard_map/ppermute | solution.py:270
  82.8 33.4 %collective-permute-start.16 = (f32[2,8,12288]{2,1,0:T(8,128)}, f32[2,8,12288]{2,1,0:T(8,128)S(1)}, u32[]{:S(2)}, u32[]{:S(2)}) collective-permute-start(f32[2,8,12288]{2,1,0:T(8,128)} %shard_sum.28), channel_id=1, source_target_pairs={{0,4},{2,6},{8,0},{10,2},{16,8},{18,10},{24,16},{26,18},{28,24},{3... | collective-permute-start | bytes 2359304 | tf_op jit(solution)/shard_map/ppermute | solution.py:270
  86.1 34.1 %collective-permute-start.7 = (f32[2,8,12288]{2,1,0:T(8,128)}, f32[2,8,12288]{2,1,0:T(8,128)S(1)}, u32[]{:S(2)}, u32[]{:S(2)}) collective-permute-start(f32[2,8,12288]{2,1,0:T(8,128)} %shard_sum.20), channel_id=1, source_target_pairs={{0,4},{2,6},{8,0},{10,2},{16,8},{18,10},{24,16},{26,18},{28,24},{3... | collective-permute-start | bytes 2359304 | tf_op jit(solution)/shard_map/ppermute | solution.py:270
  96.9 29.7 %collective-permute-start.4 = (f32[2,8,12288]{2,1,0:T(8,128)}, f32[2,8,12288]{2,1,0:T(8,128)S(1)}, u32[]{:S(2)}, u32[]{:S(2)}) collective-permute-start(f32[2,8,12288]{2,1,0:T(8,128)} %shard_sum.17), channel_id=1, source_target_pairs={{0,8},{2,10},{8,16},{10,18},{16,24},{18,26},{24,28},{26,30},{28,20... | collective-permute-start | bytes 2359304 | tf_op jit(solution)/shard_map/ppermute | solution.py:270
  113.8 29.7 %collective-permute-start.13 = (f32[2,8,12288]{2,1,0:T(8,128)}, f32[2,8,12288]{2,1,0:T(8,128)S(1)}, u32[]{:S(2)}, u32[]{:S(2)}) collective-permute-start(f32[2,8,12288]{2,1,0:T(8,128)} %shard_sum.25), channel_id=1, source_target_pairs={{0,8},{2,10},{8,16},{10,18},{16,24},{18,26},{24,28},{26,30},{28,20... | collective-permute-start | bytes 2359304 | tf_op jit(solution)/shard_map/ppermute | solution.py:270
  120.1 29.7 %collective-permute-start.17 = (f32[2,8,12288]{2,1,0:T(8,128)}, f32[2,8,12288]{2,1,0:T(8,128)S(1)}, u32[]{:S(2)}, u32[]{:S(2)}) collective-permute-start(f32[2,8,12288]{2,1,0:T(8,128)} %shard_sum.29), channel_id=1, source_target_pairs={{0,4},{2,6},{8,0},{10,2},{16,8},{18,10},{24,16},{26,18},{28,24},{3... | collective-permute-start | bytes 2359304 | tf_op jit(solution)/shard_map/ppermute | solution.py:270
  124.2 29.7 %collective-permute-start.8 = (f32[2,8,12288]{2,1,0:T(8,128)}, f32[2,8,12288]{2,1,0:T(8,128)S(1)}, u32[]{:S(2)}, u32[]{:S(2)}) collective-permute-start(f32[2,8,12288]{2,1,0:T(8,128)} %shard_sum.21), channel_id=1, source_target_pairs={{0,4},{2,6},{8,0},{10,2},{16,8},{18,10},{24,16},{26,18},{28,24},{3... | collective-permute-start | bytes 2359304 | tf_op jit(solution)/shard_map/ppermute | solution.py:270
  130.6 29.7 %collective-permute-start.5 = (f32[2,8,12288]{2,1,0:T(8,128)}, f32[2,8,12288]{2,1,0:T(8,128)S(1)}, u32[]{:S(2)}, u32[]{:S(2)}) collective-permute-start(f32[2,8,12288]{2,1,0:T(8,128)} %shard_sum.18), channel_id=1, source_target_pairs={{0,8},{2,10},{8,16},{10,18},{16,24},{18,26},{24,28},{26,30},{28,20... | collective-permute-start | bytes 2359304 | tf_op jit(solution)/shard_map/ppermute | solution.py:270
  147.5 29.7 %collective-permute-start.14 = (f32[2,8,12288]{2,1,0:T(8,128)}, f32[2,8,12288]{2,1,0:T(8,128)S(1)}, u32[]{:S(2)}, u32[]{:S(2)}) collective-permute-start(f32[2,8,12288]{2,1,0:T(8,128)} %shard_sum.26), channel_id=1, source_target_pairs={{0,8},{2,10},{8,16},{10,18},{16,24},{18,26},{24,28},{26,30},{28,20... | collective-permute-start | bytes 2359304 | tf_op jit(solution)/shard_map/ppermute | solution.py:270
  153.9 23.3 %collective-permute-start.18 = (f32[2,8,12288]{2,1,0:T(8,128)}, f32[2,8,12288]{2,1,0:T(8,128)S(1)}, u32[]{:S(2)}, u32[]{:S(2)}) collective-permute-start(f32[2,8,12288]{2,1,0:T(8,128)} %shard_sum.30), channel_id=1, source_target_pairs={{0,4},{2,6},{8,0},{10,2},{16,8},{18,10},{24,16},{26,18},{28,24},{3... | collective-permute-start | bytes 2359304 | tf_op jit(solution)/shard_map/ppermute | solution.py:270
  157.9 26.9 %collective-permute-start.9 = (f32[2,8,12288]{2,1,0:T(8,128)}, f32[2,8,12288]{2,1,0:T(8,128)S(1)}, u32[]{:S(2)}, u32[]{:S(2)}) collective-permute-start(f32[2,8,12288]{2,1,0:T(8,128)} %shard_sum.22), channel_id=1, source_target_pairs={{0,4},{2,6},{8,0},{10,2},{16,8},{18,10},{24,16},{26,18},{28,24},{3... | collective-permute-start | bytes 2359304 | tf_op jit(solution)/shard_map/ppermute | solution.py:270
  164.3 36.1 %collective-permute-start.6 = (f32[2,8,12288]{2,1,0:T(8,128)}, f32[2,8,12288]{2,1,0:T(8,128)S(1)}, u32[]{:S(2)}, u32[]{:S(2)}) collective-permute-start(f32[2,8,12288]{2,1,0:T(8,128)} %shard_sum.19), channel_id=1, source_target_pairs={{0,8},{2,10},{8,16},{10,18},{16,24},{18,26},{24,28},{26,30},{28,20... | collective-permute-start | bytes 2359304 | tf_op jit(solution)/shard_map/ppermute | solution.py:270
  182.4 41.9 %collective-permute-start.25 = (f32[2,8,12288]{2,1,0:T(8,128)}, f32[2,8,12288]{2,1,0:T(8,128)S(1)}, u32[]{:S(2)}, u32[]{:S(2)}) collective-permute-start(f32[2,8,12288]{2,1,0:T(8,128)} %get-tuple-element.25.rest_7_), channel_id=1, source_target_pairs={{0,2},{2,4},{4,6},{6,8},{8,10},{10,12},{12,14},{14,16},{16,18},{18... | collective-permute-start | bytes 2359304 | tf_op jit(solution)/shard_map/ppermute | solution.py:274
  204.8 19.5 %collective-permute-start.24 = (f32[2,8,12288]{2,1,0:T(8,128)}, f32[2,8,12288]{2,1,0:T(8,128)S(1)}, u32[]{:S(2)}, u32[]{:S(2)}) collective-permute-start(f32[2,8,12288]{2,1,0:T(8,128)} %get-tuple-element.24.rest_6_), channel_id=1, source_target_pairs={{0,2},{2,4},{4,6},{6,8},{8,10},{10,12},{12,14},{14,16},{16,18},{18... | collective-permute-start | bytes 2359304 | tf_op jit(solution)/shard_map/ppermute | solution.py:274
  208.0 4.0 %collective-permute-start.20 = (f32[8,128]{1,0:T(8,128)S(1)}, f32[8,128]{1,0:T(8,128)S(1)}, u32[]{:S(2)}, u32[]{:S(2)}) collective-permute-start(f32[8,128]{1,0:T(8,128)S(1)} %add.55), channel_id=1, source_target_pairs={{0,4},{2,6},{4,0},{6,2},{8,12},{10,14},{12,8},{14,10},{16,20},{18,... | collective-permute-start | bytes 12296 | tf_op jit(solution)/shard_map/ppermute | solution.py:213
  215.6 4.5 %collective-permute-start.22 = (f32[8,128]{1,0:T(8,128)S(1)}, f32[8,128]{1,0:T(8,128)S(1)}, u32[]{:S(2)}, u32[]{:S(2)}) collective-permute-start(f32[8,128]{1,0:T(8,128)S(1)} %add.57), channel_id=1, source_target_pairs={{0,16},{2,18},{4,20},{6,22},{8,24},{10,26},{12,28},{14,30},{16,0},... | collective-permute-start | bytes 12296 | tf_op jit(solution)/shard_map/ppermute | solution.py:213
  220.1 3.6 %collective-permute-start.23 = (f32[8,128]{1,0:T(8,128)S(1)}, f32[8,128]{1,0:T(8,128)S(1)}, u32[]{:S(2)}, u32[]{:S(2)}) collective-permute-start(f32[8,128]{1,0:T(8,128)S(1)} %add.58), channel_id=1, source_target_pairs={{0,1},{1,0},{2,3},{3,2},{4,5},{5,4},{6,7},{7,6},{8,9},{9,8},{10,11... | collective-permute-start | bytes 12296 | tf_op jit(solution)/shard_map/ppermute | solution.py:213
  (20 other events, 87.0 us)

commit v5 on v4

--- a/solution.py
+++ b/solution.py
@@ -16,7 +16,7 @@
 
 streams = 2
 lanes = 128
-room = pltpu.CompilerParams(vmem_limit_bytes=60 * 2**20)
+room = pltpu.CompilerParams(vmem_limit_bytes=64*2**20)
 
 
 def block_of(columns, most):
@@ -155,24 +155,24 @@
 def update_kernel(count, bound, scales_ref, squares_ref, *rest):
     states, grads, outs = (rest[:3], rest[3:6]), rest[6 : 6 + 2 * count], rest[6 + 2 * count :]
     step = pl.program_id(0)
-    per = pl.num_programs(0) // (2 * count)
+    per = pl.num_programs(0) // count
     factor = jnp.minimum(
         jnp.float32(1.0), bound / (jnp.sqrt(jnp.sum(squares_ref[...])) + jnp.float32(1e-06))
     )
-    for index, grad_ref in enumerate(grads):
+    for index in range(count):
 
         @pl.when(step // per == index)
-        def _(index=index, grad_ref=grad_ref):
-            who = index // count
-            new = adamw_update(
-                *[ref[...] for ref in states[who]],
-                grad_ref[...],
-                factor,
-                scales_ref[0],
-                scales_ref[1],
-            )
-            for out_ref, value in zip(outs[3 * who : 3 * who + 3], new):
-                out_ref[...] = value
+        def _(index=index):
+            for who in range(2):
+                new = adamw_update(
+                    *[ref[...] for ref in states[who]],
+                    grads[who * count + index][...],
+                    factor,
+                    scales_ref[0],
+                    scales_ref[1],
+                )
+                for out_ref, value in zip(outs[3 * who : 3 * who + 3], new):
+                    out_ref[...] = value
 
 
 def update(scales, squares, state, grads, old_copy, peer_grads, bound):
@@ -188,20 +188,42 @@
 
     return pl.pallas_call(
         functools.partial(update_kernel, count, bound),
-        grid=(2 * blocks,),
+        grid=(blocks,),
         in_specs=[
             pl.BlockSpec(memory_space=pltpu.SMEM),
             pl.BlockSpec(squares.shape, lambda i: (0, 0)),
         ]
         + [part(0, blocks)] * 3
-        + [part(blocks, blocks, row) for row in range(3)]
-        + [part(k * per, per) for k in range(2 * count)],
-        out_specs=[part(0, blocks)] * 3 + [part(blocks, blocks)] * 3,
+        + [part(0, blocks, row) for row in range(3)]
+        + [part(k * per, per) for k in range(count)] * 2,
+        out_specs=[part(0, blocks)] * 6,
         out_shape=[jax.ShapeDtypeStruct((layers, own, columns), jnp.float32)] * 6,
         compiler_params=room,
         cost_estimate=cost_of(*[state[0]] * 14),
         name="update",
     )(scales, squares, *state, *[old_copy] * 3, *grads, *peer_grads)
+
+
+def joined_kernel(*refs):
+    *parts, out_ref = refs
+    layers = parts[0].shape[0]
+    for index, part_ref in enumerate(parts):
+        out_ref[index * layers : (index + 1) * layers] = part_ref[...]
+
+
+def joined(arrays):
+    layers, own, columns = arrays[0].shape
+    size = block_of(columns, 8192)
+    return pl.pallas_call(
+        joined_kernel,
+        grid=(columns // size,),
+        in_specs=[pl.BlockSpec((layers, own, size), lambda i: (0, 0, i))] * len(arrays),
+        out_specs=pl.BlockSpec((len(arrays) * layers, own, size), lambda i: (0, 0, i)),
+        out_shape=jax.ShapeDtypeStruct((len(arrays) * layers, own, columns), jnp.float32),
+        compiler_params=room,
+        cost_estimate=cost_of(*arrays, *arrays),
+        name="joined",
+    )(*arrays)
 
 
 def total_over(value, axis):
@@ -242,7 +264,7 @@
     ]
 
     state = (params, first_moment, second_moment)
-    old_copy = lax.ppermute(jnp.concatenate(state), "dp", onward)
+    old_copy = lax.ppermute(joined(state), "dp", onward)
 
     same = jnp.eye(layers, dtype=activations.dtype)
     inputs = activations.transpose(1, 2, 0)[:, :, :, None] * same[:, None, None, :]
@@ -257,16 +279,22 @@
         theirs[k] = [lax.ppermute(give, "dp", swap) for give in gives]
     for k in range(streams):
         total = shard_sum(
-            plain_kernel, tables[0], half, keep[k], theirs[k], after=() if k else [old_copy]
+            plain_kernel, tables[0], half, keep[k], theirs[k]
         )
         sent[k] = [None, None]
         sent[k][k % 2] = lax.ppermute(total, "dp", hop(-1 if k % 2 else 1))
+    waiting = [old_copy]
     for away in range(half - 1, 0, -1):
         for k in range(streams):
             for way, by in enumerate((1, -1)):
                 arrived = [] if sent[k][way] is None else [sent[k][way]]
                 body = step_kernel if arrived else plain_kernel
-                total = shard_sum(body, tables[way], away, keep[k], theirs[k], *arrived)
+                after = []
+                if arrived:
+                    after, waiting = waiting, after
+                total = shard_sum(
+                    body, tables[way], away, keep[k], theirs[k], *arrived, after=after
+                )
                 sent[k][way] = lax.ppermute(total, "dp", hop(by))
     squares = None
     for k in range(streams):

time: 237 us -> 225 us (0.949)
  starting transfers between devices: 33.3 us -> 70.5 us
  waiting for transfers between devices: 102 us -> 64.9 us
  local copies, waits for them, and re-layouts: 13.1 us -> 0.78 us
  other arithmetic: 8.14 us -> 4.1 us
  Pallas kernels: 78.1 us -> 81.9 us
    ppermute x1, waiting for transfers between devices: 24.8 us -> 0.01 us  [local(): old_copy = lax.ppermute(joined(state), 'dp', onward)]
    ppermute x2, starting transfers between devices: 0.03 us -> 23.1 us  [local(): peer_grads[k] = lax.ppermute(grads[k], 'dp', onward)]
    ppermute x12, waiting for transfers between devices: 52.2 us -> 31.2 us  [local(): sent[k][way] = lax.ppermute(total, 'dp', hop(by))]
    ppermute x2, waiting for transfers between devices: 6.81 us -> 21.8 us  [local(): sent[k][k % 2] = lax.ppermute(total, 'dp', hop(-1 if k % 2 else 1))]
    ppermute x5, starting transfers between devices: 3.48 us -> 17.2 us  [total_over(): lax.ppermute(value, axis, [(i, i ^ bit) for i in range(peers)])]
    unnamed x37 -> x1, local copies, waits for them, and re-layouts: 12.3 us -> 0.02 us
    ppermute x12, starting transfers between devices: 16 us -> 23.5 us  [local(): sent[k][way] = lax.ppermute(total, 'dp', hop(by))]
    ppermute x2, starting transfers between devices: 10.2 us -> 3.14 us  [local(): sent[k][k % 2] = lax.ppermute(total, 'dp', hop(-1 if k % 2 else 1))]
  transfers between devices with their start and end apart: 26 -> 26, of which waited for: 16 -> 15; matrix products, arithmetic and copies ran while one was open for 2% -> 2% of each run, Pallas kernels for 29% -> 30%
where the time goes in v5:
time: 225 us; the launch traced here: 224 us
  Pallas kernels  81.9 us (36%)
  starting transfers between devices  70.5 us (31%)
  waiting for transfers between devices  64.9 us (29%)
  other arithmetic  4.1 us (2%)
    pallas_call x16, Pallas kernels, shard_sum(): pl.pallas_call(functools.partial(body, layers), grid_spec=pltpu.PrefetchS...  49.7 us
    ppermute x12, waiting for transfers between devices, local(): sent[k][way] = lax.ppermute(total, 'dp', hop(by))  31.2 us
    ppermute x12, starting transfers between devices, local(): sent[k][way] = lax.ppermute(total, 'dp', hop(by))  23.5 us
    ppermute x2, starting transfers between devices, local(): peer_grads[k] = lax.ppermute(grads[k], 'dp', onward)  23.1 us
    ppermute x2, waiting for transfers between devices, local(): sent[k][k % 2] = lax.ppermute(total, 'dp', hop(-1 if k % 2 else 1))  21.8 us
    pallas_call x2, Pallas kernels, make_terms(): pl.pallas_call(functools.partial(terms_kernel, order, layers), grid_spec=...  17.9 us
    ppermute x5, starting transfers between devices, total_over(): lax.ppermute(value, axis, [(i, i ^ bit) for i in range(peers)])  17.2 us
    pallas_call x1, Pallas kernels, update(): pl.pallas_call(functools.partial(update_kernel, count, bound), grid=(bloc...  8.99 us
  transfers between devices with their start and end apart: 26, of which 15 were waited for; matrix products, arithmetic and copies ran while one was open for 2% of the time, Pallas kernels for 30%

profile of v5, /device:TPU:0, one launch (start us, length us, event | category | flops | bytes accessed | tf_op | source)
XLA Modules:
  0.0 223.6 jit_solution(16813329172881364754)
XLA Ops:
  0.6 5.4 %joined.1 = f32[6,8,24576]{2,1,0:T(8,128)} custom-call(f32[2,8,24576]{2,1,0:T(8,128)} %rest_0_.1, f32[2,8,24576]{2,1,0:T(8,128)} %rest_1_.1, f32[2,8,24576]{2,1,0:T(8,128)} %rest_2_.1), custom_call_target="tpu_custom_call" | custom-call | bytes 9437184 | tf_op jit(solution)/shard_map/joined/pallas_call | solution.py:217
  8.3 9.0 %terms.3 = (f32[8,2,8,12288]{3,2,1,0:T(8,128)}, f32[8,8,12288]{2,1,0:T(8,128)}, f32[8,8,12288]{2,1,0:T(8,128)}) custom-call(s32[1]{0:T(128)} %bitcast.core_ref, bf16[256,256]{1,0:T(8,128)(2,1)} %copy.14.inputs_ref, bf16[1,2,128,24576]{3,2,1,0:T(8,128)(2,1)} %earlier_ref.3, bf16[128,2,24576]{2,1,0:T(2,128)(2,1)} %outgrad_ref.3), custom_call_target="tpu_custom_call" | custom-call | bytes 25165824 | tf_op jit(solution)/shard_map/terms/pallas_call | solution.py:71
  19.9 8.9 %terms.2 = (f32[8,2,8,12288]{3,2,1,0:T(8,128)}, f32[8,8,12288]{2,1,0:T(8,128)}, f32[8,8,12288]{2,1,0:T(8,128)}) custom-call(s32[1]{0:T(128)} %bitcast.core_ref, bf16[256,256]{1,0:T(8,128)(2,1)} %copy.14.inputs_ref, bf16[1,2,128,24576]{3,2,1,0:T(8,128)(2,1)} %earlier_ref.3, bf16[128,2,24576]{2,1,0:T(2,128)(2,1)} %outgrad_ref.3), custom_call_target="tpu_custom_call" | custom-call | bytes 25165824 | tf_op jit(solution)/shard_map/terms/pallas_call | solution.py:71
  34.9 4.5 %collective-permute-done.1.rest_1_ = f32[8,8,12288]{2,1,0:T(8,128)} collective-permute-done((f32[8,8,12288]{2,1,0:T(8,128)}, f32[8,8,12288]{2,1,0:T(8,128)}, u32[]{:S(2)}, u32[]{:S(2)}) %collective-permute-start.1) | collective-permute-done | bytes 3145760 | tf_op jit(solution)/shard_map/ppermute | solution.py:279
  48.9 4.1 %collective-permute-done.15.rest_2_ = f32[2,8,12288]{2,1,0:T(8,128)} collective-permute-done((f32[2,8,12288]{2,1,0:T(8,128)}, f32[2,8,12288]{2,1,0:T(8,128)}, u32[]{:S(2)}, u32[]{:S(2)}) %collective-permute-start.15) | collective-permute-done | bytes 786464 | tf_op jit(solution)/shard_map/ppermute | solution.py:285
  62.8 17.7 %collective-permute-done.2.rest_2_ = f32[2,8,12288]{2,1,0:T(8,128)} collective-permute-done((f32[2,8,12288]{2,1,0:T(8,128)}, f32[2,8,12288]{2,1,0:T(8,128)}, u32[]{:S(2)}, u32[]{:S(2)}) %collective-permute-start.2) | collective-permute-done | bytes 786464 | tf_op jit(solution)/shard_map/ppermute | solution.py:285
  80.4 3.1 %shard_sum.17 = f32[2,8,12288]{2,1,0:T(8,128)} custom-call(s32[6]{0:T(128)} %pad_add_fusion.shard_ref, f32[8,2,8,12288]{3,2,1,0:T(8,128)} %get-tuple-element.16.keep_ref, f32[8,8,12288]{2,1,0:T(8,128)} %collective-permute-done.rest_0_, f32[8,8,12288]{2,1,0:T(8,128)} %collective-permute-done.1.rest_1_, f32[2,8,12288]{2,1,0:T(8,128)} %collective-permute-done.2.rest_2_, ...), custom_call_target="tpu_custom_call" | custom-call | bytes 3145728 | tf_op jit(solution)/shard_map/shard_sum/pallas_call | solution.py:137
  84.3 13.0 %collective-permute-done.12.rest_2_ = f32[2,8,12288]{2,1,0:T(8,128)} collective-permute-done((f32[2,8,12288]{2,1,0:T(8,128)}, f32[2,8,12288]{2,1,0:T(8,128)}, u32[]{:S(2)}, u32[]{:S(2)}) %collective-permute-start.12) | collective-permute-done | bytes 786464 | tf_op jit(solution)/shard_map/ppermute | solution.py:298
  100.4 3.1 %shard_sum.29 = f32[2,8,12288]{2,1,0:T(8,128)} custom-call(s32[6]{0:T(128)} %pad_add_fusion.1.shard_ref, f32[8,2,8,12288]{3,2,1,0:T(8,128)} %get-tuple-element.20.keep_ref, f32[8,8,12288]{2,1,0:T(8,128)} %collective-permute-done.10.rest_0_, f32[8,8,12288]{2,1,0:T(8,128)} %collective-permute-done.11.rest_1_, f32[2,8,12288]{2,1,0:T(8,128)} %collective-permute-done.16.rest_2_), custom_call_target="tpu_custom_call" | custom-call | bytes 3145728 | tf_op jit(solution)/shard_map/shard_sum/pallas_call | solution.py:137
  105.5 3.1 %shard_sum.21 = f32[2,8,12288]{2,1,0:T(8,128)} custom-call(s32[6]{0:T(128)} %pad_add_fusion.1.shard_ref, f32[8,2,8,12288]{3,2,1,0:T(8,128)} %get-tuple-element.16.keep_ref, f32[8,8,12288]{2,1,0:T(8,128)} %collective-permute-done.rest_0_, f32[8,8,12288]{2,1,0:T(8,128)} %collective-permute-done.1.rest_1_, f32[2,8,12288]{2,1,0:T(8,128)} %collective-permute-done.7.rest_2_), custom_call_target="tpu_custom_call" | custom-call | bytes 3145728 | tf_op jit(solution)/shard_map/shard_sum/pallas_call | solution.py:137
  109.2 3.1 %shard_sum.18 = f32[2,8,12288]{2,1,0:T(8,128)} custom-call(s32[6]{0:T(128)} %pad_add_fusion.shard_ref, f32[8,2,8,12288]{3,2,1,0:T(8,128)} %get-tuple-element.16.keep_ref, f32[8,8,12288]{2,1,0:T(8,128)} %collective-permute-done.rest_0_, f32[8,8,12288]{2,1,0:T(8,128)} %collective-permute-done.1.rest_1_, f32[2,8,12288]{2,1,0:T(8,128)} %collective-permute-done.4.rest_2_), custom_call_target="tpu_custom_call" | custom-call | bytes 3145728 | tf_op jit(solution)/shard_map/shard_sum/pallas_call | solution.py:137
  113.8 4.7 %collective-permute-done.13.rest_2_ = f32[2,8,12288]{2,1,0:T(8,128)} collective-permute-done((f32[2,8,12288]{2,1,0:T(8,128)}, f32[2,8,12288]{2,1,0:T(8,128)}, u32[]{:S(2)}, u32[]{:S(2)}) %collective-permute-start.13) | collective-permute-done | bytes 786464 | tf_op jit(solution)/shard_map/ppermute | solution.py:298
  121.6 10.2 %collective-permute-start.14 = (f32[2,8,12288]{2,1,0:T(8,128)}, f32[2,8,12288]{2,1,0:T(8,128)}, u32[]{:S(2)}, u32[]{:S(2)}) collective-permute-start(f32[2,8,12288]{2,1,0:T(8,128)} %shard_sum.26), channel_id=1, source_target_pairs={{0,8},{2,10},{8,16},{10,18},{16,24},{18,26},{24,28},{26,30},{28,20... | collective-permute-start | bytes 2359304 | tf_op jit(solution)/shard_map/ppermute | solution.py:298
  131.8 3.1 %shard_sum.30 = f32[2,8,12288]{2,1,0:T(8,128)} custom-call(s32[6]{0:T(128)} %pad_add_fusion.1.shard_ref, f32[8,2,8,12288]{3,2,1,0:T(8,128)} %get-tuple-element.20.keep_ref, f32[8,8,12288]{2,1,0:T(8,128)} %collective-permute-done.10.rest_0_, f32[8,8,12288]{2,1,0:T(8,128)} %collective-permute-done.11.rest_1_, f32[2,8,12288]{2,1,0:T(8,128)} %collective-permute-done.17.rest_2_), custom_call_target="tpu_custom_call" | custom-call | bytes 3145728 | tf_op jit(solution)/shard_map/shard_sum/pallas_call | solution.py:137
  135.0 6.2 %collective-permute-done.8.rest_2_ = f32[2,8,12288]{2,1,0:T(8,128)} collective-permute-done((f32[2,8,12288]{2,1,0:T(8,128)}, f32[2,8,12288]{2,1,0:T(8,128)}, u32[]{:S(2)}, u32[]{:S(2)}) %collective-permute-start.8) | collective-permute-done | bytes 786464 | tf_op jit(solution)/shard_map/ppermute | solution.py:298
  146.3 3.1 %shard_sum.19 = f32[2,8,12288]{2,1,0:T(8,128)} custom-call(s32[6]{0:T(128)} %pad_add_fusion.shard_ref, f32[8,2,8,12288]{3,2,1,0:T(8,128)} %get-tuple-element.16.keep_ref, f32[8,8,12288]{2,1,0:T(8,128)} %collective-permute-done.rest_0_, f32[8,8,12288]{2,1,0:T(8,128)} %collective-permute-done.1.rest_1_, f32[2,8,12288]{2,1,0:T(8,128)} %collective-permute-done.5.rest_2_), custom_call_target="tpu_custom_call" | custom-call | bytes 3145728 | tf_op jit(solution)/shard_map/shard_sum/pallas_call | solution.py:137
  152.2 5.8 %collective-permute-done.18.rest_3_ = f32[2,8,12288]{2,1,0:T(8,128)} collective-permute-done((f32[2,8,12288]{2,1,0:T(8,128)}, f32[2,8,12288]{2,1,0:T(8,128)}, u32[]{:S(2)}, u32[]{:S(2)}) %collective-permute-start.18) | collective-permute-done | bytes 786464 | tf_op jit(solution)/shard_map/ppermute | solution.py:298
  158.0 3.5 %shard_sum.31 = (f32[2,8,12288]{2,1,0:T(8,128)}, f32[8,128]{1,0:T(8,128)}) custom-call(s32[6]{0:T(128)} %pad_add_fusion.shard_ref, f32[8,2,8,12288]{3,2,1,0:T(8,128)} %get-tuple-element.20.keep_ref, f32[8,8,12288]{2,1,0:T(8,128)} %collective-permute-done.10.rest_0_, f32[8,8,12288]{2,1,0:T(8,128)} %collective-permute-done.11.rest_1_, ...), custom_call_target="tpu_custom_call" | custom-call | bytes 3932160 | tf_op jit(solution)/shard_map/shard_sum/pallas_call | solution.py:137
  161.5 18.1 %collective-permute-start.25 = (f32[2,8,12288]{2,1,0:T(8,128)}, f32[2,8,12288]{2,1,0:T(8,128)}, u32[]{:S(2)}, u32[]{:S(2)}) collective-permute-start(f32[2,8,12288]{2,1,0:T(8,128)} %get-tuple-element.25.rest_7_), channel_id=1, source_target_pairs={{0,2},{2,4},{4,6},{6,8},{8,10},{10,12},{12,14},{14,16},{16,18},{18... | collective-permute-start | bytes 2359304 | tf_op jit(solution)/shard_map/ppermute | solution.py:302
  179.6 3.5 %shard_sum.23 = (f32[2,8,12288]{2,1,0:T(8,128)}, f32[8,128]{1,0:T(8,128)}) custom-call(s32[6]{0:T(128)} %pad_add_fusion.shard_ref, f32[8,2,8,12288]{3,2,1,0:T(8,128)} %get-tuple-element.16.keep_ref, f32[8,8,12288]{2,1,0:T(8,128)} %collective-permute-done.rest_0_, f32[8,8,12288]{2,1,0:T(8,128)} %collective-permute-done.1.rest_1_, ...), custom_call_target="tpu_custom_call" | custom-call | bytes 3932160 | tf_op jit(solution)/shard_map/shard_sum/pallas_call | solution.py:137
  183.1 5.0 %collective-permute-start.24 = (f32[2,8,12288]{2,1,0:T(8,128)}, f32[2,8,12288]{2,1,0:T(8,128)}, u32[]{:S(2)}, u32[]{:S(2)}) collective-permute-start(f32[2,8,12288]{2,1,0:T(8,128)} %get-tuple-element.24.rest_6_), channel_id=1, source_target_pairs={{0,2},{2,4},{4,6},{6,8},{8,10},{10,12},{12,14},{14,16},{16,18},{18... | collective-permute-start | bytes 2359304 | tf_op jit(solution)/shard_map/ppermute | solution.py:302
  193.7 4.2 %collective-permute-start.21 = (f32[8,128]{1,0:T(8,128)S(1)}, f32[8,128]{1,0:T(8,128)S(1)}, u32[]{:S(2)}, u32[]{:S(2)}) collective-permute-start(f32[8,128]{1,0:T(8,128)S(1)} %add.56), channel_id=1, source_target_pairs={{0,8},{2,10},{4,12},{6,14},{8,0},{10,2},{12,4},{14,6},{16,24},{18,... | collective-permute-start | bytes 12296 | tf_op jit(solution)/shard_map/ppermute | solution.py:235
  199.5 9.4 %collective-permute-start.22 = (f32[8,128]{1,0:T(8,128)S(1)}, f32[8,128]{1,0:T(8,128)S(1)}, u32[]{:S(2)}, u32[]{:S(2)}) collective-permute-start(f32[8,128]{1,0:T(8,128)S(1)} %add.57), channel_id=1, source_target_pairs={{0,16},{2,18},{4,20},{6,22},{8,24},{10,26},{12,28},{14,30},{16,0},... | collective-permute-start | bytes 12296 | tf_op jit(solution)/shard_map/ppermute | solution.py:235
  214.6 9.0 %update.1 = (f32[2,8,24576]{2,1,0:T(8,128)}, f32[2,8,24576]{2,1,0:T(8,128)}, f32[2,8,24576]{2,1,0:T(8,128)}, f32[2,8,24576]{2,1,0:T(8,128)}, f32[2,8,24576]{2,1,0:T(8,128)}, /*index=5*/f32[2,8,24576]{2,1,0:T(8,128)}) custom-call(f32[2]{0:T(128)} %pad_maximum_fusion.scales_ref, f32[8,128]{1,0:T(8,128)} %add.59.squares_ref, f32[2,8,24576]{2,1,0:T(8,128)} %rest_0_.1, ...), custom_call_target="tpu_custom_call" | custom-call | bytes 22020096 | tf_op jit(solution)/shard_map/update/pallas_call | solution.py:189
  (63 shorter events, 61.4 us)
Async XLA Ops:
  6.0 74.4 %collective-permute-start.3 = (f32[6,8,24576]{2,1,0:T(8,128)}, f32[6,8,24576]{2,1,0:T(8,128)}, u32[]{:S(2)}, u32[]{:S(2)}) collective-permute-start(f32[6,8,24576]{2,1,0:T(8,128)} %joined.1), channel_id=1, source_target_pairs={{0,2},{2,4},{4,6},{6,8},{8,10},{10,12},{12,14},{14,16},{16,18},{18... | collective-permute-start | bytes 14155784 | tf_op jit(solution)/shard_map/ppermute | solution.py:267
  17.2 12.6 %collective-permute-start.10 = (f32[8,8,12288]{2,1,0:T(8,128)}, f32[8,8,12288]{2,1,0:T(8,128)}, u32[]{:S(2)}, u32[]{:S(2)}) collective-permute-start(f32[8,8,12288]{2,1,0:T(8,128)} %get-tuple-element.21), channel_id=1, source_target_pairs={{0,2},{2,0},{4,6},{6,4},{8,10},{10,8},{12,14},{14,12},{16,18},{18,... | collective-permute-start | bytes 9437192 | tf_op jit(solution)/shard_map/ppermute | solution.py:279
  19.8 10.1 %collective-permute-start.11 = (f32[8,8,12288]{2,1,0:T(8,128)}, f32[8,8,12288]{2,1,0:T(8,128)}, u32[]{:S(2)}, u32[]{:S(2)}) collective-permute-start(f32[8,8,12288]{2,1,0:T(8,128)} %get-tuple-element.22), channel_id=1, source_target_pairs={{0,2},{2,0},{4,6},{6,4},{8,10},{10,8},{12,14},{14,12},{16,18},{18,... | collective-permute-start | bytes 9437192 | tf_op jit(solution)/shard_map/ppermute | solution.py:279
  28.8 6.1 %collective-permute-start = (f32[8,8,12288]{2,1,0:T(8,128)}, f32[8,8,12288]{2,1,0:T(8,128)}, u32[]{:S(2)}, u32[]{:S(2)}) collective-permute-start(f32[8,8,12288]{2,1,0:T(8,128)} %get-tuple-element.17), channel_id=1, source_target_pairs={{0,2},{2,0},{4,6},{6,4},{8,10},{10,8},{12,14},{14,12},{16,18},{18,... | collective-permute-start | bytes 9437192 | tf_op jit(solution)/shard_map/ppermute | solution.py:279
  29.3 10.1 %collective-permute-start.1 = (f32[8,8,12288]{2,1,0:T(8,128)}, f32[8,8,12288]{2,1,0:T(8,128)}, u32[]{:S(2)}, u32[]{:S(2)}) collective-permute-start(f32[8,8,12288]{2,1,0:T(8,128)} %get-tuple-element.18), channel_id=1, source_target_pairs={{0,2},{2,0},{4,6},{6,4},{8,10},{10,8},{12,14},{14,12},{16,18},{18,... | collective-permute-start | bytes 9437192 | tf_op jit(solution)/shard_map/ppermute | solution.py:279
  32.8 20.2 %collective-permute-start.15 = (f32[2,8,12288]{2,1,0:T(8,128)}, f32[2,8,12288]{2,1,0:T(8,128)}, u32[]{:S(2)}, u32[]{:S(2)}) collective-permute-start(f32[2,8,12288]{2,1,0:T(8,128)} %shard_sum.27), channel_id=1, source_target_pairs={{0,4},{2,6},{8,0},{10,2},{16,8},{18,10},{24,16},{26,18},{28,24},{3... | collective-permute-start | bytes 2359304 | tf_op jit(solution)/shard_map/ppermute | solution.py:285
  42.3 38.2 %collective-permute-start.2 = (f32[2,8,12288]{2,1,0:T(8,128)}, f32[2,8,12288]{2,1,0:T(8,128)}, u32[]{:S(2)}, u32[]{:S(2)}) collective-permute-start(f32[2,8,12288]{2,1,0:T(8,128)} %shard_sum.16), channel_id=1, source_target_pairs={{0,8},{2,10},{8,16},{10,18},{16,24},{18,26},{24,28},{26,30},{28,20... | collective-permute-start | bytes 2359304 | tf_op jit(solution)/shard_map/ppermute | solution.py:285
  47.3 49.9 %collective-permute-start.12 = (f32[2,8,12288]{2,1,0:T(8,128)}, f32[2,8,12288]{2,1,0:T(8,128)}, u32[]{:S(2)}, u32[]{:S(2)}) collective-permute-start(f32[2,8,12288]{2,1,0:T(8,128)} %shard_sum.24), channel_id=1, source_target_pairs={{0,8},{2,10},{8,16},{10,18},{16,24},{18,26},{24,28},{26,30},{28,20... | collective-permute-start | bytes 2359304 | tf_op jit(solution)/shard_map/ppermute | solution.py:298
  56.2 44.2 %collective-permute-start.16 = (f32[2,8,12288]{2,1,0:T(8,128)}, f32[2,8,12288]{2,1,0:T(8,128)}, u32[]{:S(2)}, u32[]{:S(2)}) collective-permute-start(f32[2,8,12288]{2,1,0:T(8,128)} %shard_sum.28), channel_id=1, source_target_pairs={{0,4},{2,6},{8,0},{10,2},{16,8},{18,10},{24,16},{26,18},{28,24},{3... | collective-permute-start | bytes 2359304 | tf_op jit(solution)/shard_map/ppermute | solution.py:298
  61.2 44.3 %collective-permute-start.7 = (f32[2,8,12288]{2,1,0:T(8,128)}, f32[2,8,12288]{2,1,0:T(8,128)}, u32[]{:S(2)}, u32[]{:S(2)}) collective-permute-start(f32[2,8,12288]{2,1,0:T(8,128)} %shard_sum.20), channel_id=1, source_target_pairs={{0,4},{2,6},{8,0},{10,2},{16,8},{18,10},{24,16},{26,18},{28,24},{3... | collective-permute-start | bytes 2359304 | tf_op jit(solution)/shard_map/ppermute | solution.py:298
  83.6 25.6 %collective-permute-start.4 = (f32[2,8,12288]{2,1,0:T(8,128)}, f32[2,8,12288]{2,1,0:T(8,128)}, u32[]{:S(2)}, u32[]{:S(2)}) collective-permute-start(f32[2,8,12288]{2,1,0:T(8,128)} %shard_sum.17), channel_id=1, source_target_pairs={{0,8},{2,10},{8,16},{10,18},{16,24},{18,26},{24,28},{26,30},{28,20... | collective-permute-start | bytes 2359304 | tf_op jit(solution)/shard_map/ppermute | solution.py:298
  100.4 18.1 %collective-permute-start.13 = (f32[2,8,12288]{2,1,0:T(8,128)}, f32[2,8,12288]{2,1,0:T(8,128)}, u32[]{:S(2)}, u32[]{:S(2)}) collective-permute-start(f32[2,8,12288]{2,1,0:T(8,128)} %shard_sum.25), channel_id=1, source_target_pairs={{0,8},{2,10},{8,16},{10,18},{16,24},{18,26},{24,28},{26,30},{28,20... | collective-permute-start | bytes 2359304 | tf_op jit(solution)/shard_map/ppermute | solution.py:298
  103.5 28.3 %collective-permute-start.17 = (f32[2,8,12288]{2,1,0:T(8,128)}, f32[2,8,12288]{2,1,0:T(8,128)}, u32[]{:S(2)}, u32[]{:S(2)}) collective-permute-start(f32[2,8,12288]{2,1,0:T(8,128)} %shard_sum.29), channel_id=1, source_target_pairs={{0,4},{2,6},{8,0},{10,2},{16,8},{18,10},{24,16},{26,18},{28,24},{3... | collective-permute-start | bytes 2359304 | tf_op jit(solution)/shard_map/ppermute | solution.py:298
  108.7 32.5 %collective-permute-start.8 = (f32[2,8,12288]{2,1,0:T(8,128)}, f32[2,8,12288]{2,1,0:T(8,128)}, u32[]{:S(2)}, u32[]{:S(2)}) collective-permute-start(f32[2,8,12288]{2,1,0:T(8,128)} %shard_sum.21), channel_id=1, source_target_pairs={{0,4},{2,6},{8,0},{10,2},{16,8},{18,10},{24,16},{26,18},{28,24},{3... | collective-permute-start | bytes 2359304 | tf_op jit(solution)/shard_map/ppermute | solution.py:298
  112.4 34.0 %collective-permute-start.5 = (f32[2,8,12288]{2,1,0:T(8,128)}, f32[2,8,12288]{2,1,0:T(8,128)}, u32[]{:S(2)}, u32[]{:S(2)}) collective-permute-start(f32[2,8,12288]{2,1,0:T(8,128)} %shard_sum.18), channel_id=1, source_target_pairs={{0,8},{2,10},{8,16},{10,18},{16,24},{18,26},{24,28},{26,30},{28,20... | collective-permute-start | bytes 2359304 | tf_op jit(solution)/shard_map/ppermute | solution.py:298
  121.6 30.6 %collective-permute-start.14 = (f32[2,8,12288]{2,1,0:T(8,128)}, f32[2,8,12288]{2,1,0:T(8,128)}, u32[]{:S(2)}, u32[]{:S(2)}) collective-permute-start(f32[2,8,12288]{2,1,0:T(8,128)} %shard_sum.26), channel_id=1, source_target_pairs={{0,8},{2,10},{8,16},{10,18},{16,24},{18,26},{24,28},{26,30},{28,20... | collective-permute-start | bytes 2359304 | tf_op jit(solution)/shard_map/ppermute | solution.py:298
  135.0 23.1 %collective-permute-start.18 = (f32[2,8,12288]{2,1,0:T(8,128)}, f32[2,8,12288]{2,1,0:T(8,128)}, u32[]{:S(2)}, u32[]{:S(2)}) collective-permute-start(f32[2,8,12288]{2,1,0:T(8,128)} %shard_sum.30), channel_id=1, source_target_pairs={{0,4},{2,6},{8,0},{10,2},{16,8},{18,10},{24,16},{26,18},{28,24},{3... | collective-permute-start | bytes 2359304 | tf_op jit(solution)/shard_map/ppermute | solution.py:298
  144.3 35.3 %collective-permute-start.9 = (f32[2,8,12288]{2,1,0:T(8,128)}, f32[2,8,12288]{2,1,0:T(8,128)}, u32[]{:S(2)}, u32[]{:S(2)}) collective-permute-start(f32[2,8,12288]{2,1,0:T(8,128)} %shard_sum.22), channel_id=1, source_target_pairs={{0,4},{2,6},{8,0},{10,2},{16,8},{18,10},{24,16},{26,18},{28,24},{3... | collective-permute-start | bytes 2359304 | tf_op jit(solution)/shard_map/ppermute | solution.py:298
  149.4 30.2 %collective-permute-start.6 = (f32[2,8,12288]{2,1,0:T(8,128)}, f32[2,8,12288]{2,1,0:T(8,128)}, u32[]{:S(2)}, u32[]{:S(2)}) collective-permute-start(f32[2,8,12288]{2,1,0:T(8,128)} %shard_sum.19), channel_id=1, source_target_pairs={{0,8},{2,10},{8,16},{10,18},{16,24},{18,26},{24,28},{26,30},{28,20... | collective-permute-start | bytes 2359304 | tf_op jit(solution)/shard_map/ppermute | solution.py:298
  161.5 53.1 %collective-permute-start.25 = (f32[2,8,12288]{2,1,0:T(8,128)}, f32[2,8,12288]{2,1,0:T(8,128)}, u32[]{:S(2)}, u32[]{:S(2)}) collective-permute-start(f32[2,8,12288]{2,1,0:T(8,128)} %get-tuple-element.25.rest_7_), channel_id=1, source_target_pairs={{0,2},{2,4},{4,6},{6,8},{8,10},{10,12},{12,14},{14,16},{16,18},{18... | collective-permute-start | bytes 2359304 | tf_op jit(solution)/shard_map/ppermute | solution.py:302
  183.1 31.6 %collective-permute-start.24 = (f32[2,8,12288]{2,1,0:T(8,128)}, f32[2,8,12288]{2,1,0:T(8,128)}, u32[]{:S(2)}, u32[]{:S(2)}) collective-permute-start(f32[2,8,12288]{2,1,0:T(8,128)} %get-tuple-element.24.rest_6_), channel_id=1, source_target_pairs={{0,2},{2,4},{4,6},{6,8},{8,10},{10,12},{12,14},{14,16},{16,18},{18... | collective-permute-start | bytes 2359304 | tf_op jit(solution)/shard_map/ppermute | solution.py:302
  189.9 3.8 %collective-permute-start.20 = (f32[8,128]{1,0:T(8,128)S(1)}, f32[8,128]{1,0:T(8,128)S(1)}, u32[]{:S(2)}, u32[]{:S(2)}) collective-permute-start(f32[8,128]{1,0:T(8,128)S(1)} %add.55), channel_id=1, source_target_pairs={{0,4},{2,6},{4,0},{6,2},{8,12},{10,14},{12,8},{14,10},{16,20},{18,... | collective-permute-start | bytes 12296 | tf_op jit(solution)/shard_map/ppermute | solution.py:235
  193.7 5.8 %collective-permute-start.21 = (f32[8,128]{1,0:T(8,128)S(1)}, f32[8,128]{1,0:T(8,128)S(1)}, u32[]{:S(2)}, u32[]{:S(2)}) collective-permute-start(f32[8,128]{1,0:T(8,128)S(1)} %add.56), channel_id=1, source_target_pairs={{0,8},{2,10},{4,12},{6,14},{8,0},{10,2},{12,4},{14,6},{16,24},{18,... | collective-permute-start | bytes 12296 | tf_op jit(solution)/shard_map/ppermute | solution.py:235
  199.5 10.9 %collective-permute-start.22 = (f32[8,128]{1,0:T(8,128)S(1)}, f32[8,128]{1,0:T(8,128)S(1)}, u32[]{:S(2)}, u32[]{:S(2)}) collective-permute-start(f32[8,128]{1,0:T(8,128)S(1)} %add.57), channel_id=1, source_target_pairs={{0,16},{2,18},{4,20},{6,22},{8,24},{10,26},{12,28},{14,30},{16,0},... | collective-permute-start | bytes 12296 | tf_op jit(solution)/shard_map/ppermute | solution.py:235
  (2 other events, 4.8 us)

commit v6 on v5

--- a/solution.py
+++ b/solution.py
@@ -213,7 +213,7 @@
 
 def joined(arrays):
     layers, own, columns = arrays[0].shape
-    size = block_of(columns, 8192)
+    size = block_of(columns, 12288)
     return pl.pallas_call(
         joined_kernel,
         grid=(columns // size,),
@@ -226,15 +226,28 @@
     )(*arrays)
 
 
-def total_over(value, axis):
-    peers = lax.axis_size(axis)
-    if peers & (peers - 1):
-        return lax.psum(value, axis)
+def total_of(value, later):
+    peers, groups = lax.axis_size("dp"), lax.axis_size("mp")
+    if peers & (peers - 1) or groups & (groups - 1) or peers < 4:
+        return lax.psum(value, ("dp", "mp")), later
+
+    def exchanged(value, axis, members, bit):
+        return value + lax.ppermute(value, axis, [(i, i ^ bit) for i in members])
+
+    value = exchanged(value, "dp", range(peers), 1)
+    value = exchanged(value, "dp", range(peers), 2)
+    value, later = lax.optimization_barrier((value, later))
+    first = [i for i in range(peers) if not i & 2]
+    bit = 4
+    while bit < peers:
+        value = exchanged(value, "dp", first, bit)
+        bit *= 2
     bit = 1
-    while bit < peers:
-        value = value + lax.ppermute(value, axis, [(i, i ^ bit) for i in range(peers)])
+    while bit < groups:
+        value = exchanged(value, "mp", range(groups), bit)
         bit *= 2
-    return value
+    passed = lax.ppermute(value, "dp", [(i, i | 2) for i in first])
+    return jnp.where(lax.axis_index("dp") & 2 == 0, value, passed), later
 
 
 def local(acc_grads, activations, cotangent, params, first_moment, second_moment, step):
@@ -299,10 +312,12 @@
     squares = None
     for k in range(streams):
         grads[k], part = shard_sum(last_kernel, tables[0], 0, keep[k], theirs[k], *sent[k])
-        peer_grads[k] = lax.ppermute(grads[k], "dp", onward)
+        if k:
+            peer_grads[k] = lax.ppermute(grads[k], "dp", onward)
         squares = part if squares is None else squares + part
 
-    squares = total_over(total_over(squares, "dp"), "mp")
+    squares, waiting = total_of(squares, grads[0])
+    peer_grads[0] = lax.ppermute(waiting, "dp", onward)
     bound = float((layers * rows * columns * lax.axis_size("mp")) ** 0.5)
     count = step.astype(jnp.float32)
     scales = jnp.concatenate(

time: 225 us -> 221 us (0.982)
  starting transfers between devices: 70.5 us -> 45.1 us
  waiting for transfers between devices: 64.9 us -> 87.3 us
    ppermute x2 -> x1, starting transfers between devices: 23.1 us -> 0.06 us  [local(): peer_grads[k] = lax.ppermute(grads[k], 'dp', onward)]
    ppermute x12, waiting for transfers between devices: 31.2 us -> 49.5 us  [local(): sent[k][way] = lax.ppermute(total, 'dp', hop(by))]
    ppermute x5 -> x7, waiting for transfers between devices: 6.71 us -> 9.85 us  [the longest x5 7.3 us: exchanged(): return value + lax.ppermute(value, axis, [(i, i ^ bit) for i in members])]
    ppermute x12, starting transfers between devices: 23.5 us -> 20.5 us  [local(): sent[k][way] = lax.ppermute(total, 'dp', hop(by))]
    ppermute x5 -> x7, starting transfers between devices: 17.2 us -> 17.9 us  [the longest x5 16.6 us: exchanged(): return value + lax.ppermute(value, axis, [(i, i ^ bit) for i in members])]
  transfers between devices with their start and end apart: 26 -> 27, of which waited for: 15 -> 17; matrix products, arithmetic and copies ran while one was open for 2% -> 2% of each run, Pallas kernels for 30% -> 29%
where the time goes in v6:
time: 221 us; the launch traced here: 220 us
  waiting for transfers between devices  87.3 us (40%)
  Pallas kernels  80.7 us (37%)
  starting transfers between devices  45.1 us (20%)
  other arithmetic  4.19 us (2%)
    pallas_call x16, Pallas kernels, shard_sum(): pl.pallas_call(functools.partial(body, layers), grid_spec=pltpu.PrefetchS...  49.7 us
    ppermute x12, waiting for transfers between devices, local(): sent[k][way] = lax.ppermute(total, 'dp', hop(by))  49.5 us
    ppermute x2, waiting for transfers between devices, local(): sent[k][k % 2] = lax.ppermute(total, 'dp', hop(-1 if k % 2 else 1))  22.9 us
    ppermute x12, starting transfers between devices, local(): sent[k][way] = lax.ppermute(total, 'dp', hop(by))  20.5 us
    pallas_call x2, Pallas kernels, make_terms(): pl.pallas_call(functools.partial(terms_kernel, order, layers), grid_spec=...  18 us
    ppermute x5, starting transfers between devices, exchanged(): return value + lax.ppermute(value, axis, [(i, i ^ bit) for i in members])  16.6 us
    pallas_call x1, Pallas kernels, update(): pl.pallas_call(functools.partial(update_kernel, count, bound), grid=(bloc...  8.98 us
    ppermute x5, waiting for transfers between devices, exchanged(): return value + lax.ppermute(value, axis, [(i, i ^ bit) for i in members])  7.3 us
  transfers between devices with their start and end apart: 27, of which 17 were waited for; matrix products, arithmetic and copies ran while one was open for 2% of the time, Pallas kernels for 29%

profile of v6, /device:TPU:0, one launch (start us, length us, event | category | flops | bytes accessed | tf_op | source)
XLA Modules:
  0.0 219.6 jit_solution(1293213862746026259)
XLA Ops:
  0.6 4.0 %joined.1 = f32[6,8,24576]{2,1,0:T(8,128)} custom-call(f32[2,8,24576]{2,1,0:T(8,128)} %rest_0_.1, f32[2,8,24576]{2,1,0:T(8,128)} %rest_1_.1, f32[2,8,24576]{2,1,0:T(8,128)} %rest_2_.1), custom_call_target="tpu_custom_call" | custom-call | bytes 9437184 | tf_op jit(solution)/shard_map/joined/pallas_call | solution.py:217
  6.9 9.0 %terms.3 = (f32[8,2,8,12288]{3,2,1,0:T(8,128)}, f32[8,8,12288]{2,1,0:T(8,128)}, f32[8,8,12288]{2,1,0:T(8,128)}) custom-call(s32[1]{0:T(128)} %bitcast.core_ref, bf16[256,256]{1,0:T(8,128)(2,1)} %copy.14.inputs_ref, bf16[1,2,128,24576]{3,2,1,0:T(8,128)(2,1)} %earlier_ref.3, bf16[128,2,24576]{2,1,0:T(2,128)(2,1)} %outgrad_ref.3), custom_call_target="tpu_custom_call" | custom-call | bytes 25165824 | tf_op jit(solution)/shard_map/terms/pallas_call | solution.py:71
  18.5 9.0 %terms.2 = (f32[8,2,8,12288]{3,2,1,0:T(8,128)}, f32[8,8,12288]{2,1,0:T(8,128)}, f32[8,8,12288]{2,1,0:T(8,128)}) custom-call(s32[1]{0:T(128)} %bitcast.core_ref, bf16[256,256]{1,0:T(8,128)(2,1)} %copy.14.inputs_ref, bf16[1,2,128,24576]{3,2,1,0:T(8,128)(2,1)} %earlier_ref.3, bf16[128,2,24576]{2,1,0:T(2,128)(2,1)} %outgrad_ref.3), custom_call_target="tpu_custom_call" | custom-call | bytes 25165824 | tf_op jit(solution)/shard_map/terms/pallas_call | solution.py:71
  33.6 4.5 %collective-permute-done.1.rest_1_ = f32[8,8,12288]{2,1,0:T(8,128)} collective-permute-done((f32[8,8,12288]{2,1,0:T(8,128)}, f32[8,8,12288]{2,1,0:T(8,128)}, u32[]{:S(2)}, u32[]{:S(2)}) %collective-permute-start.1) | collective-permute-done | bytes 3145760 | tf_op jit(solution)/shard_map/ppermute | solution.py:292
  57.0 22.1 %collective-permute-done.2.rest_2_ = f32[2,8,12288]{2,1,0:T(8,128)} collective-permute-done((f32[2,8,12288]{2,1,0:T(8,128)}, f32[2,8,12288]{2,1,0:T(8,128)}, u32[]{:S(2)}, u32[]{:S(2)}) %collective-permute-start.2) | collective-permute-done | bytes 786464 | tf_op jit(solution)/shard_map/ppermute | solution.py:298
  79.1 3.1 %shard_sum.17 = f32[2,8,12288]{2,1,0:T(8,128)} custom-call(s32[6]{0:T(128)} %pad_add_fusion.shard_ref, f32[8,2,8,12288]{3,2,1,0:T(8,128)} %get-tuple-element.18.keep_ref, f32[8,8,12288]{2,1,0:T(8,128)} %collective-permute-done.rest_0_, f32[8,8,12288]{2,1,0:T(8,128)} %collective-permute-done.1.rest_1_, f32[2,8,12288]{2,1,0:T(8,128)} %collective-permute-done.2.rest_2_, ...), custom_call_target="tpu_custom_call" | custom-call | bytes 3145728 | tf_op jit(solution)/shard_map/shard_sum/pallas_call | solution.py:137
  82.2 7.7 %collective-permute-start.4 = (f32[2,8,12288]{2,1,0:T(8,128)}, f32[2,8,12288]{2,1,0:T(8,128)}, u32[]{:S(2)}, u32[]{:S(2)}) collective-permute-start(f32[2,8,12288]{2,1,0:T(8,128)} %shard_sum.17), channel_id=1, source_target_pairs={{0,8},{2,10},{8,16},{10,18},{16,24},{18,26},{24,28},{26,30},{28,20... | collective-permute-start | bytes 2359304 | tf_op jit(solution)/shard_map/ppermute | solution.py:311
  90.0 5.9 %collective-permute-done.12.rest_2_ = f32[2,8,12288]{2,1,0:T(8,128)} collective-permute-done((f32[2,8,12288]{2,1,0:T(8,128)}, f32[2,8,12288]{2,1,0:T(8,128)}, u32[]{:S(2)}, u32[]{:S(2)}) %collective-permute-start.12) | collective-permute-done | bytes 786464 | tf_op jit(solution)/shard_map/ppermute | solution.py:311
  99.0 3.1 %shard_sum.21 = f32[2,8,12288]{2,1,0:T(8,128)} custom-call(s32[6]{0:T(128)} %pad_add_fusion.1.shard_ref, f32[8,2,8,12288]{3,2,1,0:T(8,128)} %get-tuple-element.18.keep_ref, f32[8,8,12288]{2,1,0:T(8,128)} %collective-permute-done.rest_0_, f32[8,8,12288]{2,1,0:T(8,128)} %collective-permute-done.1.rest_1_, f32[2,8,12288]{2,1,0:T(8,128)} %collective-permute-done.7.rest_2_), custom_call_target="tpu_custom_call" | custom-call | bytes 3145728 | tf_op jit(solution)/shard_map/shard_sum/pallas_call | solution.py:137
  104.2 3.1 %shard_sum.29 = f32[2,8,12288]{2,1,0:T(8,128)} custom-call(s32[6]{0:T(128)} %pad_add_fusion.1.shard_ref, f32[8,2,8,12288]{3,2,1,0:T(8,128)} %get-tuple-element.22.keep_ref, f32[8,8,12288]{2,1,0:T(8,128)} %collective-permute-done.10.rest_0_, f32[8,8,12288]{2,1,0:T(8,128)} %collective-permute-done.11.rest_1_, f32[2,8,12288]{2,1,0:T(8,128)} %collective-permute-done.16.rest_2_), custom_call_target="tpu_custom_call" | custom-call | bytes 3145728 | tf_op jit(solution)/shard_map/shard_sum/pallas_call | solution.py:137
  107.9 3.1 %shard_sum.18 = f32[2,8,12288]{2,1,0:T(8,128)} custom-call(s32[6]{0:T(128)} %pad_add_fusion.shard_ref, f32[8,2,8,12288]{3,2,1,0:T(8,128)} %get-tuple-element.18.keep_ref, f32[8,8,12288]{2,1,0:T(8,128)} %collective-permute-done.rest_0_, f32[8,8,12288]{2,1,0:T(8,128)} %collective-permute-done.1.rest_1_, f32[2,8,12288]{2,1,0:T(8,128)} %collective-permute-done.4.rest_2_), custom_call_target="tpu_custom_call" | custom-call | bytes 3145728 | tf_op jit(solution)/shard_map/shard_sum/pallas_call | solution.py:137
  112.5 8.8 %collective-permute-done.13.rest_2_ = f32[2,8,12288]{2,1,0:T(8,128)} collective-permute-done((f32[2,8,12288]{2,1,0:T(8,128)}, f32[2,8,12288]{2,1,0:T(8,128)}, u32[]{:S(2)}, u32[]{:S(2)}) %collective-permute-start.13) | collective-permute-done | bytes 786464 | tf_op jit(solution)/shard_map/ppermute | solution.py:311
  121.3 3.1 %shard_sum.26 = f32[2,8,12288]{2,1,0:T(8,128)} custom-call(s32[6]{0:T(128)} %pad_add_fusion.shard_ref, f32[8,2,8,12288]{3,2,1,0:T(8,128)} %get-tuple-element.22.keep_ref, f32[8,8,12288]{2,1,0:T(8,128)} %collective-permute-done.10.rest_0_, f32[8,8,12288]{2,1,0:T(8,128)} %collective-permute-done.11.rest_1_, f32[2,8,12288]{2,1,0:T(8,128)} %collective-permute-done.13.rest_2_), custom_call_target="tpu_custom_call" | custom-call | bytes 3145728 | tf_op jit(solution)/shard_map/shard_sum/pallas_call | solution.py:137
  124.4 3.1 %shard_sum.22 = f32[2,8,12288]{2,1,0:T(8,128)} custom-call(s32[6]{0:T(128)} %pad_add_fusion.1.shard_ref, f32[8,2,8,12288]{3,2,1,0:T(8,128)} %get-tuple-element.18.keep_ref, f32[8,8,12288]{2,1,0:T(8,128)} %collective-permute-done.rest_0_, f32[8,8,12288]{2,1,0:T(8,128)} %collective-permute-done.1.rest_1_, f32[2,8,12288]{2,1,0:T(8,128)} %collective-permute-done.8.rest_2_), custom_call_target="tpu_custom_call" | custom-call | bytes 3145728 | tf_op jit(solution)/shard_map/shard_sum/pallas_call | solution.py:137
  129.5 9.8 %collective-permute-done.17.rest_2_ = f32[2,8,12288]{2,1,0:T(8,128)} collective-permute-done((f32[2,8,12288]{2,1,0:T(8,128)}, f32[2,8,12288]{2,1,0:T(8,128)}, u32[]{:S(2)}, u32[]{:S(2)}) %collective-permute-start.17) | collective-permute-done | bytes 786464 | tf_op jit(solution)/shard_map/ppermute | solution.py:311
  145.0 3.1 %shard_sum.19 = f32[2,8,12288]{2,1,0:T(8,128)} custom-call(s32[6]{0:T(128)} %pad_add_fusion.shard_ref, f32[8,2,8,12288]{3,2,1,0:T(8,128)} %get-tuple-element.18.keep_ref, f32[8,8,12288]{2,1,0:T(8,128)} %collective-permute-done.rest_0_, f32[8,8,12288]{2,1,0:T(8,128)} %collective-permute-done.1.rest_1_, f32[2,8,12288]{2,1,0:T(8,128)} %collective-permute-done.5.rest_2_), custom_call_target="tpu_custom_call" | custom-call | bytes 3145728 | tf_op jit(solution)/shard_map/shard_sum/pallas_call | solution.py:137
  148.1 6.9 %collective-permute-done.14.rest_2_ = f32[2,8,12288]{2,1,0:T(8,128)} collective-permute-done((f32[2,8,12288]{2,1,0:T(8,128)}, f32[2,8,12288]{2,1,0:T(8,128)}, u32[]{:S(2)}, u32[]{:S(2)}) %collective-permute-start.14) | collective-permute-done | bytes 786464 | tf_op jit(solution)/shard_map/ppermute | solution.py:311
  155.0 18.1 %collective-permute-done.18.rest_3_ = f32[2,8,12288]{2,1,0:T(8,128)} collective-permute-done((f32[2,8,12288]{2,1,0:T(8,128)}, f32[2,8,12288]{2,1,0:T(8,128)}, u32[]{:S(2)}, u32[]{:S(2)}) %collective-permute-start.18) | collective-permute-done | bytes 786464 | tf_op jit(solution)/shard_map/ppermute | solution.py:311
  173.1 3.5 %shard_sum.31 = (f32[2,8,12288]{2,1,0:T(8,128)}, f32[8,128]{1,0:T(8,128)}) custom-call(s32[6]{0:T(128)} %pad_add_fusion.shard_ref, f32[8,2,8,12288]{3,2,1,0:T(8,128)} %get-tuple-element.22.keep_ref, f32[8,8,12288]{2,1,0:T(8,128)} %collective-permute-done.10.rest_0_, f32[8,8,12288]{2,1,0:T(8,128)} %collective-permute-done.11.rest_1_, ...), custom_call_target="tpu_custom_call" | custom-call | bytes 3932160 | tf_op jit(solution)/shard_map/shard_sum/pallas_call | solution.py:137
  176.6 3.5 %shard_sum.23 = (f32[2,8,12288]{2,1,0:T(8,128)}, f32[8,128]{1,0:T(8,128)}) custom-call(s32[6]{0:T(128)} %pad_add_fusion.shard_ref, f32[8,2,8,12288]{3,2,1,0:T(8,128)} %get-tuple-element.18.keep_ref, f32[8,8,12288]{2,1,0:T(8,128)} %collective-permute-done.rest_0_, f32[8,8,12288]{2,1,0:T(8,128)} %collective-permute-done.1.rest_1_, ...), custom_call_target="tpu_custom_call" | custom-call | bytes 3932160 | tf_op jit(solution)/shard_map/shard_sum/pallas_call | solution.py:137
  180.7 4.0 %collective-permute-start.19 = (f32[8,128]{1,0:T(8,128)S(1)}, f32[8,128]{1,0:T(8,128)S(1)}, u32[]{:S(2)}, u32[]{:S(2)}) collective-permute-start(f32[8,128]{1,0:T(8,128)S(1)} %add.54), channel_id=1, source_target_pairs={{0,2},{2,0},{4,6},{6,4},{8,10},{10,8},{12,14},{14,12},{16,18},{18,... | collective-permute-start | bytes 12296 | tf_op jit(solution)/shard_map/ppermute | solution.py:235
  189.4 3.4 %collective-permute-start.21 = (f32[8,128]{1,0:T(8,128)S(1)}, f32[8,128]{1,0:T(8,128)S(1)}, u32[]{:S(2)}, u32[]{:S(2)}) collective-permute-start(f32[8,128]{1,0:T(8,128)S(1)} %add.56), channel_id=1, source_target_pairs={{0,8},{2,10},{8,0},{10,2},{16,24},{18,26},{24,16},{26,18},{1,9},{3... | collective-permute-start | bytes 12296 | tf_op jit(solution)/shard_map/ppermute | solution.py:235
  194.9 5.5 %collective-permute-start.22 = (f32[8,128]{1,0:T(8,128)S(1)}, f32[8,128]{1,0:T(8,128)S(1)}, u32[]{:S(2)}, u32[]{:S(2)}) collective-permute-start(f32[8,128]{1,0:T(8,128)S(1)} %add.57), channel_id=1, source_target_pairs={{0,16},{2,18},{8,24},{10,26},{16,0},{18,2},{24,8},{26,10},{1,17},{... | collective-permute-start | bytes 12296 | tf_op jit(solution)/shard_map/ppermute | solution.py:235
  210.6 9.0 %update.1 = (f32[2,8,24576]{2,1,0:T(8,128)}, f32[2,8,24576]{2,1,0:T(8,128)}, f32[2,8,24576]{2,1,0:T(8,128)}, f32[2,8,24576]{2,1,0:T(8,128)}, f32[2,8,24576]{2,1,0:T(8,128)}, /*index=5*/f32[2,8,24576]{2,1,0:T(8,128)}) custom-call(f32[2]{0:T(128)} %pad_maximum_fusion.scales_ref, f32[8,128]{1,0:T(8,128)} %broadcast_select_fusion.squares_ref, ...), custom_call_target="tpu_custom_call" | custom-call | bytes 22020096 | tf_op jit(solution)/shard_map/update/pallas_call | solution.py:189
  (66 shorter events, 61.6 us)
Async XLA Ops:
  4.7 74.4 %collective-permute-start.3 = (f32[6,8,24576]{2,1,0:T(8,128)}, f32[6,8,24576]{2,1,0:T(8,128)}, u32[]{:S(2)}, u32[]{:S(2)}) collective-permute-start(f32[6,8,24576]{2,1,0:T(8,128)} %joined.1), channel_id=1, source_target_pairs={{0,2},{2,4},{4,6},{6,8},{8,10},{10,12},{12,14},{14,16},{16,18},{18... | collective-permute-start | bytes 14155784 | tf_op jit(solution)/shard_map/ppermute | solution.py:280
  15.9 12.7 %collective-permute-start.10 = (f32[8,8,12288]{2,1,0:T(8,128)}, f32[8,8,12288]{2,1,0:T(8,128)}, u32[]{:S(2)}, u32[]{:S(2)}) collective-permute-start(f32[8,8,12288]{2,1,0:T(8,128)} %get-tuple-element.23), channel_id=1, source_target_pairs={{0,2},{2,0},{4,6},{6,4},{8,10},{10,8},{12,14},{14,12},{16,18},{18,... | collective-permute-start | bytes 9437192 | tf_op jit(solution)/shard_map/ppermute | solution.py:292
  18.5 10.1 %collective-permute-start.11 = (f32[8,8,12288]{2,1,0:T(8,128)}, f32[8,8,12288]{2,1,0:T(8,128)}, u32[]{:S(2)}, u32[]{:S(2)}) collective-permute-start(f32[8,8,12288]{2,1,0:T(8,128)} %get-tuple-element.24), channel_id=1, source_target_pairs={{0,2},{2,0},{4,6},{6,4},{8,10},{10,8},{12,14},{14,12},{16,18},{18,... | collective-permute-start | bytes 9437192 | tf_op jit(solution)/shard_map/ppermute | solution.py:292
  27.5 6.1 %collective-permute-start = (f32[8,8,12288]{2,1,0:T(8,128)}, f32[8,8,12288]{2,1,0:T(8,128)}, u32[]{:S(2)}, u32[]{:S(2)}) collective-permute-start(f32[8,8,12288]{2,1,0:T(8,128)} %get-tuple-element.19), channel_id=1, source_target_pairs={{0,2},{2,0},{4,6},{6,4},{8,10},{10,8},{12,14},{14,12},{16,18},{18,... | collective-permute-start | bytes 9437192 | tf_op jit(solution)/shard_map/ppermute | solution.py:292
  28.0 10.1 %collective-permute-start.1 = (f32[8,8,12288]{2,1,0:T(8,128)}, f32[8,8,12288]{2,1,0:T(8,128)}, u32[]{:S(2)}, u32[]{:S(2)}) collective-permute-start(f32[8,8,12288]{2,1,0:T(8,128)} %get-tuple-element.20), channel_id=1, source_target_pairs={{0,2},{2,0},{4,6},{6,4},{8,10},{10,8},{12,14},{14,12},{16,18},{18,... | collective-permute-start | bytes 9437192 | tf_op jit(solution)/shard_map/ppermute | solution.py:292
  31.5 20.2 %collective-permute-start.15 = (f32[2,8,12288]{2,1,0:T(8,128)}, f32[2,8,12288]{2,1,0:T(8,128)}, u32[]{:S(2)}, u32[]{:S(2)}) collective-permute-start(f32[2,8,12288]{2,1,0:T(8,128)} %shard_sum.27), channel_id=1, source_target_pairs={{0,4},{2,6},{8,0},{10,2},{16,8},{18,10},{24,16},{26,18},{28,24},{3... | collective-permute-start | bytes 2359304 | tf_op jit(solution)/shard_map/ppermute | solution.py:298
  41.0 38.1 %collective-permute-start.2 = (f32[2,8,12288]{2,1,0:T(8,128)}, f32[2,8,12288]{2,1,0:T(8,128)}, u32[]{:S(2)}, u32[]{:S(2)}) collective-permute-start(f32[2,8,12288]{2,1,0:T(8,128)} %shard_sum.16), channel_id=1, source_target_pairs={{0,8},{2,10},{8,16},{10,18},{16,24},{18,26},{24,28},{26,30},{28,20... | collective-permute-start | bytes 2359304 | tf_op jit(solution)/shard_map/ppermute | solution.py:298
  46.0 49.9 %collective-permute-start.12 = (f32[2,8,12288]{2,1,0:T(8,128)}, f32[2,8,12288]{2,1,0:T(8,128)}, u32[]{:S(2)}, u32[]{:S(2)}) collective-permute-start(f32[2,8,12288]{2,1,0:T(8,128)} %shard_sum.24), channel_id=1, source_target_pairs={{0,8},{2,10},{8,16},{10,18},{16,24},{18,26},{24,28},{26,30},{28,20... | collective-permute-start | bytes 2359304 | tf_op jit(solution)/shard_map/ppermute | solution.py:311
  50.5 48.5 %collective-permute-start.7 = (f32[2,8,12288]{2,1,0:T(8,128)}, f32[2,8,12288]{2,1,0:T(8,128)}, u32[]{:S(2)}, u32[]{:S(2)}) collective-permute-start(f32[2,8,12288]{2,1,0:T(8,128)} %shard_sum.20), channel_id=1, source_target_pairs={{0,4},{2,6},{8,0},{10,2},{16,8},{18,10},{24,16},{26,18},{28,24},{3... | collective-permute-start | bytes 2359304 | tf_op jit(solution)/shard_map/ppermute | solution.py:311
  54.9 49.3 %collective-permute-start.16 = (f32[2,8,12288]{2,1,0:T(8,128)}, f32[2,8,12288]{2,1,0:T(8,128)}, u32[]{:S(2)}, u32[]{:S(2)}) collective-permute-start(f32[2,8,12288]{2,1,0:T(8,128)} %shard_sum.28), channel_id=1, source_target_pairs={{0,4},{2,6},{8,0},{10,2},{16,8},{18,10},{24,16},{26,18},{28,24},{3... | collective-permute-start | bytes 2359304 | tf_op jit(solution)/shard_map/ppermute | solution.py:311
  82.2 25.6 %collective-permute-start.4 = (f32[2,8,12288]{2,1,0:T(8,128)}, f32[2,8,12288]{2,1,0:T(8,128)}, u32[]{:S(2)}, u32[]{:S(2)}) collective-permute-start(f32[2,8,12288]{2,1,0:T(8,128)} %shard_sum.17), channel_id=1, source_target_pairs={{0,8},{2,10},{8,16},{10,18},{16,24},{18,26},{24,28},{26,30},{28,20... | collective-permute-start | bytes 2359304 | tf_op jit(solution)/shard_map/ppermute | solution.py:311
  99.0 22.2 %collective-permute-start.13 = (f32[2,8,12288]{2,1,0:T(8,128)}, f32[2,8,12288]{2,1,0:T(8,128)}, u32[]{:S(2)}, u32[]{:S(2)}) collective-permute-start(f32[2,8,12288]{2,1,0:T(8,128)} %shard_sum.25), channel_id=1, source_target_pairs={{0,8},{2,10},{8,16},{10,18},{16,24},{18,26},{24,28},{26,30},{28,20... | collective-permute-start | bytes 2359304 | tf_op jit(solution)/shard_map/ppermute | solution.py:311
  102.2 22.2 %collective-permute-start.8 = (f32[2,8,12288]{2,1,0:T(8,128)}, f32[2,8,12288]{2,1,0:T(8,128)}, u32[]{:S(2)}, u32[]{:S(2)}) collective-permute-start(f32[2,8,12288]{2,1,0:T(8,128)} %shard_sum.21), channel_id=1, source_target_pairs={{0,4},{2,6},{8,0},{10,2},{16,8},{18,10},{24,16},{26,18},{28,24},{3... | collective-permute-start | bytes 2359304 | tf_op jit(solution)/shard_map/ppermute | solution.py:311
  107.3 32.0 %collective-permute-start.17 = (f32[2,8,12288]{2,1,0:T(8,128)}, f32[2,8,12288]{2,1,0:T(8,128)}, u32[]{:S(2)}, u32[]{:S(2)}) collective-permute-start(f32[2,8,12288]{2,1,0:T(8,128)} %shard_sum.29), channel_id=1, source_target_pairs={{0,4},{2,6},{8,0},{10,2},{16,8},{18,10},{24,16},{26,18},{28,24},{3... | collective-permute-start | bytes 2359304 | tf_op jit(solution)/shard_map/ppermute | solution.py:311
  111.0 34.0 %collective-permute-start.5 = (f32[2,8,12288]{2,1,0:T(8,128)}, f32[2,8,12288]{2,1,0:T(8,128)}, u32[]{:S(2)}, u32[]{:S(2)}) collective-permute-start(f32[2,8,12288]{2,1,0:T(8,128)} %shard_sum.18), channel_id=1, source_target_pairs={{0,8},{2,10},{8,16},{10,18},{16,24},{18,26},{24,28},{26,30},{28,20... | collective-permute-start | bytes 2359304 | tf_op jit(solution)/shard_map/ppermute | solution.py:311
  124.4 30.6 %collective-permute-start.14 = (f32[2,8,12288]{2,1,0:T(8,128)}, f32[2,8,12288]{2,1,0:T(8,128)}, u32[]{:S(2)}, u32[]{:S(2)}) collective-permute-start(f32[2,8,12288]{2,1,0:T(8,128)} %shard_sum.26), channel_id=1, source_target_pairs={{0,8},{2,10},{8,16},{10,18},{16,24},{18,26},{24,28},{26,30},{28,20... | collective-permute-start | bytes 2359304 | tf_op jit(solution)/shard_map/ppermute | solution.py:311
  127.5 49.0 %collective-permute-start.9 = (f32[2,8,12288]{2,1,0:T(8,128)}, f32[2,8,12288]{2,1,0:T(8,128)}, u32[]{:S(2)}, u32[]{:S(2)}) collective-permute-start(f32[2,8,12288]{2,1,0:T(8,128)} %shard_sum.22), channel_id=1, source_target_pairs={{0,4},{2,6},{8,0},{10,2},{16,8},{18,10},{24,16},{26,18},{28,24},{3... | collective-permute-start | bytes 2359304 | tf_op jit(solution)/shard_map/ppermute | solution.py:311
  142.5 30.6 %collective-permute-start.18 = (f32[2,8,12288]{2,1,0:T(8,128)}, f32[2,8,12288]{2,1,0:T(8,128)}, u32[]{:S(2)}, u32[]{:S(2)}) collective-permute-start(f32[2,8,12288]{2,1,0:T(8,128)} %shard_sum.30), channel_id=1, source_target_pairs={{0,4},{2,6},{8,0},{10,2},{16,8},{18,10},{24,16},{26,18},{28,24},{3... | collective-permute-start | bytes 2359304 | tf_op jit(solution)/shard_map/ppermute | solution.py:311
  148.1 28.5 %collective-permute-start.6 = (f32[2,8,12288]{2,1,0:T(8,128)}, f32[2,8,12288]{2,1,0:T(8,128)}, u32[]{:S(2)}, u32[]{:S(2)}) collective-permute-start(f32[2,8,12288]{2,1,0:T(8,128)} %shard_sum.19), channel_id=1, source_target_pairs={{0,8},{2,10},{8,16},{10,18},{16,24},{18,26},{24,28},{26,30},{28,20... | collective-permute-start | bytes 2359304 | tf_op jit(solution)/shard_map/ppermute | solution.py:311
  180.7 4.8 %collective-permute-start.19 = (f32[8,128]{1,0:T(8,128)S(1)}, f32[8,128]{1,0:T(8,128)S(1)}, u32[]{:S(2)}, u32[]{:S(2)}) collective-permute-start(f32[8,128]{1,0:T(8,128)S(1)} %add.54), channel_id=1, source_target_pairs={{0,2},{2,0},{4,6},{6,4},{8,10},{10,8},{12,14},{14,12},{16,18},{18,... | collective-permute-start | bytes 12296 | tf_op jit(solution)/shard_map/ppermute | solution.py:235
  187.8 20.9 %collective-permute-start.26 = (f32[2,8,12288]{2,1,0:T(8,128)}, f32[2,8,12288]{2,1,0:T(8,128)}, u32[]{:S(2)}, u32[]{:S(2)}) collective-permute-start(f32[2,8,12288]{2,1,0:T(8,128)} %get-tuple-element.28.rest_7_), channel_id=1, source_target_pairs={{0,2},{2,4},{4,6},{6,8},{8,10},{10,12},{12,14},{14,16},{16,18},{18... | collective-permute-start | bytes 2359304 | tf_op jit(solution)/shard_map/ppermute | solution.py:316
  189.4 21.3 %collective-permute-start.25 = (f32[2,8,12288]{2,1,0:T(8,128)}, f32[2,8,12288]{2,1,0:T(8,128)}, u32[]{:S(2)}, u32[]{:S(2)}) collective-permute-start(f32[2,8,12288]{2,1,0:T(8,128)} %get-tuple-element.29.rest_6_), channel_id=1, source_target_pairs={{0,2},{2,4},{4,6},{6,8},{8,10},{10,12},{12,14},{14,16},{16,18},{18... | collective-permute-start | bytes 2359304 | tf_op jit(solution)/shard_map/ppermute | solution.py:320
  189.4 5.5 %collective-permute-start.21 = (f32[8,128]{1,0:T(8,128)S(1)}, f32[8,128]{1,0:T(8,128)S(1)}, u32[]{:S(2)}, u32[]{:S(2)}) collective-permute-start(f32[8,128]{1,0:T(8,128)S(1)} %add.56), channel_id=1, source_target_pairs={{0,8},{2,10},{8,0},{10,2},{16,24},{18,26},{24,16},{26,18},{1,9},{3... | collective-permute-start | bytes 12296 | tf_op jit(solution)/shard_map/ppermute | solution.py:235
  194.9 7.1 %collective-permute-start.22 = (f32[8,128]{1,0:T(8,128)S(1)}, f32[8,128]{1,0:T(8,128)S(1)}, u32[]{:S(2)}, u32[]{:S(2)}) collective-permute-start(f32[8,128]{1,0:T(8,128)S(1)} %add.57), channel_id=1, source_target_pairs={{0,16},{2,18},{8,24},{10,26},{16,0},{18,2},{24,8},{26,10},{1,17},{... | collective-permute-start | bytes 12296 | tf_op jit(solution)/shard_map/ppermute | solution.py:235
  (3 other events, 10.0 us)

commit v7 on v6

--- a/solution.py
+++ b/solution.py
@@ -106,21 +106,57 @@
     out_ref[...] = arrived_ref[...] + both_cores(keep_ref, theirs)
 
 
-def last_kernel(layers, shard_ref, keep_ref, *rest):
-    theirs, up_ref, down_ref = rest[:layers], rest[layers], rest[layers + 1]
-    out_ref, squares_ref = rest[-2:]
-    grad = (up_ref[...] + down_ref[...]) + both_cores(keep_ref, theirs)
-    out_ref[...] = grad
-    _, own, columns = grad.shape
-    squares = jnp.sum((grad * grad).reshape(layers, own, columns // lanes, lanes), axis=(0, 2))
-
-    @pl.when(pl.program_id(0) == 0)
+def last_kernel(streams, layers, shard_ref, *refs):
+    *refs, squares_ref = refs
+    refs, outs = refs[:-streams], refs[-streams:]
+    each = layers + 3
+    step = pl.program_id(0)
+    per = pl.num_programs(0) // streams
+
+    @pl.when(step == 0)
     def _():
-        squares_ref[...] = squares
-
-    @pl.when(pl.program_id(0) > 0)
-    def _():
-        squares_ref[...] += squares
+        squares_ref[...] = jnp.zeros_like(squares_ref)
+
+    for k in range(streams):
+
+        @pl.when(step // per == k)
+        def _(k=k):
+            keep_ref, *theirs, up_ref, down_ref = refs[k * each : (k + 1) * each]
+            grad = (up_ref[...] + down_ref[...]) + both_cores(keep_ref, theirs)
+            outs[k][...] = grad
+            _, own, columns = grad.shape
+            squares = (grad * grad).reshape(layers, own, columns // lanes, lanes)
+            squares_ref[...] += jnp.sum(squares, axis=(0, 2))
+
+
+def last_sums(shards, keep, theirs, sent):
+    streams = len(keep)
+    _, layers, own, width = keep[0].shape
+    size = block_of(width, 6144)
+    per = width // size
+    operands, specs, outs = [], [], []
+    for k in range(streams):
+        place = lambda i, k=k: jnp.clip(i - k * per, 0, per - 1)
+        operands += [keep[k], *theirs[k], *sent[k]]
+        specs += [pl.BlockSpec((1, layers, own, size), lambda i, s, at=place: (s[0], 0, 0, at(i)))]
+        specs += [pl.BlockSpec((1, own, size), lambda i, s, at=place: (s[0], 0, at(i)))] * layers
+        outs += [pl.BlockSpec((layers, own, size), lambda i, s, at=place: (0, 0, at(i)))]
+        specs += outs[-1:] * 2
+    summed = jax.ShapeDtypeStruct((layers, own, width), jnp.float32)
+    *grads, squares = pl.pallas_call(
+        functools.partial(last_kernel, streams, layers),
+        grid_spec=pltpu.PrefetchScalarGridSpec(
+            num_scalar_prefetch=1,
+            grid=(streams * per,),
+            in_specs=specs,
+            out_specs=outs + [pl.BlockSpec((own, lanes), lambda i, s: (0, 0))],
+        ),
+        out_shape=[summed] * streams + [jax.ShapeDtypeStruct((own, lanes), jnp.float32)],
+        compiler_params=room,
+        cost_estimate=cost_of(*[summed] * (5 * streams)),
+        name="last_sums",
+    )(shards, *operands)
+    return grads, squares
 
 
 def shard_sum(body, shards, which, keep, theirs, *arrived, after=()):
@@ -130,10 +166,6 @@
     layer = pl.BlockSpec((1, own, size), lambda i, shards: (shards[which], 0, i))
     whole = pl.BlockSpec((layers, own, size), lambda i, shards: (0, 0, i))
     summed = jax.ShapeDtypeStruct((layers, own, width), jnp.float32)
-    out_shape, out_specs = summed, whole
-    if body is last_kernel:
-        out_shape = [summed, jax.ShapeDtypeStruct((own, lanes), jnp.float32)]
-        out_specs = [whole, pl.BlockSpec((own, lanes), lambda i, shards: (0, 0))]
     return pl.pallas_call(
         functools.partial(body, layers),
         grid_spec=pltpu.PrefetchScalarGridSpec(
@@ -143,9 +175,9 @@
             + [layer] * layers
             + [whole] * len(arrived)
             + [pl.BlockSpec(memory_space=pl.ANY)] * len(after),
-            out_specs=out_specs,
-        ),
-        out_shape=out_shape,
+            out_specs=whole,
+        ),
+        out_shape=summed,
         compiler_params=room,
         cost_estimate=cost_of(*[summed] * (3 + len(arrived))),
         name="shard_sum",
@@ -226,28 +258,33 @@
     )(*arrays)
 
 
-def total_of(value, later):
+def total_of(value, later, last):
     peers, groups = lax.axis_size("dp"), lax.axis_size("mp")
     if peers & (peers - 1) or groups & (groups - 1) or peers < 4:
-        return lax.psum(value, ("dp", "mp")), later
-
-    def exchanged(value, axis, members, bit):
-        return value + lax.ppermute(value, axis, [(i, i ^ bit) for i in members])
+        return lax.psum(value, ("dp", "mp")), later, last
+
+    def exchanged(value, axis, members, *bits):
+        others = [lax.ppermute(value, axis, [(i, i ^ bit) for i in members]) for bit in bits]
+        return sum(others, value)
 
     value = exchanged(value, "dp", range(peers), 1)
+    value, later = lax.optimization_barrier((value, later))
     value = exchanged(value, "dp", range(peers), 2)
-    value, later = lax.optimization_barrier((value, later))
+    value, last = lax.optimization_barrier((value, last))
     first = [i for i in range(peers) if not i & 2]
     bit = 4
     while bit < peers:
-        value = exchanged(value, "dp", first, bit)
-        bit *= 2
+        if 2 * bit < peers:
+            value = exchanged(value, "dp", first, bit, 2 * bit, 3 * bit)
+        else:
+            value = exchanged(value, "dp", first, bit)
+        bit *= 4
     bit = 1
     while bit < groups:
         value = exchanged(value, "mp", range(groups), bit)
         bit *= 2
     passed = lax.ppermute(value, "dp", [(i, i | 2) for i in first])
-    return jnp.where(lax.axis_index("dp") & 2 == 0, value, passed), later
+    return jnp.where(lax.axis_index("dp") & 2 == 0, value, passed), later, last
 
 
 def local(acc_grads, activations, cotangent, params, first_moment, second_moment, step):
@@ -284,7 +321,7 @@
     inputs = inputs.reshape(layers * rows, tokens * layers)
 
     width = columns // streams
-    keep, theirs, sent, grads, peer_grads = ([None] * streams for _ in range(5))
+    keep, theirs, sent = ([None] * streams for _ in range(3))
     for k in range(streams):
         keep[k], *gives = make_terms(
             core.reshape(1), inputs, acc_grads, cotangent, order, k * width, width
@@ -309,15 +346,9 @@
                     body, tables[way], away, keep[k], theirs[k], *arrived, after=after
                 )
                 sent[k][way] = lax.ppermute(total, "dp", hop(by))
-    squares = None
-    for k in range(streams):
-        grads[k], part = shard_sum(last_kernel, tables[0], 0, keep[k], theirs[k], *sent[k])
-        if k:
-            peer_grads[k] = lax.ppermute(grads[k], "dp", onward)
-        squares = part if squares is None else squares + part
-
-    squares, waiting = total_of(squares, grads[0])
-    peer_grads[0] = lax.ppermute(waiting, "dp", onward)
+    grads, squares = last_sums(tables[0], keep, theirs, sent)
+    squares, *waiting = total_of(squares, grads[1:], grads[:1])
+    peer_grads = [lax.ppermute(value, "dp", onward) for value in waiting[1] + waiting[0]]
     bound = float((layers * rows * columns * lax.axis_size("mp")) ** 0.5)
     count = step.astype(jnp.float32)
     scales = jnp.concatenate(

time: 221 us -> 221 us (level)
  starting transfers between devices: 45.1 us -> 48.3 us
    pallas_call x16 -> x14, Pallas kernels: 49.7 us -> 42.7 us  [shard_sum(): pl.pallas_call(functools.partial(body, layers), grid_spec=pltpu.PrefetchS...]
    pallas_call x0 -> x1, Pallas kernels: none -> 6.03 us  [last_sums(): pl.pallas_call(functools.partial(last_kernel, streams, layers), grid_spec...]
    ppermute x7 -> x8, starting transfers between devices: 16.7 us -> 19.7 us  [the longest x6 19.6 us: exchanged(): lax.ppermute(value, axis, [(i, i ^ bit) for i in members])]
    ppermute x7 -> x8, waiting for transfers between devices: 9.21 us -> 7.76 us  [the longest x6 6.46 us: exchanged(): lax.ppermute(value, axis, [(i, i ^ bit) for i in members])]
  transfers between devices with their start and end apart: 27 -> 28, of which waited for: 17 -> 18; matrix products, arithmetic and copies ran while one was open for 2% -> 2% of each run, Pallas kernels for 29% -> 28%
where the time goes in v7:
time: 221 us; the launch traced here: 220 us
  waiting for transfers between devices  86 us (39%)
  Pallas kernels  79.7 us (36%)
  starting transfers between devices  48.3 us (22%)
  other arithmetic  4.09 us (2%)
    ppermute x12, waiting for transfers between devices, local(): sent[k][way] = lax.ppermute(total, 'dp', hop(by))  49.4 us
    pallas_call x14, Pallas kernels, shard_sum(): pl.pallas_call(functools.partial(body, layers), grid_spec=pltpu.PrefetchS...  42.7 us
    ppermute x2, waiting for transfers between devices, local(): sent[k][k % 2] = lax.ppermute(total, 'dp', hop(-1 if k % 2 else 1))  23 us
    ppermute x12, starting transfers between devices, local(): sent[k][way] = lax.ppermute(total, 'dp', hop(by))  20.6 us
    ppermute x6, starting transfers between devices, exchanged(): lax.ppermute(value, axis, [(i, i ^ bit) for i in members])  19.6 us
    pallas_call x2, Pallas kernels, make_terms(): pl.pallas_call(functools.partial(terms_kernel, order, layers), grid_spec=...  17.8 us
    pallas_call x1, Pallas kernels, update(): pl.pallas_call(functools.partial(update_kernel, count, bound), grid=(bloc...  9.07 us
    ppermute x6, waiting for transfers between devices, exchanged(): lax.ppermute(value, axis, [(i, i ^ bit) for i in members])  6.46 us
  transfers between devices with their start and end apart: 28, of which 18 were waited for; matrix products, arithmetic and copies ran while one was open for 2% of the time, Pallas kernels for 28%

profile of v7, /device:TPU:0, one launch (start us, length us, event | category | flops | bytes accessed | tf_op | source)
XLA Modules:
  0.0 220.3 jit_solution(8786304557118516728)
XLA Ops:
  0.6 4.0 %joined.1 = f32[6,8,24576]{2,1,0:T(8,128)} custom-call(f32[2,8,24576]{2,1,0:T(8,128)} %rest_0_.1, f32[2,8,24576]{2,1,0:T(8,128)} %rest_1_.1, f32[2,8,24576]{2,1,0:T(8,128)} %rest_2_.1), custom_call_target="tpu_custom_call" | custom-call | bytes 9437184 | tf_op jit(solution)/shard_map/joined/pallas_call | solution.py:249
  6.9 8.9 %terms.3 = (f32[8,2,8,12288]{3,2,1,0:T(8,128)}, f32[8,8,12288]{2,1,0:T(8,128)}, f32[8,8,12288]{2,1,0:T(8,128)}) custom-call(s32[1]{0:T(128)} %bitcast.core_ref, bf16[256,256]{1,0:T(8,128)(2,1)} %copy.14.inputs_ref, bf16[1,2,128,24576]{3,2,1,0:T(8,128)(2,1)} %earlier_ref.3, bf16[128,2,24576]{2,1,0:T(2,128)(2,1)} %outgrad_ref.3), custom_call_target="tpu_custom_call" | custom-call | bytes 25165824 | tf_op jit(solution)/shard_map/terms/pallas_call | solution.py:71
  18.4 8.9 %terms.2 = (f32[8,2,8,12288]{3,2,1,0:T(8,128)}, f32[8,8,12288]{2,1,0:T(8,128)}, f32[8,8,12288]{2,1,0:T(8,128)}) custom-call(s32[1]{0:T(128)} %bitcast.core_ref, bf16[256,256]{1,0:T(8,128)(2,1)} %copy.14.inputs_ref, bf16[1,2,128,24576]{3,2,1,0:T(8,128)(2,1)} %earlier_ref.3, bf16[128,2,24576]{2,1,0:T(2,128)(2,1)} %outgrad_ref.3), custom_call_target="tpu_custom_call" | custom-call | bytes 25165824 | tf_op jit(solution)/shard_map/terms/pallas_call | solution.py:71
  33.5 4.5 %collective-permute-done.1.rest_1_.refs_2_ = f32[8,8,12288]{2,1,0:T(8,128)} collective-permute-done((f32[8,8,12288]{2,1,0:T(8,128)}, f32[8,8,12288]{2,1,0:T(8,128)}, u32[]{:S(2)}, u32[]{:S(2)}) %collective-permute-start.1) | collective-permute-done | bytes 3145760 | tf_op jit(solution)/shard_map/ppermute | solution.py:329
  51.6 3.1 %shard_sum.25 = f32[2,8,12288]{2,1,0:T(8,128)} custom-call(s32[6]{0:T(128)} %pad_add_fusion.1.shard_ref, f32[8,2,8,12288]{3,2,1,0:T(8,128)} %get-tuple-element.22.keep_ref.refs_5_, f32[8,8,12288]{2,1,0:T(8,128)} %collective-permute-done.10.rest_0_.refs_6_, f32[8,8,12288]{2,1,0:T(8,128)} %collective-permute-done.11.rest_1_.refs_7_, ...), custom_call_target="tpu_custom_call" | custom-call | bytes 3145728 | tf_op jit(solution)/shard_map/shard_sum/pallas_call | solution.py:169
  56.9 22.2 %collective-permute-done.2.rest_2_ = f32[2,8,12288]{2,1,0:T(8,128)} collective-permute-done((f32[2,8,12288]{2,1,0:T(8,128)}, f32[2,8,12288]{2,1,0:T(8,128)}, u32[]{:S(2)}, u32[]{:S(2)}) %collective-permute-start.2) | collective-permute-done | bytes 786464 | tf_op jit(solution)/shard_map/ppermute | solution.py:335
  79.1 3.1 %shard_sum.15 = f32[2,8,12288]{2,1,0:T(8,128)} custom-call(s32[6]{0:T(128)} %pad_add_fusion.shard_ref, f32[8,2,8,12288]{3,2,1,0:T(8,128)} %get-tuple-element.19.keep_ref.refs_0_, f32[8,8,12288]{2,1,0:T(8,128)} %collective-permute-done.rest_0_.refs_1_, f32[8,8,12288]{2,1,0:T(8,128)} %collective-permute-done.1.rest_1_.refs_2_, ...), custom_call_target="tpu_custom_call" | custom-call | bytes 3145728 | tf_op jit(solution)/shard_map/shard_sum/pallas_call | solution.py:169
  82.2 7.9 %collective-permute-start.4 = (f32[2,8,12288]{2,1,0:T(8,128)}, f32[2,8,12288]{2,1,0:T(8,128)}, u32[]{:S(2)}, u32[]{:S(2)}) collective-permute-start(f32[2,8,12288]{2,1,0:T(8,128)} %shard_sum.15), channel_id=1, source_target_pairs={{0,8},{2,10},{8,16},{10,18},{16,24},{18,26},{24,28},{26,30},{28,20... | collective-permute-start | bytes 2359304 | tf_op jit(solution)/shard_map/ppermute | solution.py:348
  90.1 5.8 %collective-permute-done.12.rest_2_ = f32[2,8,12288]{2,1,0:T(8,128)} collective-permute-done((f32[2,8,12288]{2,1,0:T(8,128)}, f32[2,8,12288]{2,1,0:T(8,128)}, u32[]{:S(2)}, u32[]{:S(2)}) %collective-permute-start.12) | collective-permute-done | bytes 786464 | tf_op jit(solution)/shard_map/ppermute | solution.py:348
  95.9 3.1 %shard_sum.22 = f32[2,8,12288]{2,1,0:T(8,128)} custom-call(s32[6]{0:T(128)} %pad_add_fusion.shard_ref, f32[8,2,8,12288]{3,2,1,0:T(8,128)} %get-tuple-element.22.keep_ref.refs_5_, f32[8,8,12288]{2,1,0:T(8,128)} %collective-permute-done.10.rest_0_.refs_6_, f32[8,8,12288]{2,1,0:T(8,128)} %collective-permute-done.11.rest_1_.refs_7_, ...), custom_call_target="tpu_custom_call" | custom-call | bytes 3145728 | tf_op jit(solution)/shard_map/shard_sum/pallas_call | solution.py:169
  99.0 3.1 %shard_sum.19 = f32[2,8,12288]{2,1,0:T(8,128)} custom-call(s32[6]{0:T(128)} %pad_add_fusion.1.shard_ref, f32[8,2,8,12288]{3,2,1,0:T(8,128)} %get-tuple-element.19.keep_ref.refs_0_, f32[8,8,12288]{2,1,0:T(8,128)} %collective-permute-done.rest_0_.refs_1_, f32[8,8,12288]{2,1,0:T(8,128)} %collective-permute-done.1.rest_1_.refs_2_, ...), custom_call_target="tpu_custom_call" | custom-call | bytes 3145728 | tf_op jit(solution)/shard_map/shard_sum/pallas_call | solution.py:169
  104.2 3.1 %shard_sum.26 = f32[2,8,12288]{2,1,0:T(8,128)} custom-call(s32[6]{0:T(128)} %pad_add_fusion.1.shard_ref, f32[8,2,8,12288]{3,2,1,0:T(8,128)} %get-tuple-element.22.keep_ref.refs_5_, f32[8,8,12288]{2,1,0:T(8,128)} %collective-permute-done.10.rest_0_.refs_6_, f32[8,8,12288]{2,1,0:T(8,128)} %collective-permute-done.11.rest_1_.refs_7_, ...), custom_call_target="tpu_custom_call" | custom-call | bytes 3145728 | tf_op jit(solution)/shard_map/shard_sum/pallas_call | solution.py:169
  107.9 3.1 %shard_sum.16 = f32[2,8,12288]{2,1,0:T(8,128)} custom-call(s32[6]{0:T(128)} %pad_add_fusion.shard_ref, f32[8,2,8,12288]{3,2,1,0:T(8,128)} %get-tuple-element.19.keep_ref.refs_0_, f32[8,8,12288]{2,1,0:T(8,128)} %collective-permute-done.rest_0_.refs_1_, f32[8,8,12288]{2,1,0:T(8,128)} %collective-permute-done.1.rest_1_.refs_2_, ...), custom_call_target="tpu_custom_call" | custom-call | bytes 3145728 | tf_op jit(solution)/shard_map/shard_sum/pallas_call | solution.py:169
  112.5 8.8 %collective-permute-done.13.rest_2_ = f32[2,8,12288]{2,1,0:T(8,128)} collective-permute-done((f32[2,8,12288]{2,1,0:T(8,128)}, f32[2,8,12288]{2,1,0:T(8,128)}, u32[]{:S(2)}, u32[]{:S(2)}) %collective-permute-start.13) | collective-permute-done | bytes 786464 | tf_op jit(solution)/shard_map/ppermute | solution.py:348
  124.4 3.1 %shard_sum.20 = f32[2,8,12288]{2,1,0:T(8,128)} custom-call(s32[6]{0:T(128)} %pad_add_fusion.1.shard_ref, f32[8,2,8,12288]{3,2,1,0:T(8,128)} %get-tuple-element.19.keep_ref.refs_0_, f32[8,8,12288]{2,1,0:T(8,128)} %collective-permute-done.rest_0_.refs_1_, f32[8,8,12288]{2,1,0:T(8,128)} %collective-permute-done.1.rest_1_.refs_2_, ...), custom_call_target="tpu_custom_call" | custom-call | bytes 3145728 | tf_op jit(solution)/shard_map/shard_sum/pallas_call | solution.py:169
  129.5 9.8 %collective-permute-done.17.rest_2_ = f32[2,8,12288]{2,1,0:T(8,128)} collective-permute-done((f32[2,8,12288]{2,1,0:T(8,128)}, f32[2,8,12288]{2,1,0:T(8,128)}, u32[]{:S(2)}, u32[]{:S(2)}) %collective-permute-start.17) | collective-permute-done | bytes 786464 | tf_op jit(solution)/shard_map/ppermute | solution.py:348
  145.0 3.1 %shard_sum.17 = f32[2,8,12288]{2,1,0:T(8,128)} custom-call(s32[6]{0:T(128)} %pad_add_fusion.shard_ref, f32[8,2,8,12288]{3,2,1,0:T(8,128)} %get-tuple-element.19.keep_ref.refs_0_, f32[8,8,12288]{2,1,0:T(8,128)} %collective-permute-done.rest_0_.refs_1_, f32[8,8,12288]{2,1,0:T(8,128)} %collective-permute-done.1.rest_1_.refs_2_, ...), custom_call_target="tpu_custom_call" | custom-call | bytes 3145728 | tf_op jit(solution)/shard_map/shard_sum/pallas_call | solution.py:169
  148.1 6.9 %collective-permute-done.14.refs_8_ = f32[2,8,12288]{2,1,0:T(8,128)} collective-permute-done((f32[2,8,12288]{2,1,0:T(8,128)}, f32[2,8,12288]{2,1,0:T(8,128)}, u32[]{:S(2)}, u32[]{:S(2)}) %collective-permute-start.14) | collective-permute-done | bytes 786464 | tf_op jit(solution)/shard_map/ppermute | solution.py:348
  156.2 16.9 %collective-permute-done.18.refs_9_ = f32[2,8,12288]{2,1,0:T(8,128)} collective-permute-done((f32[2,8,12288]{2,1,0:T(8,128)}, f32[2,8,12288]{2,1,0:T(8,128)}, u32[]{:S(2)}, u32[]{:S(2)}) %collective-permute-start.18) | collective-permute-done | bytes 786464 | tf_op jit(solution)/shard_map/ppermute | solution.py:348
  173.1 6.0 %last_sums.1 = (f32[2,8,12288]{2,1,0:T(8,128)}, f32[2,8,12288]{2,1,0:T(8,128)}, f32[8,128]{1,0:T(8,128)}) custom-call(s32[6]{0:T(128)} %pad_add_fusion.shard_ref, f32[8,2,8,12288]{3,2,1,0:T(8,128)} %get-tuple-element.19.keep_ref.refs_0_, f32[8,8,12288]{2,1,0:T(8,128)} %collective-permute-done.rest_0_.refs_1_, ...), custom_call_target="tpu_custom_call" | custom-call | bytes 7864320 | tf_op jit(solution)/shard_map/last_sums/pallas_call | solution.py:146
  179.1 7.0 %collective-permute-start.19 = (f32[8,128]{1,0:T(8,128)}, f32[8,128]{1,0:T(8,128)S(1)}, u32[]{:S(2)}, u32[]{:S(2)}) collective-permute-start(f32[8,128]{1,0:T(8,128)} %get-tuple-element.25), channel_id=1, source_target_pairs={{0,2},{2,0},{4,6},{6,4},{8,10},{10,8},{12,14},{14,12},{16,18},{18,... | collective-permute-start | bytes 12296 | tf_op jit(solution)/shard_map/ppermute | solution.py:267
  191.4 4.2 %collective-permute-start.23 = (f32[8,128]{1,0:T(8,128)S(1)}, f32[8,128]{1,0:T(8,128)S(1)}, u32[]{:S(2)}, u32[]{:S(2)}) collective-permute-start(f32[8,128]{1,0:T(8,128)S(1)} %add.55), channel_id=1, source_target_pairs={{0,24},{2,26},{8,16},{10,18},{16,8},{18,10},{24,0},{26,2},{1,25},{... | collective-permute-start | bytes 12296 | tf_op jit(solution)/shard_map/ppermute | solution.py:267
  197.5 4.0 %collective-permute-start.21 = (f32[8,128]{1,0:T(8,128)S(1)}, f32[8,128]{1,0:T(8,128)S(1)}, u32[]{:S(2)}, u32[]{:S(2)}) collective-permute-start(f32[8,128]{1,0:T(8,128)S(1)} %add.55), channel_id=1, source_target_pairs={{0,8},{2,10},{8,0},{10,2},{16,24},{18,26},{24,16},{26,18},{1,9},{3... | collective-permute-start | bytes 12296 | tf_op jit(solution)/shard_map/ppermute | solution.py:267
  211.2 9.1 %update.1 = (f32[2,8,24576]{2,1,0:T(8,128)}, f32[2,8,24576]{2,1,0:T(8,128)}, f32[2,8,24576]{2,1,0:T(8,128)}, f32[2,8,24576]{2,1,0:T(8,128)}, f32[2,8,24576]{2,1,0:T(8,128)}, /*index=5*/f32[2,8,24576]{2,1,0:T(8,128)}) custom-call(f32[2]{0:T(128)} %pad_maximum_fusion.scales_ref, f32[8,128]{1,0:T(8,128)} %broadcast_select_fusion.squares_ref, ...), custom_call_target="tpu_custom_call" | custom-call | bytes 22020096 | tf_op jit(solution)/shard_map/update/pallas_call | solution.py:221
  (65 shorter events, 59.0 us)
Async XLA Ops:
  4.7 74.4 %collective-permute-start.3 = (f32[6,8,24576]{2,1,0:T(8,128)}, f32[6,8,24576]{2,1,0:T(8,128)}, u32[]{:S(2)}, u32[]{:S(2)}) collective-permute-start(f32[6,8,24576]{2,1,0:T(8,128)} %joined.1), channel_id=1, source_target_pairs={{0,2},{2,4},{4,6},{6,8},{8,10},{10,12},{12,14},{14,16},{16,18},{18... | collective-permute-start | bytes 14155784 | tf_op jit(solution)/shard_map/ppermute | solution.py:317
  15.8 12.7 %collective-permute-start.10 = (f32[8,8,12288]{2,1,0:T(8,128)}, f32[8,8,12288]{2,1,0:T(8,128)}, u32[]{:S(2)}, u32[]{:S(2)}) collective-permute-start(f32[8,8,12288]{2,1,0:T(8,128)} %get-tuple-element.23), channel_id=1, source_target_pairs={{0,2},{2,0},{4,6},{6,4},{8,10},{10,8},{12,14},{14,12},{16,18},{18,... | collective-permute-start | bytes 9437192 | tf_op jit(solution)/shard_map/ppermute | solution.py:329
  18.4 10.1 %collective-permute-start.11 = (f32[8,8,12288]{2,1,0:T(8,128)}, f32[8,8,12288]{2,1,0:T(8,128)}, u32[]{:S(2)}, u32[]{:S(2)}) collective-permute-start(f32[8,8,12288]{2,1,0:T(8,128)} %get-tuple-element.24), channel_id=1, source_target_pairs={{0,2},{2,0},{4,6},{6,4},{8,10},{10,8},{12,14},{14,12},{16,18},{18,... | collective-permute-start | bytes 9437192 | tf_op jit(solution)/shard_map/ppermute | solution.py:329
  27.4 6.1 %collective-permute-start = (f32[8,8,12288]{2,1,0:T(8,128)}, f32[8,8,12288]{2,1,0:T(8,128)}, u32[]{:S(2)}, u32[]{:S(2)}) collective-permute-start(f32[8,8,12288]{2,1,0:T(8,128)} %get-tuple-element.20), channel_id=1, source_target_pairs={{0,2},{2,0},{4,6},{6,4},{8,10},{10,8},{12,14},{14,12},{16,18},{18,... | collective-permute-start | bytes 9437192 | tf_op jit(solution)/shard_map/ppermute | solution.py:329
  27.9 10.1 %collective-permute-start.1 = (f32[8,8,12288]{2,1,0:T(8,128)}, f32[8,8,12288]{2,1,0:T(8,128)}, u32[]{:S(2)}, u32[]{:S(2)}) collective-permute-start(f32[8,8,12288]{2,1,0:T(8,128)} %get-tuple-element.21), channel_id=1, source_target_pairs={{0,2},{2,0},{4,6},{6,4},{8,10},{10,8},{12,14},{14,12},{16,18},{18,... | collective-permute-start | bytes 9437192 | tf_op jit(solution)/shard_map/ppermute | solution.py:329
  31.4 20.2 %collective-permute-start.15 = (f32[2,8,12288]{2,1,0:T(8,128)}, f32[2,8,12288]{2,1,0:T(8,128)}, u32[]{:S(2)}, u32[]{:S(2)}) collective-permute-start(f32[2,8,12288]{2,1,0:T(8,128)} %shard_sum.24), channel_id=1, source_target_pairs={{0,4},{2,6},{8,0},{10,2},{16,8},{18,10},{24,16},{26,18},{28,24},{3... | collective-permute-start | bytes 2359304 | tf_op jit(solution)/shard_map/ppermute | solution.py:335
  40.9 38.2 %collective-permute-start.2 = (f32[2,8,12288]{2,1,0:T(8,128)}, f32[2,8,12288]{2,1,0:T(8,128)}, u32[]{:S(2)}, u32[]{:S(2)}) collective-permute-start(f32[2,8,12288]{2,1,0:T(8,128)} %shard_sum.14), channel_id=1, source_target_pairs={{0,8},{2,10},{8,16},{10,18},{16,24},{18,26},{24,28},{26,30},{28,20... | collective-permute-start | bytes 2359304 | tf_op jit(solution)/shard_map/ppermute | solution.py:335
  45.9 50.0 %collective-permute-start.12 = (f32[2,8,12288]{2,1,0:T(8,128)}, f32[2,8,12288]{2,1,0:T(8,128)}, u32[]{:S(2)}, u32[]{:S(2)}) collective-permute-start(f32[2,8,12288]{2,1,0:T(8,128)} %shard_sum.21), channel_id=1, source_target_pairs={{0,8},{2,10},{8,16},{10,18},{16,24},{18,26},{24,28},{26,30},{28,20... | collective-permute-start | bytes 2359304 | tf_op jit(solution)/shard_map/ppermute | solution.py:348
  50.4 48.7 %collective-permute-start.7 = (f32[2,8,12288]{2,1,0:T(8,128)}, f32[2,8,12288]{2,1,0:T(8,128)}, u32[]{:S(2)}, u32[]{:S(2)}) collective-permute-start(f32[2,8,12288]{2,1,0:T(8,128)} %shard_sum.18), channel_id=1, source_target_pairs={{0,4},{2,6},{8,0},{10,2},{16,8},{18,10},{24,16},{26,18},{28,24},{3... | collective-permute-start | bytes 2359304 | tf_op jit(solution)/shard_map/ppermute | solution.py:348
  54.7 49.4 %collective-permute-start.16 = (f32[2,8,12288]{2,1,0:T(8,128)}, f32[2,8,12288]{2,1,0:T(8,128)}, u32[]{:S(2)}, u32[]{:S(2)}) collective-permute-start(f32[2,8,12288]{2,1,0:T(8,128)} %shard_sum.25), channel_id=1, source_target_pairs={{0,4},{2,6},{8,0},{10,2},{16,8},{18,10},{24,16},{26,18},{28,24},{3... | collective-permute-start | bytes 2359304 | tf_op jit(solution)/shard_map/ppermute | solution.py:348
  82.2 25.6 %collective-permute-start.4 = (f32[2,8,12288]{2,1,0:T(8,128)}, f32[2,8,12288]{2,1,0:T(8,128)}, u32[]{:S(2)}, u32[]{:S(2)}) collective-permute-start(f32[2,8,12288]{2,1,0:T(8,128)} %shard_sum.15), channel_id=1, source_target_pairs={{0,8},{2,10},{8,16},{10,18},{16,24},{18,26},{24,28},{26,30},{28,20... | collective-permute-start | bytes 2359304 | tf_op jit(solution)/shard_map/ppermute | solution.py:348
  99.0 22.2 %collective-permute-start.13 = (f32[2,8,12288]{2,1,0:T(8,128)}, f32[2,8,12288]{2,1,0:T(8,128)}, u32[]{:S(2)}, u32[]{:S(2)}) collective-permute-start(f32[2,8,12288]{2,1,0:T(8,128)} %shard_sum.22), channel_id=1, source_target_pairs={{0,8},{2,10},{8,16},{10,18},{16,24},{18,26},{24,28},{26,30},{28,20... | collective-permute-start | bytes 2359304 | tf_op jit(solution)/shard_map/ppermute | solution.py:348
  102.2 22.2 %collective-permute-start.8 = (f32[2,8,12288]{2,1,0:T(8,128)}, f32[2,8,12288]{2,1,0:T(8,128)}, u32[]{:S(2)}, u32[]{:S(2)}) collective-permute-start(f32[2,8,12288]{2,1,0:T(8,128)} %shard_sum.19), channel_id=1, source_target_pairs={{0,4},{2,6},{8,0},{10,2},{16,8},{18,10},{24,16},{26,18},{28,24},{3... | collective-permute-start | bytes 2359304 | tf_op jit(solution)/shard_map/ppermute | solution.py:348
  107.3 32.0 %collective-permute-start.17 = (f32[2,8,12288]{2,1,0:T(8,128)}, f32[2,8,12288]{2,1,0:T(8,128)}, u32[]{:S(2)}, u32[]{:S(2)}) collective-permute-start(f32[2,8,12288]{2,1,0:T(8,128)} %shard_sum.26), channel_id=1, source_target_pairs={{0,4},{2,6},{8,0},{10,2},{16,8},{18,10},{24,16},{26,18},{28,24},{3... | collective-permute-start | bytes 2359304 | tf_op jit(solution)/shard_map/ppermute | solution.py:348
  111.0 34.0 %collective-permute-start.5 = (f32[2,8,12288]{2,1,0:T(8,128)}, f32[2,8,12288]{2,1,0:T(8,128)}, u32[]{:S(2)}, u32[]{:S(2)}) collective-permute-start(f32[2,8,12288]{2,1,0:T(8,128)} %shard_sum.16), channel_id=1, source_target_pairs={{0,8},{2,10},{8,16},{10,18},{16,24},{18,26},{24,28},{26,30},{28,20... | collective-permute-start | bytes 2359304 | tf_op jit(solution)/shard_map/ppermute | solution.py:348
  124.4 30.6 %collective-permute-start.14 = (f32[2,8,12288]{2,1,0:T(8,128)}, f32[2,8,12288]{2,1,0:T(8,128)}, u32[]{:S(2)}, u32[]{:S(2)}) collective-permute-start(f32[2,8,12288]{2,1,0:T(8,128)} %shard_sum.23), channel_id=1, source_target_pairs={{0,8},{2,10},{8,16},{10,18},{16,24},{18,26},{24,28},{26,30},{28,20... | collective-permute-start | bytes 2359304 | tf_op jit(solution)/shard_map/ppermute | solution.py:348
  127.5 28.7 %collective-permute-start.9 = (f32[2,8,12288]{2,1,0:T(8,128)}, f32[2,8,12288]{2,1,0:T(8,128)}, u32[]{:S(2)}, u32[]{:S(2)}) collective-permute-start(f32[2,8,12288]{2,1,0:T(8,128)} %shard_sum.20), channel_id=1, source_target_pairs={{0,4},{2,6},{8,0},{10,2},{16,8},{18,10},{24,16},{26,18},{28,24},{3... | collective-permute-start | bytes 2359304 | tf_op jit(solution)/shard_map/ppermute | solution.py:348
  142.5 30.6 %collective-permute-start.18 = (f32[2,8,12288]{2,1,0:T(8,128)}, f32[2,8,12288]{2,1,0:T(8,128)}, u32[]{:S(2)}, u32[]{:S(2)}) collective-permute-start(f32[2,8,12288]{2,1,0:T(8,128)} %shard_sum.27), channel_id=1, source_target_pairs={{0,4},{2,6},{8,0},{10,2},{16,8},{18,10},{24,16},{26,18},{28,24},{3... | collective-permute-start | bytes 2359304 | tf_op jit(solution)/shard_map/ppermute | solution.py:348
  148.1 25.0 %collective-permute-start.6 = (f32[2,8,12288]{2,1,0:T(8,128)}, f32[2,8,12288]{2,1,0:T(8,128)}, u32[]{:S(2)}, u32[]{:S(2)}) collective-permute-start(f32[2,8,12288]{2,1,0:T(8,128)} %shard_sum.17), channel_id=1, source_target_pairs={{0,8},{2,10},{8,16},{10,18},{16,24},{18,26},{24,28},{26,30},{28,20... | collective-permute-start | bytes 2359304 | tf_op jit(solution)/shard_map/ppermute | solution.py:348
  179.1 8.0 %collective-permute-start.19 = (f32[8,128]{1,0:T(8,128)}, f32[8,128]{1,0:T(8,128)S(1)}, u32[]{:S(2)}, u32[]{:S(2)}) collective-permute-start(f32[8,128]{1,0:T(8,128)} %get-tuple-element.25), channel_id=1, source_target_pairs={{0,2},{2,0},{4,6},{6,4},{8,10},{10,8},{12,14},{14,12},{16,18},{18,... | collective-permute-start | bytes 12296 | tf_op jit(solution)/shard_map/ppermute | solution.py:267
  188.4 21.6 %collective-permute-start.27 = (f32[2,8,12288]{2,1,0:T(8,128)}, f32[2,8,12288]{2,1,0:T(8,128)}, u32[]{:S(2)}, u32[]{:S(2)}) collective-permute-start(f32[2,8,12288]{2,1,0:T(8,128)} %get-tuple-element.31.rest_7_), channel_id=1, source_target_pairs={{0,2},{2,4},{4,6},{6,8},{8,10},{10,12},{12,14},{14,16},{16,18},{18... | collective-permute-start | bytes 2359304 | tf_op jit(solution)/shard_map/ppermute | solution.py:351
  191.4 19.8 %collective-permute-start.26 = (f32[2,8,12288]{2,1,0:T(8,128)}, f32[2,8,12288]{2,1,0:T(8,128)}, u32[]{:S(2)}, u32[]{:S(2)}) collective-permute-start(f32[2,8,12288]{2,1,0:T(8,128)} %get-tuple-element.30.rest_6_), channel_id=1, source_target_pairs={{0,2},{2,4},{4,6},{6,8},{8,10},{10,12},{12,14},{14,16},{16,18},{18... | collective-permute-start | bytes 2359304 | tf_op jit(solution)/shard_map/ppermute | solution.py:351
  191.4 10.1 %collective-permute-start.23 = (f32[8,128]{1,0:T(8,128)S(1)}, f32[8,128]{1,0:T(8,128)S(1)}, u32[]{:S(2)}, u32[]{:S(2)}) collective-permute-start(f32[8,128]{1,0:T(8,128)S(1)} %add.55), channel_id=1, source_target_pairs={{0,24},{2,26},{8,16},{10,18},{16,8},{18,10},{24,0},{26,2},{1,25},{... | collective-permute-start | bytes 12296 | tf_op jit(solution)/shard_map/ppermute | solution.py:267
  195.6 6.4 %collective-permute-start.22 = (f32[8,128]{1,0:T(8,128)S(1)}, f32[8,128]{1,0:T(8,128)S(1)}, u32[]{:S(2)}, u32[]{:S(2)}) collective-permute-start(f32[8,128]{1,0:T(8,128)S(1)} %add.55), channel_id=1, source_target_pairs={{0,16},{2,18},{8,24},{10,26},{16,0},{18,2},{24,8},{26,10},{1,17},{... | collective-permute-start | bytes 12296 | tf_op jit(solution)/shard_map/ppermute | solution.py:267
  (4 other events, 15.4 us)

commit v8 on v7

--- a/solution.py
+++ b/solution.py
@@ -106,10 +106,9 @@
     out_ref[...] = arrived_ref[...] + both_cores(keep_ref, theirs)
 
 
-def last_kernel(streams, layers, shard_ref, *refs):
+def last_kernel(streams, *refs):
     *refs, squares_ref = refs
     refs, outs = refs[:-streams], refs[-streams:]
-    each = layers + 3
     step = pl.program_id(0)
     per = pl.num_programs(0) // streams
 
@@ -121,41 +120,36 @@
 
         @pl.when(step // per == k)
         def _(k=k):
-            keep_ref, *theirs, up_ref, down_ref = refs[k * each : (k + 1) * each]
-            grad = (up_ref[...] + down_ref[...]) + both_cores(keep_ref, theirs)
+            own_ref, up_ref, down_ref = refs[3 * k : 3 * k + 3]
+            grad = (up_ref[...] + down_ref[...]) + own_ref[...]
             outs[k][...] = grad
-            _, own, columns = grad.shape
+            layers, own, columns = grad.shape
             squares = (grad * grad).reshape(layers, own, columns // lanes, lanes)
             squares_ref[...] += jnp.sum(squares, axis=(0, 2))
 
 
-def last_sums(shards, keep, theirs, sent):
-    streams = len(keep)
-    _, layers, own, width = keep[0].shape
-    size = block_of(width, 6144)
+def last_sums(ours, sent):
+    streams = len(ours)
+    layers, own, width = ours[0].shape
+    size = block_of(width, 12288)
     per = width // size
-    operands, specs, outs = [], [], []
-    for k in range(streams):
-        place = lambda i, k=k: jnp.clip(i - k * per, 0, per - 1)
-        operands += [keep[k], *theirs[k], *sent[k]]
-        specs += [pl.BlockSpec((1, layers, own, size), lambda i, s, at=place: (s[0], 0, 0, at(i)))]
-        specs += [pl.BlockSpec((1, own, size), lambda i, s, at=place: (s[0], 0, at(i)))] * layers
-        outs += [pl.BlockSpec((layers, own, size), lambda i, s, at=place: (0, 0, at(i)))]
-        specs += outs[-1:] * 2
-    summed = jax.ShapeDtypeStruct((layers, own, width), jnp.float32)
+    specs = [
+        pl.BlockSpec(
+            (layers, own, size), lambda i, k=k: (0, 0, jnp.clip(i - k * per, 0, per - 1))
+        )
+        for k in range(streams)
+    ]
+    summed = jax.ShapeDtypeStruct(ours[0].shape, jnp.float32)
     *grads, squares = pl.pallas_call(
-        functools.partial(last_kernel, streams, layers),
-        grid_spec=pltpu.PrefetchScalarGridSpec(
-            num_scalar_prefetch=1,
-            grid=(streams * per,),
-            in_specs=specs,
-            out_specs=outs + [pl.BlockSpec((own, lanes), lambda i, s: (0, 0))],
-        ),
+        functools.partial(last_kernel, streams),
+        grid=(streams * per,),
+        in_specs=[spec for spec in specs for _ in range(3)],
+        out_specs=specs + [pl.BlockSpec((own, lanes), lambda i: (0, 0))],
         out_shape=[summed] * streams + [jax.ShapeDtypeStruct((own, lanes), jnp.float32)],
         compiler_params=room,
-        cost_estimate=cost_of(*[summed] * (5 * streams)),
+        cost_estimate=cost_of(*[summed] * (4 * streams)),
         name="last_sums",
-    )(shards, *operands)
+    )(*[array for k in range(streams) for array in (ours[k], *sent[k])])
     return grads, squares
 
 
@@ -184,8 +178,9 @@
     )(shards, keep, *theirs, *arrived, *after)
 
 
-def update_kernel(count, bound, scales_ref, squares_ref, *rest):
-    states, grads, outs = (rest[:3], rest[3:6]), rest[6 : 6 + 2 * count], rest[6 + 2 * count :]
+def update_kernel(count, bound, layers, scales_ref, squares_ref, *rest):
+    own, old, rest = rest[:3], rest[3 : 3 + 3 * layers], rest[3 + 3 * layers :]
+    grads, outs = rest[: 2 * count], rest[2 * count :]
     step = pl.program_id(0)
     per = pl.num_programs(0) // count
     factor = jnp.minimum(
@@ -195,80 +190,86 @@
 
         @pl.when(step // per == index)
         def _(index=index):
-            for who in range(2):
-                new = adamw_update(
-                    *[ref[...] for ref in states[who]],
-                    grads[who * count + index][...],
-                    factor,
-                    scales_ref[0],
-                    scales_ref[1],
-                )
+            states = (
+                [ref[...] for ref in own],
+                [
+                    jnp.concatenate([ref[...] for ref in old[k * layers : (k + 1) * layers]])
+                    for k in range(3)
+                ],
+            )
+            for who, state in enumerate(states):
+                grad = grads[who * count + index][...]
+                new = adamw_update(*state, grad, factor, scales_ref[0], scales_ref[1])
                 for out_ref, value in zip(outs[3 * who : 3 * who + 3], new):
                     out_ref[...] = value
 
 
-def update(scales, squares, state, grads, old_copy, peer_grads, bound):
+def update(scales, squares, state, grads, old_copy, old_last, peer_grads, bound):
     layers, own, columns = state[0].shape
     width = grads[0].shape[-1]
     count = len(grads)
     size = block_of(width, 12288)
     per, blocks = width // size, columns // size
-    shape = (layers, own, size)
-
-    def part(first, many, row=0):
-        return pl.BlockSpec(shape, lambda i: (row, 0, jnp.clip(i - first, 0, many - 1)))
+    joint = 3 * layers - 1
+
+    def part(first, many):
+        return pl.BlockSpec((layers, own, size), lambda i: (0, 0, jnp.clip(i - first, 0, many - 1)))
+
+    def layer(row):
+        return pl.BlockSpec((1, own, size), lambda i: (row, 0, i))
 
     return pl.pallas_call(
-        functools.partial(update_kernel, count, bound),
+        functools.partial(update_kernel, count, bound, layers),
         grid=(blocks,),
         in_specs=[
             pl.BlockSpec(memory_space=pltpu.SMEM),
             pl.BlockSpec(squares.shape, lambda i: (0, 0)),
         ]
         + [part(0, blocks)] * 3
-        + [part(0, blocks, row) for row in range(3)]
+        + [layer(row) for row in range(joint)]
+        + [layer(0)]
         + [part(k * per, per) for k in range(count)] * 2,
         out_specs=[part(0, blocks)] * 6,
         out_shape=[jax.ShapeDtypeStruct((layers, own, columns), jnp.float32)] * 6,
         compiler_params=room,
         cost_estimate=cost_of(*[state[0]] * 14),
         name="update",
-    )(scales, squares, *state, *[old_copy] * 3, *grads, *peer_grads)
+    )(scales, squares, *state, *[old_copy] * joint, old_last, *grads, *peer_grads)
 
 
 def joined_kernel(*refs):
     *parts, out_ref = refs
-    layers = parts[0].shape[0]
     for index, part_ref in enumerate(parts):
-        out_ref[index * layers : (index + 1) * layers] = part_ref[...]
+        out_ref[index] = part_ref[0]
 
 
 def joined(arrays):
     layers, own, columns = arrays[0].shape
     size = block_of(columns, 12288)
+    places = [(array, layer) for array in arrays for layer in range(layers)][:-1]
     return pl.pallas_call(
         joined_kernel,
         grid=(columns // size,),
-        in_specs=[pl.BlockSpec((layers, own, size), lambda i: (0, 0, i))] * len(arrays),
-        out_specs=pl.BlockSpec((len(arrays) * layers, own, size), lambda i: (0, 0, i)),
-        out_shape=jax.ShapeDtypeStruct((len(arrays) * layers, own, columns), jnp.float32),
+        in_specs=[pl.BlockSpec((1, own, size), lambda i, l=l: (l, 0, i)) for _, l in places],
+        out_specs=pl.BlockSpec((len(places), own, size), lambda i: (0, 0, i)),
+        out_shape=jax.ShapeDtypeStruct((len(places), own, columns), jnp.float32),
         compiler_params=room,
         cost_estimate=cost_of(*arrays, *arrays),
         name="joined",
-    )(*arrays)
-
-
-def total_of(value, later, last):
+    )(*[array for array, _ in places])
+
+
+def total_of(value, before, later, last):
     peers, groups = lax.axis_size("dp"), lax.axis_size("mp")
     if peers & (peers - 1) or groups & (groups - 1) or peers < 4:
-        return lax.psum(value, ("dp", "mp")), later, last
+        return lax.psum(value, ("dp", "mp")), before, later, last
 
     def exchanged(value, axis, members, *bits):
         others = [lax.ppermute(value, axis, [(i, i ^ bit) for i in members]) for bit in bits]
         return sum(others, value)
 
     value = exchanged(value, "dp", range(peers), 1)
-    value, later = lax.optimization_barrier((value, later))
+    value, before, later = lax.optimization_barrier((value, before, later))
     value = exchanged(value, "dp", range(peers), 2)
     value, last = lax.optimization_barrier((value, last))
     first = [i for i in range(peers) if not i & 2]
@@ -284,7 +285,7 @@
         value = exchanged(value, "mp", range(groups), bit)
         bit *= 2
     passed = lax.ppermute(value, "dp", [(i, i | 2) for i in first])
-    return jnp.where(lax.axis_index("dp") & 2 == 0, value, passed), later, last
+    return jnp.where(lax.axis_index("dp") & 2 == 0, value, passed), before, later, last
 
 
 def local(acc_grads, activations, cotangent, params, first_moment, second_moment, step):
@@ -334,20 +335,25 @@
         sent[k] = [None, None]
         sent[k][k % 2] = lax.ppermute(total, "dp", hop(-1 if k % 2 else 1))
     waiting = [old_copy]
+    final = [None] * (2 * streams)
     for away in range(half - 1, 0, -1):
         for k in range(streams):
             for way, by in enumerate((1, -1)):
                 arrived = [] if sent[k][way] is None else [sent[k][way]]
                 body = step_kernel if arrived else plain_kernel
                 after = []
-                if arrived:
+                if k and not arrived:
                     after, waiting = waiting, after
                 total = shard_sum(
                     body, tables[way], away, keep[k], theirs[k], *arrived, after=after
                 )
                 sent[k][way] = lax.ppermute(total, "dp", hop(by))
-    grads, squares = last_sums(tables[0], keep, theirs, sent)
-    squares, *waiting = total_of(squares, grads[1:], grads[:1])
+                final[k * 2 + way] = total
+    ours = [shard_sum(plain_kernel, tables[0], 0, keep[k], theirs[k]) for k in range(streams)]
+    left = lax.optimization_barrier((state[-1][-1:], *final))[0]
+    old_last = lax.ppermute(left, "dp", onward)
+    grads, squares = last_sums(ours, sent)
+    squares, old_last, *waiting = total_of(squares, old_last, grads[1:], grads[:1])
     peer_grads = [lax.ppermute(value, "dp", onward) for value in waiting[1] + waiting[0]]
     bound = float((layers * rows * columns * lax.axis_size("mp")) ** 0.5)
     count = step.astype(jnp.float32)
@@ -357,7 +363,7 @@
             1.0 - jnp.power(jnp.float32(beta_two), count),
         ]
     )
-    return tuple(update(scales, squares, state, grads, old_copy, peer_grads, bound))
+    return tuple(update(scales, squares, state, grads, old_copy, old_last, peer_grads, bound))
 
 
 def solution(mesh):

time: 221 us -> 222 us (level)
  waiting for transfers between devices: 86 us -> 80.8 us
  Pallas kernels: 79.7 us -> 82.9 us
    ppermute x2, waiting for transfers between devices: 23 us -> 0.01 us  [local(): sent[k][k % 2] = lax.ppermute(total, 'dp', hop(-1 if k % 2 else 1))]
    ppermute x1, waiting for transfers between devices: 0.01 us -> 13.2 us  [local(): old_copy = lax.ppermute(joined(state), 'dp', onward)]
    ppermute x6, starting transfers between devices: 19.6 us -> 13.2 us  [exchanged(): lax.ppermute(value, axis, [(i, i ^ bit) for i in members])]
    pallas_call x14 -> x16, Pallas kernels: 42.7 us -> 48.5 us  [shard_sum(): pl.pallas_call(functools.partial(body, layers), grid_spec=pltpu.PrefetchS...]
    ppermute x0 -> x1, starting transfers between devices: none -> 4.79 us  [local(): old_last = lax.ppermute(left, 'dp', onward)]
    ppermute x12, waiting for transfers between devices: 49.4 us -> 53.3 us  [local(): sent[k][way] = lax.ppermute(total, 'dp', hop(by))]
  transfers between devices with their start and end apart: 28 -> 29, of which waited for: 18 -> 16; matrix products, arithmetic and copies ran while one was open for 2% -> 3% of each run, Pallas kernels for 28% -> 32%
where the time goes in v8:
time: 222 us; the launch traced here: 221 us
  Pallas kernels  82.9 us (37%)
  waiting for transfers between devices  80.8 us (36%)
  starting transfers between devices  48.7 us (22%)
  other arithmetic  4.25 us (2%)
  local copies, waits for them, and re-layouts  2.86 us (1%)
    ppermute x12, waiting for transfers between devices, local(): sent[k][way] = lax.ppermute(total, 'dp', hop(by))  53.3 us
    pallas_call x16, Pallas kernels, shard_sum(): pl.pallas_call(functools.partial(body, layers), grid_spec=pltpu.PrefetchS...  48.5 us
    ppermute x12, starting transfers between devices, local(): sent[k][way] = lax.ppermute(total, 'dp', hop(by))  22.8 us
    pallas_call x2, Pallas kernels, make_terms(): pl.pallas_call(functools.partial(terms_kernel, order, layers), grid_spec=...  17.9 us
    ppermute x1, waiting for transfers between devices, local(): old_copy = lax.ppermute(joined(state), 'dp', onward)  13.2 us
    ppermute x6, starting transfers between devices, exchanged(): lax.ppermute(value, axis, [(i, i ^ bit) for i in members])  13.2 us
    pallas_call x1, Pallas kernels, update(): pl.pallas_call(functools.partial(update_kernel, count, bound, layers), gr...  8.88 us
    ppermute x6, waiting for transfers between devices, exchanged(): lax.ppermute(value, axis, [(i, i ^ bit) for i in members])  6.35 us
  transfers between devices with their start and end apart: 29, of which 16 were waited for; matrix products, arithmetic and copies ran while one was open for 3% of the time, Pallas kernels for 32%

profile of v8, /device:TPU:0, one launch (start us, length us, event | category | flops | bytes accessed | tf_op | source)
XLA Modules:
  0.0 221.1 jit_solution(15417513598462668847)
XLA Ops:
  0.6 3.5 %joined.1 = f32[5,8,24576]{2,1,0:T(8,128)} custom-call(f32[2,8,24576]{2,1,0:T(8,128)} %rest_0_.1, f32[2,8,24576]{2,1,0:T(8,128)} %rest_0_.1, f32[2,8,24576]{2,1,0:T(8,128)} %rest_1_.1, f32[2,8,24576]{2,1,0:T(8,128)} %rest_1_.1, f32[2,8,24576]{2,1,0:T(8,128)} %rest_2_.1), custom_call_target="tpu_custom_call" | custom-call | bytes 9437184 | tf_op jit(solution)/shard_map/joined/pallas_call | solution.py:250
  6.4 8.9 %terms.3 = (f32[8,2,8,12288]{3,2,1,0:T(8,128)}, f32[8,8,12288]{2,1,0:T(8,128)}, f32[8,8,12288]{2,1,0:T(8,128)}) custom-call(s32[1]{0:T(128)} %bitcast.core_ref, bf16[256,256]{1,0:T(8,128)(2,1)} %copy.14.inputs_ref, bf16[1,2,128,24576]{3,2,1,0:T(8,128)(2,1)} %earlier_ref.3, bf16[128,2,24576]{2,1,0:T(2,128)(2,1)} %outgrad_ref.3), custom_call_target="tpu_custom_call" | custom-call | bytes 25165824 | tf_op jit(solution)/shard_map/terms/pallas_call | solution.py:71
  18.0 9.0 %terms.2 = (f32[8,2,8,12288]{3,2,1,0:T(8,128)}, f32[8,8,12288]{2,1,0:T(8,128)}, f32[8,8,12288]{2,1,0:T(8,128)}) custom-call(s32[1]{0:T(128)} %bitcast.core_ref, bf16[256,256]{1,0:T(8,128)(2,1)} %copy.14.inputs_ref, bf16[1,2,128,24576]{3,2,1,0:T(8,128)(2,1)} %earlier_ref.3, bf16[128,2,24576]{2,1,0:T(2,128)(2,1)} %outgrad_ref.3), custom_call_target="tpu_custom_call" | custom-call | bytes 25165824 | tf_op jit(solution)/shard_map/terms/pallas_call | solution.py:71
  33.1 4.5 %collective-permute-done.1.rest_1_ = f32[8,8,12288]{2,1,0:T(8,128)} collective-permute-done((f32[8,8,12288]{2,1,0:T(8,128)}, f32[8,8,12288]{2,1,0:T(8,128)}, u32[]{:S(2)}, u32[]{:S(2)}) %collective-permute-start.1) | collective-permute-done | bytes 3145760 | tf_op jit(solution)/shard_map/ppermute | solution.py:330
  45.9 13.2 %collective-permute-done.11.rest_2_.rest_3_.rest_4_.rest_5_.rest_6_.rest_7_ = f32[5,8,24576]{2,1,0:T(8,128)} collective-permute-done((f32[5,8,24576]{2,1,0:T(8,128)}, f32[5,8,24576]{2,1,0:T(8,128)}, u32[]{:S(2)}, u32[]{:S(2)}) %collective-permute-start.11) | collective-permute-done | bytes 3932192 | tf_op jit(solution)/shard_map/ppermute | solution.py:318
  62.1 10.4 %collective-permute-start.12 = (f32[2,8,12288]{2,1,0:T(8,128)}, f32[2,8,12288]{2,1,0:T(8,128)}, u32[]{:S(2)}, u32[]{:S(2)}) collective-permute-start(f32[2,8,12288]{2,1,0:T(8,128)} %shard_sum.25), channel_id=1, source_target_pairs={{0,8},{2,10},{8,16},{10,18},{16,24},{18,26},{24,28},{26,30},{28,20... | collective-permute-start | bytes 2359304 | tf_op jit(solution)/shard_map/ppermute | solution.py:350
  72.4 3.1 %shard_sum.29 = f32[2,8,12288]{2,1,0:T(8,128)} custom-call(s32[6]{0:T(128)} %pad_add_fusion.1.shard_ref, f32[8,2,8,12288]{3,2,1,0:T(8,128)} %get-tuple-element.24.keep_ref, f32[8,8,12288]{2,1,0:T(8,128)} %collective-permute-done.9.rest_0_, f32[8,8,12288]{2,1,0:T(8,128)} %collective-permute-done.10.rest_1_, f32[2,8,12288]{2,1,0:T(8,128)} %collective-permute-done.15.rest_2_), custom_call_target="tpu_custom_call" | custom-call | bytes 3145728 | tf_op jit(solution)/shard_map/shard_sum/pallas_call | solution.py:163
  75.6 3.1 %shard_sum.18 = f32[2,8,12288]{2,1,0:T(8,128)} custom-call(s32[6]{0:T(128)} %pad_add_fusion.shard_ref, f32[8,2,8,12288]{3,2,1,0:T(8,128)} %get-tuple-element.21.keep_ref, f32[8,8,12288]{2,1,0:T(8,128)} %collective-permute-done.rest_0_, f32[8,8,12288]{2,1,0:T(8,128)} %collective-permute-done.1.rest_1_, f32[2,8,12288]{2,1,0:T(8,128)} %collective-permute-done.2.rest_2_), custom_call_target="tpu_custom_call" | custom-call | bytes 3145728 | tf_op jit(solution)/shard_map/shard_sum/pallas_call | solution.py:163
  80.7 3.1 %shard_sum.22 = f32[2,8,12288]{2,1,0:T(8,128)} custom-call(s32[6]{0:T(128)} %pad_add_fusion.1.shard_ref, f32[8,2,8,12288]{3,2,1,0:T(8,128)} %get-tuple-element.21.keep_ref, f32[8,8,12288]{2,1,0:T(8,128)} %collective-permute-done.rest_0_, f32[8,8,12288]{2,1,0:T(8,128)} %collective-permute-done.1.rest_1_, f32[2,8,12288]{2,1,0:T(8,128)} %collective-permute-done.6.rest_2_), custom_call_target="tpu_custom_call" | custom-call | bytes 3145728 | tf_op jit(solution)/shard_map/shard_sum/pallas_call | solution.py:163
  83.9 6.4 %collective-permute-done.12.rest_2_ = f32[2,8,12288]{2,1,0:T(8,128)} collective-permute-done((f32[2,8,12288]{2,1,0:T(8,128)}, f32[2,8,12288]{2,1,0:T(8,128)}, u32[]{:S(2)}, u32[]{:S(2)}) %collective-permute-start.12) | collective-permute-done | bytes 786464 | tf_op jit(solution)/shard_map/ppermute | solution.py:350
  90.2 3.1 %shard_sum.26 = f32[2,8,12288]{2,1,0:T(8,128)} custom-call(s32[6]{0:T(128)} %pad_add_fusion.shard_ref, f32[8,2,8,12288]{3,2,1,0:T(8,128)} %get-tuple-element.24.keep_ref, f32[8,8,12288]{2,1,0:T(8,128)} %collective-permute-done.9.rest_0_, f32[8,8,12288]{2,1,0:T(8,128)} %collective-permute-done.10.rest_1_, f32[2,8,12288]{2,1,0:T(8,128)} %collective-permute-done.12.rest_2_), custom_call_target="tpu_custom_call" | custom-call | bytes 3145728 | tf_op jit(solution)/shard_map/shard_sum/pallas_call | solution.py:163
  94.3 3.1 %shard_sum.30 = f32[2,8,12288]{2,1,0:T(8,128)} custom-call(s32[6]{0:T(128)} %pad_add_fusion.1.shard_ref, f32[8,2,8,12288]{3,2,1,0:T(8,128)} %get-tuple-element.24.keep_ref, f32[8,8,12288]{2,1,0:T(8,128)} %collective-permute-done.9.rest_0_, f32[8,8,12288]{2,1,0:T(8,128)} %collective-permute-done.10.rest_1_, f32[2,8,12288]{2,1,0:T(8,128)} %collective-permute-done.16.rest_2_), custom_call_target="tpu_custom_call" | custom-call | bytes 3145728 | tf_op jit(solution)/shard_map/shard_sum/pallas_call | solution.py:163
  99.5 7.6 %collective-permute-done.3.rest_2_ = f32[2,8,12288]{2,1,0:T(8,128)} collective-permute-done((f32[2,8,12288]{2,1,0:T(8,128)}, f32[2,8,12288]{2,1,0:T(8,128)}, u32[]{:S(2)}, u32[]{:S(2)}) %collective-permute-start.3) | collective-permute-done | bytes 786464 | tf_op jit(solution)/shard_map/ppermute | solution.py:350
  111.1 3.1 %shard_sum.23 = f32[2,8,12288]{2,1,0:T(8,128)} custom-call(s32[6]{0:T(128)} %pad_add_fusion.1.shard_ref, f32[8,2,8,12288]{3,2,1,0:T(8,128)} %get-tuple-element.21.keep_ref, f32[8,8,12288]{2,1,0:T(8,128)} %collective-permute-done.rest_0_, f32[8,8,12288]{2,1,0:T(8,128)} %collective-permute-done.1.rest_1_, f32[2,8,12288]{2,1,0:T(8,128)} %collective-permute-done.7.rest_2_), custom_call_target="tpu_custom_call" | custom-call | bytes 3145728 | tf_op jit(solution)/shard_map/shard_sum/pallas_call | solution.py:163
  116.3 7.6 %collective-permute-done.13.rest_2_ = f32[2,8,12288]{2,1,0:T(8,128)} collective-permute-done((f32[2,8,12288]{2,1,0:T(8,128)}, f32[2,8,12288]{2,1,0:T(8,128)}, u32[]{:S(2)}, u32[]{:S(2)}) %collective-permute-start.13) | collective-permute-done | bytes 786464 | tf_op jit(solution)/shard_map/ppermute | solution.py:350
  123.9 3.1 %shard_sum.27 = f32[2,8,12288]{2,1,0:T(8,128)} custom-call(s32[6]{0:T(128)} %pad_add_fusion.shard_ref, f32[8,2,8,12288]{3,2,1,0:T(8,128)} %get-tuple-element.24.keep_ref, f32[8,8,12288]{2,1,0:T(8,128)} %collective-permute-done.9.rest_0_, f32[8,8,12288]{2,1,0:T(8,128)} %collective-permute-done.10.rest_1_, f32[2,8,12288]{2,1,0:T(8,128)} %collective-permute-done.13.rest_2_), custom_call_target="tpu_custom_call" | custom-call | bytes 3145728 | tf_op jit(solution)/shard_map/shard_sum/pallas_call | solution.py:163
  128.0 3.1 %shard_sum.31 = f32[2,8,12288]{2,1,0:T(8,128)} custom-call(s32[6]{0:T(128)} %pad_add_fusion.1.shard_ref, f32[8,2,8,12288]{3,2,1,0:T(8,128)} %get-tuple-element.24.keep_ref, f32[8,8,12288]{2,1,0:T(8,128)} %collective-permute-done.9.rest_0_, f32[8,8,12288]{2,1,0:T(8,128)} %collective-permute-done.10.rest_1_, f32[2,8,12288]{2,1,0:T(8,128)} %collective-permute-done.17.rest_2_), custom_call_target="tpu_custom_call" | custom-call | bytes 3145728 | tf_op jit(solution)/shard_map/shard_sum/pallas_call | solution.py:163
  133.2 7.6 %collective-permute-done.4.rest_2_ = f32[2,8,12288]{2,1,0:T(8,128)} collective-permute-done((f32[2,8,12288]{2,1,0:T(8,128)}, f32[2,8,12288]{2,1,0:T(8,128)}, u32[]{:S(2)}, u32[]{:S(2)}) %collective-permute-start.4) | collective-permute-done | bytes 786464 | tf_op jit(solution)/shard_map/ppermute | solution.py:350
  146.9 4.8 %collective-permute-start.20 = (f32[1,8,24576]{2,1,0:T(8,128)}, f32[1,8,24576]{2,1,0:T(8,128)}, u32[]{:S(2)}, u32[]{:S(2)}) collective-permute-start(f32[1,8,24576]{2,1,0:T(8,128)} %slice.3), channel_id=1, source_target_pairs={{0,2},{2,4},{4,6},{6,8},{8,10},{10,12},{12,14},{14,16},{16,18},{18... | collective-permute-start | bytes 2359304 | tf_op jit(solution)/shard_map/ppermute | solution.py:354
  157.6 4.0 %collective-permute-done.18.refs_5_ = f32[2,8,12288]{2,1,0:T(8,128)} collective-permute-done((f32[2,8,12288]{2,1,0:T(8,128)}, f32[2,8,12288]{2,1,0:T(8,128)}, u32[]{:S(2)}, u32[]{:S(2)}) %collective-permute-start.18) | collective-permute-done | bytes 786464 | tf_op jit(solution)/shard_map/ppermute | solution.py:350
  161.6 20.0 %collective-permute-done.5.refs_1_ = f32[2,8,12288]{2,1,0:T(8,128)} collective-permute-done((f32[2,8,12288]{2,1,0:T(8,128)}, f32[2,8,12288]{2,1,0:T(8,128)}, u32[]{:S(2)}, u32[]{:S(2)}) %collective-permute-start.5) | collective-permute-done | bytes 786464 | tf_op jit(solution)/shard_map/ppermute | solution.py:350
  181.6 4.2 %last_sums.1 = (f32[2,8,12288]{2,1,0:T(8,128)}, f32[2,8,12288]{2,1,0:T(8,128)}, f32[8,128]{1,0:T(8,128)}) custom-call(f32[2,8,12288]{2,1,0:T(8,128)} %shard_sum.16.refs_0_, f32[2,8,12288]{2,1,0:T(8,128)} %collective-permute-done.5.refs_1_, f32[2,8,12288]{2,1,0:T(8,128)} %collective-permute-done.8.refs_2_, f32[2,8,12288]{2,1,0:T(8,128)} %shard_sum.24.refs_3_, ...), custom_call_target="tpu_custom_call" | custom-call | bytes 6291456 | tf_op jit(solution)/shard_map/last_sums/pallas_call | solution.py:143
  195.8 5.8 %collective-permute-start.22 = (f32[8,128]{1,0:T(8,128)S(1)}, f32[8,128]{1,0:T(8,128)S(1)}, u32[]{:S(2)}, u32[]{:S(2)}) collective-permute-start(f32[8,128]{1,0:T(8,128)S(1)} %add.55), channel_id=1, source_target_pairs={{0,8},{2,10},{8,0},{10,2},{16,24},{18,26},{24,16},{26,18},{1,9},{3... | collective-permute-start | bytes 12296 | tf_op jit(solution)/shard_map/ppermute | solution.py:268
  212.2 8.9 %update.1 = (f32[2,8,24576]{2,1,0:T(8,128)}, f32[2,8,24576]{2,1,0:T(8,128)}, f32[2,8,24576]{2,1,0:T(8,128)}, f32[2,8,24576]{2,1,0:T(8,128)}, f32[2,8,24576]{2,1,0:T(8,128)}, /*index=5*/f32[2,8,24576]{2,1,0:T(8,128)}) custom-call(f32[2]{0:T(128)} %pad_maximum_fusion.scales_ref, f32[8,128]{1,0:T(8,128)} %broadcast_select_fusion.squares_ref, ...), custom_call_target="tpu_custom_call" | custom-call | bytes 22020096 | tf_op jit(solution)/shard_map/update/pallas_call | solution.py:221
  (70 shorter events, 68.3 us)
Async XLA Ops:
  4.2 55.0 %collective-permute-start.11 = (f32[5,8,24576]{2,1,0:T(8,128)}, f32[5,8,24576]{2,1,0:T(8,128)}, u32[]{:S(2)}, u32[]{:S(2)}) collective-permute-start(f32[5,8,24576]{2,1,0:T(8,128)} %joined.1), channel_id=1, source_target_pairs={{0,2},{2,4},{4,6},{6,8},{8,10},{10,12},{12,14},{14,16},{16,18},{18... | collective-permute-start | bytes 11796488 | tf_op jit(solution)/shard_map/ppermute | solution.py:318
  15.4 12.7 %collective-permute-start.9 = (f32[8,8,12288]{2,1,0:T(8,128)}, f32[8,8,12288]{2,1,0:T(8,128)}, u32[]{:S(2)}, u32[]{:S(2)}) collective-permute-start(f32[8,8,12288]{2,1,0:T(8,128)} %get-tuple-element.25), channel_id=1, source_target_pairs={{0,2},{2,0},{4,6},{6,4},{8,10},{10,8},{12,14},{14,12},{16,18},{18,... | collective-permute-start | bytes 9437192 | tf_op jit(solution)/shard_map/ppermute | solution.py:330
  18.0 10.1 %collective-permute-start.10 = (f32[8,8,12288]{2,1,0:T(8,128)}, f32[8,8,12288]{2,1,0:T(8,128)}, u32[]{:S(2)}, u32[]{:S(2)}) collective-permute-start(f32[8,8,12288]{2,1,0:T(8,128)} %get-tuple-element.26), channel_id=1, source_target_pairs={{0,2},{2,0},{4,6},{6,4},{8,10},{10,8},{12,14},{14,12},{16,18},{18,... | collective-permute-start | bytes 9437192 | tf_op jit(solution)/shard_map/ppermute | solution.py:330
  27.4 10.1 %collective-permute-start.1 = (f32[8,8,12288]{2,1,0:T(8,128)}, f32[8,8,12288]{2,1,0:T(8,128)}, u32[]{:S(2)}, u32[]{:S(2)}) collective-permute-start(f32[8,8,12288]{2,1,0:T(8,128)} %get-tuple-element.23), channel_id=1, source_target_pairs={{0,2},{2,0},{4,6},{6,4},{8,10},{10,8},{12,14},{14,12},{16,18},{18,... | collective-permute-start | bytes 9437192 | tf_op jit(solution)/shard_map/ppermute | solution.py:330
  31.0 41.5 %collective-permute-start.15 = (f32[2,8,12288]{2,1,0:T(8,128)}, f32[2,8,12288]{2,1,0:T(8,128)}, u32[]{:S(2)}, u32[]{:S(2)}) collective-permute-start(f32[2,8,12288]{2,1,0:T(8,128)} %shard_sum.28), channel_id=1, source_target_pairs={{0,4},{2,6},{8,0},{10,2},{16,8},{18,10},{24,16},{26,18},{28,24},{3... | collective-permute-start | bytes 2359304 | tf_op jit(solution)/shard_map/ppermute | solution.py:336
  40.4 35.2 %collective-permute-start.2 = (f32[2,8,12288]{2,1,0:T(8,128)}, f32[2,8,12288]{2,1,0:T(8,128)}, u32[]{:S(2)}, u32[]{:S(2)}) collective-permute-start(f32[2,8,12288]{2,1,0:T(8,128)} %shard_sum.17), channel_id=1, source_target_pairs={{0,8},{2,10},{8,16},{10,18},{16,24},{18,26},{24,28},{26,30},{28,20... | collective-permute-start | bytes 2359304 | tf_op jit(solution)/shard_map/ppermute | solution.py:336
  45.5 35.2 %collective-permute-start.6 = (f32[2,8,12288]{2,1,0:T(8,128)}, f32[2,8,12288]{2,1,0:T(8,128)}, u32[]{:S(2)}, u32[]{:S(2)}) collective-permute-start(f32[2,8,12288]{2,1,0:T(8,128)} %shard_sum.21), channel_id=1, source_target_pairs={{0,4},{2,6},{8,0},{10,2},{16,8},{18,10},{24,16},{26,18},{28,24},{3... | collective-permute-start | bytes 2359304 | tf_op jit(solution)/shard_map/ppermute | solution.py:350
  62.1 28.2 %collective-permute-start.12 = (f32[2,8,12288]{2,1,0:T(8,128)}, f32[2,8,12288]{2,1,0:T(8,128)}, u32[]{:S(2)}, u32[]{:S(2)}) collective-permute-start(f32[2,8,12288]{2,1,0:T(8,128)} %shard_sum.25), channel_id=1, source_target_pairs={{0,8},{2,10},{8,16},{10,18},{16,24},{18,26},{24,28},{26,30},{28,20... | collective-permute-start | bytes 2359304 | tf_op jit(solution)/shard_map/ppermute | solution.py:350
  75.6 18.7 %collective-permute-start.16 = (f32[2,8,12288]{2,1,0:T(8,128)}, f32[2,8,12288]{2,1,0:T(8,128)}, u32[]{:S(2)}, u32[]{:S(2)}) collective-permute-start(f32[2,8,12288]{2,1,0:T(8,128)} %shard_sum.29), channel_id=1, source_target_pairs={{0,4},{2,6},{8,0},{10,2},{16,8},{18,10},{24,16},{26,18},{28,24},{3... | collective-permute-start | bytes 2359304 | tf_op jit(solution)/shard_map/ppermute | solution.py:350
  78.7 28.4 %collective-permute-start.3 = (f32[2,8,12288]{2,1,0:T(8,128)}, f32[2,8,12288]{2,1,0:T(8,128)}, u32[]{:S(2)}, u32[]{:S(2)}) collective-permute-start(f32[2,8,12288]{2,1,0:T(8,128)} %shard_sum.18), channel_id=1, source_target_pairs={{0,8},{2,10},{8,16},{10,18},{16,24},{18,26},{24,28},{26,30},{28,20... | collective-permute-start | bytes 2359304 | tf_op jit(solution)/shard_map/ppermute | solution.py:350
  83.9 27.3 %collective-permute-start.7 = (f32[2,8,12288]{2,1,0:T(8,128)}, f32[2,8,12288]{2,1,0:T(8,128)}, u32[]{:S(2)}, u32[]{:S(2)}) collective-permute-start(f32[2,8,12288]{2,1,0:T(8,128)} %shard_sum.22), channel_id=1, source_target_pairs={{0,4},{2,6},{8,0},{10,2},{16,8},{18,10},{24,16},{26,18},{28,24},{3... | collective-permute-start | bytes 2359304 | tf_op jit(solution)/shard_map/ppermute | solution.py:350
  93.4 30.6 %collective-permute-start.13 = (f32[2,8,12288]{2,1,0:T(8,128)}, f32[2,8,12288]{2,1,0:T(8,128)}, u32[]{:S(2)}, u32[]{:S(2)}) collective-permute-start(f32[2,8,12288]{2,1,0:T(8,128)} %shard_sum.26), channel_id=1, source_target_pairs={{0,8},{2,10},{8,16},{10,18},{16,24},{18,26},{24,28},{26,30},{28,20... | collective-permute-start | bytes 2359304 | tf_op jit(solution)/shard_map/ppermute | solution.py:350
  97.4 30.6 %collective-permute-start.17 = (f32[2,8,12288]{2,1,0:T(8,128)}, f32[2,8,12288]{2,1,0:T(8,128)}, u32[]{:S(2)}, u32[]{:S(2)}) collective-permute-start(f32[2,8,12288]{2,1,0:T(8,128)} %shard_sum.30), channel_id=1, source_target_pairs={{0,4},{2,6},{8,0},{10,2},{16,8},{18,10},{24,16},{26,18},{28,24},{3... | collective-permute-start | bytes 2359304 | tf_op jit(solution)/shard_map/ppermute | solution.py:350
  110.2 30.6 %collective-permute-start.4 = (f32[2,8,12288]{2,1,0:T(8,128)}, f32[2,8,12288]{2,1,0:T(8,128)}, u32[]{:S(2)}, u32[]{:S(2)}) collective-permute-start(f32[2,8,12288]{2,1,0:T(8,128)} %shard_sum.19), channel_id=1, source_target_pairs={{0,8},{2,10},{8,16},{10,18},{16,24},{18,26},{24,28},{26,30},{28,20... | collective-permute-start | bytes 2359304 | tf_op jit(solution)/shard_map/ppermute | solution.py:350
  114.3 43.2 %collective-permute-start.8 = (f32[2,8,12288]{2,1,0:T(8,128)}, f32[2,8,12288]{2,1,0:T(8,128)}, u32[]{:S(2)}, u32[]{:S(2)}) collective-permute-start(f32[2,8,12288]{2,1,0:T(8,128)} %shard_sum.23), channel_id=1, source_target_pairs={{0,4},{2,6},{8,0},{10,2},{16,8},{18,10},{24,16},{26,18},{28,24},{3... | collective-permute-start | bytes 2359304 | tf_op jit(solution)/shard_map/ppermute | solution.py:350
  127.1 30.6 %collective-permute-start.14 = (f32[2,8,12288]{2,1,0:T(8,128)}, f32[2,8,12288]{2,1,0:T(8,128)}, u32[]{:S(2)}, u32[]{:S(2)}) collective-permute-start(f32[2,8,12288]{2,1,0:T(8,128)} %shard_sum.27), channel_id=1, source_target_pairs={{0,8},{2,10},{8,16},{10,18},{16,24},{18,26},{24,28},{26,30},{28,20... | collective-permute-start | bytes 2359304 | tf_op jit(solution)/shard_map/ppermute | solution.py:350
  131.1 30.5 %collective-permute-start.18 = (f32[2,8,12288]{2,1,0:T(8,128)}, f32[2,8,12288]{2,1,0:T(8,128)}, u32[]{:S(2)}, u32[]{:S(2)}) collective-permute-start(f32[2,8,12288]{2,1,0:T(8,128)} %shard_sum.31), channel_id=1, source_target_pairs={{0,4},{2,6},{8,0},{10,2},{16,8},{18,10},{24,16},{26,18},{28,24},{3... | collective-permute-start | bytes 2359304 | tf_op jit(solution)/shard_map/ppermute | solution.py:350
  143.9 37.6 %collective-permute-start.5 = (f32[2,8,12288]{2,1,0:T(8,128)}, f32[2,8,12288]{2,1,0:T(8,128)}, u32[]{:S(2)}, u32[]{:S(2)}) collective-permute-start(f32[2,8,12288]{2,1,0:T(8,128)} %shard_sum.20), channel_id=1, source_target_pairs={{0,8},{2,10},{8,16},{10,18},{16,24},{18,26},{24,28},{26,30},{28,20... | collective-permute-start | bytes 2359304 | tf_op jit(solution)/shard_map/ppermute | solution.py:350
  146.9 40.9 %collective-permute-start.20 = (f32[1,8,24576]{2,1,0:T(8,128)}, f32[1,8,24576]{2,1,0:T(8,128)}, u32[]{:S(2)}, u32[]{:S(2)}) collective-permute-start(f32[1,8,24576]{2,1,0:T(8,128)} %slice.3), channel_id=1, source_target_pairs={{0,2},{2,4},{4,6},{6,8},{8,10},{10,12},{12,14},{14,16},{16,18},{18... | collective-permute-start | bytes 2359304 | tf_op jit(solution)/shard_map/ppermute | solution.py:354
  189.3 20.6 %collective-permute-start.28 = (f32[2,8,12288]{2,1,0:T(8,128)}, f32[2,8,12288]{2,1,0:T(8,128)}, u32[]{:S(2)}, u32[]{:S(2)}) collective-permute-start(f32[2,8,12288]{2,1,0:T(8,128)} %get-tuple-element.35.rest_10_), channel_id=1, source_target_pairs={{0,2},{2,4},{4,6},{6,8},{8,10},{10,12},{12,14},{14,16},{16,18},{18... | collective-permute-start | bytes 2359304 | tf_op jit(solution)/shard_map/ppermute | solution.py:357
  191.4 20.8 %collective-permute-start.27 = (f32[2,8,12288]{2,1,0:T(8,128)}, f32[2,8,12288]{2,1,0:T(8,128)}, u32[]{:S(2)}, u32[]{:S(2)}) collective-permute-start(f32[2,8,12288]{2,1,0:T(8,128)} %get-tuple-element.34.rest_9_), channel_id=1, source_target_pairs={{0,2},{2,4},{4,6},{6,8},{8,10},{10,12},{12,14},{14,16},{16,18},{18... | collective-permute-start | bytes 2359304 | tf_op jit(solution)/shard_map/ppermute | solution.py:357
  191.4 10.1 %collective-permute-start.24 = (f32[8,128]{1,0:T(8,128)S(1)}, f32[8,128]{1,0:T(8,128)S(1)}, u32[]{:S(2)}, u32[]{:S(2)}) collective-permute-start(f32[8,128]{1,0:T(8,128)S(1)} %add.55), channel_id=1, source_target_pairs={{0,24},{2,26},{8,16},{10,18},{16,8},{18,10},{24,0},{26,2},{1,25},{... | collective-permute-start | bytes 12296 | tf_op jit(solution)/shard_map/ppermute | solution.py:268
  193.3 8.2 %collective-permute-start.23 = (f32[8,128]{1,0:T(8,128)S(1)}, f32[8,128]{1,0:T(8,128)S(1)}, u32[]{:S(2)}, u32[]{:S(2)}) collective-permute-start(f32[8,128]{1,0:T(8,128)S(1)} %add.55), channel_id=1, source_target_pairs={{0,16},{2,18},{8,24},{10,26},{16,0},{18,2},{24,8},{26,10},{1,17},{... | collective-permute-start | bytes 12296 | tf_op jit(solution)/shard_map/ppermute | solution.py:268
  195.8 7.4 %collective-permute-start.22 = (f32[8,128]{1,0:T(8,128)S(1)}, f32[8,128]{1,0:T(8,128)S(1)}, u32[]{:S(2)}, u32[]{:S(2)}) collective-permute-start(f32[8,128]{1,0:T(8,128)S(1)} %add.55), channel_id=1, source_target_pairs={{0,8},{2,10},{8,0},{10,2},{16,24},{18,26},{24,16},{26,18},{1,9},{3... | collective-permute-start | bytes 12296 | tf_op jit(solution)/shard_map/ppermute | solution.py:268
  (5 other events, 17.3 us)

commit v9 on v8

--- a/solution.py
+++ b/solution.py
@@ -238,21 +238,23 @@
 
 
 def joined_kernel(*refs):
-    *parts, out_ref = refs
-    for index, part_ref in enumerate(parts):
+    *parts, out_ref, left_ref = refs
+    for index, part_ref in enumerate(parts[:-1]):
         out_ref[index] = part_ref[0]
+    left_ref[...] = parts[-1][...]
 
 
 def joined(arrays):
     layers, own, columns = arrays[0].shape
     size = block_of(columns, 12288)
-    places = [(array, layer) for array in arrays for layer in range(layers)][:-1]
+    places = [(array, layer) for array in arrays for layer in range(layers)]
+    joint = len(places) - 1
     return pl.pallas_call(
         joined_kernel,
         grid=(columns // size,),
         in_specs=[pl.BlockSpec((1, own, size), lambda i, l=l: (l, 0, i)) for _, l in places],
-        out_specs=pl.BlockSpec((len(places), own, size), lambda i: (0, 0, i)),
-        out_shape=jax.ShapeDtypeStruct((len(places), own, columns), jnp.float32),
+        out_specs=[pl.BlockSpec((n, own, size), lambda i: (0, 0, i)) for n in (joint, 1)],
+        out_shape=[jax.ShapeDtypeStruct((n, own, columns), jnp.float32) for n in (joint, 1)],
         compiler_params=room,
         cost_estimate=cost_of(*arrays, *arrays),
         name="joined",
@@ -315,7 +317,8 @@
     ]
 
     state = (params, first_moment, second_moment)
-    old_copy = lax.ppermute(joined(state), "dp", onward)
+    most, left = joined(state)
+    old_copy = lax.ppermute(most, "dp", onward)
 
     same = jnp.eye(layers, dtype=activations.dtype)
     inputs = activations.transpose(1, 2, 0)[:, :, :, None] * same[:, None, None, :]
@@ -335,7 +338,6 @@
         sent[k] = [None, None]
         sent[k][k % 2] = lax.ppermute(total, "dp", hop(-1 if k % 2 else 1))
     waiting = [old_copy]
-    final = [None] * (2 * streams)
     for away in range(half - 1, 0, -1):
         for k in range(streams):
             for way, by in enumerate((1, -1)):
@@ -348,9 +350,8 @@
                     body, tables[way], away, keep[k], theirs[k], *arrived, after=after
                 )
                 sent[k][way] = lax.ppermute(total, "dp", hop(by))
-                final[k * 2 + way] = total
     ours = [shard_sum(plain_kernel, tables[0], 0, keep[k], theirs[k]) for k in range(streams)]
-    left = lax.optimization_barrier((state[-1][-1:], *final))[0]
+    left, *_ = lax.optimization_barrier((left, sent, ours))
     old_last = lax.ppermute(left, "dp", onward)
     grads, squares = last_sums(ours, sent)
     squares, old_last, *waiting = total_of(squares, old_last, grads[1:], grads[:1])

time: 222 us -> 240 us (1.081)
  starting transfers between devices: 48.7 us -> 62.8 us
  waiting for transfers between devices: 80.8 us -> 86.9 us
    ppermute x12, starting transfers between devices: 22.8 us -> 32.1 us  [local(): sent[k][way] = lax.ppermute(total, 'dp', hop(by))]
    ppermute x12, waiting for transfers between devices: 53.3 us -> 45.5 us  [local(): sent[k][way] = lax.ppermute(total, 'dp', hop(by))]
    ppermute x2, waiting for transfers between devices: 0.01 us -> 5.66 us  [local(): sent[k][k % 2] = lax.ppermute(total, 'dp', hop(-1 if k % 2 else 1))]
    ppermute x1, starting transfers between devices: 4.79 us -> 9.9 us  [local(): old_last = lax.ppermute(left, 'dp', onward)]
    ppermute x1, waiting for transfers between devices: 0.01 us -> 4.24 us  [local(): old_last = lax.ppermute(left, 'dp', onward)]
    ppermute x1, waiting for transfers between devices: 13.2 us -> 16.9 us  [local(): old_copy = lax.ppermute(most, 'dp', onward)]
    ppermute x6, waiting for transfers between devices: 6.35 us -> 8.77 us  [exchanged(): lax.ppermute(value, axis, [(i, i ^ bit) for i in members])]
  transfers between devices with their start and end apart: 29 -> 29, of which waited for: 16 -> 15; matrix products, arithmetic and copies ran while one was open for 3% -> 1% of each run, Pallas kernels for 32% -> 27%
where the time goes in v9:
time: 240 us
  waiting for transfers between devices  86.9 us (36%)
  Pallas kernels  83.4 us (35%)
  starting transfers between devices  62.8 us (26%)
  other arithmetic  4.15 us (2%)
    pallas_call x16, Pallas kernels, shard_sum(): pl.pallas_call(functools.partial(body, layers), grid_spec=pltpu.PrefetchS...  48.5 us
    ppermute x12, waiting for transfers between devices, local(): sent[k][way] = lax.ppermute(total, 'dp', hop(by))  45.5 us
    ppermute x12, starting transfers between devices, local(): sent[k][way] = lax.ppermute(total, 'dp', hop(by))  32.1 us
    pallas_call x2, Pallas kernels, make_terms(): pl.pallas_call(functools.partial(terms_kernel, order, layers), grid_spec=...  17.9 us
    ppermute x1, waiting for transfers between devices, local(): old_copy = lax.ppermute(most, 'dp', onward)  16.9 us
    ppermute x6, starting transfers between devices, exchanged(): lax.ppermute(value, axis, [(i, i ^ bit) for i in members])  12.8 us
    ppermute x1, starting transfers between devices, local(): old_last = lax.ppermute(left, 'dp', onward)  9.9 us
    pallas_call x1, Pallas kernels, update(): pl.pallas_call(functools.partial(update_kernel, count, bound, layers), gr...  8.89 us
  transfers between devices with their start and end apart: 29, of which 15 were waited for; matrix products, arithmetic and copies ran while one was open for 1% of the time, Pallas kernels for 27%

profile of v9, /device:TPU:0, one launch (start us, length us, event | category | flops | bytes accessed | tf_op | source)
XLA Modules:
  0.0 239.5 jit_solution(14365674756838737150)
XLA Ops:
  2.5 9.0 %terms.3 = (f32[8,2,8,12288]{3,2,1,0:T(8,128)}, f32[8,8,12288]{2,1,0:T(8,128)}, f32[8,8,12288]{2,1,0:T(8,128)}) custom-call(s32[1]{0:T(128)} %bitcast.core_ref, bf16[256,256]{1,0:T(8,128)(2,1)} %copy.14.inputs_ref, bf16[1,2,128,24576]{3,2,1,0:T(8,128)(2,1)} %earlier_ref.3, bf16[128,2,24576]{2,1,0:T(2,128)(2,1)} %outgrad_ref.3), custom_call_target="tpu_custom_call" | custom-call | bytes 25165824 | tf_op jit(solution)/shard_map/terms/pallas_call | solution.py:71
  11.9 3.9 %joined.1 = (f32[5,8,24576]{2,1,0:T(8,128)}, f32[1,8,24576]{2,1,0:T(8,128)}) custom-call(f32[2,8,24576]{2,1,0:T(8,128)} %rest_0_.1, f32[2,8,24576]{2,1,0:T(8,128)} %rest_0_.1, f32[2,8,24576]{2,1,0:T(8,128)} %rest_1_.1, f32[2,8,24576]{2,1,0:T(8,128)} %rest_1_.1, f32[2,8,24576]{2,1,0:T(8,128)} %rest_2_.1, f32[2,8,24576]{2,1,0:T(8,128)} %rest_2_.1), custom_call_target="tpu_custom_call" | custom-call | bytes 9437184 | tf_op jit(solution)/shard_map/joined/pallas_call | solution.py:252
  16.3 9.0 %terms.2 = (f32[8,2,8,12288]{3,2,1,0:T(8,128)}, f32[8,8,12288]{2,1,0:T(8,128)}, f32[8,8,12288]{2,1,0:T(8,128)}) custom-call(s32[1]{0:T(128)} %bitcast.core_ref, bf16[256,256]{1,0:T(8,128)(2,1)} %copy.14.inputs_ref, bf16[1,2,128,24576]{3,2,1,0:T(8,128)(2,1)} %earlier_ref.3, bf16[128,2,24576]{2,1,0:T(2,128)(2,1)} %outgrad_ref.3), custom_call_target="tpu_custom_call" | custom-call | bytes 25165824 | tf_op jit(solution)/shard_map/terms/pallas_call | solution.py:71
  33.5 4.5 %collective-permute-done.1.rest_1_ = f32[8,8,12288]{2,1,0:T(8,128)} collective-permute-done((f32[8,8,12288]{2,1,0:T(8,128)}, f32[8,8,12288]{2,1,0:T(8,128)}, u32[]{:S(2)}, u32[]{:S(2)}) %collective-permute-start.1) | collective-permute-done | bytes 3145760 | tf_op jit(solution)/shard_map/ppermute | solution.py:333
  46.4 5.7 %collective-permute-done.15.rest_2_ = f32[2,8,12288]{2,1,0:T(8,128)} collective-permute-done((f32[2,8,12288]{2,1,0:T(8,128)}, f32[2,8,12288]{2,1,0:T(8,128)}, u32[]{:S(2)}, u32[]{:S(2)}) %collective-permute-start.15) | collective-permute-done | bytes 786464 | tf_op jit(solution)/shard_map/ppermute | solution.py:339
  56.9 16.9 %collective-permute-done.11.rest_2_.rest_3_.rest_4_.rest_5_.rest_6_.rest_7_ = f32[5,8,24576]{2,1,0:T(8,128)} collective-permute-done((f32[5,8,24576]{2,1,0:T(8,128)}, f32[5,8,24576]{2,1,0:T(8,128)}, u32[]{:S(2)}, u32[]{:S(2)}) %collective-permute-start.11) | collective-permute-done | bytes 3932192 | tf_op jit(solution)/shard_map/ppermute | solution.py:321
  76.6 16.7 %collective-permute-start.12 = (f32[2,8,12288]{2,1,0:T(8,128)}, f32[2,8,12288]{2,1,0:T(8,128)}, u32[]{:S(2)}, u32[]{:S(2)}) collective-permute-start(f32[2,8,12288]{2,1,0:T(8,128)} %shard_sum.25), channel_id=1, source_target_pairs={{0,8},{2,10},{8,16},{10,18},{16,24},{18,26},{24,28},{26,30},{28,20... | collective-permute-start | bytes 2359304 | tf_op jit(solution)/shard_map/ppermute | solution.py:352
  93.4 3.1 %shard_sum.18 = f32[2,8,12288]{2,1,0:T(8,128)} custom-call(s32[6]{0:T(128)} %pad_add_fusion.shard_ref, f32[8,2,8,12288]{3,2,1,0:T(8,128)} %get-tuple-element.23.keep_ref, f32[8,8,12288]{2,1,0:T(8,128)} %collective-permute-done.rest_0_, f32[8,8,12288]{2,1,0:T(8,128)} %collective-permute-done.1.rest_1_, f32[2,8,12288]{2,1,0:T(8,128)} %collective-permute-done.2.rest_2_), custom_call_target="tpu_custom_call" | custom-call | bytes 3145728 | tf_op jit(solution)/shard_map/shard_sum/pallas_call | solution.py:163
  109.9 8.7 %collective-permute-done.3.rest_2_ = f32[2,8,12288]{2,1,0:T(8,128)} collective-permute-done((f32[2,8,12288]{2,1,0:T(8,128)}, f32[2,8,12288]{2,1,0:T(8,128)}, u32[]{:S(2)}, u32[]{:S(2)}) %collective-permute-start.3) | collective-permute-done | bytes 786464 | tf_op jit(solution)/shard_map/ppermute | solution.py:352
  121.8 3.6 %collective-permute-start.4 = (f32[2,8,12288]{2,1,0:T(8,128)}, f32[2,8,12288]{2,1,0:T(8,128)}, u32[]{:S(2)}, u32[]{:S(2)}) collective-permute-start(f32[2,8,12288]{2,1,0:T(8,128)} %shard_sum.19), channel_id=1, source_target_pairs={{0,8},{2,10},{8,16},{10,18},{16,24},{18,26},{24,28},{26,30},{28,20... | collective-permute-start | bytes 2359304 | tf_op jit(solution)/shard_map/ppermute | solution.py:352
  125.4 3.1 %shard_sum.23 = f32[2,8,12288]{2,1,0:T(8,128)} custom-call(s32[6]{0:T(128)} %pad_add_fusion.1.shard_ref, f32[8,2,8,12288]{3,2,1,0:T(8,128)} %get-tuple-element.23.keep_ref, f32[8,8,12288]{2,1,0:T(8,128)} %collective-permute-done.rest_0_, f32[8,8,12288]{2,1,0:T(8,128)} %collective-permute-done.1.rest_1_, f32[2,8,12288]{2,1,0:T(8,128)} %collective-permute-done.7.rest_2_), custom_call_target="tpu_custom_call" | custom-call | bytes 3145728 | tf_op jit(solution)/shard_map/shard_sum/pallas_call | solution.py:163
  128.5 10.3 %collective-permute-done.17.rest_2_ = f32[2,8,12288]{2,1,0:T(8,128)} collective-permute-done((f32[2,8,12288]{2,1,0:T(8,128)}, f32[2,8,12288]{2,1,0:T(8,128)}, u32[]{:S(2)}, u32[]{:S(2)}) %collective-permute-start.17) | collective-permute-done | bytes 786464 | tf_op jit(solution)/shard_map/ppermute | solution.py:352
  138.8 3.2 %shard_sum.31 = f32[2,8,12288]{2,1,0:T(8,128)} custom-call(s32[6]{0:T(128)} %pad_add_fusion.1.shard_ref, f32[8,2,8,12288]{3,2,1,0:T(8,128)} %get-tuple-element.26.keep_ref, f32[8,8,12288]{2,1,0:T(8,128)} %collective-permute-done.9.rest_0_, f32[8,8,12288]{2,1,0:T(8,128)} %collective-permute-done.10.rest_1_, f32[2,8,12288]{2,1,0:T(8,128)} %collective-permute-done.17.rest_2_), custom_call_target="tpu_custom_call" | custom-call | bytes 3145728 | tf_op jit(solution)/shard_map/shard_sum/pallas_call | solution.py:163
  147.2 5.2 %collective-permute-done.4.rest_2_ = f32[2,8,12288]{2,1,0:T(8,128)} collective-permute-done((f32[2,8,12288]{2,1,0:T(8,128)}, f32[2,8,12288]{2,1,0:T(8,128)}, u32[]{:S(2)}, u32[]{:S(2)}) %collective-permute-start.4) | collective-permute-done | bytes 786464 | tf_op jit(solution)/shard_map/ppermute | solution.py:352
  155.5 3.6 %collective-permute-start.5 = (f32[2,8,12288]{2,1,0:T(8,128)}, f32[2,8,12288]{2,1,0:T(8,128)}, u32[]{:S(2)}, u32[]{:S(2)}) collective-permute-start(f32[2,8,12288]{2,1,0:T(8,128)} %shard_sum.20), channel_id=1, source_target_pairs={{0,8},{2,10},{8,16},{10,18},{16,24},{18,26},{24,28},{26,30},{28,20... | collective-permute-start | bytes 2359304 | tf_op jit(solution)/shard_map/ppermute | solution.py:352
  164.8 6.5 %collective-permute-done.18.refs_5_ = f32[2,8,12288]{2,1,0:T(8,128)} collective-permute-done((f32[2,8,12288]{2,1,0:T(8,128)}, f32[2,8,12288]{2,1,0:T(8,128)}, u32[]{:S(2)}, u32[]{:S(2)}) %collective-permute-start.18) | collective-permute-done | bytes 786464 | tf_op jit(solution)/shard_map/ppermute | solution.py:352
  171.4 14.7 %collective-permute-done.5.refs_1_ = f32[2,8,12288]{2,1,0:T(8,128)} collective-permute-done((f32[2,8,12288]{2,1,0:T(8,128)}, f32[2,8,12288]{2,1,0:T(8,128)}, u32[]{:S(2)}, u32[]{:S(2)}) %collective-permute-start.5) | collective-permute-done | bytes 786464 | tf_op jit(solution)/shard_map/ppermute | solution.py:352
  186.1 9.9 %collective-permute-start.20 = (f32[1,8,24576]{2,1,0:T(8,128)}, f32[1,8,24576]{2,1,0:T(8,128)}, u32[]{:S(2)}, u32[]{:S(2)}) collective-permute-start(f32[1,8,24576]{2,1,0:T(8,128)} %get-tuple-element.32), channel_id=1, source_target_pairs={{0,2},{2,4},{4,6},{6,8},{8,10},{10,12},{12,14},{14,16},{16,18},{18... | collective-permute-start | bytes 2359304 | tf_op jit(solution)/shard_map/ppermute | solution.py:355
  196.0 4.2 %last_sums.1 = (f32[2,8,12288]{2,1,0:T(8,128)}, f32[2,8,12288]{2,1,0:T(8,128)}, f32[8,128]{1,0:T(8,128)}) custom-call(f32[2,8,12288]{2,1,0:T(8,128)} %shard_sum.16.refs_0_, f32[2,8,12288]{2,1,0:T(8,128)} %collective-permute-done.5.refs_1_, f32[2,8,12288]{2,1,0:T(8,128)} %collective-permute-done.8.refs_2_, f32[2,8,12288]{2,1,0:T(8,128)} %shard_sum.24.refs_3_, ...), custom_call_target="tpu_custom_call" | custom-call | bytes 6291456 | tf_op jit(solution)/shard_map/last_sums/pallas_call | solution.py:143
  202.2 4.2 %collective-permute-done.20.rest_8_ = f32[1,8,24576]{2,1,0:T(8,128)} collective-permute-done((f32[1,8,24576]{2,1,0:T(8,128)}, f32[1,8,24576]{2,1,0:T(8,128)}, u32[]{:S(2)}, u32[]{:S(2)}) %collective-permute-start.20) | collective-permute-done | bytes 786464 | tf_op jit(solution)/shard_map/ppermute | solution.py:355
  210.1 3.7 %collective-permute-start.22 = (f32[8,128]{1,0:T(8,128)S(1)}, f32[8,128]{1,0:T(8,128)S(1)}, u32[]{:S(2)}, u32[]{:S(2)}) collective-permute-start(f32[8,128]{1,0:T(8,128)S(1)} %add.55), channel_id=1, source_target_pairs={{0,8},{2,10},{8,0},{10,2},{16,24},{18,26},{24,16},{26,18},{1,9},{3... | collective-permute-start | bytes 12296 | tf_op jit(solution)/shard_map/ppermute | solution.py:270
  216.5 3.7 %collective-permute-start.24 = (f32[8,128]{1,0:T(8,128)S(1)}, f32[8,128]{1,0:T(8,128)S(1)}, u32[]{:S(2)}, u32[]{:S(2)}) collective-permute-start(f32[8,128]{1,0:T(8,128)S(1)} %add.55), channel_id=1, source_target_pairs={{0,24},{2,26},{8,16},{10,18},{16,8},{18,10},{24,0},{26,2},{1,25},{... | collective-permute-start | bytes 12296 | tf_op jit(solution)/shard_map/ppermute | solution.py:270
  220.2 3.6 %collective-permute-done.24 = f32[8,128]{1,0:T(8,128)S(1)} collective-permute-done((f32[8,128]{1,0:T(8,128)S(1)}, f32[8,128]{1,0:T(8,128)S(1)}, u32[]{:S(2)}, u32[]{:S(2)}) %collective-permute-start.24) | collective-permute-done | bytes 4128 | tf_op jit(solution)/shard_map/ppermute | solution.py:270
  230.6 8.9 %update.1 = (f32[2,8,24576]{2,1,0:T(8,128)}, f32[2,8,24576]{2,1,0:T(8,128)}, f32[2,8,24576]{2,1,0:T(8,128)}, f32[2,8,24576]{2,1,0:T(8,128)}, f32[2,8,24576]{2,1,0:T(8,128)}, /*index=5*/f32[2,8,24576]{2,1,0:T(8,128)}) custom-call(f32[2]{0:T(128)} %pad_maximum_fusion.scales_ref, f32[8,128]{1,0:T(8,128)} %broadcast_select_fusion.squares_ref, ...), custom_call_target="tpu_custom_call" | custom-call | bytes 22020096 | tf_op jit(solution)/shard_map/update/pallas_call | solution.py:221
  (69 shorter events, 72.1 us)
Async XLA Ops:
  11.4 17.1 %collective-permute-start.10 = (f32[8,8,12288]{2,1,0:T(8,128)}, f32[8,8,12288]{2,1,0:T(8,128)}, u32[]{:S(2)}, u32[]{:S(2)}) collective-permute-start(f32[8,8,12288]{2,1,0:T(8,128)} %get-tuple-element.28), channel_id=1, source_target_pairs={{0,2},{2,0},{4,6},{6,4},{8,10},{10,8},{12,14},{14,12},{16,18},{18,... | collective-permute-start | bytes 9437192 | tf_op jit(solution)/shard_map/ppermute | solution.py:333
  11.9 16.7 %collective-permute-start.9 = (f32[8,8,12288]{2,1,0:T(8,128)}, f32[8,8,12288]{2,1,0:T(8,128)}, u32[]{:S(2)}, u32[]{:S(2)}) collective-permute-start(f32[8,8,12288]{2,1,0:T(8,128)} %get-tuple-element.27), channel_id=1, source_target_pairs={{0,2},{2,0},{4,6},{6,4},{8,10},{10,8},{12,14},{14,12},{16,18},{18,... | collective-permute-start | bytes 9437192 | tf_op jit(solution)/shard_map/ppermute | solution.py:333
  15.8 57.9 %collective-permute-start.11 = (f32[5,8,24576]{2,1,0:T(8,128)}, f32[5,8,24576]{2,1,0:T(8,128)}, u32[]{:S(2)}, u32[]{:S(2)}) collective-permute-start(f32[5,8,24576]{2,1,0:T(8,128)} %get-tuple-element.29), channel_id=1, source_target_pairs={{0,2},{2,4},{4,6},{6,8},{8,10},{10,12},{12,14},{14,16},{16,18},{18... | collective-permute-start | bytes 11796488 | tf_op jit(solution)/shard_map/ppermute | solution.py:321
  25.3 8.2 %collective-permute-start = (f32[8,8,12288]{2,1,0:T(8,128)}, f32[8,8,12288]{2,1,0:T(8,128)}, u32[]{:S(2)}, u32[]{:S(2)}) collective-permute-start(f32[8,8,12288]{2,1,0:T(8,128)} %get-tuple-element.24), channel_id=1, source_target_pairs={{0,2},{2,0},{4,6},{6,4},{8,10},{10,8},{12,14},{14,12},{16,18},{18,... | collective-permute-start | bytes 9437192 | tf_op jit(solution)/shard_map/ppermute | solution.py:333
  27.9 10.1 %collective-permute-start.1 = (f32[8,8,12288]{2,1,0:T(8,128)}, f32[8,8,12288]{2,1,0:T(8,128)}, u32[]{:S(2)}, u32[]{:S(2)}) collective-permute-start(f32[8,8,12288]{2,1,0:T(8,128)} %get-tuple-element.25), channel_id=1, source_target_pairs={{0,2},{2,0},{4,6},{6,4},{8,10},{10,8},{12,14},{14,12},{16,18},{18,... | collective-permute-start | bytes 9437192 | tf_op jit(solution)/shard_map/ppermute | solution.py:333
  31.4 20.7 %collective-permute-start.15 = (f32[2,8,12288]{2,1,0:T(8,128)}, f32[2,8,12288]{2,1,0:T(8,128)}, u32[]{:S(2)}, u32[]{:S(2)}) collective-permute-start(f32[2,8,12288]{2,1,0:T(8,128)} %shard_sum.28), channel_id=1, source_target_pairs={{0,4},{2,6},{8,0},{10,2},{16,8},{18,10},{24,16},{26,18},{28,24},{3... | collective-permute-start | bytes 2359304 | tf_op jit(solution)/shard_map/ppermute | solution.py:339
  40.9 52.5 %collective-permute-start.2 = (f32[2,8,12288]{2,1,0:T(8,128)}, f32[2,8,12288]{2,1,0:T(8,128)}, u32[]{:S(2)}, u32[]{:S(2)}) collective-permute-start(f32[2,8,12288]{2,1,0:T(8,128)} %shard_sum.17), channel_id=1, source_target_pairs={{0,8},{2,10},{8,16},{10,18},{16,24},{18,26},{24,28},{26,30},{28,20... | collective-permute-start | bytes 2359304 | tf_op jit(solution)/shard_map/ppermute | solution.py:339
  45.9 52.1 %collective-permute-start.6 = (f32[2,8,12288]{2,1,0:T(8,128)}, f32[2,8,12288]{2,1,0:T(8,128)}, u32[]{:S(2)}, u32[]{:S(2)}) collective-permute-start(f32[2,8,12288]{2,1,0:T(8,128)} %shard_sum.21), channel_id=1, source_target_pairs={{0,4},{2,6},{8,0},{10,2},{16,8},{18,10},{24,16},{26,18},{28,24},{3... | collective-permute-start | bytes 2359304 | tf_op jit(solution)/shard_map/ppermute | solution.py:352
  55.2 46.5 %collective-permute-start.16 = (f32[2,8,12288]{2,1,0:T(8,128)}, f32[2,8,12288]{2,1,0:T(8,128)}, u32[]{:S(2)}, u32[]{:S(2)}) collective-permute-start(f32[2,8,12288]{2,1,0:T(8,128)} %shard_sum.29), channel_id=1, source_target_pairs={{0,4},{2,6},{8,0},{10,2},{16,8},{18,10},{24,16},{26,18},{28,24},{3... | collective-permute-start | bytes 2359304 | tf_op jit(solution)/shard_map/ppermute | solution.py:352
  76.6 28.2 %collective-permute-start.12 = (f32[2,8,12288]{2,1,0:T(8,128)}, f32[2,8,12288]{2,1,0:T(8,128)}, u32[]{:S(2)}, u32[]{:S(2)}) collective-permute-start(f32[2,8,12288]{2,1,0:T(8,128)} %shard_sum.25), channel_id=1, source_target_pairs={{0,8},{2,10},{8,16},{10,18},{16,24},{18,26},{24,28},{26,30},{28,20... | collective-permute-start | bytes 2359304 | tf_op jit(solution)/shard_map/ppermute | solution.py:352
  96.5 22.2 %collective-permute-start.3 = (f32[2,8,12288]{2,1,0:T(8,128)}, f32[2,8,12288]{2,1,0:T(8,128)}, u32[]{:S(2)}, u32[]{:S(2)}) collective-permute-start(f32[2,8,12288]{2,1,0:T(8,128)} %shard_sum.18), channel_id=1, source_target_pairs={{0,8},{2,10},{8,16},{10,18},{16,24},{18,26},{24,28},{26,30},{28,20... | collective-permute-start | bytes 2359304 | tf_op jit(solution)/shard_map/ppermute | solution.py:352
  101.2 24.2 %collective-permute-start.7 = (f32[2,8,12288]{2,1,0:T(8,128)}, f32[2,8,12288]{2,1,0:T(8,128)}, u32[]{:S(2)}, u32[]{:S(2)}) collective-permute-start(f32[2,8,12288]{2,1,0:T(8,128)} %shard_sum.22), channel_id=1, source_target_pairs={{0,4},{2,6},{8,0},{10,2},{16,8},{18,10},{24,16},{26,18},{28,24},{3... | collective-permute-start | bytes 2359304 | tf_op jit(solution)/shard_map/ppermute | solution.py:352
  104.8 34.1 %collective-permute-start.17 = (f32[2,8,12288]{2,1,0:T(8,128)}, f32[2,8,12288]{2,1,0:T(8,128)}, u32[]{:S(2)}, u32[]{:S(2)}) collective-permute-start(f32[2,8,12288]{2,1,0:T(8,128)} %shard_sum.30), channel_id=1, source_target_pairs={{0,4},{2,6},{8,0},{10,2},{16,8},{18,10},{24,16},{26,18},{28,24},{3... | collective-permute-start | bytes 2359304 | tf_op jit(solution)/shard_map/ppermute | solution.py:352
  107.9 34.5 %collective-permute-start.13 = (f32[2,8,12288]{2,1,0:T(8,128)}, f32[2,8,12288]{2,1,0:T(8,128)}, u32[]{:S(2)}, u32[]{:S(2)}) collective-permute-start(f32[2,8,12288]{2,1,0:T(8,128)} %shard_sum.26), channel_id=1, source_target_pairs={{0,8},{2,10},{8,16},{10,18},{16,24},{18,26},{24,28},{26,30},{28,20... | collective-permute-start | bytes 2359304 | tf_op jit(solution)/shard_map/ppermute | solution.py:352
  121.8 30.6 %collective-permute-start.4 = (f32[2,8,12288]{2,1,0:T(8,128)}, f32[2,8,12288]{2,1,0:T(8,128)}, u32[]{:S(2)}, u32[]{:S(2)}) collective-permute-start(f32[2,8,12288]{2,1,0:T(8,128)} %shard_sum.19), channel_id=1, source_target_pairs={{0,8},{2,10},{8,16},{10,18},{16,24},{18,26},{24,28},{26,30},{28,20... | collective-permute-start | bytes 2359304 | tf_op jit(solution)/shard_map/ppermute | solution.py:352
  128.5 36.3 %collective-permute-start.8 = (f32[2,8,12288]{2,1,0:T(8,128)}, f32[2,8,12288]{2,1,0:T(8,128)}, u32[]{:S(2)}, u32[]{:S(2)}) collective-permute-start(f32[2,8,12288]{2,1,0:T(8,128)} %shard_sum.23), channel_id=1, source_target_pairs={{0,4},{2,6},{8,0},{10,2},{16,8},{18,10},{24,16},{26,18},{28,24},{3... | collective-permute-start | bytes 2359304 | tf_op jit(solution)/shard_map/ppermute | solution.py:352
  142.0 29.4 %collective-permute-start.18 = (f32[2,8,12288]{2,1,0:T(8,128)}, f32[2,8,12288]{2,1,0:T(8,128)}, u32[]{:S(2)}, u32[]{:S(2)}) collective-permute-start(f32[2,8,12288]{2,1,0:T(8,128)} %shard_sum.31), channel_id=1, source_target_pairs={{0,4},{2,6},{8,0},{10,2},{16,8},{18,10},{24,16},{26,18},{28,24},{3... | collective-permute-start | bytes 2359304 | tf_op jit(solution)/shard_map/ppermute | solution.py:352
  145.6 25.8 %collective-permute-start.14 = (f32[2,8,12288]{2,1,0:T(8,128)}, f32[2,8,12288]{2,1,0:T(8,128)}, u32[]{:S(2)}, u32[]{:S(2)}) collective-permute-start(f32[2,8,12288]{2,1,0:T(8,128)} %shard_sum.27), channel_id=1, source_target_pairs={{0,8},{2,10},{8,16},{10,18},{16,24},{18,26},{24,28},{26,30},{28,20... | collective-permute-start | bytes 2359304 | tf_op jit(solution)/shard_map/ppermute | solution.py:352
  155.5 30.6 %collective-permute-start.5 = (f32[2,8,12288]{2,1,0:T(8,128)}, f32[2,8,12288]{2,1,0:T(8,128)}, u32[]{:S(2)}, u32[]{:S(2)}) collective-permute-start(f32[2,8,12288]{2,1,0:T(8,128)} %shard_sum.20), channel_id=1, source_target_pairs={{0,8},{2,10},{8,16},{10,18},{16,24},{18,26},{24,28},{26,30},{28,20... | collective-permute-start | bytes 2359304 | tf_op jit(solution)/shard_map/ppermute | solution.py:352
  186.1 20.4 %collective-permute-start.20 = (f32[1,8,24576]{2,1,0:T(8,128)}, f32[1,8,24576]{2,1,0:T(8,128)}, u32[]{:S(2)}, u32[]{:S(2)}) collective-permute-start(f32[1,8,24576]{2,1,0:T(8,128)} %get-tuple-element.32), channel_id=1, source_target_pairs={{0,2},{2,4},{4,6},{6,8},{8,10},{10,12},{12,14},{14,16},{16,18},{18... | collective-permute-start | bytes 2359304 | tf_op jit(solution)/shard_map/ppermute | solution.py:355
  207.6 23.0 %collective-permute-start.28 = (f32[2,8,12288]{2,1,0:T(8,128)}, f32[2,8,12288]{2,1,0:T(8,128)}, u32[]{:S(2)}, u32[]{:S(2)}) collective-permute-start(f32[2,8,12288]{2,1,0:T(8,128)} %get-tuple-element.39.rest_10_), channel_id=1, source_target_pairs={{0,2},{2,4},{4,6},{6,8},{8,10},{10,12},{12,14},{14,16},{16,18},{18... | collective-permute-start | bytes 2359304 | tf_op jit(solution)/shard_map/ppermute | solution.py:358
  210.1 20.6 %collective-permute-start.27 = (f32[2,8,12288]{2,1,0:T(8,128)}, f32[2,8,12288]{2,1,0:T(8,128)}, u32[]{:S(2)}, u32[]{:S(2)}) collective-permute-start(f32[2,8,12288]{2,1,0:T(8,128)} %get-tuple-element.38.rest_9_), channel_id=1, source_target_pairs={{0,2},{2,4},{4,6},{6,8},{8,10},{10,12},{12,14},{14,16},{16,18},{18... | collective-permute-start | bytes 2359304 | tf_op jit(solution)/shard_map/ppermute | solution.py:358
  210.1 10.1 %collective-permute-start.22 = (f32[8,128]{1,0:T(8,128)S(1)}, f32[8,128]{1,0:T(8,128)S(1)}, u32[]{:S(2)}, u32[]{:S(2)}) collective-permute-start(f32[8,128]{1,0:T(8,128)S(1)} %add.55), channel_id=1, source_target_pairs={{0,8},{2,10},{8,0},{10,2},{16,24},{18,26},{24,16},{26,18},{1,9},{3... | collective-permute-start | bytes 12296 | tf_op jit(solution)/shard_map/ppermute | solution.py:270
  216.5 7.3 %collective-permute-start.24 = (f32[8,128]{1,0:T(8,128)S(1)}, f32[8,128]{1,0:T(8,128)S(1)}, u32[]{:S(2)}, u32[]{:S(2)}) collective-permute-start(f32[8,128]{1,0:T(8,128)S(1)} %add.55), channel_id=1, source_target_pairs={{0,24},{2,26},{8,16},{10,18},{16,8},{18,10},{24,0},{26,2},{1,25},{... | collective-permute-start | bytes 12296 | tf_op jit(solution)/shard_map/ppermute | solution.py:270
  (5 other events, 17.7 us)

commit v10 on v9

--- a/solution.py
+++ b/solution.py
@@ -333,27 +333,21 @@
         theirs[k] = [lax.ppermute(give, "dp", swap) for give in gives]
     for k in range(streams):
         total = shard_sum(
-            plain_kernel, tables[0], half, keep[k], theirs[k]
+            plain_kernel, tables[0], half, keep[k], theirs[k], after=[old_copy] if k else []
         )
         sent[k] = [None, None]
         sent[k][k % 2] = lax.ppermute(total, "dp", hop(-1 if k % 2 else 1))
-    waiting = [old_copy]
     for away in range(half - 1, 0, -1):
         for k in range(streams):
             for way, by in enumerate((1, -1)):
                 arrived = [] if sent[k][way] is None else [sent[k][way]]
                 body = step_kernel if arrived else plain_kernel
-                after = []
-                if k and not arrived:
-                    after, waiting = waiting, after
-                total = shard_sum(
-                    body, tables[way], away, keep[k], theirs[k], *arrived, after=after
-                )
+                total = shard_sum(body, tables[way], away, keep[k], theirs[k], *arrived)
                 sent[k][way] = lax.ppermute(total, "dp", hop(by))
     ours = [shard_sum(plain_kernel, tables[0], 0, keep[k], theirs[k]) for k in range(streams)]
-    left, *_ = lax.optimization_barrier((left, sent, ours))
+    grads, squares = last_sums(ours, sent)
+    left, squares = lax.optimization_barrier((left, squares))
     old_last = lax.ppermute(left, "dp", onward)
-    grads, squares = last_sums(ours, sent)
     squares, old_last, *waiting = total_of(squares, old_last, grads[1:], grads[:1])
     peer_grads = [lax.ppermute(value, "dp", onward) for value in waiting[1] + waiting[0]]
     bound = float((layers * rows * columns * lax.axis_size("mp")) ** 0.5)

time: 240 us -> 235 us (0.979)
  starting transfers between devices: 62.8 us -> 37.7 us
  waiting for transfers between devices: 86.9 us -> 105 us
    ppermute x12, starting transfers between devices: 32.1 us -> 16.5 us  [local(): sent[k][way] = lax.ppermute(total, 'dp', hop(by))]
    ppermute x1, waiting for transfers between devices: 4.24 us -> 15.5 us  [local(): old_last = lax.ppermute(left, 'dp', onward)]
    ppermute x1, starting transfers between devices: 9.9 us -> 0.01 us  [local(): old_last = lax.ppermute(left, 'dp', onward)]
    ppermute x1, waiting for transfers between devices: 16.9 us -> 24.3 us  [local(): old_copy = lax.ppermute(most, 'dp', onward)]
    ppermute x6, waiting for transfers between devices: 8.77 us -> 11.3 us  [exchanged(): lax.ppermute(value, axis, [(i, i ^ bit) for i in members])]
  transfers between devices with their start and end apart: 29 -> 29, of which waited for: 15 -> 21; matrix products, arithmetic and copies ran while one was open for 1% -> 3% of each run, Pallas kernels for 27% -> 28%
where the time goes in v10:
time: 235 us; the launch traced here: 234 us
  waiting for transfers between devices  105 us (45%)
  Pallas kernels  83.5 us (36%)
  starting transfers between devices  37.7 us (16%)
  other arithmetic  5.34 us (2%)
    pallas_call x16, Pallas kernels, shard_sum(): pl.pallas_call(functools.partial(body, layers), grid_spec=pltpu.PrefetchS...  48.5 us
    ppermute x12, waiting for transfers between devices, local(): sent[k][way] = lax.ppermute(total, 'dp', hop(by))  45.1 us
    ppermute x1, waiting for transfers between devices, local(): old_copy = lax.ppermute(most, 'dp', onward)  24.3 us
    pallas_call x2, Pallas kernels, make_terms(): pl.pallas_call(functools.partial(terms_kernel, order, layers), grid_spec=...  18 us
    ppermute x12, starting transfers between devices, local(): sent[k][way] = lax.ppermute(total, 'dp', hop(by))  16.5 us
    ppermute x1, waiting for transfers between devices, local(): old_last = lax.ppermute(left, 'dp', onward)  15.5 us
    ppermute x6, starting transfers between devices, exchanged(): lax.ppermute(value, axis, [(i, i ^ bit) for i in members])  14.8 us
    ppermute x6, waiting for transfers between devices, exchanged(): lax.ppermute(value, axis, [(i, i ^ bit) for i in members])  11.3 us
  transfers between devices with their start and end apart: 29, of which 21 were waited for; matrix products, arithmetic and copies ran while one was open for 3% of the time, Pallas kernels for 28%

profile of v10, /device:TPU:0, one launch (start us, length us, event | category | flops | bytes accessed | tf_op | source)
XLA Modules:
  0.0 234.2 jit_solution(16789806815910750425)
XLA Ops:
  0.6 3.9 %joined.1 = (f32[5,8,24576]{2,1,0:T(8,128)}, f32[1,8,24576]{2,1,0:T(8,128)}) custom-call(f32[2,8,24576]{2,1,0:T(8,128)} %rest_0_.1, f32[2,8,24576]{2,1,0:T(8,128)} %rest_0_.1, f32[2,8,24576]{2,1,0:T(8,128)} %rest_1_.1, f32[2,8,24576]{2,1,0:T(8,128)} %rest_1_.1, f32[2,8,24576]{2,1,0:T(8,128)} %rest_2_.1, f32[2,8,24576]{2,1,0:T(8,128)} %rest_2_.1), custom_call_target="tpu_custom_call" | custom-call | bytes 9437184 | tf_op jit(solution)/shard_map/joined/pallas_call | solution.py:252
  6.8 9.0 %terms.2 = (f32[8,2,8,12288]{3,2,1,0:T(8,128)}, f32[8,8,12288]{2,1,0:T(8,128)}, f32[8,8,12288]{2,1,0:T(8,128)}) custom-call(s32[1]{0:T(128)} %bitcast.core_ref, bf16[256,256]{1,0:T(8,128)(2,1)} %copy.14.inputs_ref, bf16[1,2,128,24576]{3,2,1,0:T(8,128)(2,1)} %earlier_ref.3, bf16[128,2,24576]{2,1,0:T(2,128)(2,1)} %outgrad_ref.3), custom_call_target="tpu_custom_call" | custom-call | bytes 25165824 | tf_op jit(solution)/shard_map/terms/pallas_call | solution.py:71
  18.4 9.0 %terms.3 = (f32[8,2,8,12288]{3,2,1,0:T(8,128)}, f32[8,8,12288]{2,1,0:T(8,128)}, f32[8,8,12288]{2,1,0:T(8,128)}) custom-call(s32[1]{0:T(128)} %bitcast.core_ref, bf16[256,256]{1,0:T(8,128)(2,1)} %copy.14.inputs_ref, bf16[1,2,128,24576]{3,2,1,0:T(8,128)(2,1)} %earlier_ref.3, bf16[128,2,24576]{2,1,0:T(2,128)(2,1)} %outgrad_ref.3), custom_call_target="tpu_custom_call" | custom-call | bytes 25165824 | tf_op jit(solution)/shard_map/terms/pallas_call | solution.py:71
  33.5 4.5 %collective-permute-done.9.rest_0_ = f32[8,8,12288]{2,1,0:T(8,128)} collective-permute-done((f32[8,8,12288]{2,1,0:T(8,128)}, f32[8,8,12288]{2,1,0:T(8,128)}, u32[]{:S(2)}, u32[]{:S(2)}) %collective-permute-start.9) | collective-permute-done | bytes 3145760 | tf_op jit(solution)/shard_map/ppermute | solution.py:333
  38.0 24.3 %collective-permute-done.14.rest_2_.rest_3_.rest_4_.rest_5_.rest_6_.rest_7_ = f32[5,8,24576]{2,1,0:T(8,128)} collective-permute-done((f32[5,8,24576]{2,1,0:T(8,128)}, f32[5,8,24576]{2,1,0:T(8,128)}, u32[]{:S(2)}, u32[]{:S(2)}) %collective-permute-start.14) | collective-permute-done | bytes 3932192 | tf_op jit(solution)/shard_map/ppermute | solution.py:321
  74.7 3.1 %shard_sum.18 = f32[2,8,12288]{2,1,0:T(8,128)} custom-call(s32[6]{0:T(128)} %pad_add_fusion.shard_ref, f32[8,2,8,12288]{3,2,1,0:T(8,128)} %get-tuple-element.25.keep_ref, f32[8,8,12288]{2,1,0:T(8,128)} %collective-permute-done.rest_0_, f32[8,8,12288]{2,1,0:T(8,128)} %collective-permute-done.1.rest_1_, f32[2,8,12288]{2,1,0:T(8,128)} %collective-permute-done.2.rest_2_), custom_call_target="tpu_custom_call" | custom-call | bytes 3145728 | tf_op jit(solution)/shard_map/shard_sum/pallas_call | solution.py:163
  79.9 3.6 %collective-permute-done.15.rest_2_ = f32[2,8,12288]{2,1,0:T(8,128)} collective-permute-done((f32[2,8,12288]{2,1,0:T(8,128)}, f32[2,8,12288]{2,1,0:T(8,128)}, u32[]{:S(2)}, u32[]{:S(2)}) %collective-permute-start.15) | collective-permute-done | bytes 786464 | tf_op jit(solution)/shard_map/ppermute | solution.py:339
  89.3 3.1 %shard_sum.26 = f32[2,8,12288]{2,1,0:T(8,128)} custom-call(s32[6]{0:T(128)} %pad_add_fusion.shard_ref, f32[8,2,8,12288]{3,2,1,0:T(8,128)} %get-tuple-element.28.keep_ref, f32[8,8,12288]{2,1,0:T(8,128)} %collective-permute-done.9.rest_0_, f32[8,8,12288]{2,1,0:T(8,128)} %collective-permute-done.10.rest_1_, f32[2,8,12288]{2,1,0:T(8,128)} %collective-permute-done.11.rest_2_), custom_call_target="tpu_custom_call" | custom-call | bytes 3145728 | tf_op jit(solution)/shard_map/shard_sum/pallas_call | solution.py:163
  92.5 7.8 %collective-permute-done.6.rest_2_ = f32[2,8,12288]{2,1,0:T(8,128)} collective-permute-done((f32[2,8,12288]{2,1,0:T(8,128)}, f32[2,8,12288]{2,1,0:T(8,128)}, u32[]{:S(2)}, u32[]{:S(2)}) %collective-permute-start.6) | collective-permute-done | bytes 786464 | tf_op jit(solution)/shard_map/ppermute | solution.py:346
  106.2 3.1 %shard_sum.19 = f32[2,8,12288]{2,1,0:T(8,128)} custom-call(s32[6]{0:T(128)} %pad_add_fusion.shard_ref, f32[8,2,8,12288]{3,2,1,0:T(8,128)} %get-tuple-element.25.keep_ref, f32[8,8,12288]{2,1,0:T(8,128)} %collective-permute-done.rest_0_, f32[8,8,12288]{2,1,0:T(8,128)} %collective-permute-done.1.rest_1_, f32[2,8,12288]{2,1,0:T(8,128)} %collective-permute-done.3.rest_2_), custom_call_target="tpu_custom_call" | custom-call | bytes 3145728 | tf_op jit(solution)/shard_map/shard_sum/pallas_call | solution.py:163
  109.3 7.8 %collective-permute-done.16.rest_2_ = f32[2,8,12288]{2,1,0:T(8,128)} collective-permute-done((f32[2,8,12288]{2,1,0:T(8,128)}, f32[2,8,12288]{2,1,0:T(8,128)}, u32[]{:S(2)}, u32[]{:S(2)}) %collective-permute-start.16) | collective-permute-done | bytes 786464 | tf_op jit(solution)/shard_map/ppermute | solution.py:346
  123.0 3.1 %shard_sum.27 = f32[2,8,12288]{2,1,0:T(8,128)} custom-call(s32[6]{0:T(128)} %pad_add_fusion.shard_ref, f32[8,2,8,12288]{3,2,1,0:T(8,128)} %get-tuple-element.28.keep_ref, f32[8,8,12288]{2,1,0:T(8,128)} %collective-permute-done.9.rest_0_, f32[8,8,12288]{2,1,0:T(8,128)} %collective-permute-done.10.rest_1_, f32[2,8,12288]{2,1,0:T(8,128)} %collective-permute-done.12.rest_2_), custom_call_target="tpu_custom_call" | custom-call | bytes 3145728 | tf_op jit(solution)/shard_map/shard_sum/pallas_call | solution.py:163
  126.2 7.8 %collective-permute-done.7.rest_2_ = f32[2,8,12288]{2,1,0:T(8,128)} collective-permute-done((f32[2,8,12288]{2,1,0:T(8,128)}, f32[2,8,12288]{2,1,0:T(8,128)}, u32[]{:S(2)}, u32[]{:S(2)}) %collective-permute-start.7) | collective-permute-done | bytes 786464 | tf_op jit(solution)/shard_map/ppermute | solution.py:346
  143.0 7.8 %collective-permute-done.17.rest_2_ = f32[2,8,12288]{2,1,0:T(8,128)} collective-permute-done((f32[2,8,12288]{2,1,0:T(8,128)}, f32[2,8,12288]{2,1,0:T(8,128)}, u32[]{:S(2)}, u32[]{:S(2)}) %collective-permute-start.17) | collective-permute-done | bytes 786464 | tf_op jit(solution)/shard_map/ppermute | solution.py:346
  150.9 3.2 %shard_sum.31 = f32[2,8,12288]{2,1,0:T(8,128)} custom-call(s32[6]{0:T(128)} %pad_add_fusion.1.shard_ref, f32[8,2,8,12288]{3,2,1,0:T(8,128)} %get-tuple-element.28.keep_ref, f32[8,8,12288]{2,1,0:T(8,128)} %collective-permute-done.9.rest_0_, f32[8,8,12288]{2,1,0:T(8,128)} %collective-permute-done.10.rest_1_, f32[2,8,12288]{2,1,0:T(8,128)} %collective-permute-done.17.rest_2_), custom_call_target="tpu_custom_call" | custom-call | bytes 3145728 | tf_op jit(solution)/shard_map/shard_sum/pallas_call | solution.py:163
  162.2 4.2 %collective-permute-done.8.refs_2_ = f32[2,8,12288]{2,1,0:T(8,128)} collective-permute-done((f32[2,8,12288]{2,1,0:T(8,128)}, f32[2,8,12288]{2,1,0:T(8,128)}, u32[]{:S(2)}, u32[]{:S(2)}) %collective-permute-start.8) | collective-permute-done | bytes 786464 | tf_op jit(solution)/shard_map/ppermute | solution.py:346
  166.5 5.2 %collective-permute-done.5.refs_1_ = f32[2,8,12288]{2,1,0:T(8,128)} collective-permute-done((f32[2,8,12288]{2,1,0:T(8,128)}, f32[2,8,12288]{2,1,0:T(8,128)}, u32[]{:S(2)}, u32[]{:S(2)}) %collective-permute-start.5) | collective-permute-done | bytes 786464 | tf_op jit(solution)/shard_map/ppermute | solution.py:346
  171.7 3.2 %collective-permute-done.18.refs_5_ = f32[2,8,12288]{2,1,0:T(8,128)} collective-permute-done((f32[2,8,12288]{2,1,0:T(8,128)}, f32[2,8,12288]{2,1,0:T(8,128)}, u32[]{:S(2)}, u32[]{:S(2)}) %collective-permute-start.18) | collective-permute-done | bytes 786464 | tf_op jit(solution)/shard_map/ppermute | solution.py:346
  174.9 4.2 %last_sums.1 = (f32[2,8,12288]{2,1,0:T(8,128)}, f32[2,8,12288]{2,1,0:T(8,128)}, f32[8,128]{1,0:T(8,128)}) custom-call(f32[2,8,12288]{2,1,0:T(8,128)} %shard_sum.16.refs_0_, f32[2,8,12288]{2,1,0:T(8,128)} %collective-permute-done.5.refs_1_, f32[2,8,12288]{2,1,0:T(8,128)} %collective-permute-done.8.refs_2_, f32[2,8,12288]{2,1,0:T(8,128)} %shard_sum.24.refs_3_, ...), custom_call_target="tpu_custom_call" | custom-call | bytes 6291456 | tf_op jit(solution)/shard_map/last_sums/pallas_call | solution.py:143
  182.4 15.5 %collective-permute-done.20.rest_8_ = f32[1,8,24576]{2,1,0:T(8,128)} collective-permute-done((f32[1,8,24576]{2,1,0:T(8,128)}, f32[1,8,24576]{2,1,0:T(8,128)}, u32[]{:S(2)}, u32[]{:S(2)}) %collective-permute-start.20) | collective-permute-done | bytes 786464 | tf_op jit(solution)/shard_map/ppermute | solution.py:350
  197.9 3.6 %collective-permute-done.21 = f32[8,128]{1,0:T(8,128)S(1)} collective-permute-done((f32[8,128]{1,0:T(8,128)S(1)}, f32[8,128]{1,0:T(8,128)S(1)}, u32[]{:S(2)}, u32[]{:S(2)}) %collective-permute-start.21) | collective-permute-done | bytes 4128 | tf_op jit(solution)/shard_map/ppermute | solution.py:270
  203.4 7.8 %collective-permute-start.23 = (f32[8,128]{1,0:T(8,128)S(1)}, f32[8,128]{1,0:T(8,128)S(1)}, u32[]{:S(2)}, u32[]{:S(2)}) collective-permute-start(f32[8,128]{1,0:T(8,128)S(1)} %add.55), channel_id=1, source_target_pairs={{0,16},{2,18},{8,24},{10,26},{16,0},{18,2},{24,8},{26,10},{1,17},{... | collective-permute-start | bytes 12296 | tf_op jit(solution)/shard_map/ppermute | solution.py:270
  213.2 5.3 %collective-permute-done.24 = f32[8,128]{1,0:T(8,128)S(1)} collective-permute-done((f32[8,128]{1,0:T(8,128)S(1)}, f32[8,128]{1,0:T(8,128)S(1)}, u32[]{:S(2)}, u32[]{:S(2)}) %collective-permute-start.24) | collective-permute-done | bytes 4128 | tf_op jit(solution)/shard_map/ppermute | solution.py:270
  225.3 8.9 %update.1 = (f32[2,8,24576]{2,1,0:T(8,128)}, f32[2,8,24576]{2,1,0:T(8,128)}, f32[2,8,24576]{2,1,0:T(8,128)}, f32[2,8,24576]{2,1,0:T(8,128)}, f32[2,8,24576]{2,1,0:T(8,128)}, /*index=5*/f32[2,8,24576]{2,1,0:T(8,128)}) custom-call(f32[2]{0:T(128)} %pad_maximum_fusion.scales_ref, f32[8,128]{1,0:T(8,128)} %broadcast_select_fusion.squares_ref, ...), custom_call_target="tpu_custom_call" | custom-call | bytes 22020096 | tf_op jit(solution)/shard_map/update/pallas_call | solution.py:221
  (69 shorter events, 73.5 us)
Async XLA Ops:
  4.6 57.7 %collective-permute-start.14 = (f32[5,8,24576]{2,1,0:T(8,128)}, f32[5,8,24576]{2,1,0:T(8,128)}, u32[]{:S(2)}, u32[]{:S(2)}) collective-permute-start(f32[5,8,24576]{2,1,0:T(8,128)} %get-tuple-element.31), channel_id=1, source_target_pairs={{0,2},{2,4},{4,6},{6,8},{8,10},{10,12},{12,14},{14,16},{16,18},{18... | collective-permute-start | bytes 11796488 | tf_op jit(solution)/shard_map/ppermute | solution.py:321
  15.8 12.7 %collective-permute-start = (f32[8,8,12288]{2,1,0:T(8,128)}, f32[8,8,12288]{2,1,0:T(8,128)}, u32[]{:S(2)}, u32[]{:S(2)}) collective-permute-start(f32[8,8,12288]{2,1,0:T(8,128)} %get-tuple-element.26), channel_id=1, source_target_pairs={{0,2},{2,0},{4,6},{6,4},{8,10},{10,8},{12,14},{14,12},{16,18},{18,... | collective-permute-start | bytes 9437192 | tf_op jit(solution)/shard_map/ppermute | solution.py:333
  18.4 10.1 %collective-permute-start.1 = (f32[8,8,12288]{2,1,0:T(8,128)}, f32[8,8,12288]{2,1,0:T(8,128)}, u32[]{:S(2)}, u32[]{:S(2)}) collective-permute-start(f32[8,8,12288]{2,1,0:T(8,128)} %get-tuple-element.27), channel_id=1, source_target_pairs={{0,2},{2,0},{4,6},{6,4},{8,10},{10,8},{12,14},{14,12},{16,18},{18,... | collective-permute-start | bytes 9437192 | tf_op jit(solution)/shard_map/ppermute | solution.py:333
  27.9 10.1 %collective-permute-start.9 = (f32[8,8,12288]{2,1,0:T(8,128)}, f32[8,8,12288]{2,1,0:T(8,128)}, u32[]{:S(2)}, u32[]{:S(2)}) collective-permute-start(f32[8,8,12288]{2,1,0:T(8,128)} %get-tuple-element.29), channel_id=1, source_target_pairs={{0,2},{2,0},{4,6},{6,4},{8,10},{10,8},{12,14},{14,12},{16,18},{18,... | collective-permute-start | bytes 9437192 | tf_op jit(solution)/shard_map/ppermute | solution.py:333
  31.4 43.3 %collective-permute-start.2 = (f32[2,8,12288]{2,1,0:T(8,128)}, f32[2,8,12288]{2,1,0:T(8,128)}, u32[]{:S(2)}, u32[]{:S(2)}) collective-permute-start(f32[2,8,12288]{2,1,0:T(8,128)} %shard_sum.17), channel_id=1, source_target_pairs={{0,8},{2,10},{8,16},{10,18},{16,24},{18,26},{24,28},{26,30},{28,20... | collective-permute-start | bytes 2359304 | tf_op jit(solution)/shard_map/ppermute | solution.py:339
  65.1 18.3 %collective-permute-start.15 = (f32[2,8,12288]{2,1,0:T(8,128)}, f32[2,8,12288]{2,1,0:T(8,128)}, u32[]{:S(2)}, u32[]{:S(2)}) collective-permute-start(f32[2,8,12288]{2,1,0:T(8,128)} %shard_sum.28), channel_id=1, source_target_pairs={{0,4},{2,6},{8,0},{10,2},{16,8},{18,10},{24,16},{26,18},{28,24},{3... | collective-permute-start | bytes 2359304 | tf_op jit(solution)/shard_map/ppermute | solution.py:339
  68.5 20.8 %collective-permute-start.11 = (f32[2,8,12288]{2,1,0:T(8,128)}, f32[2,8,12288]{2,1,0:T(8,128)}, u32[]{:S(2)}, u32[]{:S(2)}) collective-permute-start(f32[2,8,12288]{2,1,0:T(8,128)} %shard_sum.25), channel_id=1, source_target_pairs={{0,8},{2,10},{8,16},{10,18},{16,24},{18,26},{24,28},{26,30},{28,20... | collective-permute-start | bytes 2359304 | tf_op jit(solution)/shard_map/ppermute | solution.py:346
  74.7 25.6 %collective-permute-start.6 = (f32[2,8,12288]{2,1,0:T(8,128)}, f32[2,8,12288]{2,1,0:T(8,128)}, u32[]{:S(2)}, u32[]{:S(2)}) collective-permute-start(f32[2,8,12288]{2,1,0:T(8,128)} %shard_sum.21), channel_id=1, source_target_pairs={{0,4},{2,6},{8,0},{10,2},{16,8},{18,10},{24,16},{26,18},{28,24},{3... | collective-permute-start | bytes 2359304 | tf_op jit(solution)/shard_map/ppermute | solution.py:346
  77.8 28.4 %collective-permute-start.3 = (f32[2,8,12288]{2,1,0:T(8,128)}, f32[2,8,12288]{2,1,0:T(8,128)}, u32[]{:S(2)}, u32[]{:S(2)}) collective-permute-start(f32[2,8,12288]{2,1,0:T(8,128)} %shard_sum.18), channel_id=1, source_target_pairs={{0,8},{2,10},{8,16},{10,18},{16,24},{18,26},{24,28},{26,30},{28,20... | collective-permute-start | bytes 2359304 | tf_op jit(solution)/shard_map/ppermute | solution.py:346
  86.6 30.6 %collective-permute-start.16 = (f32[2,8,12288]{2,1,0:T(8,128)}, f32[2,8,12288]{2,1,0:T(8,128)}, u32[]{:S(2)}, u32[]{:S(2)}) collective-permute-start(f32[2,8,12288]{2,1,0:T(8,128)} %shard_sum.29), channel_id=1, source_target_pairs={{0,4},{2,6},{8,0},{10,2},{16,8},{18,10},{24,16},{26,18},{28,24},{3... | collective-permute-start | bytes 2359304 | tf_op jit(solution)/shard_map/ppermute | solution.py:346
  92.5 30.6 %collective-permute-start.12 = (f32[2,8,12288]{2,1,0:T(8,128)}, f32[2,8,12288]{2,1,0:T(8,128)}, u32[]{:S(2)}, u32[]{:S(2)}) collective-permute-start(f32[2,8,12288]{2,1,0:T(8,128)} %shard_sum.26), channel_id=1, source_target_pairs={{0,8},{2,10},{8,16},{10,18},{16,24},{18,26},{24,28},{26,30},{28,20... | collective-permute-start | bytes 2359304 | tf_op jit(solution)/shard_map/ppermute | solution.py:346
  103.4 30.6 %collective-permute-start.7 = (f32[2,8,12288]{2,1,0:T(8,128)}, f32[2,8,12288]{2,1,0:T(8,128)}, u32[]{:S(2)}, u32[]{:S(2)}) collective-permute-start(f32[2,8,12288]{2,1,0:T(8,128)} %shard_sum.22), channel_id=1, source_target_pairs={{0,4},{2,6},{8,0},{10,2},{16,8},{18,10},{24,16},{26,18},{28,24},{3... | collective-permute-start | bytes 2359304 | tf_op jit(solution)/shard_map/ppermute | solution.py:346
  109.3 30.6 %collective-permute-start.4 = (f32[2,8,12288]{2,1,0:T(8,128)}, f32[2,8,12288]{2,1,0:T(8,128)}, u32[]{:S(2)}, u32[]{:S(2)}) collective-permute-start(f32[2,8,12288]{2,1,0:T(8,128)} %shard_sum.19), channel_id=1, source_target_pairs={{0,8},{2,10},{8,16},{10,18},{16,24},{18,26},{24,28},{26,30},{28,20... | collective-permute-start | bytes 2359304 | tf_op jit(solution)/shard_map/ppermute | solution.py:346
  120.3 30.6 %collective-permute-start.17 = (f32[2,8,12288]{2,1,0:T(8,128)}, f32[2,8,12288]{2,1,0:T(8,128)}, u32[]{:S(2)}, u32[]{:S(2)}) collective-permute-start(f32[2,8,12288]{2,1,0:T(8,128)} %shard_sum.30), channel_id=1, source_target_pairs={{0,4},{2,6},{8,0},{10,2},{16,8},{18,10},{24,16},{26,18},{28,24},{3... | collective-permute-start | bytes 2359304 | tf_op jit(solution)/shard_map/ppermute | solution.py:346
  126.2 36.1 %collective-permute-start.13 = (f32[2,8,12288]{2,1,0:T(8,128)}, f32[2,8,12288]{2,1,0:T(8,128)}, u32[]{:S(2)}, u32[]{:S(2)}) collective-permute-start(f32[2,8,12288]{2,1,0:T(8,128)} %shard_sum.27), channel_id=1, source_target_pairs={{0,8},{2,10},{8,16},{10,18},{16,24},{18,26},{24,28},{26,30},{28,20... | collective-permute-start | bytes 2359304 | tf_op jit(solution)/shard_map/ppermute | solution.py:346
  137.1 29.3 %collective-permute-start.8 = (f32[2,8,12288]{2,1,0:T(8,128)}, f32[2,8,12288]{2,1,0:T(8,128)}, u32[]{:S(2)}, u32[]{:S(2)}) collective-permute-start(f32[2,8,12288]{2,1,0:T(8,128)} %shard_sum.23), channel_id=1, source_target_pairs={{0,4},{2,6},{8,0},{10,2},{16,8},{18,10},{24,16},{26,18},{28,24},{3... | collective-permute-start | bytes 2359304 | tf_op jit(solution)/shard_map/ppermute | solution.py:346
  143.0 28.6 %collective-permute-start.5 = (f32[2,8,12288]{2,1,0:T(8,128)}, f32[2,8,12288]{2,1,0:T(8,128)}, u32[]{:S(2)}, u32[]{:S(2)}) collective-permute-start(f32[2,8,12288]{2,1,0:T(8,128)} %shard_sum.20), channel_id=1, source_target_pairs={{0,8},{2,10},{8,16},{10,18},{16,24},{18,26},{24,28},{26,30},{28,20... | collective-permute-start | bytes 2359304 | tf_op jit(solution)/shard_map/ppermute | solution.py:346
  154.0 20.9 %collective-permute-start.18 = (f32[2,8,12288]{2,1,0:T(8,128)}, f32[2,8,12288]{2,1,0:T(8,128)}, u32[]{:S(2)}, u32[]{:S(2)}) collective-permute-start(f32[2,8,12288]{2,1,0:T(8,128)} %shard_sum.31), channel_id=1, source_target_pairs={{0,4},{2,6},{8,0},{10,2},{16,8},{18,10},{24,16},{26,18},{28,24},{3... | collective-permute-start | bytes 2359304 | tf_op jit(solution)/shard_map/ppermute | solution.py:346
  179.1 18.8 %collective-permute-start.20 = (f32[1,8,24576]{2,1,0:T(8,128)}, f32[1,8,24576]{2,1,0:T(8,128)}, u32[]{:S(2)}, u32[]{:S(2)}) collective-permute-start(f32[1,8,24576]{2,1,0:T(8,128)} %get-tuple-element.34), channel_id=1, source_target_pairs={{0,2},{2,4},{4,6},{6,8},{8,10},{10,12},{12,14},{14,16},{16,18},{18... | collective-permute-start | bytes 2359304 | tf_op jit(solution)/shard_map/ppermute | solution.py:350
  197.9 27.4 %collective-permute-start.28 = (f32[2,8,12288]{2,1,0:T(8,128)}, f32[2,8,12288]{2,1,0:T(8,128)}, u32[]{:S(2)}, u32[]{:S(2)}) collective-permute-start(f32[2,8,12288]{2,1,0:T(8,128)} %get-tuple-element.41.rest_10_), channel_id=1, source_target_pairs={{0,2},{2,4},{4,6},{6,8},{8,10},{10,12},{12,14},{14,16},{16,18},{18... | collective-permute-start | bytes 2359304 | tf_op jit(solution)/shard_map/ppermute | solution.py:352
  201.5 23.8 %collective-permute-start.27 = (f32[2,8,12288]{2,1,0:T(8,128)}, f32[2,8,12288]{2,1,0:T(8,128)}, u32[]{:S(2)}, u32[]{:S(2)}) collective-permute-start(f32[2,8,12288]{2,1,0:T(8,128)} %get-tuple-element.40.rest_9_), channel_id=1, source_target_pairs={{0,2},{2,4},{4,6},{6,8},{8,10},{10,12},{12,14},{14,16},{16,18},{18... | collective-permute-start | bytes 2359304 | tf_op jit(solution)/shard_map/ppermute | solution.py:352
  201.5 11.6 %collective-permute-start.22 = (f32[8,128]{1,0:T(8,128)S(1)}, f32[8,128]{1,0:T(8,128)S(1)}, u32[]{:S(2)}, u32[]{:S(2)}) collective-permute-start(f32[8,128]{1,0:T(8,128)S(1)} %add.55), channel_id=1, source_target_pairs={{0,8},{2,10},{8,0},{10,2},{16,24},{18,26},{24,16},{26,18},{1,9},{3... | collective-permute-start | bytes 12296 | tf_op jit(solution)/shard_map/ppermute | solution.py:270
  203.4 9.7 %collective-permute-start.23 = (f32[8,128]{1,0:T(8,128)S(1)}, f32[8,128]{1,0:T(8,128)S(1)}, u32[]{:S(2)}, u32[]{:S(2)}) collective-permute-start(f32[8,128]{1,0:T(8,128)S(1)} %add.55), channel_id=1, source_target_pairs={{0,16},{2,18},{8,24},{10,26},{16,0},{18,2},{24,8},{26,10},{1,17},{... | collective-permute-start | bytes 12296 | tf_op jit(solution)/shard_map/ppermute | solution.py:270
  211.2 7.3 %collective-permute-start.24 = (f32[8,128]{1,0:T(8,128)S(1)}, f32[8,128]{1,0:T(8,128)S(1)}, u32[]{:S(2)}, u32[]{:S(2)}) collective-permute-start(f32[8,128]{1,0:T(8,128)S(1)} %add.55), channel_id=1, source_target_pairs={{0,24},{2,26},{8,16},{10,18},{16,8},{18,10},{24,0},{26,2},{1,25},{... | collective-permute-start | bytes 12296 | tf_op jit(solution)/shard_map/ppermute | solution.py:270
  (5 other events, 18.6 us)

commit v11 on v7

--- a/solution.py
+++ b/solution.py
@@ -106,10 +106,9 @@
     out_ref[...] = arrived_ref[...] + both_cores(keep_ref, theirs)
 
 
-def last_kernel(streams, layers, shard_ref, *refs):
+def last_kernel(streams, *refs):
     *refs, squares_ref = refs
     refs, outs = refs[:-streams], refs[-streams:]
-    each = layers + 3
     step = pl.program_id(0)
     per = pl.num_programs(0) // streams
 
@@ -121,41 +120,36 @@
 
         @pl.when(step // per == k)
         def _(k=k):
-            keep_ref, *theirs, up_ref, down_ref = refs[k * each : (k + 1) * each]
-            grad = (up_ref[...] + down_ref[...]) + both_cores(keep_ref, theirs)
+            own_ref, up_ref, down_ref = refs[3 * k : 3 * k + 3]
+            grad = (up_ref[...] + down_ref[...]) + own_ref[...]
             outs[k][...] = grad
-            _, own, columns = grad.shape
+            layers, own, columns = grad.shape
             squares = (grad * grad).reshape(layers, own, columns // lanes, lanes)
             squares_ref[...] += jnp.sum(squares, axis=(0, 2))
 
 
-def last_sums(shards, keep, theirs, sent):
-    streams = len(keep)
-    _, layers, own, width = keep[0].shape
-    size = block_of(width, 6144)
+def last_sums(ours, sent):
+    streams = len(ours)
+    layers, own, width = ours[0].shape
+    size = block_of(width, 12288)
     per = width // size
-    operands, specs, outs = [], [], []
-    for k in range(streams):
-        place = lambda i, k=k: jnp.clip(i - k * per, 0, per - 1)
-        operands += [keep[k], *theirs[k], *sent[k]]
-        specs += [pl.BlockSpec((1, layers, own, size), lambda i, s, at=place: (s[0], 0, 0, at(i)))]
-        specs += [pl.BlockSpec((1, own, size), lambda i, s, at=place: (s[0], 0, at(i)))] * layers
-        outs += [pl.BlockSpec((layers, own, size), lambda i, s, at=place: (0, 0, at(i)))]
-        specs += outs[-1:] * 2
-    summed = jax.ShapeDtypeStruct((layers, own, width), jnp.float32)
+    specs = [
+        pl.BlockSpec(
+            (layers, own, size), lambda i, k=k: (0, 0, jnp.clip(i - k * per, 0, per - 1))
+        )
+        for k in range(streams)
+    ]
+    summed = jax.ShapeDtypeStruct(ours[0].shape, jnp.float32)
     *grads, squares = pl.pallas_call(
-        functools.partial(last_kernel, streams, layers),
-        grid_spec=pltpu.PrefetchScalarGridSpec(
-            num_scalar_prefetch=1,
-            grid=(streams * per,),
-            in_specs=specs,
-            out_specs=outs + [pl.BlockSpec((own, lanes), lambda i, s: (0, 0))],
-        ),
+        functools.partial(last_kernel, streams),
+        grid=(streams * per,),
+        in_specs=[spec for spec in specs for _ in range(3)],
+        out_specs=specs + [pl.BlockSpec((own, lanes), lambda i: (0, 0))],
         out_shape=[summed] * streams + [jax.ShapeDtypeStruct((own, lanes), jnp.float32)],
         compiler_params=room,
-        cost_estimate=cost_of(*[summed] * (5 * streams)),
+        cost_estimate=cost_of(*[summed] * (4 * streams)),
         name="last_sums",
-    )(shards, *operands)
+    )(*[array for k in range(streams) for array in (ours[k], *sent[k])])
     return grads, squares
 
 
@@ -263,9 +257,8 @@
     if peers & (peers - 1) or groups & (groups - 1) or peers < 4:
         return lax.psum(value, ("dp", "mp")), later, last
 
-    def exchanged(value, axis, members, *bits):
-        others = [lax.ppermute(value, axis, [(i, i ^ bit) for i in members]) for bit in bits]
-        return sum(others, value)
+    def exchanged(value, axis, members, bit):
+        return value + lax.ppermute(value, axis, [(i, i ^ bit) for i in members])
 
     value = exchanged(value, "dp", range(peers), 1)
     value, later = lax.optimization_barrier((value, later))
@@ -274,11 +267,8 @@
     first = [i for i in range(peers) if not i & 2]
     bit = 4
     while bit < peers:
-        if 2 * bit < peers:
-            value = exchanged(value, "dp", first, bit, 2 * bit, 3 * bit)
-        else:
-            value = exchanged(value, "dp", first, bit)
-        bit *= 4
+        value = exchanged(value, "dp", first, bit)
+        bit *= 2
     bit = 1
     while bit < groups:
         value = exchanged(value, "mp", range(groups), bit)
@@ -346,7 +336,8 @@
                     body, tables[way], away, keep[k], theirs[k], *arrived, after=after
                 )
                 sent[k][way] = lax.ppermute(total, "dp", hop(by))
-    grads, squares = last_sums(tables[0], keep, theirs, sent)
+    ours = [shard_sum(plain_kernel, tables[0], 0, keep[k], theirs[k]) for k in range(streams)]
+    grads, squares = last_sums(ours, sent)
     squares, *waiting = total_of(squares, grads[1:], grads[:1])
     peer_grads = [lax.ppermute(value, "dp", onward) for value in waiting[1] + waiting[0]]
     bound = float((layers * rows * columns * lax.axis_size("mp")) ** 0.5)

time: 221 us -> 219 us (level)
  starting transfers between devices: 48.3 us -> 42.7 us
  Pallas kernels: 79.7 us -> 83.5 us
    pallas_call x14 -> x16, Pallas kernels: 42.7 us -> 48.5 us  [shard_sum(): pl.pallas_call(functools.partial(body, layers), grid_spec=pltpu.PrefetchS...]
    ppermute x12, waiting for transfers between devices: 49.4 us -> 43.7 us  [local(): sent[k][way] = lax.ppermute(total, 'dp', hop(by))]
    ppermute x6 -> x5, waiting for transfers between devices: 6.46 us -> 12.1 us  [exchanged(): return value + lax.ppermute(value, axis, [(i, i ^ bit) for i in members])]
    ppermute x6 -> x5, starting transfers between devices: 19.6 us -> 14.1 us  [exchanged(): return value + lax.ppermute(value, axis, [(i, i ^ bit) for i in members])]
  transfers between devices with their start and end apart: 28 -> 27, of which waited for: 18 -> 18; matrix products, arithmetic and copies ran while one was open for 2% -> 2% of each run, Pallas kernels for 28% -> 30%
where the time goes in v11:
time: 219 us; the launch traced here: 218 us
  waiting for transfers between devices  85.6 us (39%)
  Pallas kernels  83.5 us (38%)
  starting transfers between devices  42.7 us (19%)
  other arithmetic  4.26 us (2%)
    pallas_call x16, Pallas kernels, shard_sum(): pl.pallas_call(functools.partial(body, layers), grid_spec=pltpu.PrefetchS...  48.5 us
    ppermute x12, waiting for transfers between devices, local(): sent[k][way] = lax.ppermute(total, 'dp', hop(by))  43.7 us
    ppermute x2, waiting for transfers between devices, local(): sent[k][k % 2] = lax.ppermute(total, 'dp', hop(-1 if k % 2 else 1))  23 us
    ppermute x12, starting transfers between devices, local(): sent[k][way] = lax.ppermute(total, 'dp', hop(by))  20.6 us
    pallas_call x2, Pallas kernels, make_terms(): pl.pallas_call(functools.partial(terms_kernel, order, layers), grid_spec=...  17.8 us
    ppermute x5, starting transfers between devices, exchanged(): return value + lax.ppermute(value, axis, [(i, i ^ bit) for i in members])  14.1 us
    ppermute x5, waiting for transfers between devices, exchanged(): return value + lax.ppermute(value, axis, [(i, i ^ bit) for i in members])  12.1 us
    pallas_call x1, Pallas kernels, update(): pl.pallas_call(functools.partial(update_kernel, count, bound), grid=(bloc...  9.05 us
  transfers between devices with their start and end apart: 27, of which 18 were waited for; matrix products, arithmetic and copies ran while one was open for 2% of the time, Pallas kernels for 30%

profile of v11, /device:TPU:0, one launch (start us, length us, event | category | flops | bytes accessed | tf_op | source)
XLA Modules:
  0.0 218.3 jit_solution(2913826092664113459)
XLA Ops:
  0.6 4.0 %joined.1 = f32[6,8,24576]{2,1,0:T(8,128)} custom-call(f32[2,8,24576]{2,1,0:T(8,128)} %rest_0_.1, f32[2,8,24576]{2,1,0:T(8,128)} %rest_1_.1, f32[2,8,24576]{2,1,0:T(8,128)} %rest_2_.1), custom_call_target="tpu_custom_call" | custom-call | bytes 9437184 | tf_op jit(solution)/shard_map/joined/pallas_call | solution.py:243
  6.9 8.9 %terms.3 = (f32[8,2,8,12288]{3,2,1,0:T(8,128)}, f32[8,8,12288]{2,1,0:T(8,128)}, f32[8,8,12288]{2,1,0:T(8,128)}) custom-call(s32[1]{0:T(128)} %bitcast.core_ref, bf16[256,256]{1,0:T(8,128)(2,1)} %copy.14.inputs_ref, bf16[1,2,128,24576]{3,2,1,0:T(8,128)(2,1)} %earlier_ref.3, bf16[128,2,24576]{2,1,0:T(2,128)(2,1)} %outgrad_ref.3), custom_call_target="tpu_custom_call" | custom-call | bytes 25165824 | tf_op jit(solution)/shard_map/terms/pallas_call | solution.py:71
  18.4 8.9 %terms.2 = (f32[8,2,8,12288]{3,2,1,0:T(8,128)}, f32[8,8,12288]{2,1,0:T(8,128)}, f32[8,8,12288]{2,1,0:T(8,128)}) custom-call(s32[1]{0:T(128)} %bitcast.core_ref, bf16[256,256]{1,0:T(8,128)(2,1)} %copy.14.inputs_ref, bf16[1,2,128,24576]{3,2,1,0:T(8,128)(2,1)} %earlier_ref.3, bf16[128,2,24576]{2,1,0:T(2,128)(2,1)} %outgrad_ref.3), custom_call_target="tpu_custom_call" | custom-call | bytes 25165824 | tf_op jit(solution)/shard_map/terms/pallas_call | solution.py:71
  33.5 4.5 %collective-permute-done.1.rest_1_ = f32[8,8,12288]{2,1,0:T(8,128)} collective-permute-done((f32[8,8,12288]{2,1,0:T(8,128)}, f32[8,8,12288]{2,1,0:T(8,128)}, u32[]{:S(2)}, u32[]{:S(2)}) %collective-permute-start.1) | collective-permute-done | bytes 3145760 | tf_op jit(solution)/shard_map/ppermute | solution.py:319
  51.6 3.1 %shard_sum.29 = f32[2,8,12288]{2,1,0:T(8,128)} custom-call(s32[6]{0:T(128)} %pad_add_fusion.1.shard_ref, f32[8,2,8,12288]{3,2,1,0:T(8,128)} %get-tuple-element.22.keep_ref, f32[8,8,12288]{2,1,0:T(8,128)} %collective-permute-done.10.rest_0_, f32[8,8,12288]{2,1,0:T(8,128)} %collective-permute-done.11.rest_1_, f32[2,8,12288]{2,1,0:T(8,128)} %collective-permute-done.15.rest_2_), custom_call_target="tpu_custom_call" | custom-call | bytes 3145728 | tf_op jit(solution)/shard_map/shard_sum/pallas_call | solution.py:163
  56.9 22.2 %collective-permute-done.2.rest_2_ = f32[2,8,12288]{2,1,0:T(8,128)} collective-permute-done((f32[2,8,12288]{2,1,0:T(8,128)}, f32[2,8,12288]{2,1,0:T(8,128)}, u32[]{:S(2)}, u32[]{:S(2)}) %collective-permute-start.2) | collective-permute-done | bytes 786464 | tf_op jit(solution)/shard_map/ppermute | solution.py:325
  79.1 3.1 %shard_sum.18 = f32[2,8,12288]{2,1,0:T(8,128)} custom-call(s32[6]{0:T(128)} %pad_add_fusion.shard_ref, f32[8,2,8,12288]{3,2,1,0:T(8,128)} %get-tuple-element.19.keep_ref, f32[8,8,12288]{2,1,0:T(8,128)} %collective-permute-done.rest_0_, f32[8,8,12288]{2,1,0:T(8,128)} %collective-permute-done.1.rest_1_, f32[2,8,12288]{2,1,0:T(8,128)} %collective-permute-done.2.rest_2_, ...), custom_call_target="tpu_custom_call" | custom-call | bytes 3145728 | tf_op jit(solution)/shard_map/shard_sum/pallas_call | solution.py:163
  82.2 7.8 %collective-permute-start.4 = (f32[2,8,12288]{2,1,0:T(8,128)}, f32[2,8,12288]{2,1,0:T(8,128)}, u32[]{:S(2)}, u32[]{:S(2)}) collective-permute-start(f32[2,8,12288]{2,1,0:T(8,128)} %shard_sum.18), channel_id=1, source_target_pairs={{0,8},{2,10},{8,16},{10,18},{16,24},{18,26},{24,28},{26,30},{28,20... | collective-permute-start | bytes 2359304 | tf_op jit(solution)/shard_map/ppermute | solution.py:338
  90.1 5.8 %collective-permute-done.12.rest_2_ = f32[2,8,12288]{2,1,0:T(8,128)} collective-permute-done((f32[2,8,12288]{2,1,0:T(8,128)}, f32[2,8,12288]{2,1,0:T(8,128)}, u32[]{:S(2)}, u32[]{:S(2)}) %collective-permute-start.12) | collective-permute-done | bytes 786464 | tf_op jit(solution)/shard_map/ppermute | solution.py:338
  95.9 3.1 %shard_sum.26 = f32[2,8,12288]{2,1,0:T(8,128)} custom-call(s32[6]{0:T(128)} %pad_add_fusion.shard_ref, f32[8,2,8,12288]{3,2,1,0:T(8,128)} %get-tuple-element.22.keep_ref, f32[8,8,12288]{2,1,0:T(8,128)} %collective-permute-done.10.rest_0_, f32[8,8,12288]{2,1,0:T(8,128)} %collective-permute-done.11.rest_1_, f32[2,8,12288]{2,1,0:T(8,128)} %collective-permute-done.12.rest_2_), custom_call_target="tpu_custom_call" | custom-call | bytes 3145728 | tf_op jit(solution)/shard_map/shard_sum/pallas_call | solution.py:163
  99.0 3.1 %shard_sum.22 = f32[2,8,12288]{2,1,0:T(8,128)} custom-call(s32[6]{0:T(128)} %pad_add_fusion.1.shard_ref, f32[8,2,8,12288]{3,2,1,0:T(8,128)} %get-tuple-element.19.keep_ref, f32[8,8,12288]{2,1,0:T(8,128)} %collective-permute-done.rest_0_, f32[8,8,12288]{2,1,0:T(8,128)} %collective-permute-done.1.rest_1_, f32[2,8,12288]{2,1,0:T(8,128)} %collective-permute-done.7.rest_2_), custom_call_target="tpu_custom_call" | custom-call | bytes 3145728 | tf_op jit(solution)/shard_map/shard_sum/pallas_call | solution.py:163
  104.2 3.1 %shard_sum.30 = f32[2,8,12288]{2,1,0:T(8,128)} custom-call(s32[6]{0:T(128)} %pad_add_fusion.1.shard_ref, f32[8,2,8,12288]{3,2,1,0:T(8,128)} %get-tuple-element.22.keep_ref, f32[8,8,12288]{2,1,0:T(8,128)} %collective-permute-done.10.rest_0_, f32[8,8,12288]{2,1,0:T(8,128)} %collective-permute-done.11.rest_1_, f32[2,8,12288]{2,1,0:T(8,128)} %collective-permute-done.16.rest_2_), custom_call_target="tpu_custom_call" | custom-call | bytes 3145728 | tf_op jit(solution)/shard_map/shard_sum/pallas_call | solution.py:163
  107.9 3.1 %shard_sum.19 = f32[2,8,12288]{2,1,0:T(8,128)} custom-call(s32[6]{0:T(128)} %pad_add_fusion.shard_ref, f32[8,2,8,12288]{3,2,1,0:T(8,128)} %get-tuple-element.19.keep_ref, f32[8,8,12288]{2,1,0:T(8,128)} %collective-permute-done.rest_0_, f32[8,8,12288]{2,1,0:T(8,128)} %collective-permute-done.1.rest_1_, f32[2,8,12288]{2,1,0:T(8,128)} %collective-permute-done.4.rest_2_), custom_call_target="tpu_custom_call" | custom-call | bytes 3145728 | tf_op jit(solution)/shard_map/shard_sum/pallas_call | solution.py:163
  112.5 8.8 %collective-permute-done.13.rest_2_ = f32[2,8,12288]{2,1,0:T(8,128)} collective-permute-done((f32[2,8,12288]{2,1,0:T(8,128)}, f32[2,8,12288]{2,1,0:T(8,128)}, u32[]{:S(2)}, u32[]{:S(2)}) %collective-permute-start.13) | collective-permute-done | bytes 786464 | tf_op jit(solution)/shard_map/ppermute | solution.py:338
  121.2 3.1 %shard_sum.27 = f32[2,8,12288]{2,1,0:T(8,128)} custom-call(s32[6]{0:T(128)} %pad_add_fusion.shard_ref, f32[8,2,8,12288]{3,2,1,0:T(8,128)} %get-tuple-element.22.keep_ref, f32[8,8,12288]{2,1,0:T(8,128)} %collective-permute-done.10.rest_0_, f32[8,8,12288]{2,1,0:T(8,128)} %collective-permute-done.11.rest_1_, f32[2,8,12288]{2,1,0:T(8,128)} %collective-permute-done.13.rest_2_), custom_call_target="tpu_custom_call" | custom-call | bytes 3145728 | tf_op jit(solution)/shard_map/shard_sum/pallas_call | solution.py:163
  124.4 3.1 %shard_sum.23 = f32[2,8,12288]{2,1,0:T(8,128)} custom-call(s32[6]{0:T(128)} %pad_add_fusion.1.shard_ref, f32[8,2,8,12288]{3,2,1,0:T(8,128)} %get-tuple-element.19.keep_ref, f32[8,8,12288]{2,1,0:T(8,128)} %collective-permute-done.rest_0_, f32[8,8,12288]{2,1,0:T(8,128)} %collective-permute-done.1.rest_1_, f32[2,8,12288]{2,1,0:T(8,128)} %collective-permute-done.8.rest_2_), custom_call_target="tpu_custom_call" | custom-call | bytes 3145728 | tf_op jit(solution)/shard_map/shard_sum/pallas_call | solution.py:163
  129.5 9.8 %collective-permute-done.17.rest_2_ = f32[2,8,12288]{2,1,0:T(8,128)} collective-permute-done((f32[2,8,12288]{2,1,0:T(8,128)}, f32[2,8,12288]{2,1,0:T(8,128)}, u32[]{:S(2)}, u32[]{:S(2)}) %collective-permute-start.17) | collective-permute-done | bytes 786464 | tf_op jit(solution)/shard_map/ppermute | solution.py:338
  144.9 3.1 %shard_sum.20 = f32[2,8,12288]{2,1,0:T(8,128)} custom-call(s32[6]{0:T(128)} %pad_add_fusion.shard_ref, f32[8,2,8,12288]{3,2,1,0:T(8,128)} %get-tuple-element.19.keep_ref, f32[8,8,12288]{2,1,0:T(8,128)} %collective-permute-done.rest_0_, f32[8,8,12288]{2,1,0:T(8,128)} %collective-permute-done.1.rest_1_, f32[2,8,12288]{2,1,0:T(8,128)} %collective-permute-done.5.rest_2_), custom_call_target="tpu_custom_call" | custom-call | bytes 3145728 | tf_op jit(solution)/shard_map/shard_sum/pallas_call | solution.py:163
  156.2 16.9 %collective-permute-done.18.refs_5_ = f32[2,8,12288]{2,1,0:T(8,128)} collective-permute-done((f32[2,8,12288]{2,1,0:T(8,128)}, f32[2,8,12288]{2,1,0:T(8,128)}, u32[]{:S(2)}, u32[]{:S(2)}) %collective-permute-start.18) | collective-permute-done | bytes 786464 | tf_op jit(solution)/shard_map/ppermute | solution.py:338
  173.0 4.2 %last_sums.1 = (f32[2,8,12288]{2,1,0:T(8,128)}, f32[2,8,12288]{2,1,0:T(8,128)}, f32[8,128]{1,0:T(8,128)}) custom-call(f32[2,8,12288]{2,1,0:T(8,128)} %shard_sum.16.refs_0_, f32[2,8,12288]{2,1,0:T(8,128)} %collective-permute-done.6.refs_1_, f32[2,8,12288]{2,1,0:T(8,128)} %collective-permute-done.9.refs_2_, f32[2,8,12288]{2,1,0:T(8,128)} %shard_sum.24.refs_3_, ...), custom_call_target="tpu_custom_call" | custom-call | bytes 6291456 | tf_op jit(solution)/shard_map/last_sums/pallas_call | solution.py:143
  177.2 6.9 %collective-permute-start.19 = (f32[8,128]{1,0:T(8,128)}, f32[8,128]{1,0:T(8,128)S(1)}, u32[]{:S(2)}, u32[]{:S(2)}) collective-permute-start(f32[8,128]{1,0:T(8,128)} %get-tuple-element.25), channel_id=1, source_target_pairs={{0,2},{2,0},{4,6},{6,4},{8,10},{10,8},{12,14},{14,12},{16,18},{18,... | collective-permute-start | bytes 12296 | tf_op jit(solution)/shard_map/ppermute | solution.py:261
  191.4 3.6 %collective-permute-done.21 = f32[8,128]{1,0:T(8,128)S(1)} collective-permute-done((f32[8,128]{1,0:T(8,128)S(1)}, f32[8,128]{1,0:T(8,128)S(1)}, u32[]{:S(2)}, u32[]{:S(2)}) %collective-permute-start.21) | collective-permute-done | bytes 4128 | tf_op jit(solution)/shard_map/ppermute | solution.py:261
  197.7 3.7 %collective-permute-done.22 = f32[8,128]{1,0:T(8,128)S(1)} collective-permute-done((f32[8,128]{1,0:T(8,128)S(1)}, f32[8,128]{1,0:T(8,128)S(1)}, u32[]{:S(2)}, u32[]{:S(2)}) %collective-permute-start.22) | collective-permute-done | bytes 4128 | tf_op jit(solution)/shard_map/ppermute | solution.py:261
  209.3 9.1 %update.1 = (f32[2,8,24576]{2,1,0:T(8,128)}, f32[2,8,24576]{2,1,0:T(8,128)}, f32[2,8,24576]{2,1,0:T(8,128)}, f32[2,8,24576]{2,1,0:T(8,128)}, f32[2,8,24576]{2,1,0:T(8,128)}, /*index=5*/f32[2,8,24576]{2,1,0:T(8,128)}) custom-call(f32[2]{0:T(128)} %pad_maximum_fusion.scales_ref, f32[8,128]{1,0:T(8,128)} %broadcast_select_fusion.squares_ref, ...), custom_call_target="tpu_custom_call" | custom-call | bytes 22020096 | tf_op jit(solution)/shard_map/update/pallas_call | solution.py:215
  (66 shorter events, 63.7 us)
Async XLA Ops:
  4.6 74.4 %collective-permute-start.3 = (f32[6,8,24576]{2,1,0:T(8,128)}, f32[6,8,24576]{2,1,0:T(8,128)}, u32[]{:S(2)}, u32[]{:S(2)}) collective-permute-start(f32[6,8,24576]{2,1,0:T(8,128)} %joined.1), channel_id=1, source_target_pairs={{0,2},{2,4},{4,6},{6,8},{8,10},{10,12},{12,14},{14,16},{16,18},{18... | collective-permute-start | bytes 14155784 | tf_op jit(solution)/shard_map/ppermute | solution.py:307
  15.8 12.7 %collective-permute-start.10 = (f32[8,8,12288]{2,1,0:T(8,128)}, f32[8,8,12288]{2,1,0:T(8,128)}, u32[]{:S(2)}, u32[]{:S(2)}) collective-permute-start(f32[8,8,12288]{2,1,0:T(8,128)} %get-tuple-element.23), channel_id=1, source_target_pairs={{0,2},{2,0},{4,6},{6,4},{8,10},{10,8},{12,14},{14,12},{16,18},{18,... | collective-permute-start | bytes 9437192 | tf_op jit(solution)/shard_map/ppermute | solution.py:319
  18.4 10.1 %collective-permute-start.11 = (f32[8,8,12288]{2,1,0:T(8,128)}, f32[8,8,12288]{2,1,0:T(8,128)}, u32[]{:S(2)}, u32[]{:S(2)}) collective-permute-start(f32[8,8,12288]{2,1,0:T(8,128)} %get-tuple-element.24), channel_id=1, source_target_pairs={{0,2},{2,0},{4,6},{6,4},{8,10},{10,8},{12,14},{14,12},{16,18},{18,... | collective-permute-start | bytes 9437192 | tf_op jit(solution)/shard_map/ppermute | solution.py:319
  27.3 6.1 %collective-permute-start = (f32[8,8,12288]{2,1,0:T(8,128)}, f32[8,8,12288]{2,1,0:T(8,128)}, u32[]{:S(2)}, u32[]{:S(2)}) collective-permute-start(f32[8,8,12288]{2,1,0:T(8,128)} %get-tuple-element.20), channel_id=1, source_target_pairs={{0,2},{2,0},{4,6},{6,4},{8,10},{10,8},{12,14},{14,12},{16,18},{18,... | collective-permute-start | bytes 9437192 | tf_op jit(solution)/shard_map/ppermute | solution.py:319
  27.8 10.1 %collective-permute-start.1 = (f32[8,8,12288]{2,1,0:T(8,128)}, f32[8,8,12288]{2,1,0:T(8,128)}, u32[]{:S(2)}, u32[]{:S(2)}) collective-permute-start(f32[8,8,12288]{2,1,0:T(8,128)} %get-tuple-element.21), channel_id=1, source_target_pairs={{0,2},{2,0},{4,6},{6,4},{8,10},{10,8},{12,14},{14,12},{16,18},{18,... | collective-permute-start | bytes 9437192 | tf_op jit(solution)/shard_map/ppermute | solution.py:319
  31.4 20.2 %collective-permute-start.15 = (f32[2,8,12288]{2,1,0:T(8,128)}, f32[2,8,12288]{2,1,0:T(8,128)}, u32[]{:S(2)}, u32[]{:S(2)}) collective-permute-start(f32[2,8,12288]{2,1,0:T(8,128)} %shard_sum.28), channel_id=1, source_target_pairs={{0,4},{2,6},{8,0},{10,2},{16,8},{18,10},{24,16},{26,18},{28,24},{3... | collective-permute-start | bytes 2359304 | tf_op jit(solution)/shard_map/ppermute | solution.py:325
  40.8 38.3 %collective-permute-start.2 = (f32[2,8,12288]{2,1,0:T(8,128)}, f32[2,8,12288]{2,1,0:T(8,128)}, u32[]{:S(2)}, u32[]{:S(2)}) collective-permute-start(f32[2,8,12288]{2,1,0:T(8,128)} %shard_sum.17), channel_id=1, source_target_pairs={{0,8},{2,10},{8,16},{10,18},{16,24},{18,26},{24,28},{26,30},{28,20... | collective-permute-start | bytes 2359304 | tf_op jit(solution)/shard_map/ppermute | solution.py:325
  46.0 49.9 %collective-permute-start.12 = (f32[2,8,12288]{2,1,0:T(8,128)}, f32[2,8,12288]{2,1,0:T(8,128)}, u32[]{:S(2)}, u32[]{:S(2)}) collective-permute-start(f32[2,8,12288]{2,1,0:T(8,128)} %shard_sum.25), channel_id=1, source_target_pairs={{0,8},{2,10},{8,16},{10,18},{16,24},{18,26},{24,28},{26,30},{28,20... | collective-permute-start | bytes 2359304 | tf_op jit(solution)/shard_map/ppermute | solution.py:338
  50.4 48.6 %collective-permute-start.7 = (f32[2,8,12288]{2,1,0:T(8,128)}, f32[2,8,12288]{2,1,0:T(8,128)}, u32[]{:S(2)}, u32[]{:S(2)}) collective-permute-start(f32[2,8,12288]{2,1,0:T(8,128)} %shard_sum.21), channel_id=1, source_target_pairs={{0,4},{2,6},{8,0},{10,2},{16,8},{18,10},{24,16},{26,18},{28,24},{3... | collective-permute-start | bytes 2359304 | tf_op jit(solution)/shard_map/ppermute | solution.py:338
  54.7 49.4 %collective-permute-start.16 = (f32[2,8,12288]{2,1,0:T(8,128)}, f32[2,8,12288]{2,1,0:T(8,128)}, u32[]{:S(2)}, u32[]{:S(2)}) collective-permute-start(f32[2,8,12288]{2,1,0:T(8,128)} %shard_sum.29), channel_id=1, source_target_pairs={{0,4},{2,6},{8,0},{10,2},{16,8},{18,10},{24,16},{26,18},{28,24},{3... | collective-permute-start | bytes 2359304 | tf_op jit(solution)/shard_map/ppermute | solution.py:338
  82.2 25.6 %collective-permute-start.4 = (f32[2,8,12288]{2,1,0:T(8,128)}, f32[2,8,12288]{2,1,0:T(8,128)}, u32[]{:S(2)}, u32[]{:S(2)}) collective-permute-start(f32[2,8,12288]{2,1,0:T(8,128)} %shard_sum.18), channel_id=1, source_target_pairs={{0,8},{2,10},{8,16},{10,18},{16,24},{18,26},{24,28},{26,30},{28,20... | collective-permute-start | bytes 2359304 | tf_op jit(solution)/shard_map/ppermute | solution.py:338
  99.0 22.2 %collective-permute-start.13 = (f32[2,8,12288]{2,1,0:T(8,128)}, f32[2,8,12288]{2,1,0:T(8,128)}, u32[]{:S(2)}, u32[]{:S(2)}) collective-permute-start(f32[2,8,12288]{2,1,0:T(8,128)} %shard_sum.26), channel_id=1, source_target_pairs={{0,8},{2,10},{8,16},{10,18},{16,24},{18,26},{24,28},{26,30},{28,20... | collective-permute-start | bytes 2359304 | tf_op jit(solution)/shard_map/ppermute | solution.py:338
  102.2 22.2 %collective-permute-start.8 = (f32[2,8,12288]{2,1,0:T(8,128)}, f32[2,8,12288]{2,1,0:T(8,128)}, u32[]{:S(2)}, u32[]{:S(2)}) collective-permute-start(f32[2,8,12288]{2,1,0:T(8,128)} %shard_sum.22), channel_id=1, source_target_pairs={{0,4},{2,6},{8,0},{10,2},{16,8},{18,10},{24,16},{26,18},{28,24},{3... | collective-permute-start | bytes 2359304 | tf_op jit(solution)/shard_map/ppermute | solution.py:338
  107.3 32.0 %collective-permute-start.17 = (f32[2,8,12288]{2,1,0:T(8,128)}, f32[2,8,12288]{2,1,0:T(8,128)}, u32[]{:S(2)}, u32[]{:S(2)}) collective-permute-start(f32[2,8,12288]{2,1,0:T(8,128)} %shard_sum.30), channel_id=1, source_target_pairs={{0,4},{2,6},{8,0},{10,2},{16,8},{18,10},{24,16},{26,18},{28,24},{3... | collective-permute-start | bytes 2359304 | tf_op jit(solution)/shard_map/ppermute | solution.py:338
  111.0 34.0 %collective-permute-start.5 = (f32[2,8,12288]{2,1,0:T(8,128)}, f32[2,8,12288]{2,1,0:T(8,128)}, u32[]{:S(2)}, u32[]{:S(2)}) collective-permute-start(f32[2,8,12288]{2,1,0:T(8,128)} %shard_sum.19), channel_id=1, source_target_pairs={{0,8},{2,10},{8,16},{10,18},{16,24},{18,26},{24,28},{26,30},{28,20... | collective-permute-start | bytes 2359304 | tf_op jit(solution)/shard_map/ppermute | solution.py:338
  124.4 30.6 %collective-permute-start.14 = (f32[2,8,12288]{2,1,0:T(8,128)}, f32[2,8,12288]{2,1,0:T(8,128)}, u32[]{:S(2)}, u32[]{:S(2)}) collective-permute-start(f32[2,8,12288]{2,1,0:T(8,128)} %shard_sum.27), channel_id=1, source_target_pairs={{0,8},{2,10},{8,16},{10,18},{16,24},{18,26},{24,28},{26,30},{28,20... | collective-permute-start | bytes 2359304 | tf_op jit(solution)/shard_map/ppermute | solution.py:338
  127.5 28.7 %collective-permute-start.9 = (f32[2,8,12288]{2,1,0:T(8,128)}, f32[2,8,12288]{2,1,0:T(8,128)}, u32[]{:S(2)}, u32[]{:S(2)}) collective-permute-start(f32[2,8,12288]{2,1,0:T(8,128)} %shard_sum.23), channel_id=1, source_target_pairs={{0,4},{2,6},{8,0},{10,2},{16,8},{18,10},{24,16},{26,18},{28,24},{3... | collective-permute-start | bytes 2359304 | tf_op jit(solution)/shard_map/ppermute | solution.py:338
  142.5 30.6 %collective-permute-start.18 = (f32[2,8,12288]{2,1,0:T(8,128)}, f32[2,8,12288]{2,1,0:T(8,128)}, u32[]{:S(2)}, u32[]{:S(2)}) collective-permute-start(f32[2,8,12288]{2,1,0:T(8,128)} %shard_sum.31), channel_id=1, source_target_pairs={{0,4},{2,6},{8,0},{10,2},{16,8},{18,10},{24,16},{26,18},{28,24},{3... | collective-permute-start | bytes 2359304 | tf_op jit(solution)/shard_map/ppermute | solution.py:338
  148.1 25.0 %collective-permute-start.6 = (f32[2,8,12288]{2,1,0:T(8,128)}, f32[2,8,12288]{2,1,0:T(8,128)}, u32[]{:S(2)}, u32[]{:S(2)}) collective-permute-start(f32[2,8,12288]{2,1,0:T(8,128)} %shard_sum.20), channel_id=1, source_target_pairs={{0,8},{2,10},{8,16},{10,18},{16,24},{18,26},{24,28},{26,30},{28,20... | collective-permute-start | bytes 2359304 | tf_op jit(solution)/shard_map/ppermute | solution.py:338
  177.2 8.0 %collective-permute-start.19 = (f32[8,128]{1,0:T(8,128)}, f32[8,128]{1,0:T(8,128)S(1)}, u32[]{:S(2)}, u32[]{:S(2)}) collective-permute-start(f32[8,128]{1,0:T(8,128)} %get-tuple-element.25), channel_id=1, source_target_pairs={{0,2},{2,0},{4,6},{6,4},{8,10},{10,8},{12,14},{14,12},{16,18},{18,... | collective-permute-start | bytes 12296 | tf_op jit(solution)/shard_map/ppermute | solution.py:261
  186.4 21.7 %collective-permute-start.26 = (f32[2,8,12288]{2,1,0:T(8,128)}, f32[2,8,12288]{2,1,0:T(8,128)}, u32[]{:S(2)}, u32[]{:S(2)}) collective-permute-start(f32[2,8,12288]{2,1,0:T(8,128)} %get-tuple-element.31.rest_7_), channel_id=1, source_target_pairs={{0,2},{2,4},{4,6},{6,8},{8,10},{10,12},{12,14},{14,16},{16,18},{18... | collective-permute-start | bytes 2359304 | tf_op jit(solution)/shard_map/ppermute | solution.py:342
  189.5 19.8 %collective-permute-start.25 = (f32[2,8,12288]{2,1,0:T(8,128)}, f32[2,8,12288]{2,1,0:T(8,128)}, u32[]{:S(2)}, u32[]{:S(2)}) collective-permute-start(f32[2,8,12288]{2,1,0:T(8,128)} %get-tuple-element.30.rest_6_), channel_id=1, source_target_pairs={{0,2},{2,4},{4,6},{6,8},{8,10},{10,12},{12,14},{14,16},{16,18},{18... | collective-permute-start | bytes 2359304 | tf_op jit(solution)/shard_map/ppermute | solution.py:342
  189.5 5.5 %collective-permute-start.21 = (f32[8,128]{1,0:T(8,128)S(1)}, f32[8,128]{1,0:T(8,128)S(1)}, u32[]{:S(2)}, u32[]{:S(2)}) collective-permute-start(f32[8,128]{1,0:T(8,128)S(1)} %add.52), channel_id=1, source_target_pairs={{0,8},{2,10},{8,0},{10,2},{16,24},{18,26},{24,16},{26,18},{1,9},{3... | collective-permute-start | bytes 12296 | tf_op jit(solution)/shard_map/ppermute | solution.py:261
  195.0 6.4 %collective-permute-start.22 = (f32[8,128]{1,0:T(8,128)S(1)}, f32[8,128]{1,0:T(8,128)S(1)}, u32[]{:S(2)}, u32[]{:S(2)}) collective-permute-start(f32[8,128]{1,0:T(8,128)S(1)} %add.53), channel_id=1, source_target_pairs={{0,16},{2,18},{8,24},{10,26},{16,0},{18,2},{24,8},{26,10},{1,17},{... | collective-permute-start | bytes 12296 | tf_op jit(solution)/shard_map/ppermute | solution.py:261
  (3 other events, 9.8 us)

commit v12 on v11

--- a/solution.py
+++ b/solution.py
@@ -44,8 +44,10 @@
     return (weights_new, first_new, second_new)
 
 
-def terms_kernel(order, layers, core_ref, inputs_ref, earlier_ref, outgrad_ref, *rest):
-    keep_ref, gives = rest[-1 - layers], rest[-layers:]
+def terms_kernel(order, layers, held, core_ref, inputs_ref, earlier_ref, outgrad_ref, *rest):
+    keep_ref, *gives = rest[held:]
+    halves = len(gives) // layers
+    here = pl.program_id(0) // (pl.num_programs(0) // halves)
     core = core_ref[0]
     tokens, _, columns = outgrad_ref.shape
     rows = earlier_ref.shape[2]
@@ -58,18 +60,25 @@
         term = term.reshape(chips, 2, rows // (2 * chips), columns)
         for place, chip in enumerate(order):
             keep_ref[place, layer] = jnp.where(core == 0, term[chip, 0], term[chip, 1])
-            gives[layer][place] = jnp.where(core == 0, term[chip, 1], term[chip, 0])
-
-
-def make_terms(core, inputs, earlier, outgrad, order, start, width):
+            given = jnp.where(core == 0, term[chip, 1], term[chip, 0])
+            for index in range(halves):
+
+                @pl.when(here == index)
+                def _(index=index, given=given, layer=layer, place=place):
+                    gives[layer * halves + index][place] = given
+
+
+def make_terms(core, inputs, earlier, outgrad, order, start, width, after):
     _, layers, rows, _ = earlier.shape
     tokens = outgrad.shape[0]
     chips = len(order)
     own = rows // (2 * chips)
-    size = block_of(width, 6144)
+    half = width // 2
+    size = block_of(half, 6144)
+    per = half // size
     first = start // size
     return pl.pallas_call(
-        functools.partial(terms_kernel, order, layers),
+        functools.partial(terms_kernel, order, layers, len(after)),
         grid_spec=pltpu.PrefetchScalarGridSpec(
             num_scalar_prefetch=1,
             grid=(width // size,),
@@ -77,32 +86,48 @@
                 pl.BlockSpec(inputs.shape, lambda i, core: (0, 0)),
                 pl.BlockSpec((1, layers, rows, size), lambda i, core: (0, 0, 0, first + i)),
                 pl.BlockSpec((tokens, layers, size), lambda i, core: (0, 0, first + i)),
-            ],
+            ]
+            + [pl.BlockSpec(memory_space=pl.ANY)] * len(after),
             out_specs=[pl.BlockSpec((chips, layers, own, size), lambda i, core: (0, 0, 0, i))]
-            + [pl.BlockSpec((chips, own, size), lambda i, core: (0, 0, i))] * layers,
+            + [
+                pl.BlockSpec(
+                    (chips, own, size), lambda i, core, h=h: (0, 0, jnp.clip(i - h * per, 0, per - 1))
+                )
+                for h in range(2)
+            ]
+            * layers,
         ),
         out_shape=[jax.ShapeDtypeStruct((chips, layers, own, width), jnp.float32)]
-        + [jax.ShapeDtypeStruct((chips, own, width), jnp.float32)] * layers,
+        + [jax.ShapeDtypeStruct((chips, own, half), jnp.float32)] * (2 * layers),
         compiler_params=room,
         cost_estimate=cost_of(
             jax.ShapeDtypeStruct((layers, rows + tokens, width), earlier.dtype),
             jax.ShapeDtypeStruct((layers, rows, width), jnp.float32),
         ),
         name="terms",
-    )(core, inputs, earlier, outgrad)
+    )(core, inputs, earlier, outgrad, *after)
 
 
 def both_cores(keep_ref, theirs):
-    return jnp.stack([keep_ref[0, layer] + theirs_ref[0] for layer, theirs_ref in enumerate(theirs)])
-
-
-def plain_kernel(layers, shard_ref, keep_ref, *rest):
-    theirs, out_ref = rest[:layers], rest[-1]
+    layers = keep_ref.shape[1]
+    halves = len(theirs) // layers
+    here = pl.program_id(0) // (pl.num_programs(0) // halves)
+    rows = []
+    for layer in range(layers):
+        row = theirs[layer * halves][0]
+        for index in range(1, halves):
+            row = jnp.where(here == index, theirs[layer * halves + index][0], row)
+        rows.append(keep_ref[0, layer] + row)
+    return jnp.stack(rows)
+
+
+def plain_kernel(parts, shard_ref, keep_ref, *rest):
+    theirs, out_ref = rest[:parts], rest[-1]
     out_ref[...] = both_cores(keep_ref, theirs)
 
 
-def step_kernel(layers, shard_ref, keep_ref, *rest):
-    theirs, arrived_ref, out_ref = rest[:layers], rest[layers], rest[-1]
+def step_kernel(parts, shard_ref, keep_ref, *rest):
+    theirs, arrived_ref, out_ref = rest[:parts], rest[parts], rest[-1]
     out_ref[...] = arrived_ref[...] + both_cores(keep_ref, theirs)
 
 
@@ -155,18 +180,26 @@
 
 def shard_sum(body, shards, which, keep, theirs, *arrived, after=()):
     _, layers, own, width = keep.shape
-    size = block_of(width, 6144)
+    half = theirs[0].shape[-1]
+    size = block_of(half, 6144)
+    per, halves = half // size, width // half
     chosen = pl.BlockSpec((1, layers, own, size), lambda i, shards: (shards[which], 0, 0, i))
-    layer = pl.BlockSpec((1, own, size), lambda i, shards: (shards[which], 0, i))
+    pieces = [
+        pl.BlockSpec(
+            (1, own, size),
+            lambda i, shards, h=h: (shards[which], 0, jnp.clip(i - h * per, 0, per - 1)),
+        )
+        for h in range(halves)
+    ]
     whole = pl.BlockSpec((layers, own, size), lambda i, shards: (0, 0, i))
     summed = jax.ShapeDtypeStruct((layers, own, width), jnp.float32)
     return pl.pallas_call(
-        functools.partial(body, layers),
+        functools.partial(body, len(theirs)),
         grid_spec=pltpu.PrefetchScalarGridSpec(
             num_scalar_prefetch=1,
             grid=(width // size,),
             in_specs=[chosen]
-            + [layer] * layers
+            + pieces * layers
             + [whole] * len(arrived)
             + [pl.BlockSpec(memory_space=pl.ANY)] * len(after),
             out_specs=whole,
@@ -201,7 +234,7 @@
                     out_ref[...] = value
 
 
-def update(scales, squares, state, grads, old_copy, peer_grads, bound):
+def update(scales, squares, state, grads, old_params, old_moments, peer_grads, bound):
     layers, own, columns = state[0].shape
     width = grads[0].shape[-1]
     count = len(grads)
@@ -219,15 +252,15 @@
             pl.BlockSpec(memory_space=pltpu.SMEM),
             pl.BlockSpec(squares.shape, lambda i: (0, 0)),
         ]
-        + [part(0, blocks)] * 3
-        + [part(0, blocks, row) for row in range(3)]
+        + [part(0, blocks)] * 4
+        + [part(0, blocks, row) for row in range(2)]
         + [part(k * per, per) for k in range(count)] * 2,
         out_specs=[part(0, blocks)] * 6,
         out_shape=[jax.ShapeDtypeStruct((layers, own, columns), jnp.float32)] * 6,
         compiler_params=room,
         cost_estimate=cost_of(*[state[0]] * 14),
         name="update",
-    )(scales, squares, *state, *[old_copy] * 3, *grads, *peer_grads)
+    )(scales, squares, *state, old_params, *[old_moments] * 2, *grads, *peer_grads)
 
 
 def joined_kernel(*refs):
@@ -304,7 +337,9 @@
     ]
 
     state = (params, first_moment, second_moment)
-    old_copy = lax.ppermute(joined(state), "dp", onward)
+    old_params = lax.ppermute(params, "dp", onward)
+    moments = joined(state[1:])
+    old_moments = lax.ppermute(moments, "dp", onward)
 
     same = jnp.eye(layers, dtype=activations.dtype)
     inputs = activations.transpose(1, 2, 0)[:, :, :, None] * same[:, None, None, :]
@@ -314,7 +349,8 @@
     keep, theirs, sent = ([None] * streams for _ in range(3))
     for k in range(streams):
         keep[k], *gives = make_terms(
-            core.reshape(1), inputs, acc_grads, cotangent, order, k * width, width
+            core.reshape(1), inputs, acc_grads, cotangent, order, k * width, width,
+            [[moments], [old_params], []][min(k, 2)],
         )
         theirs[k] = [lax.ppermute(give, "dp", swap) for give in gives]
     for k in range(streams):
@@ -323,7 +359,7 @@
         )
         sent[k] = [None, None]
         sent[k][k % 2] = lax.ppermute(total, "dp", hop(-1 if k % 2 else 1))
-    waiting = [old_copy]
+    waiting = [old_moments]
     for away in range(half - 1, 0, -1):
         for k in range(streams):
             for way, by in enumerate((1, -1)):
@@ -348,7 +384,7 @@
             1.0 - jnp.power(jnp.float32(beta_two), count),
         ]
     )
-    return tuple(update(scales, squares, state, grads, old_copy, peer_grads, bound))
+    return tuple(update(scales, squares, state, grads, old_params, old_moments, peer_grads, bound))
 
 
 def solution(mesh):

time: 219 us -> 228 us (1.041)
  waiting for transfers between devices: 85.6 us -> 107 us
  starting transfers between devices: 42.7 us -> 25.1 us
  Pallas kernels: 83.5 us -> 88.1 us
    ppermute x12, waiting for transfers between devices: 43.7 us -> 57.9 us  [local(): sent[k][way] = lax.ppermute(total, 'dp', hop(by))]
    ppermute x12, starting transfers between devices: 20.6 us -> 10.2 us  [local(): sent[k][way] = lax.ppermute(total, 'dp', hop(by))]
    ppermute x5, starting transfers between devices: 14.1 us -> 6.69 us  [exchanged(): return value + lax.ppermute(value, axis, [(i, i ^ bit) for i in members])]
    pallas_call x18, Pallas kernels: 66.3 us -> 71.8 us  [the longest x16 49.4 us: shard_sum(): pl.pallas_call(functools.partial(body, len(theirs)), grid_spec=pltpu.Pref...]
    ppermute x1 -> x2, waiting for transfers between devices: 0.01 us -> 4.04 us  [the longest x1 4.04 us: local(): old_params = lax.ppermute(params, 'dp', onward)]
    ppermute x2, waiting for transfers between devices: 23 us -> 25.3 us  [local(): sent[k][k % 2] = lax.ppermute(total, 'dp', hop(-1 if k % 2 else 1))]
    ppermute x4 -> x8, waiting for transfers between devices: 5.07 us -> 5.37 us  [local(): theirs[k] = [lax.ppermute(give, 'dp', swap) for give in gives]]
  transfers between devices with their start and end apart: 27 -> 32, of which waited for: 18 -> 18; matrix products, arithmetic and copies ran while one was open for 2% -> 2% of each run, Pallas kernels for 30% -> 33%
where the time goes in v12:
time: 228 us; the launch traced here: 227 us
  waiting for transfers between devices  107 us (47%)
  Pallas kernels  88.1 us (39%)
  starting transfers between devices  25.1 us (11%)
  other arithmetic  4.28 us (2%)
    ppermute x12, waiting for transfers between devices, local(): sent[k][way] = lax.ppermute(total, 'dp', hop(by))  57.9 us
    pallas_call x16, Pallas kernels, shard_sum(): pl.pallas_call(functools.partial(body, len(theirs)), grid_spec=pltpu.Pref...  49.4 us
    ppermute x2, waiting for transfers between devices, local(): sent[k][k % 2] = lax.ppermute(total, 'dp', hop(-1 if k % 2 else 1))  25.3 us
    pallas_call x2, Pallas kernels, make_terms(): pl.pallas_call(functools.partial(terms_kernel, order, layers, len(after))...  22.3 us
    ppermute x5, waiting for transfers between devices, exchanged(): return value + lax.ppermute(value, axis, [(i, i ^ bit) for i in members])  13 us
    ppermute x12, starting transfers between devices, local(): sent[k][way] = lax.ppermute(total, 'dp', hop(by))  10.2 us
    pallas_call x1, Pallas kernels, update(): pl.pallas_call(functools.partial(update_kernel, count, bound), grid=(bloc...  8.99 us
    ppermute x5, starting transfers between devices, exchanged(): return value + lax.ppermute(value, axis, [(i, i ^ bit) for i in members])  6.69 us
  transfers between devices with their start and end apart: 32, of which 18 were waited for; matrix products, arithmetic and copies ran while one was open for 2% of the time, Pallas kernels for 33%

profile of v12, /device:TPU:0, one launch (start us, length us, event | category | flops | bytes accessed | tf_op | source)
XLA Modules:
  0.0 227.2 jit_solution(2878454119460668760)
XLA Ops:
  3.0 3.2 %joined.1.rest_0_ = f32[4,8,24576]{2,1,0:T(8,128)} custom-call(f32[2,8,24576]{2,1,0:T(8,128)} %rest_1_.1, f32[2,8,24576]{2,1,0:T(8,128)} %rest_2_.1), custom_call_target="tpu_custom_call" | custom-call | bytes 6291456 | tf_op jit(solution)/shard_map/joined/pallas_call | solution.py:276
  6.1 11.2 %terms.2 = (f32[8,2,8,12288]{3,2,1,0:T(8,128)}, f32[8,8,6144]{2,1,0:T(8,128)}, f32[8,8,6144]{2,1,0:T(8,128)}, f32[8,8,6144]{2,1,0:T(8,128)}, f32[8,8,6144]{2,1,0:T(8,128)}) custom-call(s32[1]{0:T(128)} %bitcast.core_ref, bf16[256,256]{1,0:T(8,128)(2,1)} %copy.14.inputs_ref, bf16[1,2,128,24576]{3,2,1,0:T(8,128)(2,1)} %earlier_ref.3, ...), custom_call_target="tpu_custom_call" | custom-call | bytes 25165824 | tf_op jit(solution)/shard_map/terms/pallas_call | solution.py:80
  20.5 4.0 %collective-permute-done.12.rest_0_.rest_3_ = f32[2,8,24576]{2,1,0:T(8,128)} collective-permute-done((f32[2,8,24576]{2,1,0:T(8,128)}, f32[2,8,24576]{2,1,0:T(8,128)}, u32[]{:S(2)}, u32[]{:S(2)}) %collective-permute-start.12) | collective-permute-done | bytes 1572896 | tf_op jit(solution)/shard_map/ppermute | solution.py:340
  24.5 11.2 %terms.3 = (f32[8,2,8,12288]{3,2,1,0:T(8,128)}, f32[8,8,6144]{2,1,0:T(8,128)}, f32[8,8,6144]{2,1,0:T(8,128)}, f32[8,8,6144]{2,1,0:T(8,128)}, f32[8,8,6144]{2,1,0:T(8,128)}) custom-call(s32[1]{0:T(128)} %bitcast.core_ref, bf16[256,256]{1,0:T(8,128)(2,1)} %copy.14.inputs_ref, bf16[1,2,128,24576]{3,2,1,0:T(8,128)(2,1)} %earlier_ref.3, ...), custom_call_target="tpu_custom_call" | custom-call | bytes 25165824 | tf_op jit(solution)/shard_map/terms/pallas_call | solution.py:80
  55.8 25.3 %collective-permute-done.4.rest_4_ = f32[2,8,12288]{2,1,0:T(8,128)} collective-permute-done((f32[2,8,12288]{2,1,0:T(8,128)}, f32[2,8,12288]{2,1,0:T(8,128)}, u32[]{:S(2)}, u32[]{:S(2)}) %collective-permute-start.4) | collective-permute-done | bytes 786464 | tf_op jit(solution)/shard_map/ppermute | solution.py:361
  81.1 3.2 %shard_sum.18 = f32[2,8,12288]{2,1,0:T(8,128)} custom-call(s32[6]{0:T(128)} %pad_add_fusion.shard_ref, f32[8,2,8,12288]{3,2,1,0:T(8,128)} %get-tuple-element.23.keep_ref, f32[8,8,6144]{2,1,0:T(8,128)} %collective-permute-done.rest_0_, f32[8,8,6144]{2,1,0:T(8,128)} %collective-permute-done.1.rest_1_, f32[8,8,6144]{2,1,0:T(8,128)} %collective-permute-done.2.rest_2_, ...), custom_call_target="tpu_custom_call" | custom-call | bytes 3145728 | tf_op jit(solution)/shard_map/shard_sum/pallas_call | solution.py:196
  87.2 3.2 %shard_sum.29 = f32[2,8,12288]{2,1,0:T(8,128)} custom-call(s32[6]{0:T(128)} %pad_add_fusion.1.shard_ref, f32[8,2,8,12288]{3,2,1,0:T(8,128)} %get-tuple-element.28.keep_ref, f32[8,8,6144]{2,1,0:T(8,128)} %collective-permute-done.13.rest_0_, f32[8,8,6144]{2,1,0:T(8,128)} %collective-permute-done.14.rest_1_, f32[8,8,6144]{2,1,0:T(8,128)} %collective-permute-done.15.rest_2_, ...), custom_call_target="tpu_custom_call" | custom-call | bytes 3145728 | tf_op jit(solution)/shard_map/shard_sum/pallas_call | solution.py:196
  92.4 3.2 %shard_sum.22 = f32[2,8,12288]{2,1,0:T(8,128)} custom-call(s32[6]{0:T(128)} %pad_add_fusion.1.shard_ref, f32[8,2,8,12288]{3,2,1,0:T(8,128)} %get-tuple-element.23.keep_ref, f32[8,8,6144]{2,1,0:T(8,128)} %collective-permute-done.rest_0_, f32[8,8,6144]{2,1,0:T(8,128)} %collective-permute-done.1.rest_1_, f32[8,8,6144]{2,1,0:T(8,128)} %collective-permute-done.2.rest_2_, ...), custom_call_target="tpu_custom_call" | custom-call | bytes 3145728 | tf_op jit(solution)/shard_map/shard_sum/pallas_call | solution.py:196
  97.6 7.4 %collective-permute-done.6.rest_4_ = f32[2,8,12288]{2,1,0:T(8,128)} collective-permute-done((f32[2,8,12288]{2,1,0:T(8,128)}, f32[2,8,12288]{2,1,0:T(8,128)}, u32[]{:S(2)}, u32[]{:S(2)}) %collective-permute-start.6) | collective-permute-done | bytes 786464 | tf_op jit(solution)/shard_map/ppermute | solution.py:374
  105.0 3.2 %shard_sum.19 = f32[2,8,12288]{2,1,0:T(8,128)} custom-call(s32[6]{0:T(128)} %pad_add_fusion.shard_ref, f32[8,2,8,12288]{3,2,1,0:T(8,128)} %get-tuple-element.23.keep_ref, f32[8,8,6144]{2,1,0:T(8,128)} %collective-permute-done.rest_0_, f32[8,8,6144]{2,1,0:T(8,128)} %collective-permute-done.1.rest_1_, f32[8,8,6144]{2,1,0:T(8,128)} %collective-permute-done.2.rest_2_, ...), custom_call_target="tpu_custom_call" | custom-call | bytes 3145728 | tf_op jit(solution)/shard_map/shard_sum/pallas_call | solution.py:196
  108.2 13.7 %collective-permute-done.17.rest_4_ = f32[2,8,12288]{2,1,0:T(8,128)} collective-permute-done((f32[2,8,12288]{2,1,0:T(8,128)}, f32[2,8,12288]{2,1,0:T(8,128)}, u32[]{:S(2)}, u32[]{:S(2)}) %collective-permute-start.17) | collective-permute-done | bytes 786464 | tf_op jit(solution)/shard_map/ppermute | solution.py:374
  121.8 3.2 %shard_sum.26 = f32[2,8,12288]{2,1,0:T(8,128)} custom-call(s32[6]{0:T(128)} %pad_add_fusion.shard_ref, f32[8,2,8,12288]{3,2,1,0:T(8,128)} %get-tuple-element.28.keep_ref, f32[8,8,6144]{2,1,0:T(8,128)} %collective-permute-done.13.rest_0_, f32[8,8,6144]{2,1,0:T(8,128)} %collective-permute-done.14.rest_1_, f32[8,8,6144]{2,1,0:T(8,128)} %collective-permute-done.15.rest_2_, ...), custom_call_target="tpu_custom_call" | custom-call | bytes 3145728 | tf_op jit(solution)/shard_map/shard_sum/pallas_call | solution.py:196
  125.0 3.2 %shard_sum.30 = f32[2,8,12288]{2,1,0:T(8,128)} custom-call(s32[6]{0:T(128)} %pad_add_fusion.1.shard_ref, f32[8,2,8,12288]{3,2,1,0:T(8,128)} %get-tuple-element.28.keep_ref, f32[8,8,6144]{2,1,0:T(8,128)} %collective-permute-done.13.rest_0_, f32[8,8,6144]{2,1,0:T(8,128)} %collective-permute-done.14.rest_1_, f32[8,8,6144]{2,1,0:T(8,128)} %collective-permute-done.15.rest_2_, ...), custom_call_target="tpu_custom_call" | custom-call | bytes 3145728 | tf_op jit(solution)/shard_map/shard_sum/pallas_call | solution.py:196
  130.2 3.2 %shard_sum.23 = f32[2,8,12288]{2,1,0:T(8,128)} custom-call(s32[6]{0:T(128)} %pad_add_fusion.1.shard_ref, f32[8,2,8,12288]{3,2,1,0:T(8,128)} %get-tuple-element.23.keep_ref, f32[8,8,6144]{2,1,0:T(8,128)} %collective-permute-done.rest_0_, f32[8,8,6144]{2,1,0:T(8,128)} %collective-permute-done.1.rest_1_, f32[8,8,6144]{2,1,0:T(8,128)} %collective-permute-done.2.rest_2_, ...), custom_call_target="tpu_custom_call" | custom-call | bytes 3145728 | tf_op jit(solution)/shard_map/shard_sum/pallas_call | solution.py:196
  134.0 4.7 %collective-permute-done.7.rest_4_ = f32[2,8,12288]{2,1,0:T(8,128)} collective-permute-done((f32[2,8,12288]{2,1,0:T(8,128)}, f32[2,8,12288]{2,1,0:T(8,128)}, u32[]{:S(2)}, u32[]{:S(2)}) %collective-permute-start.7) | collective-permute-done | bytes 786464 | tf_op jit(solution)/shard_map/ppermute | solution.py:374
  138.7 3.2 %shard_sum.20 = f32[2,8,12288]{2,1,0:T(8,128)} custom-call(s32[6]{0:T(128)} %pad_add_fusion.shard_ref, f32[8,2,8,12288]{3,2,1,0:T(8,128)} %get-tuple-element.23.keep_ref, f32[8,8,6144]{2,1,0:T(8,128)} %collective-permute-done.rest_0_, f32[8,8,6144]{2,1,0:T(8,128)} %collective-permute-done.1.rest_1_, f32[8,8,6144]{2,1,0:T(8,128)} %collective-permute-done.2.rest_2_, ...), custom_call_target="tpu_custom_call" | custom-call | bytes 3145728 | tf_op jit(solution)/shard_map/shard_sum/pallas_call | solution.py:196
  141.9 13.7 %collective-permute-done.18.rest_4_ = f32[2,8,12288]{2,1,0:T(8,128)} collective-permute-done((f32[2,8,12288]{2,1,0:T(8,128)}, f32[2,8,12288]{2,1,0:T(8,128)}, u32[]{:S(2)}, u32[]{:S(2)}) %collective-permute-start.18) | collective-permute-done | bytes 786464 | tf_op jit(solution)/shard_map/ppermute | solution.py:374
  155.5 3.2 %shard_sum.27 = f32[2,8,12288]{2,1,0:T(8,128)} custom-call(s32[6]{0:T(128)} %pad_add_fusion.shard_ref, f32[8,2,8,12288]{3,2,1,0:T(8,128)} %get-tuple-element.28.keep_ref, f32[8,8,6144]{2,1,0:T(8,128)} %collective-permute-done.13.rest_0_, f32[8,8,6144]{2,1,0:T(8,128)} %collective-permute-done.14.rest_1_, f32[8,8,6144]{2,1,0:T(8,128)} %collective-permute-done.15.rest_2_, ...), custom_call_target="tpu_custom_call" | custom-call | bytes 3145728 | tf_op jit(solution)/shard_map/shard_sum/pallas_call | solution.py:196
  158.7 3.2 %shard_sum.31 = f32[2,8,12288]{2,1,0:T(8,128)} custom-call(s32[6]{0:T(128)} %pad_add_fusion.1.shard_ref, f32[8,2,8,12288]{3,2,1,0:T(8,128)} %get-tuple-element.28.keep_ref, f32[8,8,6144]{2,1,0:T(8,128)} %collective-permute-done.13.rest_0_, f32[8,8,6144]{2,1,0:T(8,128)} %collective-permute-done.14.rest_1_, f32[8,8,6144]{2,1,0:T(8,128)} %collective-permute-done.15.rest_2_, ...), custom_call_target="tpu_custom_call" | custom-call | bytes 3145728 | tf_op jit(solution)/shard_map/shard_sum/pallas_call | solution.py:196
  172.4 15.9 %collective-permute-done.19.refs_4_ = f32[2,8,12288]{2,1,0:T(8,128)} collective-permute-done((f32[2,8,12288]{2,1,0:T(8,128)}, f32[2,8,12288]{2,1,0:T(8,128)}, u32[]{:S(2)}, u32[]{:S(2)}) %collective-permute-start.19) | collective-permute-done | bytes 786464 | tf_op jit(solution)/shard_map/ppermute | solution.py:374
  188.3 4.2 %last_sums.1 = (f32[2,8,12288]{2,1,0:T(8,128)}, f32[2,8,12288]{2,1,0:T(8,128)}, f32[8,128]{1,0:T(8,128)}) custom-call(f32[2,8,12288]{2,1,0:T(8,128)} %shard_sum.16.refs_0_, f32[2,8,12288]{2,1,0:T(8,128)} %collective-permute-done.8.refs_1_, f32[2,8,12288]{2,1,0:T(8,128)} %collective-permute-done.11.refs_2_, f32[2,8,12288]{2,1,0:T(8,128)} %shard_sum.24.refs_3_, ...), custom_call_target="tpu_custom_call" | custom-call | bytes 6291456 | tf_op jit(solution)/shard_map/last_sums/pallas_call | solution.py:168
  200.4 3.3 %collective-permute-done.26 = f32[8,128]{1,0:T(8,128)S(1)} collective-permute-done((f32[8,128]{1,0:T(8,128)S(1)}, f32[8,128]{1,0:T(8,128)S(1)}, u32[]{:S(2)}, u32[]{:S(2)}) %collective-permute-start.26) | collective-permute-done | bytes 4128 | tf_op jit(solution)/shard_map/ppermute | solution.py:294
  205.6 4.5 %collective-permute-done.27 = f32[8,128]{1,0:T(8,128)S(1)} collective-permute-done((f32[8,128]{1,0:T(8,128)S(1)}, f32[8,128]{1,0:T(8,128)S(1)}, u32[]{:S(2)}, u32[]{:S(2)}) %collective-permute-start.27) | collective-permute-done | bytes 4128 | tf_op jit(solution)/shard_map/ppermute | solution.py:294
  218.0 9.0 %update.1 = (f32[2,8,24576]{2,1,0:T(8,128)}, f32[2,8,24576]{2,1,0:T(8,128)}, f32[2,8,24576]{2,1,0:T(8,128)}, f32[2,8,24576]{2,1,0:T(8,128)}, f32[2,8,24576]{2,1,0:T(8,128)}, /*index=5*/f32[2,8,24576]{2,1,0:T(8,128)}) custom-call(f32[2]{0:T(128)} %pad_maximum_fusion.scales_ref, f32[8,128]{1,0:T(8,128)} %broadcast_select_fusion.squares_ref, ...), custom_call_target="tpu_custom_call" | custom-call | bytes 22020096 | tf_op jit(solution)/shard_map/update/pallas_call | solution.py:248
  (76 shorter events, 62.6 us)
Async XLA Ops:
  0.6 23.9 %collective-permute-start.12 = (f32[2,8,24576]{2,1,0:T(8,128)}, f32[2,8,24576]{2,1,0:T(8,128)}, u32[]{:S(2)}, u32[]{:S(2)}) collective-permute-start(f32[2,8,24576]{2,1,0:T(8,128)} %rest_0_.1), channel_id=1, source_target_pairs={{0,2},{2,4},{4,6},{6,8},{8,10},{10,12},{12,14},{14,16},{16,18},{18... | collective-permute-start | bytes 4718600 | tf_op jit(solution)/shard_map/ppermute | solution.py:340
  17.3 18.4 %collective-permute-start = (f32[8,8,6144]{2,1,0:T(8,128)}, f32[8,8,6144]{2,1,0:T(8,128)}, u32[]{:S(2)}, u32[]{:S(2)}) collective-permute-start(f32[8,8,6144]{2,1,0:T(8,128)} %get-tuple-element.24), channel_id=1, source_target_pairs={{0,2},{2,0},{4,6},{6,4},{8,10},{10,8},{12,14},{14,12},{16,18},{18,... | collective-permute-start | bytes 4718600 | tf_op jit(solution)/shard_map/ppermute | solution.py:355
  19.9 15.9 %collective-permute-start.1 = (f32[8,8,6144]{2,1,0:T(8,128)}, f32[8,8,6144]{2,1,0:T(8,128)}, u32[]{:S(2)}, u32[]{:S(2)}) collective-permute-start(f32[8,8,6144]{2,1,0:T(8,128)} %get-tuple-element.25), channel_id=1, source_target_pairs={{0,2},{2,0},{4,6},{6,4},{8,10},{10,8},{12,14},{14,12},{16,18},{18,... | collective-permute-start | bytes 4718600 | tf_op jit(solution)/shard_map/ppermute | solution.py:355
  20.0 16.3 %collective-permute-start.2 = (f32[8,8,6144]{2,1,0:T(8,128)}, f32[8,8,6144]{2,1,0:T(8,128)}, u32[]{:S(2)}, u32[]{:S(2)}) collective-permute-start(f32[8,8,6144]{2,1,0:T(8,128)} %get-tuple-element.26), channel_id=1, source_target_pairs={{0,2},{2,0},{4,6},{6,4},{8,10},{10,8},{12,14},{14,12},{16,18},{18,... | collective-permute-start | bytes 4718600 | tf_op jit(solution)/shard_map/ppermute | solution.py:355
  20.4 16.0 %collective-permute-start.3 = (f32[8,8,6144]{2,1,0:T(8,128)}, f32[8,8,6144]{2,1,0:T(8,128)}, u32[]{:S(2)}, u32[]{:S(2)}) collective-permute-start(f32[8,8,6144]{2,1,0:T(8,128)} %get-tuple-element.27), channel_id=1, source_target_pairs={{0,2},{2,0},{4,6},{6,4},{8,10},{10,8},{12,14},{14,12},{16,18},{18,... | collective-permute-start | bytes 4718600 | tf_op jit(solution)/shard_map/ppermute | solution.py:355
  24.5 56.6 %collective-permute-start.5 = (f32[4,8,24576]{2,1,0:T(8,128)}, f32[4,8,24576]{2,1,0:T(8,128)}, u32[]{:S(2)}, u32[]{:S(2)}) collective-permute-start(f32[4,8,24576]{2,1,0:T(8,128)} %joined.1.rest_0_), channel_id=1, source_target_pairs={{0,2},{2,4},{4,6},{6,8},{8,10},{10,12},{12,14},{14,16},{16,18},{18... | collective-permute-start | bytes 9437192 | tf_op jit(solution)/shard_map/ppermute | solution.py:342
  36.3 7.7 %collective-permute-start.15 = (f32[8,8,6144]{2,1,0:T(8,128)}, f32[8,8,6144]{2,1,0:T(8,128)}, u32[]{:S(2)}, u32[]{:S(2)}) collective-permute-start(f32[8,8,6144]{2,1,0:T(8,128)} %get-tuple-element.31), channel_id=1, source_target_pairs={{0,2},{2,0},{4,6},{6,4},{8,10},{10,8},{12,14},{14,12},{16,18},{18,... | collective-permute-start | bytes 4718600 | tf_op jit(solution)/shard_map/ppermute | solution.py:355
  36.4 9.9 %collective-permute-start.16 = (f32[8,8,6144]{2,1,0:T(8,128)}, f32[8,8,6144]{2,1,0:T(8,128)}, u32[]{:S(2)}, u32[]{:S(2)}) collective-permute-start(f32[8,8,6144]{2,1,0:T(8,128)} %get-tuple-element.32), channel_id=1, source_target_pairs={{0,2},{2,0},{4,6},{6,4},{8,10},{10,8},{12,14},{14,12},{16,18},{18,... | collective-permute-start | bytes 4718600 | tf_op jit(solution)/shard_map/ppermute | solution.py:355
  40.4 40.7 %collective-permute-start.4 = (f32[2,8,12288]{2,1,0:T(8,128)}, f32[2,8,12288]{2,1,0:T(8,128)}, u32[]{:S(2)}, u32[]{:S(2)}) collective-permute-start(f32[2,8,12288]{2,1,0:T(8,128)} %shard_sum.17), channel_id=1, source_target_pairs={{0,8},{2,10},{8,16},{10,18},{16,24},{18,26},{24,28},{26,30},{28,20... | collective-permute-start | bytes 2359304 | tf_op jit(solution)/shard_map/ppermute | solution.py:361
  49.2 38.0 %collective-permute-start.20 = (f32[2,8,12288]{2,1,0:T(8,128)}, f32[2,8,12288]{2,1,0:T(8,128)}, u32[]{:S(2)}, u32[]{:S(2)}) collective-permute-start(f32[2,8,12288]{2,1,0:T(8,128)} %shard_sum.28), channel_id=1, source_target_pairs={{0,4},{2,6},{8,0},{10,2},{16,8},{18,10},{24,16},{26,18},{28,24},{3... | collective-permute-start | bytes 2359304 | tf_op jit(solution)/shard_map/ppermute | solution.py:361
  54.2 38.2 %collective-permute-start.9 = (f32[2,8,12288]{2,1,0:T(8,128)}, f32[2,8,12288]{2,1,0:T(8,128)}, u32[]{:S(2)}, u32[]{:S(2)}) collective-permute-start(f32[2,8,12288]{2,1,0:T(8,128)} %shard_sum.21), channel_id=1, source_target_pairs={{0,4},{2,6},{8,0},{10,2},{16,8},{18,10},{24,16},{26,18},{28,24},{3... | collective-permute-start | bytes 2359304 | tf_op jit(solution)/shard_map/ppermute | solution.py:374
  84.3 20.7 %collective-permute-start.6 = (f32[2,8,12288]{2,1,0:T(8,128)}, f32[2,8,12288]{2,1,0:T(8,128)}, u32[]{:S(2)}, u32[]{:S(2)}) collective-permute-start(f32[2,8,12288]{2,1,0:T(8,128)} %shard_sum.18), channel_id=1, source_target_pairs={{0,8},{2,10},{8,16},{10,18},{16,24},{18,26},{24,28},{26,30},{28,20... | collective-permute-start | bytes 2359304 | tf_op jit(solution)/shard_map/ppermute | solution.py:374
  87.2 34.6 %collective-permute-start.17 = (f32[2,8,12288]{2,1,0:T(8,128)}, f32[2,8,12288]{2,1,0:T(8,128)}, u32[]{:S(2)}, u32[]{:S(2)}) collective-permute-start(f32[2,8,12288]{2,1,0:T(8,128)} %shard_sum.25), channel_id=1, source_target_pairs={{0,8},{2,10},{8,16},{10,18},{16,24},{18,26},{24,28},{26,30},{28,20... | collective-permute-start | bytes 2359304 | tf_op jit(solution)/shard_map/ppermute | solution.py:374
  90.4 34.6 %collective-permute-start.21 = (f32[2,8,12288]{2,1,0:T(8,128)}, f32[2,8,12288]{2,1,0:T(8,128)}, u32[]{:S(2)}, u32[]{:S(2)}) collective-permute-start(f32[2,8,12288]{2,1,0:T(8,128)} %shard_sum.29), channel_id=1, source_target_pairs={{0,4},{2,6},{8,0},{10,2},{16,8},{18,10},{24,16},{26,18},{28,24},{3... | collective-permute-start | bytes 2359304 | tf_op jit(solution)/shard_map/ppermute | solution.py:374
  95.6 34.6 %collective-permute-start.10 = (f32[2,8,12288]{2,1,0:T(8,128)}, f32[2,8,12288]{2,1,0:T(8,128)}, u32[]{:S(2)}, u32[]{:S(2)}) collective-permute-start(f32[2,8,12288]{2,1,0:T(8,128)} %shard_sum.22), channel_id=1, source_target_pairs={{0,4},{2,6},{8,0},{10,2},{16,8},{18,10},{24,16},{26,18},{28,24},{3... | collective-permute-start | bytes 2359304 | tf_op jit(solution)/shard_map/ppermute | solution.py:374
  108.2 30.5 %collective-permute-start.7 = (f32[2,8,12288]{2,1,0:T(8,128)}, f32[2,8,12288]{2,1,0:T(8,128)}, u32[]{:S(2)}, u32[]{:S(2)}) collective-permute-start(f32[2,8,12288]{2,1,0:T(8,128)} %shard_sum.19), channel_id=1, source_target_pairs={{0,8},{2,10},{8,16},{10,18},{16,24},{18,26},{24,28},{26,30},{28,20... | collective-permute-start | bytes 2359304 | tf_op jit(solution)/shard_map/ppermute | solution.py:374
  125.0 30.5 %collective-permute-start.18 = (f32[2,8,12288]{2,1,0:T(8,128)}, f32[2,8,12288]{2,1,0:T(8,128)}, u32[]{:S(2)}, u32[]{:S(2)}) collective-permute-start(f32[2,8,12288]{2,1,0:T(8,128)} %shard_sum.26), channel_id=1, source_target_pairs={{0,8},{2,10},{8,16},{10,18},{16,24},{18,26},{24,28},{26,30},{28,20... | collective-permute-start | bytes 2359304 | tf_op jit(solution)/shard_map/ppermute | solution.py:374
  128.2 30.5 %collective-permute-start.22 = (f32[2,8,12288]{2,1,0:T(8,128)}, f32[2,8,12288]{2,1,0:T(8,128)}, u32[]{:S(2)}, u32[]{:S(2)}) collective-permute-start(f32[2,8,12288]{2,1,0:T(8,128)} %shard_sum.30), channel_id=1, source_target_pairs={{0,4},{2,6},{8,0},{10,2},{16,8},{18,10},{24,16},{26,18},{28,24},{3... | collective-permute-start | bytes 2359304 | tf_op jit(solution)/shard_map/ppermute | solution.py:374
  133.4 36.4 %collective-permute-start.11 = (f32[2,8,12288]{2,1,0:T(8,128)}, f32[2,8,12288]{2,1,0:T(8,128)}, u32[]{:S(2)}, u32[]{:S(2)}) collective-permute-start(f32[2,8,12288]{2,1,0:T(8,128)} %shard_sum.23), channel_id=1, source_target_pairs={{0,4},{2,6},{8,0},{10,2},{16,8},{18,10},{24,16},{26,18},{28,24},{3... | collective-permute-start | bytes 2359304 | tf_op jit(solution)/shard_map/ppermute | solution.py:374
  141.9 30.5 %collective-permute-start.8 = (f32[2,8,12288]{2,1,0:T(8,128)}, f32[2,8,12288]{2,1,0:T(8,128)}, u32[]{:S(2)}, u32[]{:S(2)}) collective-permute-start(f32[2,8,12288]{2,1,0:T(8,128)} %shard_sum.20), channel_id=1, source_target_pairs={{0,8},{2,10},{8,16},{10,18},{16,24},{18,26},{24,28},{26,30},{28,20... | collective-permute-start | bytes 2359304 | tf_op jit(solution)/shard_map/ppermute | solution.py:374
  158.7 29.6 %collective-permute-start.19 = (f32[2,8,12288]{2,1,0:T(8,128)}, f32[2,8,12288]{2,1,0:T(8,128)}, u32[]{:S(2)}, u32[]{:S(2)}) collective-permute-start(f32[2,8,12288]{2,1,0:T(8,128)} %shard_sum.27), channel_id=1, source_target_pairs={{0,8},{2,10},{8,16},{10,18},{16,24},{18,26},{24,28},{26,30},{28,20... | collective-permute-start | bytes 2359304 | tf_op jit(solution)/shard_map/ppermute | solution.py:374
  161.9 26.4 %collective-permute-start.23 = (f32[2,8,12288]{2,1,0:T(8,128)}, f32[2,8,12288]{2,1,0:T(8,128)}, u32[]{:S(2)}, u32[]{:S(2)}) collective-permute-start(f32[2,8,12288]{2,1,0:T(8,128)} %shard_sum.31), channel_id=1, source_target_pairs={{0,4},{2,6},{8,0},{10,2},{16,8},{18,10},{24,16},{26,18},{28,24},{3... | collective-permute-start | bytes 2359304 | tf_op jit(solution)/shard_map/ppermute | solution.py:374
  195.2 21.7 %collective-permute-start.31 = (f32[2,8,12288]{2,1,0:T(8,128)}, f32[2,8,12288]{2,1,0:T(8,128)}, u32[]{:S(2)}, u32[]{:S(2)}) collective-permute-start(f32[2,8,12288]{2,1,0:T(8,128)} %get-tuple-element.39.rest_7_), channel_id=1, source_target_pairs={{0,2},{2,4},{4,6},{6,8},{8,10},{10,12},{12,14},{14,16},{16,18},{18... | collective-permute-start | bytes 2359304 | tf_op jit(solution)/shard_map/ppermute | solution.py:378
  198.2 19.8 %collective-permute-start.30 = (f32[2,8,12288]{2,1,0:T(8,128)}, f32[2,8,12288]{2,1,0:T(8,128)}, u32[]{:S(2)}, u32[]{:S(2)}) collective-permute-start(f32[2,8,12288]{2,1,0:T(8,128)} %get-tuple-element.38.rest_6_), channel_id=1, source_target_pairs={{0,2},{2,4},{4,6},{6,8},{8,10},{10,12},{12,14},{14,16},{16,18},{18... | collective-permute-start | bytes 2359304 | tf_op jit(solution)/shard_map/ppermute | solution.py:378
  (8 other events, 33.7 us)

commit v13 on v11

--- a/solution.py
+++ b/solution.py
@@ -178,12 +178,13 @@
     )(shards, keep, *theirs, *arrived, *after)
 
 
-def update_kernel(count, bound, scales_ref, squares_ref, *rest):
+def update_kernel(count, bound, scales_ref, squares_ref, passed_ref, *rest):
     states, grads, outs = (rest[:3], rest[3:6]), rest[6 : 6 + 2 * count], rest[6 + 2 * count :]
     step = pl.program_id(0)
     per = pl.num_programs(0) // count
+    squares = jnp.where(scales_ref[2] == 0.0, squares_ref[...], passed_ref[...])
     factor = jnp.minimum(
-        jnp.float32(1.0), bound / (jnp.sqrt(jnp.sum(squares_ref[...])) + jnp.float32(1e-06))
+        jnp.float32(1.0), bound / (jnp.sqrt(jnp.sum(squares)) + jnp.float32(1e-06))
     )
     for index in range(count):
 
@@ -217,8 +218,8 @@
         grid=(blocks,),
         in_specs=[
             pl.BlockSpec(memory_space=pltpu.SMEM),
-            pl.BlockSpec(squares.shape, lambda i: (0, 0)),
         ]
+        + [pl.BlockSpec(squares[0].shape, lambda i: (0, 0))] * 2
         + [part(0, blocks)] * 3
         + [part(0, blocks, row) for row in range(3)]
         + [part(k * per, per) for k in range(count)] * 2,
@@ -227,7 +228,7 @@
         compiler_params=room,
         cost_estimate=cost_of(*[state[0]] * 14),
         name="update",
-    )(scales, squares, *state, *[old_copy] * 3, *grads, *peer_grads)
+    )(scales, *squares, *state, *[old_copy] * 3, *grads, *peer_grads)
 
 
 def joined_kernel(*refs):
@@ -255,7 +256,8 @@
 def total_of(value, later, last):
     peers, groups = lax.axis_size("dp"), lax.axis_size("mp")
     if peers & (peers - 1) or groups & (groups - 1) or peers < 4:
-        return lax.psum(value, ("dp", "mp")), later, last
+        total = lax.psum(value, ("dp", "mp"))
+        return (total, total), later, last
 
     def exchanged(value, axis, members, bit):
         return value + lax.ppermute(value, axis, [(i, i ^ bit) for i in members])
@@ -274,7 +276,7 @@
         value = exchanged(value, "mp", range(groups), bit)
         bit *= 2
     passed = lax.ppermute(value, "dp", [(i, i | 2) for i in first])
-    return jnp.where(lax.axis_index("dp") & 2 == 0, value, passed), later, last
+    return (value, passed), later, last
 
 
 def local(acc_grads, activations, cotangent, params, first_moment, second_moment, step):
@@ -346,6 +348,7 @@
         [
             1.0 - jnp.power(jnp.float32(beta_one), count),
             1.0 - jnp.power(jnp.float32(beta_two), count),
+            (chip % 2).astype(jnp.float32).reshape(1),
         ]
     )
     return tuple(update(scales, squares, state, grads, old_copy, peer_grads, bound))

time: 219 us -> 219 us (level)
  transfers between devices with their start and end apart: 27 -> 27, of which waited for: 18 -> 17; matrix products, arithmetic and copies ran while one was open for 2% -> 2% of each run, Pallas kernels for 30% -> 30%
where the time goes in v13:
time: 219 us; the launch traced here: 218 us
  waiting for transfers between devices  85 us (39%)
  Pallas kernels  83.5 us (38%)
  starting transfers between devices  42.6 us (19%)
  other arithmetic  3.67 us (2%)
    pallas_call x16, Pallas kernels, shard_sum(): pl.pallas_call(functools.partial(body, layers), grid_spec=pltpu.PrefetchS...  48.5 us
    ppermute x12, waiting for transfers between devices, local(): sent[k][way] = lax.ppermute(total, 'dp', hop(by))  43.7 us
    ppermute x2, waiting for transfers between devices, local(): sent[k][k % 2] = lax.ppermute(total, 'dp', hop(-1 if k % 2 else 1))  23 us
    ppermute x12, starting transfers between devices, local(): sent[k][way] = lax.ppermute(total, 'dp', hop(by))  20.5 us
    pallas_call x2, Pallas kernels, make_terms(): pl.pallas_call(functools.partial(terms_kernel, order, layers), grid_spec=...  17.9 us
    ppermute x5, starting transfers between devices, exchanged(): return value + lax.ppermute(value, axis, [(i, i ^ bit) for i in members])  14.1 us
    ppermute x5, waiting for transfers between devices, exchanged(): return value + lax.ppermute(value, axis, [(i, i ^ bit) for i in members])  12.1 us
    pallas_call x1, Pallas kernels, update(): pl.pallas_call(functools.partial(update_kernel, count, bound), grid=(bloc...  9 us
  transfers between devices with their start and end apart: 27, of which 17 were waited for; matrix products, arithmetic and copies ran while one was open for 2% of the time, Pallas kernels for 30%

profile of v13, /device:TPU:0, one launch (start us, length us, event | category | flops | bytes accessed | tf_op | source)
XLA Modules:
  0.0 218.3 jit_solution(519757780518425599)
XLA Ops:
  0.6 4.0 %joined.1 = f32[6,8,24576]{2,1,0:T(8,128)} custom-call(f32[2,8,24576]{2,1,0:T(8,128)} %rest_0_.1, f32[2,8,24576]{2,1,0:T(8,128)} %rest_1_.1, f32[2,8,24576]{2,1,0:T(8,128)} %rest_2_.1), custom_call_target="tpu_custom_call" | custom-call | bytes 9437184 | tf_op jit(solution)/shard_map/joined/pallas_call | solution.py:244
  6.9 8.9 %terms.3 = (f32[8,2,8,12288]{3,2,1,0:T(8,128)}, f32[8,8,12288]{2,1,0:T(8,128)}, f32[8,8,12288]{2,1,0:T(8,128)}) custom-call(s32[1]{0:T(128)} %bitcast.1.core_ref, bf16[256,256]{1,0:T(8,128)(2,1)} %copy.14.inputs_ref, bf16[1,2,128,24576]{3,2,1,0:T(8,128)(2,1)} %earlier_ref.3, bf16[128,2,24576]{2,1,0:T(2,128)(2,1)} %outgrad_ref.3), custom_call_target="tpu_custom_call" | custom-call | bytes 25165824 | tf_op jit(solution)/shard_map/terms/pallas_call | solution.py:71
  18.4 9.0 %terms.2 = (f32[8,2,8,12288]{3,2,1,0:T(8,128)}, f32[8,8,12288]{2,1,0:T(8,128)}, f32[8,8,12288]{2,1,0:T(8,128)}) custom-call(s32[1]{0:T(128)} %bitcast.1.core_ref, bf16[256,256]{1,0:T(8,128)(2,1)} %copy.14.inputs_ref, bf16[1,2,128,24576]{3,2,1,0:T(8,128)(2,1)} %earlier_ref.3, bf16[128,2,24576]{2,1,0:T(2,128)(2,1)} %outgrad_ref.3), custom_call_target="tpu_custom_call" | custom-call | bytes 25165824 | tf_op jit(solution)/shard_map/terms/pallas_call | solution.py:71
  33.5 4.5 %collective-permute-done.1.rest_1_ = f32[8,8,12288]{2,1,0:T(8,128)} collective-permute-done((f32[8,8,12288]{2,1,0:T(8,128)}, f32[8,8,12288]{2,1,0:T(8,128)}, u32[]{:S(2)}, u32[]{:S(2)}) %collective-permute-start.1) | collective-permute-done | bytes 3145760 | tf_op jit(solution)/shard_map/ppermute | solution.py:321
  51.7 3.1 %shard_sum.29 = f32[2,8,12288]{2,1,0:T(8,128)} custom-call(s32[6]{0:T(128)} %pad_add_fusion.1.shard_ref, f32[8,2,8,12288]{3,2,1,0:T(8,128)} %get-tuple-element.22.keep_ref, f32[8,8,12288]{2,1,0:T(8,128)} %collective-permute-done.10.rest_0_, f32[8,8,12288]{2,1,0:T(8,128)} %collective-permute-done.11.rest_1_, f32[2,8,12288]{2,1,0:T(8,128)} %collective-permute-done.15.rest_2_), custom_call_target="tpu_custom_call" | custom-call | bytes 3145728 | tf_op jit(solution)/shard_map/shard_sum/pallas_call | solution.py:163
  56.9 22.1 %collective-permute-done.2.rest_2_ = f32[2,8,12288]{2,1,0:T(8,128)} collective-permute-done((f32[2,8,12288]{2,1,0:T(8,128)}, f32[2,8,12288]{2,1,0:T(8,128)}, u32[]{:S(2)}, u32[]{:S(2)}) %collective-permute-start.2) | collective-permute-done | bytes 786464 | tf_op jit(solution)/shard_map/ppermute | solution.py:327
  79.1 3.1 %shard_sum.18 = f32[2,8,12288]{2,1,0:T(8,128)} custom-call(s32[6]{0:T(128)} %pad_add_fusion.shard_ref, f32[8,2,8,12288]{3,2,1,0:T(8,128)} %get-tuple-element.19.keep_ref, f32[8,8,12288]{2,1,0:T(8,128)} %collective-permute-done.rest_0_, f32[8,8,12288]{2,1,0:T(8,128)} %collective-permute-done.1.rest_1_, f32[2,8,12288]{2,1,0:T(8,128)} %collective-permute-done.2.rest_2_, ...), custom_call_target="tpu_custom_call" | custom-call | bytes 3145728 | tf_op jit(solution)/shard_map/shard_sum/pallas_call | solution.py:163
  82.2 7.8 %collective-permute-start.4 = (f32[2,8,12288]{2,1,0:T(8,128)}, f32[2,8,12288]{2,1,0:T(8,128)}, u32[]{:S(2)}, u32[]{:S(2)}) collective-permute-start(f32[2,8,12288]{2,1,0:T(8,128)} %shard_sum.18), channel_id=1, source_target_pairs={{0,8},{2,10},{8,16},{10,18},{16,24},{18,26},{24,28},{26,30},{28,20... | collective-permute-start | bytes 2359304 | tf_op jit(solution)/shard_map/ppermute | solution.py:340
  90.0 5.9 %collective-permute-done.12.rest_2_ = f32[2,8,12288]{2,1,0:T(8,128)} collective-permute-done((f32[2,8,12288]{2,1,0:T(8,128)}, f32[2,8,12288]{2,1,0:T(8,128)}, u32[]{:S(2)}, u32[]{:S(2)}) %collective-permute-start.12) | collective-permute-done | bytes 786464 | tf_op jit(solution)/shard_map/ppermute | solution.py:340
  95.9 3.1 %shard_sum.26 = f32[2,8,12288]{2,1,0:T(8,128)} custom-call(s32[6]{0:T(128)} %pad_add_fusion.shard_ref, f32[8,2,8,12288]{3,2,1,0:T(8,128)} %get-tuple-element.22.keep_ref, f32[8,8,12288]{2,1,0:T(8,128)} %collective-permute-done.10.rest_0_, f32[8,8,12288]{2,1,0:T(8,128)} %collective-permute-done.11.rest_1_, f32[2,8,12288]{2,1,0:T(8,128)} %collective-permute-done.12.rest_2_), custom_call_target="tpu_custom_call" | custom-call | bytes 3145728 | tf_op jit(solution)/shard_map/shard_sum/pallas_call | solution.py:163
  99.0 3.1 %shard_sum.22 = f32[2,8,12288]{2,1,0:T(8,128)} custom-call(s32[6]{0:T(128)} %pad_add_fusion.1.shard_ref, f32[8,2,8,12288]{3,2,1,0:T(8,128)} %get-tuple-element.19.keep_ref, f32[8,8,12288]{2,1,0:T(8,128)} %collective-permute-done.rest_0_, f32[8,8,12288]{2,1,0:T(8,128)} %collective-permute-done.1.rest_1_, f32[2,8,12288]{2,1,0:T(8,128)} %collective-permute-done.7.rest_2_), custom_call_target="tpu_custom_call" | custom-call | bytes 3145728 | tf_op jit(solution)/shard_map/shard_sum/pallas_call | solution.py:163
  104.2 3.1 %shard_sum.30 = f32[2,8,12288]{2,1,0:T(8,128)} custom-call(s32[6]{0:T(128)} %pad_add_fusion.1.shard_ref, f32[8,2,8,12288]{3,2,1,0:T(8,128)} %get-tuple-element.22.keep_ref, f32[8,8,12288]{2,1,0:T(8,128)} %collective-permute-done.10.rest_0_, f32[8,8,12288]{2,1,0:T(8,128)} %collective-permute-done.11.rest_1_, f32[2,8,12288]{2,1,0:T(8,128)} %collective-permute-done.16.rest_2_), custom_call_target="tpu_custom_call" | custom-call | bytes 3145728 | tf_op jit(solution)/shard_map/shard_sum/pallas_call | solution.py:163
  107.9 3.1 %shard_sum.19 = f32[2,8,12288]{2,1,0:T(8,128)} custom-call(s32[6]{0:T(128)} %pad_add_fusion.shard_ref, f32[8,2,8,12288]{3,2,1,0:T(8,128)} %get-tuple-element.19.keep_ref, f32[8,8,12288]{2,1,0:T(8,128)} %collective-permute-done.rest_0_, f32[8,8,12288]{2,1,0:T(8,128)} %collective-permute-done.1.rest_1_, f32[2,8,12288]{2,1,0:T(8,128)} %collective-permute-done.4.rest_2_), custom_call_target="tpu_custom_call" | custom-call | bytes 3145728 | tf_op jit(solution)/shard_map/shard_sum/pallas_call | solution.py:163
  112.4 8.8 %collective-permute-done.13.rest_2_ = f32[2,8,12288]{2,1,0:T(8,128)} collective-permute-done((f32[2,8,12288]{2,1,0:T(8,128)}, f32[2,8,12288]{2,1,0:T(8,128)}, u32[]{:S(2)}, u32[]{:S(2)}) %collective-permute-start.13) | collective-permute-done | bytes 786464 | tf_op jit(solution)/shard_map/ppermute | solution.py:340
  121.2 3.1 %shard_sum.27 = f32[2,8,12288]{2,1,0:T(8,128)} custom-call(s32[6]{0:T(128)} %pad_add_fusion.shard_ref, f32[8,2,8,12288]{3,2,1,0:T(8,128)} %get-tuple-element.22.keep_ref, f32[8,8,12288]{2,1,0:T(8,128)} %collective-permute-done.10.rest_0_, f32[8,8,12288]{2,1,0:T(8,128)} %collective-permute-done.11.rest_1_, f32[2,8,12288]{2,1,0:T(8,128)} %collective-permute-done.13.rest_2_), custom_call_target="tpu_custom_call" | custom-call | bytes 3145728 | tf_op jit(solution)/shard_map/shard_sum/pallas_call | solution.py:163
  124.4 3.1 %shard_sum.23 = f32[2,8,12288]{2,1,0:T(8,128)} custom-call(s32[6]{0:T(128)} %pad_add_fusion.1.shard_ref, f32[8,2,8,12288]{3,2,1,0:T(8,128)} %get-tuple-element.19.keep_ref, f32[8,8,12288]{2,1,0:T(8,128)} %collective-permute-done.rest_0_, f32[8,8,12288]{2,1,0:T(8,128)} %collective-permute-done.1.rest_1_, f32[2,8,12288]{2,1,0:T(8,128)} %collective-permute-done.8.rest_2_), custom_call_target="tpu_custom_call" | custom-call | bytes 3145728 | tf_op jit(solution)/shard_map/shard_sum/pallas_call | solution.py:163
  129.5 9.8 %collective-permute-done.17.rest_2_ = f32[2,8,12288]{2,1,0:T(8,128)} collective-permute-done((f32[2,8,12288]{2,1,0:T(8,128)}, f32[2,8,12288]{2,1,0:T(8,128)}, u32[]{:S(2)}, u32[]{:S(2)}) %collective-permute-start.17) | collective-permute-done | bytes 786464 | tf_op jit(solution)/shard_map/ppermute | solution.py:340
  144.9 3.1 %shard_sum.20 = f32[2,8,12288]{2,1,0:T(8,128)} custom-call(s32[6]{0:T(128)} %pad_add_fusion.shard_ref, f32[8,2,8,12288]{3,2,1,0:T(8,128)} %get-tuple-element.19.keep_ref, f32[8,8,12288]{2,1,0:T(8,128)} %collective-permute-done.rest_0_, f32[8,8,12288]{2,1,0:T(8,128)} %collective-permute-done.1.rest_1_, f32[2,8,12288]{2,1,0:T(8,128)} %collective-permute-done.5.rest_2_), custom_call_target="tpu_custom_call" | custom-call | bytes 3145728 | tf_op jit(solution)/shard_map/shard_sum/pallas_call | solution.py:163
  156.2 16.9 %collective-permute-done.18.refs_5_ = f32[2,8,12288]{2,1,0:T(8,128)} collective-permute-done((f32[2,8,12288]{2,1,0:T(8,128)}, f32[2,8,12288]{2,1,0:T(8,128)}, u32[]{:S(2)}, u32[]{:S(2)}) %collective-permute-start.18) | collective-permute-done | bytes 786464 | tf_op jit(solution)/shard_map/ppermute | solution.py:340
  173.0 4.2 %last_sums.1 = (f32[2,8,12288]{2,1,0:T(8,128)}, f32[2,8,12288]{2,1,0:T(8,128)}, f32[8,128]{1,0:T(8,128)}) custom-call(f32[2,8,12288]{2,1,0:T(8,128)} %shard_sum.16.refs_0_, f32[2,8,12288]{2,1,0:T(8,128)} %collective-permute-done.6.refs_1_, f32[2,8,12288]{2,1,0:T(8,128)} %collective-permute-done.9.refs_2_, f32[2,8,12288]{2,1,0:T(8,128)} %shard_sum.24.refs_3_, ...), custom_call_target="tpu_custom_call" | custom-call | bytes 6291456 | tf_op jit(solution)/shard_map/last_sums/pallas_call | solution.py:143
  177.2 6.9 %collective-permute-start.19 = (f32[8,128]{1,0:T(8,128)}, f32[8,128]{1,0:T(8,128)S(1)}, u32[]{:S(2)}, u32[]{:S(2)}) collective-permute-start(f32[8,128]{1,0:T(8,128)} %get-tuple-element.25), channel_id=1, source_target_pairs={{0,2},{2,0},{4,6},{6,4},{8,10},{10,8},{12,14},{14,12},{16,18},{18,... | collective-permute-start | bytes 12296 | tf_op jit(solution)/shard_map/ppermute | solution.py:263
  191.4 3.6 %collective-permute-done.21 = f32[8,128]{1,0:T(8,128)S(1)} collective-permute-done((f32[8,128]{1,0:T(8,128)S(1)}, f32[8,128]{1,0:T(8,128)S(1)}, u32[]{:S(2)}, u32[]{:S(2)}) %collective-permute-start.21) | collective-permute-done | bytes 4128 | tf_op jit(solution)/shard_map/ppermute | solution.py:263
  197.7 3.7 %collective-permute-done.22 = f32[8,128]{1,0:T(8,128)S(1)} collective-permute-done((f32[8,128]{1,0:T(8,128)S(1)}, f32[8,128]{1,0:T(8,128)S(1)}, u32[]{:S(2)}, u32[]{:S(2)}) %collective-permute-start.22) | collective-permute-done | bytes 4128 | tf_op jit(solution)/shard_map/ppermute | solution.py:263
  209.3 9.0 %update.1 = (f32[2,8,24576]{2,1,0:T(8,128)}, f32[2,8,24576]{2,1,0:T(8,128)}, f32[2,8,24576]{2,1,0:T(8,128)}, f32[2,8,24576]{2,1,0:T(8,128)}, f32[2,8,24576]{2,1,0:T(8,128)}, /*index=5*/f32[2,8,24576]{2,1,0:T(8,128)}) custom-call(f32[3]{0:T(128)} %pad_maximum_fusion.scales_ref, f32[8,128]{1,0:T(8,128)} %copy-done, f32[8,128]{1,0:T(8,128)} %copy-done.1, ...), custom_call_target="tpu_custom_call" | custom-call | bytes 22020096 | tf_op jit(solution)/shard_map/update/pallas_call | solution.py:216
  (69 shorter events, 63.7 us)
Async XLA Ops:
  4.6 74.4 %collective-permute-start.3 = (f32[6,8,24576]{2,1,0:T(8,128)}, f32[6,8,24576]{2,1,0:T(8,128)}, u32[]{:S(2)}, u32[]{:S(2)}) collective-permute-start(f32[6,8,24576]{2,1,0:T(8,128)} %joined.1), channel_id=1, source_target_pairs={{0,2},{2,4},{4,6},{6,8},{8,10},{10,12},{12,14},{14,16},{16,18},{18... | collective-permute-start | bytes 14155784 | tf_op jit(solution)/shard_map/ppermute | solution.py:309
  15.8 12.8 %collective-permute-start.10 = (f32[8,8,12288]{2,1,0:T(8,128)}, f32[8,8,12288]{2,1,0:T(8,128)}, u32[]{:S(2)}, u32[]{:S(2)}) collective-permute-start(f32[8,8,12288]{2,1,0:T(8,128)} %get-tuple-element.23), channel_id=1, source_target_pairs={{0,2},{2,0},{4,6},{6,4},{8,10},{10,8},{12,14},{14,12},{16,18},{18,... | collective-permute-start | bytes 9437192 | tf_op jit(solution)/shard_map/ppermute | solution.py:321
  18.4 10.2 %collective-permute-start.11 = (f32[8,8,12288]{2,1,0:T(8,128)}, f32[8,8,12288]{2,1,0:T(8,128)}, u32[]{:S(2)}, u32[]{:S(2)}) collective-permute-start(f32[8,8,12288]{2,1,0:T(8,128)} %get-tuple-element.24), channel_id=1, source_target_pairs={{0,2},{2,0},{4,6},{6,4},{8,10},{10,8},{12,14},{14,12},{16,18},{18,... | collective-permute-start | bytes 9437192 | tf_op jit(solution)/shard_map/ppermute | solution.py:321
  27.4 6.1 %collective-permute-start = (f32[8,8,12288]{2,1,0:T(8,128)}, f32[8,8,12288]{2,1,0:T(8,128)}, u32[]{:S(2)}, u32[]{:S(2)}) collective-permute-start(f32[8,8,12288]{2,1,0:T(8,128)} %get-tuple-element.20), channel_id=1, source_target_pairs={{0,2},{2,0},{4,6},{6,4},{8,10},{10,8},{12,14},{14,12},{16,18},{18,... | collective-permute-start | bytes 9437192 | tf_op jit(solution)/shard_map/ppermute | solution.py:321
  27.9 10.1 %collective-permute-start.1 = (f32[8,8,12288]{2,1,0:T(8,128)}, f32[8,8,12288]{2,1,0:T(8,128)}, u32[]{:S(2)}, u32[]{:S(2)}) collective-permute-start(f32[8,8,12288]{2,1,0:T(8,128)} %get-tuple-element.21), channel_id=1, source_target_pairs={{0,2},{2,0},{4,6},{6,4},{8,10},{10,8},{12,14},{14,12},{16,18},{18,... | collective-permute-start | bytes 9437192 | tf_op jit(solution)/shard_map/ppermute | solution.py:321
  31.5 20.3 %collective-permute-start.15 = (f32[2,8,12288]{2,1,0:T(8,128)}, f32[2,8,12288]{2,1,0:T(8,128)}, u32[]{:S(2)}, u32[]{:S(2)}) collective-permute-start(f32[2,8,12288]{2,1,0:T(8,128)} %shard_sum.28), channel_id=1, source_target_pairs={{0,4},{2,6},{8,0},{10,2},{16,8},{18,10},{24,16},{26,18},{28,24},{3... | collective-permute-start | bytes 2359304 | tf_op jit(solution)/shard_map/ppermute | solution.py:327
  40.9 38.2 %collective-permute-start.2 = (f32[2,8,12288]{2,1,0:T(8,128)}, f32[2,8,12288]{2,1,0:T(8,128)}, u32[]{:S(2)}, u32[]{:S(2)}) collective-permute-start(f32[2,8,12288]{2,1,0:T(8,128)} %shard_sum.17), channel_id=1, source_target_pairs={{0,8},{2,10},{8,16},{10,18},{16,24},{18,26},{24,28},{26,30},{28,20... | collective-permute-start | bytes 2359304 | tf_op jit(solution)/shard_map/ppermute | solution.py:327
  46.0 49.9 %collective-permute-start.12 = (f32[2,8,12288]{2,1,0:T(8,128)}, f32[2,8,12288]{2,1,0:T(8,128)}, u32[]{:S(2)}, u32[]{:S(2)}) collective-permute-start(f32[2,8,12288]{2,1,0:T(8,128)} %shard_sum.25), channel_id=1, source_target_pairs={{0,8},{2,10},{8,16},{10,18},{16,24},{18,26},{24,28},{26,30},{28,20... | collective-permute-start | bytes 2359304 | tf_op jit(solution)/shard_map/ppermute | solution.py:340
  50.4 48.6 %collective-permute-start.7 = (f32[2,8,12288]{2,1,0:T(8,128)}, f32[2,8,12288]{2,1,0:T(8,128)}, u32[]{:S(2)}, u32[]{:S(2)}) collective-permute-start(f32[2,8,12288]{2,1,0:T(8,128)} %shard_sum.21), channel_id=1, source_target_pairs={{0,4},{2,6},{8,0},{10,2},{16,8},{18,10},{24,16},{26,18},{28,24},{3... | collective-permute-start | bytes 2359304 | tf_op jit(solution)/shard_map/ppermute | solution.py:340
  54.8 49.3 %collective-permute-start.16 = (f32[2,8,12288]{2,1,0:T(8,128)}, f32[2,8,12288]{2,1,0:T(8,128)}, u32[]{:S(2)}, u32[]{:S(2)}) collective-permute-start(f32[2,8,12288]{2,1,0:T(8,128)} %shard_sum.29), channel_id=1, source_target_pairs={{0,4},{2,6},{8,0},{10,2},{16,8},{18,10},{24,16},{26,18},{28,24},{3... | collective-permute-start | bytes 2359304 | tf_op jit(solution)/shard_map/ppermute | solution.py:340
  82.2 25.6 %collective-permute-start.4 = (f32[2,8,12288]{2,1,0:T(8,128)}, f32[2,8,12288]{2,1,0:T(8,128)}, u32[]{:S(2)}, u32[]{:S(2)}) collective-permute-start(f32[2,8,12288]{2,1,0:T(8,128)} %shard_sum.18), channel_id=1, source_target_pairs={{0,8},{2,10},{8,16},{10,18},{16,24},{18,26},{24,28},{26,30},{28,20... | collective-permute-start | bytes 2359304 | tf_op jit(solution)/shard_map/ppermute | solution.py:340
  99.0 22.2 %collective-permute-start.13 = (f32[2,8,12288]{2,1,0:T(8,128)}, f32[2,8,12288]{2,1,0:T(8,128)}, u32[]{:S(2)}, u32[]{:S(2)}) collective-permute-start(f32[2,8,12288]{2,1,0:T(8,128)} %shard_sum.26), channel_id=1, source_target_pairs={{0,8},{2,10},{8,16},{10,18},{16,24},{18,26},{24,28},{26,30},{28,20... | collective-permute-start | bytes 2359304 | tf_op jit(solution)/shard_map/ppermute | solution.py:340
  102.1 22.2 %collective-permute-start.8 = (f32[2,8,12288]{2,1,0:T(8,128)}, f32[2,8,12288]{2,1,0:T(8,128)}, u32[]{:S(2)}, u32[]{:S(2)}) collective-permute-start(f32[2,8,12288]{2,1,0:T(8,128)} %shard_sum.22), channel_id=1, source_target_pairs={{0,4},{2,6},{8,0},{10,2},{16,8},{18,10},{24,16},{26,18},{28,24},{3... | collective-permute-start | bytes 2359304 | tf_op jit(solution)/shard_map/ppermute | solution.py:340
  107.3 32.0 %collective-permute-start.17 = (f32[2,8,12288]{2,1,0:T(8,128)}, f32[2,8,12288]{2,1,0:T(8,128)}, u32[]{:S(2)}, u32[]{:S(2)}) collective-permute-start(f32[2,8,12288]{2,1,0:T(8,128)} %shard_sum.30), channel_id=1, source_target_pairs={{0,4},{2,6},{8,0},{10,2},{16,8},{18,10},{24,16},{26,18},{28,24},{3... | collective-permute-start | bytes 2359304 | tf_op jit(solution)/shard_map/ppermute | solution.py:340
  111.0 34.0 %collective-permute-start.5 = (f32[2,8,12288]{2,1,0:T(8,128)}, f32[2,8,12288]{2,1,0:T(8,128)}, u32[]{:S(2)}, u32[]{:S(2)}) collective-permute-start(f32[2,8,12288]{2,1,0:T(8,128)} %shard_sum.19), channel_id=1, source_target_pairs={{0,8},{2,10},{8,16},{10,18},{16,24},{18,26},{24,28},{26,30},{28,20... | collective-permute-start | bytes 2359304 | tf_op jit(solution)/shard_map/ppermute | solution.py:340
  124.4 30.6 %collective-permute-start.14 = (f32[2,8,12288]{2,1,0:T(8,128)}, f32[2,8,12288]{2,1,0:T(8,128)}, u32[]{:S(2)}, u32[]{:S(2)}) collective-permute-start(f32[2,8,12288]{2,1,0:T(8,128)} %shard_sum.27), channel_id=1, source_target_pairs={{0,8},{2,10},{8,16},{10,18},{16,24},{18,26},{24,28},{26,30},{28,20... | collective-permute-start | bytes 2359304 | tf_op jit(solution)/shard_map/ppermute | solution.py:340
  127.5 28.7 %collective-permute-start.9 = (f32[2,8,12288]{2,1,0:T(8,128)}, f32[2,8,12288]{2,1,0:T(8,128)}, u32[]{:S(2)}, u32[]{:S(2)}) collective-permute-start(f32[2,8,12288]{2,1,0:T(8,128)} %shard_sum.23), channel_id=1, source_target_pairs={{0,4},{2,6},{8,0},{10,2},{16,8},{18,10},{24,16},{26,18},{28,24},{3... | collective-permute-start | bytes 2359304 | tf_op jit(solution)/shard_map/ppermute | solution.py:340
  142.5 30.6 %collective-permute-start.18 = (f32[2,8,12288]{2,1,0:T(8,128)}, f32[2,8,12288]{2,1,0:T(8,128)}, u32[]{:S(2)}, u32[]{:S(2)}) collective-permute-start(f32[2,8,12288]{2,1,0:T(8,128)} %shard_sum.31), channel_id=1, source_target_pairs={{0,4},{2,6},{8,0},{10,2},{16,8},{18,10},{24,16},{26,18},{28,24},{3... | collective-permute-start | bytes 2359304 | tf_op jit(solution)/shard_map/ppermute | solution.py:340
  148.1 25.0 %collective-permute-start.6 = (f32[2,8,12288]{2,1,0:T(8,128)}, f32[2,8,12288]{2,1,0:T(8,128)}, u32[]{:S(2)}, u32[]{:S(2)}) collective-permute-start(f32[2,8,12288]{2,1,0:T(8,128)} %shard_sum.20), channel_id=1, source_target_pairs={{0,8},{2,10},{8,16},{10,18},{16,24},{18,26},{24,28},{26,30},{28,20... | collective-permute-start | bytes 2359304 | tf_op jit(solution)/shard_map/ppermute | solution.py:340
  177.2 8.0 %collective-permute-start.19 = (f32[8,128]{1,0:T(8,128)}, f32[8,128]{1,0:T(8,128)S(1)}, u32[]{:S(2)}, u32[]{:S(2)}) collective-permute-start(f32[8,128]{1,0:T(8,128)} %get-tuple-element.25), channel_id=1, source_target_pairs={{0,2},{2,0},{4,6},{6,4},{8,10},{10,8},{12,14},{14,12},{16,18},{18,... | collective-permute-start | bytes 12296 | tf_op jit(solution)/shard_map/ppermute | solution.py:263
  186.4 22.3 %collective-permute-start.26 = (f32[2,8,12288]{2,1,0:T(8,128)}, f32[2,8,12288]{2,1,0:T(8,128)}, u32[]{:S(2)}, u32[]{:S(2)}) collective-permute-start(f32[2,8,12288]{2,1,0:T(8,128)} %get-tuple-element.31.rest_7_), channel_id=1, source_target_pairs={{0,2},{2,4},{4,6},{6,8},{8,10},{10,12},{12,14},{14,16},{16,18},{18... | collective-permute-start | bytes 2359304 | tf_op jit(solution)/shard_map/ppermute | solution.py:344
  189.5 19.8 %collective-permute-start.25 = (f32[2,8,12288]{2,1,0:T(8,128)}, f32[2,8,12288]{2,1,0:T(8,128)}, u32[]{:S(2)}, u32[]{:S(2)}) collective-permute-start(f32[2,8,12288]{2,1,0:T(8,128)} %get-tuple-element.30.rest_6_), channel_id=1, source_target_pairs={{0,2},{2,4},{4,6},{6,8},{8,10},{10,12},{12,14},{14,16},{16,18},{18... | collective-permute-start | bytes 2359304 | tf_op jit(solution)/shard_map/ppermute | solution.py:344
  189.5 5.5 %collective-permute-start.21 = (f32[8,128]{1,0:T(8,128)S(1)}, f32[8,128]{1,0:T(8,128)S(1)}, u32[]{:S(2)}, u32[]{:S(2)}) collective-permute-start(f32[8,128]{1,0:T(8,128)S(1)} %add.53), channel_id=1, source_target_pairs={{0,8},{2,10},{8,0},{10,2},{16,24},{18,26},{24,16},{26,18},{1,9},{3... | collective-permute-start | bytes 12296 | tf_op jit(solution)/shard_map/ppermute | solution.py:263
  195.0 6.4 %collective-permute-start.22 = (f32[8,128]{1,0:T(8,128)S(1)}, f32[8,128]{1,0:T(8,128)S(1)}, u32[]{:S(2)}, u32[]{:S(2)}) collective-permute-start(f32[8,128]{1,0:T(8,128)S(1)} %add.54), channel_id=1, source_target_pairs={{0,16},{2,18},{8,24},{10,26},{16,0},{18,2},{24,8},{26,10},{1,17},{... | collective-permute-start | bytes 12296 | tf_op jit(solution)/shard_map/ppermute | solution.py:263
  (5 other events, 11.0 us)

commit v14 on v13

--- a/solution.py
+++ b/solution.py
@@ -340,8 +340,8 @@
                 sent[k][way] = lax.ppermute(total, "dp", hop(by))
     ours = [shard_sum(plain_kernel, tables[0], 0, keep[k], theirs[k]) for k in range(streams)]
     grads, squares = last_sums(ours, sent)
-    squares, *waiting = total_of(squares, grads[1:], grads[:1])
-    peer_grads = [lax.ppermute(value, "dp", onward) for value in waiting[1] + waiting[0]]
+    squares, *waiting = total_of(squares, [], grads)
+    peer_grads = [lax.ppermute(value, "dp", onward) for value in waiting[0] + waiting[1]]
     bound = float((layers * rows * columns * lax.axis_size("mp")) ** 0.5)
     count = step.astype(jnp.float32)
     scales = jnp.concatenate(

time: 219 us -> 222 us (1.014)
    ppermute x2, waiting for transfers between devices: 0.53 us -> 2.86 us  [local(): lax.ppermute(value, 'dp', onward)]
where the time goes in v14:
time: 222 us; the launch traced here: 221 us
  waiting for transfers between devices  86.5 us (39%)
  Pallas kernels  83.5 us (38%)
  starting transfers between devices  44.2 us (20%)
  other arithmetic  3.67 us (2%)
    pallas_call x16, Pallas kernels, shard_sum(): pl.pallas_call(functools.partial(body, layers), grid_spec=pltpu.PrefetchS...  48.5 us
    ppermute x12, waiting for transfers between devices, local(): sent[k][way] = lax.ppermute(total, 'dp', hop(by))  43.7 us
    ppermute x2, waiting for transfers between devices, local(): sent[k][k % 2] = lax.ppermute(total, 'dp', hop(-1 if k % 2 else 1))  23 us
    ppermute x12, starting transfers between devices, local(): sent[k][way] = lax.ppermute(total, 'dp', hop(by))  20.5 us
    pallas_call x2, Pallas kernels, make_terms(): pl.pallas_call(functools.partial(terms_kernel, order, layers), grid_spec=...  17.9 us
    ppermute x5, starting transfers between devices, exchanged(): return value + lax.ppermute(value, axis, [(i, i ^ bit) for i in members])  15.1 us
    ppermute x5, waiting for transfers between devices, exchanged(): return value + lax.ppermute(value, axis, [(i, i ^ bit) for i in members])  11.2 us
    pallas_call x1, Pallas kernels, update(): pl.pallas_call(functools.partial(update_kernel, count, bound), grid=(bloc...  9 us
  transfers between devices with their start and end apart: 27, of which 17 were waited for; matrix products, arithmetic and copies ran while one was open for 2% of the time, Pallas kernels for 30%

profile of v14, /device:TPU:0, one launch (start us, length us, event | category | flops | bytes accessed | tf_op | source)
XLA Modules:
  0.0 221.3 jit_solution(14285309188399103967)
XLA Ops:
  0.6 4.0 %joined.1 = f32[6,8,24576]{2,1,0:T(8,128)} custom-call(f32[2,8,24576]{2,1,0:T(8,128)} %rest_0_.1, f32[2,8,24576]{2,1,0:T(8,128)} %rest_1_.1, f32[2,8,24576]{2,1,0:T(8,128)} %rest_2_.1), custom_call_target="tpu_custom_call" | custom-call | bytes 9437184 | tf_op jit(solution)/shard_map/joined/pallas_call | solution.py:244
  6.9 8.9 %terms.3 = (f32[8,2,8,12288]{3,2,1,0:T(8,128)}, f32[8,8,12288]{2,1,0:T(8,128)}, f32[8,8,12288]{2,1,0:T(8,128)}) custom-call(s32[1]{0:T(128)} %bitcast.1.core_ref, bf16[256,256]{1,0:T(8,128)(2,1)} %copy.14.inputs_ref, bf16[1,2,128,24576]{3,2,1,0:T(8,128)(2,1)} %earlier_ref.3, bf16[128,2,24576]{2,1,0:T(2,128)(2,1)} %outgrad_ref.3), custom_call_target="tpu_custom_call" | custom-call | bytes 25165824 | tf_op jit(solution)/shard_map/terms/pallas_call | solution.py:71
  18.4 9.0 %terms.2 = (f32[8,2,8,12288]{3,2,1,0:T(8,128)}, f32[8,8,12288]{2,1,0:T(8,128)}, f32[8,8,12288]{2,1,0:T(8,128)}) custom-call(s32[1]{0:T(128)} %bitcast.1.core_ref, bf16[256,256]{1,0:T(8,128)(2,1)} %copy.14.inputs_ref, bf16[1,2,128,24576]{3,2,1,0:T(8,128)(2,1)} %earlier_ref.3, bf16[128,2,24576]{2,1,0:T(2,128)(2,1)} %outgrad_ref.3), custom_call_target="tpu_custom_call" | custom-call | bytes 25165824 | tf_op jit(solution)/shard_map/terms/pallas_call | solution.py:71
  33.5 4.5 %collective-permute-done.1.rest_1_ = f32[8,8,12288]{2,1,0:T(8,128)} collective-permute-done((f32[8,8,12288]{2,1,0:T(8,128)}, f32[8,8,12288]{2,1,0:T(8,128)}, u32[]{:S(2)}, u32[]{:S(2)}) %collective-permute-start.1) | collective-permute-done | bytes 3145760 | tf_op jit(solution)/shard_map/ppermute | solution.py:321
  51.7 3.1 %shard_sum.29 = f32[2,8,12288]{2,1,0:T(8,128)} custom-call(s32[6]{0:T(128)} %pad_add_fusion.1.shard_ref, f32[8,2,8,12288]{3,2,1,0:T(8,128)} %get-tuple-element.21.keep_ref, f32[8,8,12288]{2,1,0:T(8,128)} %collective-permute-done.10.rest_0_, f32[8,8,12288]{2,1,0:T(8,128)} %collective-permute-done.11.rest_1_, f32[2,8,12288]{2,1,0:T(8,128)} %collective-permute-done.15.rest_2_), custom_call_target="tpu_custom_call" | custom-call | bytes 3145728 | tf_op jit(solution)/shard_map/shard_sum/pallas_call | solution.py:163
  56.9 22.1 %collective-permute-done.2.rest_2_ = f32[2,8,12288]{2,1,0:T(8,128)} collective-permute-done((f32[2,8,12288]{2,1,0:T(8,128)}, f32[2,8,12288]{2,1,0:T(8,128)}, u32[]{:S(2)}, u32[]{:S(2)}) %collective-permute-start.2) | collective-permute-done | bytes 786464 | tf_op jit(solution)/shard_map/ppermute | solution.py:327
  79.1 3.1 %shard_sum.18 = f32[2,8,12288]{2,1,0:T(8,128)} custom-call(s32[6]{0:T(128)} %pad_add_fusion.shard_ref, f32[8,2,8,12288]{3,2,1,0:T(8,128)} %get-tuple-element.18.keep_ref, f32[8,8,12288]{2,1,0:T(8,128)} %collective-permute-done.rest_0_, f32[8,8,12288]{2,1,0:T(8,128)} %collective-permute-done.1.rest_1_, f32[2,8,12288]{2,1,0:T(8,128)} %collective-permute-done.2.rest_2_, ...), custom_call_target="tpu_custom_call" | custom-call | bytes 3145728 | tf_op jit(solution)/shard_map/shard_sum/pallas_call | solution.py:163
  82.2 7.8 %collective-permute-start.4 = (f32[2,8,12288]{2,1,0:T(8,128)}, f32[2,8,12288]{2,1,0:T(8,128)}, u32[]{:S(2)}, u32[]{:S(2)}) collective-permute-start(f32[2,8,12288]{2,1,0:T(8,128)} %shard_sum.18), channel_id=1, source_target_pairs={{0,8},{2,10},{8,16},{10,18},{16,24},{18,26},{24,28},{26,30},{28,20... | collective-permute-start | bytes 2359304 | tf_op jit(solution)/shard_map/ppermute | solution.py:340
  90.0 5.9 %collective-permute-done.12.rest_2_ = f32[2,8,12288]{2,1,0:T(8,128)} collective-permute-done((f32[2,8,12288]{2,1,0:T(8,128)}, f32[2,8,12288]{2,1,0:T(8,128)}, u32[]{:S(2)}, u32[]{:S(2)}) %collective-permute-start.12) | collective-permute-done | bytes 786464 | tf_op jit(solution)/shard_map/ppermute | solution.py:340
  95.9 3.1 %shard_sum.26 = f32[2,8,12288]{2,1,0:T(8,128)} custom-call(s32[6]{0:T(128)} %pad_add_fusion.shard_ref, f32[8,2,8,12288]{3,2,1,0:T(8,128)} %get-tuple-element.21.keep_ref, f32[8,8,12288]{2,1,0:T(8,128)} %collective-permute-done.10.rest_0_, f32[8,8,12288]{2,1,0:T(8,128)} %collective-permute-done.11.rest_1_, f32[2,8,12288]{2,1,0:T(8,128)} %collective-permute-done.12.rest_2_), custom_call_target="tpu_custom_call" | custom-call | bytes 3145728 | tf_op jit(solution)/shard_map/shard_sum/pallas_call | solution.py:163
  99.0 3.1 %shard_sum.22 = f32[2,8,12288]{2,1,0:T(8,128)} custom-call(s32[6]{0:T(128)} %pad_add_fusion.1.shard_ref, f32[8,2,8,12288]{3,2,1,0:T(8,128)} %get-tuple-element.18.keep_ref, f32[8,8,12288]{2,1,0:T(8,128)} %collective-permute-done.rest_0_, f32[8,8,12288]{2,1,0:T(8,128)} %collective-permute-done.1.rest_1_, f32[2,8,12288]{2,1,0:T(8,128)} %collective-permute-done.7.rest_2_), custom_call_target="tpu_custom_call" | custom-call | bytes 3145728 | tf_op jit(solution)/shard_map/shard_sum/pallas_call | solution.py:163
  104.2 3.1 %shard_sum.30 = f32[2,8,12288]{2,1,0:T(8,128)} custom-call(s32[6]{0:T(128)} %pad_add_fusion.1.shard_ref, f32[8,2,8,12288]{3,2,1,0:T(8,128)} %get-tuple-element.21.keep_ref, f32[8,8,12288]{2,1,0:T(8,128)} %collective-permute-done.10.rest_0_, f32[8,8,12288]{2,1,0:T(8,128)} %collective-permute-done.11.rest_1_, f32[2,8,12288]{2,1,0:T(8,128)} %collective-permute-done.16.rest_2_), custom_call_target="tpu_custom_call" | custom-call | bytes 3145728 | tf_op jit(solution)/shard_map/shard_sum/pallas_call | solution.py:163
  107.9 3.1 %shard_sum.19 = f32[2,8,12288]{2,1,0:T(8,128)} custom-call(s32[6]{0:T(128)} %pad_add_fusion.shard_ref, f32[8,2,8,12288]{3,2,1,0:T(8,128)} %get-tuple-element.18.keep_ref, f32[8,8,12288]{2,1,0:T(8,128)} %collective-permute-done.rest_0_, f32[8,8,12288]{2,1,0:T(8,128)} %collective-permute-done.1.rest_1_, f32[2,8,12288]{2,1,0:T(8,128)} %collective-permute-done.4.rest_2_), custom_call_target="tpu_custom_call" | custom-call | bytes 3145728 | tf_op jit(solution)/shard_map/shard_sum/pallas_call | solution.py:163
  112.4 8.8 %collective-permute-done.13.rest_2_ = f32[2,8,12288]{2,1,0:T(8,128)} collective-permute-done((f32[2,8,12288]{2,1,0:T(8,128)}, f32[2,8,12288]{2,1,0:T(8,128)}, u32[]{:S(2)}, u32[]{:S(2)}) %collective-permute-start.13) | collective-permute-done | bytes 786464 | tf_op jit(solution)/shard_map/ppermute | solution.py:340
  121.2 3.1 %shard_sum.27 = f32[2,8,12288]{2,1,0:T(8,128)} custom-call(s32[6]{0:T(128)} %pad_add_fusion.shard_ref, f32[8,2,8,12288]{3,2,1,0:T(8,128)} %get-tuple-element.21.keep_ref, f32[8,8,12288]{2,1,0:T(8,128)} %collective-permute-done.10.rest_0_, f32[8,8,12288]{2,1,0:T(8,128)} %collective-permute-done.11.rest_1_, f32[2,8,12288]{2,1,0:T(8,128)} %collective-permute-done.13.rest_2_), custom_call_target="tpu_custom_call" | custom-call | bytes 3145728 | tf_op jit(solution)/shard_map/shard_sum/pallas_call | solution.py:163
  124.4 3.1 %shard_sum.23 = f32[2,8,12288]{2,1,0:T(8,128)} custom-call(s32[6]{0:T(128)} %pad_add_fusion.1.shard_ref, f32[8,2,8,12288]{3,2,1,0:T(8,128)} %get-tuple-element.18.keep_ref, f32[8,8,12288]{2,1,0:T(8,128)} %collective-permute-done.rest_0_, f32[8,8,12288]{2,1,0:T(8,128)} %collective-permute-done.1.rest_1_, f32[2,8,12288]{2,1,0:T(8,128)} %collective-permute-done.8.rest_2_), custom_call_target="tpu_custom_call" | custom-call | bytes 3145728 | tf_op jit(solution)/shard_map/shard_sum/pallas_call | solution.py:163
  129.5 9.8 %collective-permute-done.17.rest_2_ = f32[2,8,12288]{2,1,0:T(8,128)} collective-permute-done((f32[2,8,12288]{2,1,0:T(8,128)}, f32[2,8,12288]{2,1,0:T(8,128)}, u32[]{:S(2)}, u32[]{:S(2)}) %collective-permute-start.17) | collective-permute-done | bytes 786464 | tf_op jit(solution)/shard_map/ppermute | solution.py:340
  144.9 3.1 %shard_sum.20 = f32[2,8,12288]{2,1,0:T(8,128)} custom-call(s32[6]{0:T(128)} %pad_add_fusion.shard_ref, f32[8,2,8,12288]{3,2,1,0:T(8,128)} %get-tuple-element.18.keep_ref, f32[8,8,12288]{2,1,0:T(8,128)} %collective-permute-done.rest_0_, f32[8,8,12288]{2,1,0:T(8,128)} %collective-permute-done.1.rest_1_, f32[2,8,12288]{2,1,0:T(8,128)} %collective-permute-done.5.rest_2_), custom_call_target="tpu_custom_call" | custom-call | bytes 3145728 | tf_op jit(solution)/shard_map/shard_sum/pallas_call | solution.py:163
  156.2 16.9 %collective-permute-done.18.refs_5_ = f32[2,8,12288]{2,1,0:T(8,128)} collective-permute-done((f32[2,8,12288]{2,1,0:T(8,128)}, f32[2,8,12288]{2,1,0:T(8,128)}, u32[]{:S(2)}, u32[]{:S(2)}) %collective-permute-start.18) | collective-permute-done | bytes 786464 | tf_op jit(solution)/shard_map/ppermute | solution.py:340
  173.0 4.2 %last_sums.1 = (f32[2,8,12288]{2,1,0:T(8,128)}, f32[2,8,12288]{2,1,0:T(8,128)}, f32[8,128]{1,0:T(8,128)}) custom-call(f32[2,8,12288]{2,1,0:T(8,128)} %shard_sum.16.refs_0_, f32[2,8,12288]{2,1,0:T(8,128)} %collective-permute-done.6.refs_1_, f32[2,8,12288]{2,1,0:T(8,128)} %collective-permute-done.9.refs_2_, f32[2,8,12288]{2,1,0:T(8,128)} %shard_sum.24.refs_3_, ...), custom_call_target="tpu_custom_call" | custom-call | bytes 6291456 | tf_op jit(solution)/shard_map/last_sums/pallas_call | solution.py:143
  177.2 6.9 %collective-permute-start.19 = (f32[8,128]{1,0:T(8,128)}, f32[8,128]{1,0:T(8,128)S(1)}, u32[]{:S(2)}, u32[]{:S(2)}) collective-permute-start(f32[8,128]{1,0:T(8,128)} %get-tuple-element.24), channel_id=1, source_target_pairs={{0,2},{2,0},{4,6},{6,4},{8,10},{10,8},{12,14},{14,12},{16,18},{18,... | collective-permute-start | bytes 12296 | tf_op jit(solution)/shard_map/ppermute | solution.py:263
  195.6 3.2 %collective-permute-start.22 = (f32[8,128]{1,0:T(8,128)S(1)}, f32[8,128]{1,0:T(8,128)S(1)}, u32[]{:S(2)}, u32[]{:S(2)}) collective-permute-start(f32[8,128]{1,0:T(8,128)S(1)} %add.54), channel_id=1, source_target_pairs={{0,16},{2,18},{8,24},{10,26},{16,0},{18,2},{24,8},{26,10},{1,17},{... | collective-permute-start | bytes 12296 | tf_op jit(solution)/shard_map/ppermute | solution.py:263
  198.8 3.3 %collective-permute-done.22 = f32[8,128]{1,0:T(8,128)S(1)} collective-permute-done((f32[8,128]{1,0:T(8,128)S(1)}, f32[8,128]{1,0:T(8,128)S(1)}, u32[]{:S(2)}, u32[]{:S(2)}) %collective-permute-start.22) | collective-permute-done | bytes 4128 | tf_op jit(solution)/shard_map/ppermute | solution.py:263
  212.3 9.0 %update.1 = (f32[2,8,24576]{2,1,0:T(8,128)}, f32[2,8,24576]{2,1,0:T(8,128)}, f32[2,8,24576]{2,1,0:T(8,128)}, f32[2,8,24576]{2,1,0:T(8,128)}, f32[2,8,24576]{2,1,0:T(8,128)}, /*index=5*/f32[2,8,24576]{2,1,0:T(8,128)}) custom-call(f32[3]{0:T(128)} %pad_maximum_fusion.scales_ref, f32[8,128]{1,0:T(8,128)} %copy-done, f32[8,128]{1,0:T(8,128)} %copy-done.1, ...), custom_call_target="tpu_custom_call" | custom-call | bytes 22020096 | tf_op jit(solution)/shard_map/update/pallas_call | solution.py:216
  (69 shorter events, 67.6 us)
Async XLA Ops:
  4.6 74.4 %collective-permute-start.3 = (f32[6,8,24576]{2,1,0:T(8,128)}, f32[6,8,24576]{2,1,0:T(8,128)}, u32[]{:S(2)}, u32[]{:S(2)}) collective-permute-start(f32[6,8,24576]{2,1,0:T(8,128)} %joined.1), channel_id=1, source_target_pairs={{0,2},{2,4},{4,6},{6,8},{8,10},{10,12},{12,14},{14,16},{16,18},{18... | collective-permute-start | bytes 14155784 | tf_op jit(solution)/shard_map/ppermute | solution.py:309
  15.8 12.8 %collective-permute-start.10 = (f32[8,8,12288]{2,1,0:T(8,128)}, f32[8,8,12288]{2,1,0:T(8,128)}, u32[]{:S(2)}, u32[]{:S(2)}) collective-permute-start(f32[8,8,12288]{2,1,0:T(8,128)} %get-tuple-element.22), channel_id=1, source_target_pairs={{0,2},{2,0},{4,6},{6,4},{8,10},{10,8},{12,14},{14,12},{16,18},{18,... | collective-permute-start | bytes 9437192 | tf_op jit(solution)/shard_map/ppermute | solution.py:321
  18.4 10.2 %collective-permute-start.11 = (f32[8,8,12288]{2,1,0:T(8,128)}, f32[8,8,12288]{2,1,0:T(8,128)}, u32[]{:S(2)}, u32[]{:S(2)}) collective-permute-start(f32[8,8,12288]{2,1,0:T(8,128)} %get-tuple-element.23), channel_id=1, source_target_pairs={{0,2},{2,0},{4,6},{6,4},{8,10},{10,8},{12,14},{14,12},{16,18},{18,... | collective-permute-start | bytes 9437192 | tf_op jit(solution)/shard_map/ppermute | solution.py:321
  27.4 6.1 %collective-permute-start = (f32[8,8,12288]{2,1,0:T(8,128)}, f32[8,8,12288]{2,1,0:T(8,128)}, u32[]{:S(2)}, u32[]{:S(2)}) collective-permute-start(f32[8,8,12288]{2,1,0:T(8,128)} %get-tuple-element.19), channel_id=1, source_target_pairs={{0,2},{2,0},{4,6},{6,4},{8,10},{10,8},{12,14},{14,12},{16,18},{18,... | collective-permute-start | bytes 9437192 | tf_op jit(solution)/shard_map/ppermute | solution.py:321
  27.9 10.1 %collective-permute-start.1 = (f32[8,8,12288]{2,1,0:T(8,128)}, f32[8,8,12288]{2,1,0:T(8,128)}, u32[]{:S(2)}, u32[]{:S(2)}) collective-permute-start(f32[8,8,12288]{2,1,0:T(8,128)} %get-tuple-element.20), channel_id=1, source_target_pairs={{0,2},{2,0},{4,6},{6,4},{8,10},{10,8},{12,14},{14,12},{16,18},{18,... | collective-permute-start | bytes 9437192 | tf_op jit(solution)/shard_map/ppermute | solution.py:321
  31.5 20.3 %collective-permute-start.15 = (f32[2,8,12288]{2,1,0:T(8,128)}, f32[2,8,12288]{2,1,0:T(8,128)}, u32[]{:S(2)}, u32[]{:S(2)}) collective-permute-start(f32[2,8,12288]{2,1,0:T(8,128)} %shard_sum.28), channel_id=1, source_target_pairs={{0,4},{2,6},{8,0},{10,2},{16,8},{18,10},{24,16},{26,18},{28,24},{3... | collective-permute-start | bytes 2359304 | tf_op jit(solution)/shard_map/ppermute | solution.py:327
  40.9 38.2 %collective-permute-start.2 = (f32[2,8,12288]{2,1,0:T(8,128)}, f32[2,8,12288]{2,1,0:T(8,128)}, u32[]{:S(2)}, u32[]{:S(2)}) collective-permute-start(f32[2,8,12288]{2,1,0:T(8,128)} %shard_sum.17), channel_id=1, source_target_pairs={{0,8},{2,10},{8,16},{10,18},{16,24},{18,26},{24,28},{26,30},{28,20... | collective-permute-start | bytes 2359304 | tf_op jit(solution)/shard_map/ppermute | solution.py:327
  46.0 49.9 %collective-permute-start.12 = (f32[2,8,12288]{2,1,0:T(8,128)}, f32[2,8,12288]{2,1,0:T(8,128)}, u32[]{:S(2)}, u32[]{:S(2)}) collective-permute-start(f32[2,8,12288]{2,1,0:T(8,128)} %shard_sum.25), channel_id=1, source_target_pairs={{0,8},{2,10},{8,16},{10,18},{16,24},{18,26},{24,28},{26,30},{28,20... | collective-permute-start | bytes 2359304 | tf_op jit(solution)/shard_map/ppermute | solution.py:340
  50.4 48.6 %collective-permute-start.7 = (f32[2,8,12288]{2,1,0:T(8,128)}, f32[2,8,12288]{2,1,0:T(8,128)}, u32[]{:S(2)}, u32[]{:S(2)}) collective-permute-start(f32[2,8,12288]{2,1,0:T(8,128)} %shard_sum.21), channel_id=1, source_target_pairs={{0,4},{2,6},{8,0},{10,2},{16,8},{18,10},{24,16},{26,18},{28,24},{3... | collective-permute-start | bytes 2359304 | tf_op jit(solution)/shard_map/ppermute | solution.py:340
  54.8 49.3 %collective-permute-start.16 = (f32[2,8,12288]{2,1,0:T(8,128)}, f32[2,8,12288]{2,1,0:T(8,128)}, u32[]{:S(2)}, u32[]{:S(2)}) collective-permute-start(f32[2,8,12288]{2,1,0:T(8,128)} %shard_sum.29), channel_id=1, source_target_pairs={{0,4},{2,6},{8,0},{10,2},{16,8},{18,10},{24,16},{26,18},{28,24},{3... | collective-permute-start | bytes 2359304 | tf_op jit(solution)/shard_map/ppermute | solution.py:340
  82.2 25.6 %collective-permute-start.4 = (f32[2,8,12288]{2,1,0:T(8,128)}, f32[2,8,12288]{2,1,0:T(8,128)}, u32[]{:S(2)}, u32[]{:S(2)}) collective-permute-start(f32[2,8,12288]{2,1,0:T(8,128)} %shard_sum.18), channel_id=1, source_target_pairs={{0,8},{2,10},{8,16},{10,18},{16,24},{18,26},{24,28},{26,30},{28,20... | collective-permute-start | bytes 2359304 | tf_op jit(solution)/shard_map/ppermute | solution.py:340
  99.0 22.2 %collective-permute-start.13 = (f32[2,8,12288]{2,1,0:T(8,128)}, f32[2,8,12288]{2,1,0:T(8,128)}, u32[]{:S(2)}, u32[]{:S(2)}) collective-permute-start(f32[2,8,12288]{2,1,0:T(8,128)} %shard_sum.26), channel_id=1, source_target_pairs={{0,8},{2,10},{8,16},{10,18},{16,24},{18,26},{24,28},{26,30},{28,20... | collective-permute-start | bytes 2359304 | tf_op jit(solution)/shard_map/ppermute | solution.py:340
  102.1 22.2 %collective-permute-start.8 = (f32[2,8,12288]{2,1,0:T(8,128)}, f32[2,8,12288]{2,1,0:T(8,128)}, u32[]{:S(2)}, u32[]{:S(2)}) collective-permute-start(f32[2,8,12288]{2,1,0:T(8,128)} %shard_sum.22), channel_id=1, source_target_pairs={{0,4},{2,6},{8,0},{10,2},{16,8},{18,10},{24,16},{26,18},{28,24},{3... | collective-permute-start | bytes 2359304 | tf_op jit(solution)/shard_map/ppermute | solution.py:340
  107.3 32.0 %collective-permute-start.17 = (f32[2,8,12288]{2,1,0:T(8,128)}, f32[2,8,12288]{2,1,0:T(8,128)}, u32[]{:S(2)}, u32[]{:S(2)}) collective-permute-start(f32[2,8,12288]{2,1,0:T(8,128)} %shard_sum.30), channel_id=1, source_target_pairs={{0,4},{2,6},{8,0},{10,2},{16,8},{18,10},{24,16},{26,18},{28,24},{3... | collective-permute-start | bytes 2359304 | tf_op jit(solution)/shard_map/ppermute | solution.py:340
  111.0 34.0 %collective-permute-start.5 = (f32[2,8,12288]{2,1,0:T(8,128)}, f32[2,8,12288]{2,1,0:T(8,128)}, u32[]{:S(2)}, u32[]{:S(2)}) collective-permute-start(f32[2,8,12288]{2,1,0:T(8,128)} %shard_sum.19), channel_id=1, source_target_pairs={{0,8},{2,10},{8,16},{10,18},{16,24},{18,26},{24,28},{26,30},{28,20... | collective-permute-start | bytes 2359304 | tf_op jit(solution)/shard_map/ppermute | solution.py:340
  124.4 30.6 %collective-permute-start.14 = (f32[2,8,12288]{2,1,0:T(8,128)}, f32[2,8,12288]{2,1,0:T(8,128)}, u32[]{:S(2)}, u32[]{:S(2)}) collective-permute-start(f32[2,8,12288]{2,1,0:T(8,128)} %shard_sum.27), channel_id=1, source_target_pairs={{0,8},{2,10},{8,16},{10,18},{16,24},{18,26},{24,28},{26,30},{28,20... | collective-permute-start | bytes 2359304 | tf_op jit(solution)/shard_map/ppermute | solution.py:340
  127.5 28.7 %collective-permute-start.9 = (f32[2,8,12288]{2,1,0:T(8,128)}, f32[2,8,12288]{2,1,0:T(8,128)}, u32[]{:S(2)}, u32[]{:S(2)}) collective-permute-start(f32[2,8,12288]{2,1,0:T(8,128)} %shard_sum.23), channel_id=1, source_target_pairs={{0,4},{2,6},{8,0},{10,2},{16,8},{18,10},{24,16},{26,18},{28,24},{3... | collective-permute-start | bytes 2359304 | tf_op jit(solution)/shard_map/ppermute | solution.py:340
  142.5 30.6 %collective-permute-start.18 = (f32[2,8,12288]{2,1,0:T(8,128)}, f32[2,8,12288]{2,1,0:T(8,128)}, u32[]{:S(2)}, u32[]{:S(2)}) collective-permute-start(f32[2,8,12288]{2,1,0:T(8,128)} %shard_sum.31), channel_id=1, source_target_pairs={{0,4},{2,6},{8,0},{10,2},{16,8},{18,10},{24,16},{26,18},{28,24},{3... | collective-permute-start | bytes 2359304 | tf_op jit(solution)/shard_map/ppermute | solution.py:340
  148.1 25.0 %collective-permute-start.6 = (f32[2,8,12288]{2,1,0:T(8,128)}, f32[2,8,12288]{2,1,0:T(8,128)}, u32[]{:S(2)}, u32[]{:S(2)}) collective-permute-start(f32[2,8,12288]{2,1,0:T(8,128)} %shard_sum.20), channel_id=1, source_target_pairs={{0,8},{2,10},{8,16},{10,18},{16,24},{18,26},{24,28},{26,30},{28,20... | collective-permute-start | bytes 2359304 | tf_op jit(solution)/shard_map/ppermute | solution.py:340
  177.2 8.0 %collective-permute-start.19 = (f32[8,128]{1,0:T(8,128)}, f32[8,128]{1,0:T(8,128)S(1)}, u32[]{:S(2)}, u32[]{:S(2)}) collective-permute-start(f32[8,128]{1,0:T(8,128)} %get-tuple-element.24), channel_id=1, source_target_pairs={{0,2},{2,0},{4,6},{6,4},{8,10},{10,8},{12,14},{14,12},{16,18},{18,... | collective-permute-start | bytes 12296 | tf_op jit(solution)/shard_map/ppermute | solution.py:263
  189.5 20.0 %collective-permute-start.25 = (f32[2,8,12288]{2,1,0:T(8,128)}, f32[2,8,12288]{2,1,0:T(8,128)}, u32[]{:S(2)}, u32[]{:S(2)}) collective-permute-start(f32[2,8,12288]{2,1,0:T(8,128)} %get-tuple-element.28.rest_6_), channel_id=1, source_target_pairs={{0,2},{2,4},{4,6},{6,8},{8,10},{10,12},{12,14},{14,16},{16,18},{18... | collective-permute-start | bytes 2359304 | tf_op jit(solution)/shard_map/ppermute | solution.py:344
  189.5 22.9 %collective-permute-start.26 = (f32[2,8,12288]{2,1,0:T(8,128)}, f32[2,8,12288]{2,1,0:T(8,128)}, u32[]{:S(2)}, u32[]{:S(2)}) collective-permute-start(f32[2,8,12288]{2,1,0:T(8,128)} %get-tuple-element.29.rest_7_), channel_id=1, source_target_pairs={{0,2},{2,4},{4,6},{6,8},{8,10},{10,12},{12,14},{14,16},{16,18},{18... | collective-permute-start | bytes 2359304 | tf_op jit(solution)/shard_map/ppermute | solution.py:344
  190.2 5.5 %collective-permute-start.21 = (f32[8,128]{1,0:T(8,128)S(1)}, f32[8,128]{1,0:T(8,128)S(1)}, u32[]{:S(2)}, u32[]{:S(2)}) collective-permute-start(f32[8,128]{1,0:T(8,128)S(1)} %add.53), channel_id=1, source_target_pairs={{0,8},{2,10},{8,0},{10,2},{16,24},{18,26},{24,16},{26,18},{1,9},{3... | collective-permute-start | bytes 12296 | tf_op jit(solution)/shard_map/ppermute | solution.py:263
  195.6 6.4 %collective-permute-start.22 = (f32[8,128]{1,0:T(8,128)S(1)}, f32[8,128]{1,0:T(8,128)S(1)}, u32[]{:S(2)}, u32[]{:S(2)}) collective-permute-start(f32[8,128]{1,0:T(8,128)S(1)} %add.54), channel_id=1, source_target_pairs={{0,16},{2,18},{8,24},{10,26},{16,0},{18,2},{24,8},{26,10},{1,17},{... | collective-permute-start | bytes 12296 | tf_op jit(solution)/shard_map/ppermute | solution.py:263
  (5 other events, 11.0 us)
